TPU v7x, 32 devices: a whole 2x2x4 slice. The times are simulated.
32 devices in a mesh: seq: 8 (over z, core), fsdp: 4 (over y, x).
Axes of the slice: x: 2, y: 2, z: 4, core: 2. Of those that a mesh axis runs over, the one named last changes fastest.
Arguments:
- inputs: bfloat16 [4, 2048, 2048], P('fsdp', 'seq'), may hold values from -6 to 6
- cotangent: bfloat16 [4, 2048, 2048], P('fsdp', 'seq'), may hold values from -6 to 6
- w_inward: float32 [2048, 2560], P(('seq', 'fsdp')), may hold values from -0.125 to 0.125
- w_outward: float32 [2048, 2048], P(('seq', 'fsdp')), may hold values from -1 to 1
- w_gate_up: float32 [2048, 11264], P(('seq', 'fsdp')), may hold values from -0.125 to 0.125
- w_down: float32 [2048, 5632], P(('seq', 'fsdp')), may hold values from -0.078125 to 0.078125
- gains: float32 [2, 2048], P(None, ('seq', 'fsdp')), may hold values from 0.5 to 1.5
- first_inward: float32 [2048, 2560], P(('seq', 'fsdp')), may hold values from -64 to 64
- first_outward: float32 [2048, 2048], P(('seq', 'fsdp')), may hold values from -3 to 3
- first_gate_up: float32 [2048, 11264], P(('seq', 'fsdp')), may hold values from -16 to 16
- first_down: float32 [2048, 5632], P(('seq', 'fsdp')), may hold values from -32 to 32
- first_gains: float32 [2, 2048], P(None, ('seq', 'fsdp')), may hold values from -128 to 128
- second_inward: float32 [2048, 2560], P(('seq', 'fsdp')), may hold values from 430.8992 to 1723.5968
- second_outward: float32 [2048, 2048], P(('seq', 'fsdp')), may hold values from 1.077248 to 4.308992
- second_gate_up: float32 [2048, 11264], P(('seq', 'fsdp')), may hold values from 38.78093 to 155.15648
- second_down: float32 [2048, 5632], P(('seq', 'fsdp')), may hold values from 107.7248 to 430.8992
- second_gains: float32 [2, 2048], P(None, ('seq', 'fsdp')), may hold values from 1723.5968 to 6894.387
Outputs:
- output: bfloat16 [4, 2048, 2048], P('fsdp', 'seq')
- input_grad: float32 [4, 2048, 2048], P('fsdp', 'seq')
- first_inward_new: float32 [2048, 2560], P(('seq', 'fsdp'))
- second_inward_new: float32 [2048, 2560], P(('seq', 'fsdp'))
- inward_new: float32 [2048, 2560], P(('seq', 'fsdp'))
- first_outward_new: float32 [2048, 2048], P(('seq', 'fsdp'))
- second_outward_new: float32 [2048, 2048], P(('seq', 'fsdp'))
- outward_new: float32 [2048, 2048], P(('seq', 'fsdp'))
- first_gate_up_new: float32 [2048, 11264], P(('seq', 'fsdp'))
- second_gate_up_new: float32 [2048, 11264], P(('seq', 'fsdp'))
- gate_up_new: float32 [2048, 11264], P(('seq', 'fsdp'))
- first_down_new: float32 [2048, 5632], P(('seq', 'fsdp'))
- second_down_new: float32 [2048, 5632], P(('seq', 'fsdp'))
- down_new: float32 [2048, 5632], P(('seq', 'fsdp'))
- first_gains_new: float32 [2, 2048], P(None, ('seq', 'fsdp'))
- second_gains_new: float32 [2, 2048], P(None, ('seq', 'fsdp'))
- gains_new: float32 [2, 2048], P(None, ('seq', 'fsdp'))
All inputs are finite; a program needn't handle non-finite values.
Results may differ from a plain program's by a relative error of at most 0.015.
Values may be sent and summed in bfloat16 or wider, within the bound.
A program may use at most 640 MiB of HBM per device.

v0:
```python
import jax
import jax.numpy as jnp
from jax import lax
from jax.sharding import PartitionSpec as P

D = 2048
FF = 5632
HEADS = 32
KV_HEADS = 4
HEAD_DIM = 64
STEP = 10


epsilon = 1e-05
adam_epsilon = 1e-08
beta_first = 0.9
beta_second = 0.95
rope_base = 10000.0
weight_decay = 0.1
masked_value = -1e30


def rotate(field, position, sign):
    half = field.shape[-1] // 2
    exponent = jnp.arange(half).astype(jnp.float32) * (-2.0 / field.shape[-1])
    frequency = jnp.power(rope_base, exponent)
    angle = position[:, None] * frequency[None, :]
    cosine = jnp.cos(angle)[:, None, :]
    sine = sign * jnp.sin(angle)[:, None, :]
    first = field[..., :half]
    second = field[..., half:]
    return jnp.concatenate(
        [first * cosine - second * sine, second * cosine + first * sine], axis=-1
    )


def rms_scale(rows):
    return lax.rsqrt(jnp.mean(rows * rows, axis=-1, keepdims=True) + epsilon)


def norm_back(rows, scale_rows, gain, grad):
    weighted = grad * gain
    row_grad = scale_rows * weighted - rows * scale_rows**3 * jnp.mean(
        weighted * rows, axis=-1, keepdims=True
    )
    gain_grad = jnp.sum(grad * rows * scale_rows, axis=0)
    return (row_grad, gain_grad)


def outer(left, right):
    return lax.dot_general(
        left, right, (((0,), (0,)), ((), ())), preferred_element_type=jnp.float32
    )


def against(left, right):
    return lax.dot_general(
        left, right, (((1,), (1,)), ((), ())), preferred_element_type=jnp.float32
    )


def masked_scores(query_block, key_rows, query_place, key_place):
    scores = jnp.einsum(
        "rhd,md->hrm", query_block, key_rows, preferred_element_type=jnp.float32
    ) * key_rows.shape[-1] ** (-0.5)
    allowed = key_place[None, None, :] <= query_place[None, :, None]
    return jnp.where(allowed, scores, masked_value)


def attend_forward(query_block, key_rows, value_rows, query_place, key_place):
    scores = masked_scores(query_block, key_rows, query_place, key_place)
    largest = jnp.max(scores, axis=-1, keepdims=True)
    weights = jnp.exp(scores - largest)
    total = jnp.sum(weights, axis=-1, keepdims=True)
    shares = (weights / total).astype(jnp.bfloat16)
    mixed = jnp.einsum("hrm,md->rhd", shares, value_rows, preferred_element_type=jnp.float32)
    return (mixed.astype(jnp.bfloat16), (largest + jnp.log(total))[..., 0])


def attend_backward(
    query_block, key_rows, value_rows, grad_block, query_place, key_place, log_total
):
    scale = key_rows.shape[-1] ** (-0.5)
    scores = masked_scores(query_block, key_rows, query_place, key_place)
    shares = jnp.exp(scores - log_total[..., None])
    value_grad = jnp.einsum(
        "hrm,rhd->md", shares.astype(jnp.bfloat16), grad_block, preferred_element_type=jnp.float32
    )
    share_grad = jnp.einsum(
        "rhd,md->hrm", grad_block, value_rows, preferred_element_type=jnp.float32
    )
    inner = jnp.sum(shares * share_grad, axis=-1, keepdims=True)
    score_grad = (shares * (share_grad - inner)).astype(jnp.bfloat16)
    query_grad = (
        jnp.einsum("hrm,md->rhd", score_grad, key_rows, preferred_element_type=jnp.float32) * scale
    )
    key_grad = (
        jnp.einsum("hrm,rhd->md", score_grad, query_block, preferred_element_type=jnp.float32)
        * scale
    )
    return (query_grad, key_grad, value_grad)


def adam_update(weight, first, second, grad, rate, decay):
    first_new = beta_first * first + (1.0 - beta_first) * grad
    second_new = beta_second * second + (1.0 - beta_second) * grad * grad
    first_hat = first_new / (1.0 - beta_first**STEP)
    second_hat = second_new / (1.0 - beta_second**STEP)
    weight_new = weight - rate * (
        first_hat / (jnp.sqrt(second_hat) + adam_epsilon) + decay * weight
    )
    return (first_new, second_new, weight_new)


def body(
    inputs,
    cotangent,
    w_inward,
    w_outward,
    w_gate_up,
    w_down,
    gains,
    first_inward,
    first_outward,
    first_gate_up,
    first_down,
    first_gains,
    second_inward,
    second_outward,
    second_gate_up,
    second_down,
    second_gains,
):
    rows = inputs[0].astype(jnp.float32)
    upstream = cotangent[0]
    local = rows.shape[0]
    group = lax.axis_size("seq")
    heads_here = HEADS // group
    copies = group // KV_HEADS
    kv_width = KV_HEADS * HEAD_DIM
    head_cols = heads_here * HEAD_DIM
    inward_cols = D + 2 * kv_width
    position = (lax.axis_index("seq") * local + jnp.arange(local)).astype(jnp.float32)
    inward_full, outward_full, gains_full = (
        lax.all_gather(w_inward.astype(jnp.bfloat16), ("seq", "fsdp"), axis=0, tiled=True),
        lax.all_gather(w_outward.astype(jnp.bfloat16), ("seq", "fsdp"), axis=0, tiled=True),
        lax.all_gather(gains.astype(jnp.bfloat16), ("seq", "fsdp"), axis=1, tiled=True),
    )
    gain_first = gains_full[0].astype(jnp.float32)
    gain_second = gains_full[1].astype(jnp.float32)
    scale_first = rms_scale(rows)
    normed = (rows * scale_first * gain_first).astype(jnp.bfloat16)
    mixed = jnp.dot(normed, inward_full, preferred_element_type=jnp.float32)
    query = rotate(mixed[:, :D].reshape(local, HEADS, HEAD_DIM), position, 1.0).astype(jnp.bfloat16)
    key = rotate(
        mixed[:, D : D + kv_width].reshape(local, KV_HEADS, HEAD_DIM), position, 1.0
    ).astype(jnp.bfloat16)
    value = mixed[:, D + kv_width :].reshape(local, KV_HEADS, HEAD_DIM).astype(jnp.bfloat16)
    packed = jnp.concatenate(
        [
            query.reshape(local, group, head_cols),
            jnp.repeat(key, copies, axis=1),
            jnp.repeat(value, copies, axis=1),
        ],
        axis=-1,
    )
    arrived = lax.all_to_all(packed, "seq", split_axis=1, concat_axis=0, tiled=True)
    length = arrived.shape[0]
    arrived = arrived.reshape(length, head_cols + 2 * HEAD_DIM)
    query_here = arrived[:, :head_cols].reshape(length, heads_here, HEAD_DIM)
    key_here = arrived[:, head_cols : head_cols + HEAD_DIM]
    value_here = arrived[:, head_cols + HEAD_DIM :]
    block = min(512 // heads_here, length)
    blocks = length // block
    every = jnp.arange(length)

    def forward_block(index):
        start = index * block
        piece = lax.dynamic_slice_in_dim(query_here, start, block, 0)
        return attend_forward(piece, key_here, value_here, start + jnp.arange(block), every)

    mixed_blocks, log_blocks = lax.map(forward_block, jnp.arange(blocks))
    attended = lax.all_to_all(
        mixed_blocks.reshape(length, 1, head_cols), "seq", split_axis=0, concat_axis=1, tiled=True
    ).reshape(local, D)
    branch = jnp.dot(attended, outward_full, preferred_element_type=jnp.float32)
    middle = rows + branch
    scale_second = rms_scale(middle)
    normed_second = (middle * scale_second * gain_second).astype(jnp.bfloat16)
    local_gate_up = w_gate_up.astype(jnp.bfloat16)
    local_down = w_down.astype(jnp.bfloat16)
    columns = normed_second
    gate_up = jnp.dot(
        columns,
        lax.all_gather(local_gate_up, ("seq", "fsdp"), axis=0, tiled=True),
        preferred_element_type=jnp.float32,
    )
    gate = gate_up[:, :FF]
    up_part = gate_up[:, FF:]
    sigmoid = jax.nn.sigmoid(gate)
    hidden = (gate * sigmoid * up_part).astype(jnp.bfloat16)
    result = middle + against(
        hidden, lax.all_gather(local_down, ("seq", "fsdp"), axis=0, tiled=True)
    )
    columns = upstream
    hidden_grad = jnp.dot(
        columns,
        lax.all_gather(local_down, ("seq", "fsdp"), axis=0, tiled=True),
        preferred_element_type=jnp.float32,
    )
    gate_grad = hidden_grad * up_part * sigmoid * (1.0 + gate * (1.0 - sigmoid))
    up_grad = hidden_grad * gate * sigmoid
    gate_up_grad = jnp.concatenate([gate_grad, up_grad], axis=-1).astype(jnp.bfloat16)
    normed_second_grad = against(
        gate_up_grad, lax.all_gather(local_gate_up, ("seq", "fsdp"), axis=0, tiled=True)
    )
    middle_back, gain_second_grad = norm_back(middle, scale_second, gain_second, normed_second_grad)
    middle_grad = upstream.astype(jnp.float32) + middle_back
    normed_rows = normed_second
    feed_sum = lax.psum_scatter(
        jnp.concatenate([outer(normed_rows, gate_up_grad), outer(upstream, hidden)], axis=1),
        ("seq", "fsdp"),
        scatter_dimension=0,
        tiled=True,
    )
    branch_low = middle_grad.astype(jnp.bfloat16)
    inward_back, outward_back = (
        lax.all_gather(w_inward.astype(jnp.bfloat16), ("seq", "fsdp"), axis=0, tiled=True),
        lax.all_gather(w_outward.astype(jnp.bfloat16), ("seq", "fsdp"), axis=0, tiled=True),
    )
    attended_grad = against(branch_low, outward_back).astype(jnp.bfloat16)
    grad_here = lax.all_to_all(
        attended_grad.reshape(local, group, head_cols),
        "seq",
        split_axis=1,
        concat_axis=0,
        tiled=True,
    ).reshape(length, heads_here, HEAD_DIM)

    def backward_block(carry, index):
        start = index * block
        piece = lax.dynamic_slice_in_dim(query_here, start, block, 0)
        grad_piece = lax.dynamic_slice_in_dim(grad_here, start, block, 0)
        query_part, key_part, value_part = attend_backward(
            piece,
            key_here,
            value_here,
            grad_piece,
            start + jnp.arange(block),
            every,
            log_blocks[index],
        )
        return ((carry[0] + key_part, carry[1] + value_part), query_part)

    empty = jnp.zeros((length, HEAD_DIM), jnp.float32)
    (key_sum, value_sum), query_parts = lax.scan(backward_block, (empty, empty), jnp.arange(blocks))
    returned = jnp.concatenate(
        [query_parts.reshape(length, head_cols), key_sum, value_sum], axis=-1
    ).astype(jnp.bfloat16)
    back = lax.all_to_all(
        returned.reshape(length, 1, head_cols + 2 * HEAD_DIM),
        "seq",
        split_axis=0,
        concat_axis=1,
        tiled=True,
    ).astype(jnp.float32)
    query_grad = rotate(back[:, :, :head_cols].reshape(local, HEADS, HEAD_DIM), position, -1.0)
    key_grad = rotate(
        jnp.sum(
            back[:, :, head_cols : head_cols + HEAD_DIM].reshape(local, KV_HEADS, copies, HEAD_DIM),
            axis=2,
        ),
        position,
        -1.0,
    )
    value_grad = jnp.sum(
        back[:, :, head_cols + HEAD_DIM :].reshape(local, KV_HEADS, copies, HEAD_DIM), axis=2
    )
    inward_grad = jnp.concatenate(
        [
            query_grad.reshape(local, D),
            key_grad.reshape(local, kv_width),
            value_grad.reshape(local, kv_width),
        ],
        axis=-1,
    ).astype(jnp.bfloat16)
    normed_grad = against(inward_grad, inward_back)
    rows_back, gain_first_grad = norm_back(rows, scale_first, gain_first, normed_grad)
    input_grad = middle_grad + rows_back
    gain_grads = jnp.stack([gain_first_grad, gain_second_grad], axis=1)
    normed_rows = normed
    attention_sum = lax.psum_scatter(
        jnp.concatenate(
            [outer(normed_rows, inward_grad), outer(attended, branch_low), gain_grads], axis=1
        ),
        ("seq", "fsdp"),
        scatter_dimension=0,
        tiled=True,
    )
    inward_sum = attention_sum[:, :inward_cols]
    outward_sum = attention_sum[:, inward_cols : inward_cols + D]
    gains_sum = jnp.transpose(attention_sum[:, inward_cols + D :])
    gate_up_sum = feed_sum[:, : 2 * FF]
    down_sum = feed_sum[:, 2 * FF :]
    first_inward_new, second_inward_new, inward_new = adam_update(
        w_inward, first_inward, second_inward, inward_sum, 0.02, weight_decay
    )
    first_outward_new, second_outward_new, outward_new = adam_update(
        w_outward, first_outward, second_outward, outward_sum, 0.15, weight_decay
    )
    first_gate_up_new, second_gate_up_new, gate_up_new = adam_update(
        w_gate_up, first_gate_up, second_gate_up, gate_up_sum, 0.02, weight_decay
    )
    first_down_new, second_down_new, down_new = adam_update(
        w_down, first_down, second_down, down_sum, 0.015, weight_decay
    )
    first_gains_new, second_gains_new, gains_new = adam_update(
        gains, first_gains, second_gains, gains_sum, 0.6, 0.0
    )
    return (
        result[None].astype(jnp.bfloat16),
        input_grad[None],
        first_inward_new,
        second_inward_new,
        inward_new,
        first_outward_new,
        second_outward_new,
        outward_new,
        first_gate_up_new,
        second_gate_up_new,
        gate_up_new,
        first_down_new,
        second_down_new,
        down_new,
        first_gains_new,
        second_gains_new,
        gains_new,
    )


def solution(mesh):
    in_specs = (
        P("fsdp", "seq", None),
        P("fsdp", "seq", None),
        P(("seq", "fsdp"), None),
        P(("seq", "fsdp"), None),
        P(("seq", "fsdp"), None),
        P(("seq", "fsdp"), None),
        P(None, ("seq", "fsdp")),
        P(("seq", "fsdp"), None),
        P(("seq", "fsdp"), None),
        P(("seq", "fsdp"), None),
        P(("seq", "fsdp"), None),
        P(None, ("seq", "fsdp")),
        P(("seq", "fsdp"), None),
        P(("seq", "fsdp"), None),
        P(("seq", "fsdp"), None),
        P(("seq", "fsdp"), None),
        P(None, ("seq", "fsdp")),
    )
    out_specs = (
        P("fsdp", "seq", None),
        P("fsdp", "seq", None),
        P(("seq", "fsdp"), None),
        P(("seq", "fsdp"), None),
        P(("seq", "fsdp"), None),
        P(("seq", "fsdp"), None),
        P(("seq", "fsdp"), None),
        P(("seq", "fsdp"), None),
        P(("seq", "fsdp"), None),
        P(("seq", "fsdp"), None),
        P(("seq", "fsdp"), None),
        P(("seq", "fsdp"), None),
        P(("seq", "fsdp"), None),
        P(("seq", "fsdp"), None),
        P(None, ("seq", "fsdp")),
        P(None, ("seq", "fsdp")),
        P(None, ("seq", "fsdp")),
    )
    return jax.shard_map(body, mesh=mesh, in_specs=in_specs, out_specs=out_specs, check_vma=False)
```

profile of v0, /device:TPU:9, one launch (start us, length us, event | category | flops | bytes accessed | tf_op | source)
XLA Modules:
  0.0 3621.1 jit_solution(3560100942954621972)
XLA Ops:
  11.0 3.1 convert_element_type.126
  14.2 51.5 %all-gather = bf16[32,64,2]{1,2,0:T(2,128)(2,1)S(1)} all-gather(bf16[1,64,2]{1,2,0:T(2,128)(2,1)S(1)} %convert_bitcast_fusion.3), channel_id=1, replica_groups=mesh['seq'=8,'fsdp'=4] {'seq','fsdp'}, dimensions={0}, use_global_device_ids=true | all-gather | bytes 8448 | tf_op jit(solution)/shard_map/all_gather | solution.py:147
  68.4 31.3 all-gather.6.cloned.1.call-done
  99.7 5.7 fusion.66
  119.6 4.0 all-to-all-start
  126.2 60.6 %all-to-all-done = bf16[256,8,384]{0,2,1:T(8,128)(2,1)S(1)} async-done(((bf16[256,8,384]{0,2,1:T(8,128)(2,1)}), bf16[256,8,384]{0,2,1:T(8,128)(2,1)S(1)}, u32[]{:S(2)}, u32[]{:S(2)}) %all-to-all-start) | async-done | bytes 1572896 | tf_op jit(solution)/shard_map/all_to_all | solution.py:167
  194.8 97.4 %while.28 = (s32[]{:T(128)}, bf16[16,128,4,64]{1,3,2,0:T(8,128)(2,1)}, f32[16,4,128]{2,1,0:T(4,128)}, s32[16]{0:T(128)S(1)}, bf16[2048,4,64]{0,2,1:T(8,128)(2,1)...) while((s32[]{:T(128)}, ...), condition=%wide.region_4.5_spmd.clone, body=%wide.region_1.4_spmd.clone.sunk | while | flops 281312896 | bytes 14304447 | solution.py:182
  292.3 4.2 copy.331
  296.5 8.2 reshape.396
  305.3 11.6 reduce
  317.2 58.2 %all_to_all.54 = bf16[8,2,32768]{2,1,0:T(2,128)(2,1)} all-to-all(bf16[8,2,32768]{2,1,0:T(2,128)(2,1)S(1)} %reshape.399), channel_id=1, replica_groups=mesh['seq'=8,'fsdp'=4] {'seq'}, dimensions={0} | all-to-all | bytes 2097152 | tf_op jit(solution)/shard_map/all_to_all | solution.py:183
  375.3 4.3 reshape.400
  383.1 6.5 multiply_reduce_fusion.2
  390.1 76.3 %all-gather.10.cloned.1.call-done = bf16[2048,11264]{1,0:T(8,128)(2,1)} async-done(((bf16[64,11264]{1,0:T(8,128)(2,1)}), bf16[2048,11264]{1,0:T(8,128)(2,1)}) %all-gather.10.cloned.1.call-update) | async-done | bytes 46137360 | tf_op jit(solution)/shard_map/all_gather | solution.py:195
  466.4 23.1 fusion.74
  489.4 129.8 %all-gather.12.cloned.1.call-done = bf16[2048,5632]{1,0:T(8,128)(2,1)} async-done(((bf16[64,5632]{1,0:T(8,128)(2,1)}), bf16[2048,5632]{1,0:T(8,128)(2,1)}) %all-gather.12.cloned.1.call-update) | async-done | bytes 23068688 | tf_op jit(solution)/shard_map/all_gather | solution.py:203
  619.2 19.7 multiply_convert_fusion.1
  638.9 19.6 convolution_bitcast_fusion.2
  658.5 34.8 fusion.39
  693.3 89.0 %pad_maximum_fusion = f32[2048,16896]{1,0:T(8,128)} fusion(f32[2048,5632]{1,0:T(8,128)} %convolution_bitcast_fusion.2, f32[2048,11264]{1,0:T(8,128)} %fusion.39), kind=kLoop, calls=%fused_computation.53 | loop fusion | flops 34603008 | bytes 276824064 | tf_op jit(solution)/shard_map/concatenate | solution.py:221
  782.3 22.9 multiply_reduce_fusion
  807.6 6.7 convolution_convert_fusion
  815.3 6.8 all-to-all-start.2
  822.2 37.3 %all-to-all-done.2 = bf16[256,8,256]{2,0,1:T(8,128)(2,1)} async-done(((bf16[256,8,256]{2,0,1:T(8,128)(2,1)}), bf16[256,8,256]{2,0,1:T(8,128)(2,1)}, u32[]{:S(2)}, u32[]{:S(2)}) %all-to-all-start.2) | async-done | bytes 1048608 | tf_op jit(solution)/shard_map/all_to_all | solution.py:232
  859.5 2.7 copy.300
  864.6 207.6 %while.29 = (s32[]{:T(128)}, f32[2048,64]{0,1:T(8,128)S(1)}, f32[2048,64]{0,1:T(8,128)S(1)}, bf16[16,128,4,64]{1,3,2,0:T(8,128)(2,1)}, s32[16]{0:T(128)S(1)}, /*...) while((s32[]{:T(128)}, f32[2048,64]{0,1:T(8,128)S(1)}, ...), condition=%wide.region_9.10_spmd.clone, body=%wide.region_7.9_spmd.clone.sunk | while | flops 681475712 | bytes 35269908 | solution.py:256
  883.4 2.5 fusion.126
  896.3 2.5 fusion.126
  909.3 2.5 fusion.126
  922.3 2.5 fusion.126
  935.2 2.5 fusion.126
  948.2 2.5 fusion.126
  961.1 2.5 fusion.126
  974.1 2.5 fusion.126
  1000.1 2.5 fusion.126
  1013.1 2.5 fusion.126
  1052.0 2.5 fusion.126
  1065.0 2.5 fusion.126
  1072.1 2.9 copy.303
  1079.8 4.0 reduce.1
  1083.8 2.6 copy.344
  1086.3 3.8 reshape.401
  1090.1 4.5 all-to-all-start.3
  1096.1 9.7 fusion.62
  1105.9 39.9 %all-to-all-done.3 = bf16[8,2,49152]{2,1,0:T(2,128)(2,1)} async-done(((bf16[8,2,49152]{2,1,0:T(2,128)(2,1)}), bf16[8,2,49152]{2,1,0:T(2,128)(2,1)}, u32[]{:S(2)}, u32[]{:S(2)}) %all-to-all-start.3) | async-done | bytes 1572896 | tf_op jit(solution)/shard_map/all_to_all | solution.py:260
  1145.8 6.5 reshape.402
  1157.8 2.9 copy.306
  1165.8 9.2 fusion.53
  1176.4 10.3 fusion.60
  1186.7 42.7 %concatenate.61 = f32[2048,4610]{1,0:T(8,128)} concatenate(f32[2048,2560]{1,0:T(8,128)} %fusion.60, f32[2048,2048]{1,0:T(8,128)} %fusion.62, f32[2048,1]{1,0:T(8,128)} %copy.312, f32[2048,1]{1,0:T(8,128)} %copy.313), dimensions={1} | concatenate | bytes 75530240 | tf_op jit(solution)/shard_map/concatenate | solution.py:293
  1231.8 2.6 copy.317
  1239.1 2.6 copy.310
  1241.7 2.6 copy.315
  1244.2 12.8 fusion.43
  1257.1 4.2 fusion.50
  1261.3 1508.0 %all-reduce.3.cloned.1.call-done = f32[2048,16896]{1,0:T(8,128)} async-done(((f32[2048,16896]{1,0:T(8,128)}), f32[2048,16896]{1,0:T(8,128)}) %all-reduce.3.cloned.1.call-update) | async-done | bytes 138412048
  2769.3 6.1 multiply_subtract_fusion.1
  2775.4 6.8 multiply_subtract_fusion
  2782.3 806.1 %reduce-scatter.4.cloned.1.call-done = f32[64,4610]{1,0:T(8,128)} async-done(((f32[2048,4610]{1,0:T(8,128)}), f32[64,4610]{1,0:T(8,128)}) %reduce-scatter.4.cloned.1.call-update) | async-done | bytes 1180176
  3591.6 3.6 multiply_subtract_fusion.3
  3598.7 2.5 copy.326
  3602.7 4.3 multiply_subtract_fusion.2
  3607.0 2.6 copy.325
  3609.6 2.6 copy.324
  (441 shorter events, 299.0 us)
Async XLA Ops:
  7.2 92.5 %all-gather.6.cloned.1.call-start = ((), (), s32[]{:S(2)}) async-start(), calls=%async_computation.5 | async-start | bytes 10813440 | tf_op jit(solution)/shard_map/all_gather | solution.py:145
  9.1 374.0 %all-gather.8.cloned.1.call-start = ((), (), s32[]{:S(2)}) async-start(), calls=%async_computation.6 | async-start | bytes 8650752 | tf_op jit(solution)/shard_map/all_gather | solution.py:146
  11.0 3.2 copy-start.38
  11.0 56.5 %copy-start.2 = (bf16[1,256,2048]{2,1,0:T(8,128)(2,1)S(1)}, bf16[1,256,2048]{2,1,0:T(8,128)(2,1)}, u32[]{:S(2)}) copy-start(bf16[1,256,2048]{2,1,0:T(8,128)(2,1)} %param.21) | copy-start | bytes 3145732
  11.0 455.4 %all-gather.10.cloned.1.call-start = ((), (), s32[]{:S(2)}) async-start(), calls=%async_computation.7 | async-start | bytes 47579136 | tf_op jit(solution)/shard_map/all_gather | solution.py:195
  66.6 33.0 copy-start.30
  66.6 38.7 %copy-start.24 = (f32[256,32]{0,1:T(8,128)}, f32[256,32]{0,1:T(8,128)S(1)}, u32[]{:S(2)}) copy-start(f32[256,32]{0,1:T(8,128)S(1)} %get-tuple-element.491) | copy-start | bytes 98308
  66.7 48.3 %copy-start.22 = (f32[256,32]{1,0:T(8,128)}, f32[256,32]{1,0:T(8,128)S(1)}, u32[]{:S(2)}) copy-start(f32[256,32]{1,0:T(8,128)S(1)} %copy.287) | copy-start | bytes 98308
  68.4 37.0 %copy-start.34 = (f32[256]{0:T(256)}, f32[256]{0:T(256)S(1)}, u32[]{:S(2)}) copy-start(f32[256]{0:T(256)S(1)} %get-tuple-element.493) | copy-start | bytes 3076
  68.4 37.0 %copy-start.32 = (f32[1,2048]{1,0:T(1,128)}, f32[1,2048]{1,0:T(1,128)S(1)}, u32[]{:S(2)}) copy-start(f32[1,2048]{1,0:T(1,128)S(1)} %get-tuple-element.488) | copy-start | bytes 24580
  112.1 5.2 copy-start.25
  112.1 5.2 copy-start.31
  117.3 0.9 copy-start.28
  117.3 1.0 copy-start.27
  119.6 67.2 %all-to-all-start = ((bf16[256,8,384]{0,2,1:T(8,128)(2,1)}), bf16[256,8,384]{0,2,1:T(8,128)(2,1)S(1)}, u32[]{:S(2)}, u32[]{:S(2)}) async-start(bf16[256,8,384]{0,2,1:T(8,128)(2,1)} %pad_maximum_fusion.4), calls=%async_computation | async-start | bytes 3145728 | tf_op jit(solution)/shard_map/all_to_all | solution.py:167
  123.6 495.6 %all-gather.12.cloned.1.call-start = ((), (), s32[]{:S(2)}) async-start(), calls=%async_computation.8 | async-start | bytes 23789568 | tf_op jit(solution)/shard_map/all_gather | solution.py:203
  125.9 2643.4 %all-reduce.3.cloned.1.call-start = ((), (), s32[]{:S(2)}) async-start(), calls=%async_computation.10 | async-start | bytes 276824064
  186.7 1.1 copy-start.9
  292.3 12.5 copy-start
  292.3 12.5 copy-start.8
  292.3 12.5 copy-start.19
  466.4 152.8 %copy-start.13 = (bf16[1,256,2048]{2,1,0:T(8,128)(2,1)S(1)}, bf16[1,256,2048]{2,1,0:T(8,128)(2,1)}, u32[]{:S(2)}) copy-start(bf16[1,256,2048]{2,1,0:T(8,128)(2,1)} %param.22) | copy-start | bytes 3145732
  782.3 23.0 copy-start.14
  782.3 23.0 copy-start.37
  807.6 6.7 copy-start.4
  815.3 44.1 %all-to-all-start.2 = ((bf16[256,8,256]{2,0,1:T(8,128)(2,1)}), bf16[256,8,256]{2,0,1:T(8,128)(2,1)}, u32[]{:S(2)}, u32[]{:S(2)}) async-start(bf16[256,8,256]{2,0,1:T(8,128)(2,1)} %bitcast.179), calls=%async_computation.2 | async-start | bytes 2097152 | tf_op jit(solution)/shard_map/all_to_all | solution.py:232
  859.5 5.1 copy-start.1
  1077.3 1.2 copy-start.18
  1090.1 4.5 copy-start.29
  1090.1 6.0 copy-start.6
  1090.1 55.6 %all-to-all-start.3 = ((bf16[8,2,49152]{2,1,0:T(2,128)(2,1)}), bf16[8,2,49152]{2,1,0:T(2,128)(2,1)}, u32[]{:S(2)}, u32[]{:S(2)}) async-start(bf16[8,2,49152]{2,1,0:T(2,128)(2,1)} %reshape.401), calls=%async_computation.3 | async-start | bytes 3145728 | tf_op jit(solution)/shard_map/all_to_all | solution.py:260
  1094.7 2493.7 %reduce-scatter.4.cloned.1.call-start = ((), (), s32[]{:S(2)}) async-start(), calls=%async_computation.9 | async-start | bytes 40009728
  1154.7 1.6 copy-start.5
  1160.7 2.2 copy-start.23
  1162.9 0.8 copy-start.26
  1163.6 2.1 copy-start.3
  1163.7 2.1 copy-start.33
  1163.7 2.1 copy-start.35
  1165.7 9.3 copy-start.17
  1244.2 12.8 copy-start.36
  1261.3 1514.1 %copy-start.7 = (f32[64,11264]{1,0:T(8,128)S(1)}, f32[64,11264]{1,0:T(8,128)}, u32[]{:S(2)}) copy-start(f32[64,11264]{1,0:T(8,128)} %param.25) | copy-start | bytes 8650756
  2769.3 6.1 copy-start.20
  2769.3 6.1 copy-start.21
  2782.3 809.4 %copy-start.15 = (f32[64,2048]{0,1:T(8,128)S(1)}, f32[64,2048]{0,1:T(8,128)}, u32[]{:S(2)}) copy-start(f32[64,2048]{0,1:T(8,128)} %copy.321) | copy-start | bytes 1572868
  2782.3 809.4 %copy-start.16 = (f32[64,2048]{0,1:T(8,128)S(1)}, f32[64,2048]{0,1:T(8,128)}, u32[]{:S(2)}) copy-start(f32[64,2048]{0,1:T(8,128)} %copy.318) | copy-start | bytes 1572868
  3598.7 2.5 slice-start
  3598.7 4.0 copy-start.10
  3598.7 4.0 copy-start.11
  3607.0 5.2 copy-start.12
  3609.6 3.8 copy-start.39
  3609.6 3.8 copy-start.40
  3609.6 3.8 copy-start.41
Sparse Core Ops, SparseCore 0:
  11.5 88.1 all-gather.5
  103.1 92.8 all-gather.7
  199.4 266.9 all-gather.9
  469.7 149.4 all-gather.11
  782.4 1986.8 all-reduce.2
  2771.5 816.8 reduce-scatter.3
where the time goes:
time: 3630 us; the launch traced here: 3620 us
  waiting for transfers between devices  2690 us (74%)
  matrix products  362 us (10%)
  other arithmetic  194 us (5%)
  local copies, waits for them, and re-layouts  182 us (5%)
  blocking collectives  110 us (3%)
  loops' own time  53.1 us (1%)
    unnamed x8, waiting for transfers between devices  2310 us
    all_gather x1, waiting for transfers between devices, body(): lax.all_gather(local_down, ('seq', 'fsdp'), axis=0, tiled=True)  130 us
    concatenate x1, other arithmetic, body(): jnp.concatenate([outer(normed_rows, gate_up_grad), outer(upstream, hidden...  89 us
    all_gather x1, waiting for transfers between devices, body(): lax.all_gather(local_gate_up, ('seq', 'fsdp'), axis=0, tiled=True)  76.3 us
    dot_general x4, matrix products, outer(): lax.dot_general(left, right, (((0,), (0,)), ((), ())), preferred_element_...  74.4 us
  transfers between devices with their start and end apart: 9, of which 8 were waited for; matrix products, arithmetic and copies ran while one was open for 15% of the time, Pallas kernels for 0%

commit v1 on v0

v1 whole, which is shorter than its diff:
```python
import functools

import jax
import jax.numpy as jnp
from jax import lax
from jax.experimental import pallas as pl
from jax.experimental.pallas import tpu as pltpu
from jax.sharding import PartitionSpec as P

D = 2048
FF = 5632
HEADS = 32
KV_HEADS = 4
HEAD_DIM = 64
STEP = 10


epsilon = 1e-05
adam_epsilon = 1e-08
beta_first = 0.9
beta_second = 0.95
rope_base = 10000.0
weight_decay = 0.1
masked_value = -1e30


def rotate(field, position, sign):
    half = field.shape[-1] // 2
    exponent = jnp.arange(half).astype(jnp.float32) * (-2.0 / field.shape[-1])
    frequency = jnp.power(rope_base, exponent)
    angle = position[:, None] * frequency[None, :]
    cosine = jnp.cos(angle)[:, None, :]
    sine = sign * jnp.sin(angle)[:, None, :]
    first = field[..., :half]
    second = field[..., half:]
    return jnp.concatenate(
        [first * cosine - second * sine, second * cosine + first * sine], axis=-1
    )


def rms_scale(rows):
    return lax.rsqrt(jnp.mean(rows * rows, axis=-1, keepdims=True) + epsilon)


def norm_back(rows, scale_rows, gain, grad):
    weighted = grad * gain
    row_grad = scale_rows * weighted - rows * scale_rows**3 * jnp.mean(
        weighted * rows, axis=-1, keepdims=True
    )
    gain_grad = jnp.sum(grad * rows * scale_rows, axis=0)
    return (row_grad, gain_grad)


def dot(left, right):
    return jnp.dot(left, right, preferred_element_type=jnp.float32)


def outer(left, right):
    return lax.dot_general(
        left, right, (((0,), (0,)), ((), ())), preferred_element_type=jnp.float32
    )


def against(left, right):
    return lax.dot_general(
        left, right, (((1,), (1,)), ((), ())), preferred_element_type=jnp.float32
    )


def stack_heads(field, heads):
    return jnp.concatenate(
        [field[:, h * HEAD_DIM : (h + 1) * HEAD_DIM] for h in range(heads)], axis=0
    )


def unstack_heads(field, heads):
    rows = field.shape[0] // heads
    return jnp.concatenate([field[h * rows : (h + 1) * rows] for h in range(heads)], axis=1)


def masked_scores(keys, queries, start, first, block):
    scores = against(keys, queries)
    key_place = start + lax.broadcasted_iota(jnp.int32, scores.shape, 0)
    query_place = first + lax.rem(lax.broadcasted_iota(jnp.int32, scores.shape, 1), block)
    return jnp.where(key_place <= query_place, scores, masked_value)


def forward_kernel(query_ref, kv_ref, out_ref, log_ref, *, heads, block):
    index = pl.program_id(0)
    queries = stack_heads(query_ref[...], heads) * jnp.bfloat16(HEAD_DIM**-0.5)
    width = heads * block

    def step(j, carry, masked):
        largest, total, mixed = carry
        start = pl.multiple_of(j * block, block)
        kv = kv_ref[pl.ds(start, block), :]
        keys, values = kv[:, :HEAD_DIM], kv[:, HEAD_DIM:]
        if masked:
            scores = masked_scores(keys, queries, start, index * block, block)
        else:
            scores = against(keys, queries)
        new = jnp.maximum(largest, jnp.max(scores, axis=0, keepdims=True))
        fade = jnp.exp(largest - new)
        weights = jnp.exp(scores - new)
        total = total * fade + jnp.sum(weights, axis=0, keepdims=True)
        mixed = mixed * fade + outer(values, weights.astype(jnp.bfloat16))
        return new, total, mixed

    carry = (
        jnp.full((1, width), masked_value, jnp.float32),
        jnp.zeros((1, width), jnp.float32),
        jnp.zeros((HEAD_DIM, width), jnp.float32),
    )
    carry = lax.fori_loop(0, index, lambda j, c: step(j, c, False), carry)
    largest, total, mixed = step(index, carry, True)
    log_ref[0] = largest + jnp.log(total)
    out_ref[...] = unstack_heads((mixed / total).T, heads).astype(out_ref.dtype)


def backward_kernel(
    query_ref, kv_ref, grad_ref, out_ref, log_ref, query_grad_ref, kv_grad_ref,
    key_sum, value_sum, *, heads, block
):
    index = pl.program_id(0)
    scale = HEAD_DIM**-0.5

    @pl.when(index == 0)
    def _():
        key_sum[...] = jnp.zeros_like(key_sum)
        value_sum[...] = jnp.zeros_like(value_sum)

    queries = stack_heads(query_ref[...], heads) * jnp.bfloat16(scale)
    grads = stack_heads(grad_ref[...], heads)
    mixed = stack_heads(out_ref[...], heads)
    inner = jnp.sum(
        (grads.astype(jnp.float32) * mixed.astype(jnp.float32)).T, axis=0, keepdims=True
    )
    log_total = log_ref[0]

    def step(j, query_grad, masked):
        start = pl.multiple_of(j * block, block)
        place = pl.ds(start, block)
        kv = kv_ref[place, :]
        keys, values = kv[:, :HEAD_DIM], kv[:, HEAD_DIM:]
        if masked:
            scores = masked_scores(keys, queries, start, index * block, block)
        else:
            scores = against(keys, queries)
        shares = jnp.exp(scores - log_total)
        share_grad = against(values, grads)
        score_grad = (shares * (share_grad - inner)).astype(jnp.bfloat16)
        value_sum[place, :] += dot(shares.astype(jnp.bfloat16), grads)
        key_sum[place, :] += dot(score_grad, queries)
        return query_grad + outer(keys, score_grad)

    query_grad = lax.fori_loop(
        0,
        index,
        lambda j, c: step(j, c, False),
        jnp.zeros((HEAD_DIM, heads * block), jnp.float32),
    )
    query_grad = step(index, query_grad, True)
    query_grad_ref[...] = unstack_heads((query_grad * scale).T, heads).astype(jnp.bfloat16)

    @pl.when(index == pl.num_programs(0) - 1)
    def _():
        kv_grad_ref[...] = jnp.concatenate([key_sum[...], value_sum[...]], axis=1).astype(
            jnp.bfloat16
        )


def attention_specs(length, width, heads, block):
    rows = pl.BlockSpec((block, width), lambda i: (i, 0))
    kv = pl.BlockSpec((length, 2 * HEAD_DIM), lambda i: (0, width // (2 * HEAD_DIM)))
    logs = pl.BlockSpec((1, 1, heads * block), lambda i: (i, 0, 0))
    return rows, kv, logs


def attend_forward(packed, heads, block):
    length, width = packed.shape[0], heads * HEAD_DIM
    rows, kv, logs = attention_specs(length, width, heads, block)
    pairs = heads * length * length // 2
    return pl.pallas_call(
        functools.partial(forward_kernel, heads=heads, block=block),
        grid=(length // block,),
        in_specs=[rows, kv],
        out_specs=[rows, logs],
        out_shape=[
            jax.ShapeDtypeStruct((length, width), jnp.bfloat16),
            jax.ShapeDtypeStruct((length // block, 1, heads * block), jnp.float32),
        ],
        compiler_params=pltpu.CompilerParams(vmem_limit_bytes=48 << 20),
        cost_estimate=pl.CostEstimate(
            flops=pairs * HEAD_DIM * 16, bytes_accessed=length * 4 * width, transcendentals=pairs
        ),
    )(packed, packed)


def attend_backward(packed, grads, mixed, logs_in, heads, block):
    length, width = packed.shape[0], heads * HEAD_DIM
    rows, kv, logs = attention_specs(length, width, heads, block)
    pairs = heads * length * length // 2
    return pl.pallas_call(
        functools.partial(backward_kernel, heads=heads, block=block),
        grid=(length // block,),
        in_specs=[rows, kv, rows, rows, logs],
        out_specs=[rows, pl.BlockSpec((length, 2 * HEAD_DIM), lambda i: (0, 0))],
        out_shape=[
            jax.ShapeDtypeStruct((length, width), jnp.bfloat16),
            jax.ShapeDtypeStruct((length, 2 * HEAD_DIM), jnp.bfloat16),
        ],
        scratch_shapes=[
            pltpu.VMEM((length, HEAD_DIM), jnp.float32),
            pltpu.VMEM((length, HEAD_DIM), jnp.float32),
        ],
        compiler_params=pltpu.CompilerParams(vmem_limit_bytes=48 << 20),
        cost_estimate=pl.CostEstimate(
            flops=pairs * HEAD_DIM * 40, bytes_accessed=length * 8 * width, transcendentals=pairs
        ),
    )(packed, packed, grads, mixed, logs_in)


def swap(piece, axis, offset):
    size = lax.axis_size(axis)
    return lax.ppermute(piece, axis, [(i, i ^ offset) for i in range(size)])


def gather_swap(piece, axis):
    return [piece] + [swap(piece, axis, d) for d in range(1, lax.axis_size(axis))]


def exchange_swap(stack, axis):
    me = lax.axis_index(axis)
    pieces = [
        lax.dynamic_index_in_dim(stack, me ^ d, 0, keepdims=False)
        for d in range(lax.axis_size(axis))
    ]
    return [pieces[0]] + [swap(p, axis, d) for d, p in enumerate(pieces) if d]


def reduce_swap(parts, axis):
    total = parts[0].astype(jnp.float32)
    for d in range(1, len(parts)):
        total = total + swap(parts[d], axis, d).astype(jnp.float32)
    return total


def in_order(pieces, axis):
    me = lax.axis_index(axis)
    stack = jnp.stack(pieces)
    return [
        lax.dynamic_index_in_dim(stack, j ^ me, 0, keepdims=False) for j in range(len(pieces))
    ]


def return_columns(partial):
    mine = lax.psum_scatter(partial, "seq", scatter_dimension=0, tiled=True)
    size = lax.axis_size("fsdp")
    stack = mine.reshape(size, mine.shape[0] // size, mine.shape[1])
    return in_order(exchange_swap(stack, "fsdp"), "fsdp")


def adam_update(weight, first, second, grad, rate, decay):
    first_new = beta_first * first + (1.0 - beta_first) * grad
    second_new = beta_second * second + (1.0 - beta_second) * grad * grad
    first_hat = first_new / (1.0 - beta_first**STEP)
    second_hat = second_new / (1.0 - beta_second**STEP)
    weight_new = weight - rate * (
        first_hat / (jnp.sqrt(second_hat) + adam_epsilon) + decay * weight
    )
    return (first_new, second_new, weight_new)


def body(
    inputs,
    cotangent,
    w_inward,
    w_outward,
    w_gate_up,
    w_down,
    gains,
    first_inward,
    first_outward,
    first_gate_up,
    first_down,
    first_gains,
    second_inward,
    second_outward,
    second_gate_up,
    second_down,
    second_gains,
):
    rows = inputs[0].astype(jnp.float32)
    upstream = cotangent[0]
    local = rows.shape[0]
    group = lax.axis_size("seq")
    slices = lax.axis_size("fsdp")
    heads_here = HEADS // group
    copies = group // KV_HEADS
    kv_width = KV_HEADS * HEAD_DIM
    head_cols = heads_here * HEAD_DIM
    inward_cols = D + 2 * kv_width
    ff_cols = FF // slices
    depth = w_inward.shape[0]
    position = (lax.axis_index("seq") * local + jnp.arange(local)).astype(jnp.float32)

    low_inward = w_inward.astype(jnp.bfloat16)
    low_gains = jnp.pad(jnp.transpose(gains.astype(jnp.bfloat16)), ((0, 0), (0, 126)))
    inward_gains = lax.all_gather(
        jnp.concatenate([low_inward, low_gains], axis=1), ("seq", "fsdp"), axis=0, tiled=True
    )
    inward_full = inward_gains[:, :inward_cols]
    gain_first = inward_gains[:, inward_cols].astype(jnp.float32)
    gain_second = inward_gains[:, inward_cols + 1].astype(jnp.float32)
    outward_full = lax.all_gather(
        w_outward.astype(jnp.bfloat16), ("seq", "fsdp"), axis=0, tiled=True
    )

    low_feed = jnp.concatenate(
        [
            w_gate_up.astype(jnp.bfloat16).reshape(depth, 2, slices, ff_cols),
            w_down.astype(jnp.bfloat16).reshape(depth, 1, slices, ff_cols),
        ],
        axis=1,
    )
    low_feed = low_feed.transpose(2, 0, 1, 3).reshape(slices, depth, 3 * ff_cols)
    low_feed = lax.all_to_all(low_feed, "fsdp", 0, 0, tiled=True).reshape(
        slices * depth, 3 * ff_cols
    )
    gate_up_slice = lax.all_gather(low_feed[:, : 2 * ff_cols], "seq", axis=0, tiled=True)
    down_slice = lax.all_gather(low_feed[:, 2 * ff_cols :], "seq", axis=0, tiled=True)

    scale_first = rms_scale(rows)
    normed = (rows * scale_first * gain_first).astype(jnp.bfloat16)
    mixed = dot(normed, inward_full)
    query = rotate(mixed[:, :D].reshape(local, HEADS, HEAD_DIM), position, 1.0).astype(jnp.bfloat16)
    key = rotate(
        mixed[:, D : D + kv_width].reshape(local, KV_HEADS, HEAD_DIM), position, 1.0
    ).astype(jnp.bfloat16)
    value = mixed[:, D + kv_width :].reshape(local, KV_HEADS, HEAD_DIM).astype(jnp.bfloat16)
    packed = jnp.concatenate(
        [
            query.reshape(local, group, head_cols),
            jnp.repeat(key, copies, axis=1),
            jnp.repeat(value, copies, axis=1),
        ],
        axis=-1,
    ).transpose(1, 0, 2)
    arrived = lax.all_to_all(packed, "seq", 0, 0, tiled=True)
    length = group * local
    arrived = arrived.reshape(length, head_cols + 2 * HEAD_DIM)
    block = min(512, length)
    mixed_here, logs = attend_forward(arrived, heads_here, block)
    attended = lax.all_to_all(
        mixed_here.reshape(group, local, head_cols), "seq", 0, 0, tiled=True
    )
    attended = attended.transpose(1, 0, 2).reshape(local, D)
    middle = rows + dot(attended, outward_full)
    scale_second = rms_scale(middle)
    normed_second = (middle * scale_second * gain_second).astype(jnp.bfloat16)

    upstream_blocks = gather_swap(upstream, "fsdp")
    upstream_all = jnp.concatenate(upstream_blocks, axis=0)
    normed_all = jnp.concatenate(gather_swap(normed_second, "fsdp"), axis=0)
    gate_up = dot(normed_all, gate_up_slice)
    gate = gate_up[:, :ff_cols]
    up_part = gate_up[:, ff_cols:]
    sigmoid = jax.nn.sigmoid(gate)
    hidden = (gate * sigmoid * up_part).astype(jnp.bfloat16)
    hidden_grad = dot(upstream_all, down_slice)
    gate_grad = hidden_grad * up_part * sigmoid * (1.0 + gate * (1.0 - sigmoid))
    up_grad = hidden_grad * gate * sigmoid
    gate_up_grad = jnp.concatenate([gate_grad, up_grad], axis=-1).astype(jnp.bfloat16)

    def send_back(part):
        part = part.astype(jnp.bfloat16)
        return reduce_swap(
            [part[d * local : (d + 1) * local] for d in range(slices)], "fsdp"
        )

    normed_second_grad = send_back(against(gate_up_grad, gate_up_slice))
    result = middle + send_back(against(hidden, down_slice))
    down_back = return_columns(outer(upstream_all, hidden).astype(jnp.bfloat16))
    gate_up_back = return_columns(outer(normed_all, gate_up_grad).astype(jnp.bfloat16))

    middle_back, gain_second_grad = norm_back(middle, scale_second, gain_second, normed_second_grad)
    middle_grad = upstream.astype(jnp.float32) + middle_back
    branch_low = middle_grad.astype(jnp.bfloat16)
    attended_grad = against(branch_low, outward_full).astype(jnp.bfloat16)
    grad_here = lax.all_to_all(
        attended_grad.reshape(local, group, head_cols).transpose(1, 0, 2), "seq", 0, 0, tiled=True
    ).reshape(length, head_cols)
    query_part, kv_part = attend_backward(arrived, grad_here, mixed_here, logs, heads_here, block)
    back = lax.all_to_all(
        jnp.concatenate([query_part, kv_part], axis=-1).reshape(group, local, -1),
        "seq",
        0,
        0,
        tiled=True,
    ).astype(jnp.float32)
    query_grad = rotate(
        back[:, :, :head_cols].transpose(1, 0, 2).reshape(local, HEADS, HEAD_DIM), position, -1.0
    )

    def sum_copies(field):
        field = field.reshape(KV_HEADS, copies, local, HEAD_DIM)
        return jnp.sum(field, axis=1).transpose(1, 0, 2)

    key_grad = rotate(
        sum_copies(back[:, :, head_cols : head_cols + HEAD_DIM]), position, -1.0
    )
    value_grad = sum_copies(back[:, :, head_cols + HEAD_DIM :])
    inward_grad = jnp.concatenate(
        [
            query_grad.reshape(local, D),
            key_grad.reshape(local, kv_width),
            value_grad.reshape(local, kv_width),
        ],
        axis=-1,
    ).astype(jnp.bfloat16)
    normed_grad = against(inward_grad, inward_full)
    rows_back, gain_first_grad = norm_back(rows, scale_first, gain_first, normed_grad)
    input_grad = middle_grad + rows_back

    def column_slices(field):
        width = field.shape[1] // slices
        return field.reshape(local, slices, width).transpose(1, 0, 2)

    attended_all = jnp.concatenate(gather_swap(attended, "fsdp"), axis=0)
    branch_all = jnp.concatenate(exchange_swap(column_slices(branch_low), "fsdp"), axis=0)
    outward_back = return_columns(outer(attended_all, branch_all).astype(jnp.bfloat16))
    first_all = jnp.concatenate(gather_swap(normed, "fsdp"), axis=0)
    inward_grad_all = jnp.concatenate(exchange_swap(column_slices(inward_grad), "fsdp"), axis=0)
    inward_back = return_columns(outer(first_all, inward_grad_all).astype(jnp.bfloat16))

    gain_grads = jnp.stack([gain_first_grad, gain_second_grad], axis=1)
    gains_sum = jnp.transpose(
        lax.psum_scatter(gain_grads, ("seq", "fsdp"), scatter_dimension=0, tiled=True)
    )
    inward_sum = jnp.concatenate(inward_back, axis=1).astype(jnp.float32)
    outward_sum = jnp.concatenate(outward_back, axis=1).astype(jnp.float32)
    gate_up_sum = jnp.concatenate(
        [piece[:, :ff_cols] for piece in gate_up_back]
        + [piece[:, ff_cols:] for piece in gate_up_back],
        axis=1,
    ).astype(jnp.float32)
    down_sum = jnp.concatenate(down_back, axis=1).astype(jnp.float32)
    first_inward_new, second_inward_new, inward_new = adam_update(
        w_inward, first_inward, second_inward, inward_sum, 0.02, weight_decay
    )
    first_outward_new, second_outward_new, outward_new = adam_update(
        w_outward, first_outward, second_outward, outward_sum, 0.15, weight_decay
    )
    first_gate_up_new, second_gate_up_new, gate_up_new = adam_update(
        w_gate_up, first_gate_up, second_gate_up, gate_up_sum, 0.02, weight_decay
    )
    first_down_new, second_down_new, down_new = adam_update(
        w_down, first_down, second_down, down_sum, 0.015, weight_decay
    )
    first_gains_new, second_gains_new, gains_new = adam_update(
        gains, first_gains, second_gains, gains_sum, 0.6, 0.0
    )
    return (
        result[None].astype(jnp.bfloat16),
        input_grad[None],
        first_inward_new,
        second_inward_new,
        inward_new,
        first_outward_new,
        second_outward_new,
        outward_new,
        first_gate_up_new,
        second_gate_up_new,
        gate_up_new,
        first_down_new,
        second_down_new,
        down_new,
        first_gains_new,
        second_gains_new,
        gains_new,
    )


def solution(mesh):
    in_specs = (
        P("fsdp", "seq", None),
        P("fsdp", "seq", None),
        P(("seq", "fsdp"), None),
        P(("seq", "fsdp"), None),
        P(("seq", "fsdp"), None),
        P(("seq", "fsdp"), None),
        P(None, ("seq", "fsdp")),
        P(("seq", "fsdp"), None),
        P(("seq", "fsdp"), None),
        P(("seq", "fsdp"), None),
        P(("seq", "fsdp"), None),
        P(None, ("seq", "fsdp")),
        P(("seq", "fsdp"), None),
        P(("seq", "fsdp"), None),
        P(("seq", "fsdp"), None),
        P(("seq", "fsdp"), None),
        P(None, ("seq", "fsdp")),
    )
    out_specs = (
        P("fsdp", "seq", None),
        P("fsdp", "seq", None),
        P(("seq", "fsdp"), None),
        P(("seq", "fsdp"), None),
        P(("seq", "fsdp"), None),
        P(("seq", "fsdp"), None),
        P(("seq", "fsdp"), None),
        P(("seq", "fsdp"), None),
        P(("seq", "fsdp"), None),
        P(("seq", "fsdp"), None),
        P(("seq", "fsdp"), None),
        P(("seq", "fsdp"), None),
        P(("seq", "fsdp"), None),
        P(("seq", "fsdp"), None),
        P(None, ("seq", "fsdp")),
        P(None, ("seq", "fsdp")),
        P(None, ("seq", "fsdp")),
    )
    return jax.shard_map(body, mesh=mesh, in_specs=in_specs, out_specs=out_specs, check_vma=False)
```

time: 3630 us -> 1070 us (0.29)
  waiting for transfers between devices: 2690 us -> 678 us
  matrix products: 362 us -> 129 us
  other arithmetic: 194 us -> 40.3 us
  local copies, waits for them, and re-layouts: 182 us -> 46.1 us
  blocking collectives: 110 us -> 39 us
  loops' own time: 53.1 us -> 0 us
  Pallas kernels: 0 us -> 52.2 us
  starting transfers between devices: 15.7 us -> 65 us
    unnamed x8 -> x10, waiting for transfers between devices: 2310 us -> 46 us
    reduce_scatter x0 -> x4, waiting for transfers between devices: none -> 215 us  [return_columns(): mine = lax.psum_scatter(partial, 'seq', scatter_dimension=0, tiled=True)]
    ppermute x0 -> x36, waiting for transfers between devices: none -> 197 us  [swap(): return lax.ppermute(piece, axis, [(i, i ^ offset) for i in range(size)])]
    dot_general x116 -> x4, matrix products: 236 us -> 50.2 us  [dot(): return jnp.dot(left, right, preferred_element_type=jnp.float32)]
    all_gather x3, waiting for transfers between devices: 237 us -> 77.5 us  [the longest x1 43.2 us: body(): lax.all_gather(jnp.concatenate([low_inward, low_gains], axis=1), ('seq',...]
    concatenate x5 -> x2, other arithmetic: 95.5 us -> 0.92 us  [the longest x1 0.76 us: body(): jnp.concatenate([low_inward, low_gains], axis=1)]
    another operation x2 -> x0, loops' own time: 53.1 us -> none  [the longest x1 42.3 us: body(): lax.scan(backward_block, (empty, empty), jnp.arange(blocks))]
    pallas_call x0 -> x2, Pallas kernels: none -> 52.2 us  [the longest x1 33.3 us: attend_backward(): pl.pallas_call(functools.partial(backward_kernel, heads=heads, block=bloc...]
  transfers between devices with their start and end apart: 9 -> 49, of which waited for: 8 -> 34; matrix products, arithmetic and copies ran while one was open for 15% -> 15% of each run, Pallas kernels for 0% -> 5%
where the time goes in v1:
time: 1070 us; the launch traced here: 1060 us
  waiting for transfers between devices  678 us (63%)
  matrix products  129 us (12%)
  starting transfers between devices  65 us (6%)
  Pallas kernels  52.2 us (5%)
  local copies, waits for them, and re-layouts  46.1 us (4%)
  other arithmetic  40.3 us (4%)
  blocking collectives  39 us (4%)
  between operations  15 us (1%)
    reduce_scatter x4, waiting for transfers between devices, return_columns(): mine = lax.psum_scatter(partial, 'seq', scatter_dimension=0, tiled=True)  215 us
    ppermute x36, waiting for transfers between devices, swap(): return lax.ppermute(piece, axis, [(i, i ^ offset) for i in range(size)])  197 us
    all_to_all x1, waiting for transfers between devices, body(): arrived = lax.all_to_all(packed, 'seq', 0, 0, tiled=True)  62.2 us
    dot_general x4, matrix products, dot(): return jnp.dot(left, right, preferred_element_type=jnp.float32)  50.2 us
    all_to_all x1, waiting for transfers between devices, body(): lax.all_to_all(mixed_here.reshape(group, local, head_cols), 'seq', 0, 0,...  49.7 us
    unnamed x10, waiting for transfers between devices  46 us
    all_gather x1, waiting for transfers between devices, body(): lax.all_gather(jnp.concatenate([low_inward, low_gains], axis=1), ('seq',...  43.2 us
    dot_general x4, matrix products, outer(): lax.dot_general(left, right, (((0,), (0,)), ((), ())), preferred_element_...  42.9 us
  transfers between devices with their start and end apart: 49, of which 34 were waited for; matrix products, arithmetic and copies ran while one was open for 15% of the time, Pallas kernels for 5%

profile of v1, /device:TPU:9, one launch (start us, length us, event | category | flops | bytes accessed | tf_op | source)
XLA Modules:
  0.0 1064.3 jit_solution(6666710231731218455)
XLA Ops:
  10.2 1.8 convert_element_type.170
  13.3 3.2 reshape.275
  16.5 2.2 copy.63
  20.3 3.0 maximum_bitcast_fusion
  23.3 3.0 reshape.277
  26.3 39.0 %all_to_all.25 = bf16[4,64,4224]{2,1,0:T(8,128)(2,1)S(1)} all-to-all(bf16[4,64,4224]{2,1,0:T(8,128)(2,1)} %reshape.277), channel_id=1, replica_groups=mesh['seq'=8,'fsdp'=4] {'fsdp'}, dimensions={0} | all-to-all | bytes 4325376 | tf_op jit(solution)/shard_map/all_to_all | solution.py:327
  68.7 43.2 %all-gather.5.cloned.1.call-done = bf16[2048,2688]{1,0:T(8,128)(2,1)} async-done(((bf16[64,2688]{1,0:T(8,128)(2,1)}), bf16[2048,2688]{1,0:T(8,128)(2,1)}) %all-gather.5.cloned.1.call-update) | async-done | bytes 11010064 | tf_op jit(solution)/shard_map/all_gather | solution.py:309
  111.9 1.8 convert_reduce_fusion
  115.5 5.9 fusion.2
  123.7 2.9 copy.58
  126.9 1.9 subtract_convert_fusion
  130.2 4.9 all-to-all-start
  136.0 62.2 %all-to-all-done = bf16[8,256,384]{1,2,0:T(8,128)(2,1)} async-done(((bf16[8,256,384]{1,2,0:T(8,128)(2,1)}), bf16[8,256,384]{1,2,0:T(8,128)(2,1)}, u32[]{:S(2)}, u32[]{:S(2)}) %all-to-all-start) | async-done | bytes 1572896 | tf_op jit(solution)/shard_map/all_to_all | solution.py:349
  198.2 1.9 copy.61
  200.1 18.9 %shard_map.296 = (bf16[2048,256]{1,0:T(8,128)(2,1)S(1)}, f32[4,1,2048]{2,1,0:T(1,128)S(1)}) custom-call(bf16[2048,384]{1,0:T(8,128)(2,1)S(1)} %bitcast.165, bf16[2048,384]{1,0:T(8,128)(2,1)S(1)} %bitcast.166), custom_call_target="tpu_custom_call" | custom-call | flops 8589934592 | bytes 2097152 | tf_op jit(solution)/shard_map/pallas_call | solution.py:183
  220.4 10.0 all-to-all-start.1
  230.4 49.7 %all-to-all-done.1 = bf16[8,256,256]{1,2,0:T(8,128)(2,1)} async-done(((bf16[8,256,256]{1,2,0:T(8,128)(2,1)}), bf16[8,256,256]{1,2,0:T(8,128)(2,1)}, u32[]{:S(2)}, u32[]{:S(2)}) %all-to-all-start.1) | async-done | bytes 1048608 | tf_op jit(solution)/shard_map/all_to_all | solution.py:354
  280.1 6.6 multiply_reduce_fusion.2
  293.3 20.3 %collective-permute-done = bf16[256,2048]{1,0:T(8,128)(2,1)} collective-permute-done((bf16[256,2048]{1,0:T(8,128)(2,1)}, bf16[256,2048]{1,0:T(8,128)(2,1)}, u32[]{:S(2)}, u32[]{:S(2)}) %collective-permute-start) | collective-permute-done | bytes 1048608 | tf_op jit(solution)/shard_map/ppermute | solution.py:225
  315.0 18.5 %all-gather.9.cloned.1.call-done = bf16[2048,2816]{1,0:T(8,128)(2,1)} async-done(((bf16[256,2816]{1,0:T(8,128)(2,1)}), bf16[2048,2816]{1,0:T(8,128)(2,1)}) %all-gather.9.cloned.1.call-update) | async-done | bytes 11534352 | tf_op jit(solution)/shard_map/all_gather | solution.py:330
  333.5 3.6 collective-permute-done.2
  337.1 21.3 %fusion.56 = f32[1024,2816]{1,0:T(8,128)} fusion(bf16[2048,2816]{1,0:T(8,128)(2,1)} %all-gather.9.cloned.1.call-done, bf16[256,2048]{1,0:T(8,128)(2,1)} %collective-permute-done.2, bf16[256,2048]{1,0:T(8,128)(2,1)} %collective-permute-done.1, bf16[256,2048]{1,0:T(8,128)(2,1)} %collective-permute-done, bf16[256,2048]{1,0:T(8,128)(2,1)} %multiply_convert_fusion.3), kind=kOutput, calls=%fused_computation.102 | convolution fusion | flops 11827937280 | bytes 27262976 | tf_op jit(solution)/shard_map/dot_general | solution.py:55
  359.4 22.6 %collective-permute-done.8 = bf16[256,2048]{1,0:T(8,128)(2,1)} collective-permute-done((bf16[256,2048]{1,0:T(8,128)(2,1)}, bf16[256,2048]{1,0:T(8,128)(2,1)}, u32[]{:S(2)}, u32[]{:S(2)}) %collective-permute-start.8) | collective-permute-done | bytes 1048608 | tf_op jit(solution)/shard_map/ppermute | solution.py:225
  382.1 15.9 %all-gather.11.cloned.1.call-done = bf16[2048,1408]{1,0:T(8,128)(2,1)} async-done(((bf16[256,1408]{1,0:T(8,128)(2,1)}), bf16[2048,1408]{1,0:T(8,128)(2,1)}) %all-gather.11.cloned.1.call-update) | async-done | bytes 5767184 | tf_op jit(solution)/shard_map/all_gather | solution.py:331
  397.9 16.5 %multiply_convert_fusion.1 = (bf16[1024,1408]{1,0:T(8,128)(2,1)S(1)}, bf16[1024,1408]{1,0:T(8,128)(2,1)}, bf16[1024,1408]{1,0:T(8,128)(2,1)}) fusion(f32[1024,2816]{1,0:T(8,128)} %fusion.56, bf16[2048,1408]{1,0:T(8,128)(2,1)} %all-gather.11.cloned.1.call-done, bf16[256,2048]{1,0:T(8,128)(2,1)} %collective-permute-done.8, ...), kind=kOutput, calls=%fused_computation.8 | convolution fusion | flops 5945425920 | bytes 30146560 | tf_op jit(solution)/shard_map/dot_general | solution.py:55
  416.0 15.8 %convolution_convert_fusion.2 = bf16[1024,2048]{1,0:T(8,128)(2,1)S(1)} fusion(bf16[2048,2816]{1,0:T(8,128)(2,1)} %all-gather.9.cloned.1.call-done, bf16[1024,1408]{1,0:T(8,128)(2,1)} %get-tuple-element.51, bf16[1024,1408]{1,0:T(8,128)(2,1)S(1)} %get-tuple-element.50), kind=kOutput, calls=%fused_computation.36 | convolution fusion | flops 11824791552 | bytes 21495808 | tf_op jit(solution)/shard_map/dot_general | solution.py:65
  435.0 8.3 convolution_convert_fusion.3
  446.0 33.3 %collective-permute-done.10 = bf16[256,2048]{1,0:T(8,128)(2,1)S(1)} collective-permute-done((bf16[256,2048]{1,0:T(8,128)(2,1)S(1)}, bf16[256,2048]{1,0:T(8,128)(2,1)S(1)}, u32[]{:S(2)}, u32[]{:S(2)}) %collective-permute-start.10) | collective-permute-done | bytes 1048608 | tf_op jit(solution)/shard_map/ppermute | solution.py:225
  479.3 2.1 collective-permute-start.5
  482.7 20.0 %collective-permute-done.3 = bf16[256,2048]{1,0:T(8,128)(2,1)S(1)} collective-permute-done((bf16[256,2048]{1,0:T(8,128)(2,1)S(1)}, bf16[256,2048]{1,0:T(8,128)(2,1)S(1)}, u32[]{:S(2)}, u32[]{:S(2)}) %collective-permute-start.3) | collective-permute-done | bytes 1048608 | tf_op jit(solution)/shard_map/ppermute | solution.py:225
  502.7 23.4 %collective-permute-done.5 = bf16[256,2048]{1,0:T(8,128)(2,1)S(1)} collective-permute-done((bf16[256,2048]{1,0:T(8,128)(2,1)S(1)}, bf16[256,2048]{1,0:T(8,128)(2,1)S(1)}, u32[]{:S(2)}, u32[]{:S(2)}) %collective-permute-start.5) | collective-permute-done | bytes 1048608 | tf_op jit(solution)/shard_map/ppermute | solution.py:225
  526.1 4.9 fusion.82
  531.0 2.4 convolution_convert_fusion.4
  534.4 7.6 all-to-all-start.3
  544.7 20.4 %all-to-all-done.3 = bf16[8,256,256]{2,1,0:T(8,128)(2,1)} async-done(((bf16[8,256,256]{2,1,0:T(8,128)(2,1)}), bf16[8,256,256]{2,1,0:T(8,128)(2,1)}, u32[]{:S(2)}, u32[]{:S(2)}) %all-to-all-start.3) | async-done | bytes 1048608 | tf_op jit(solution)/shard_map/all_to_all | solution.py:390
  565.1 33.3 %shard_map.297 = (bf16[2048,256]{1,0:T(8,128)(2,1)S(1)}, bf16[2048,128]{1,0:T(8,128)(2,1)S(1)}) custom-call(bf16[2048,384]{1,0:T(8,128)(2,1)S(1)} %bitcast.167, bf16[2048,384]{1,0:T(8,128)(2,1)S(1)} %bitcast.168, bf16[2048,256]{1,0:T(8,128)(2,1)} %bitcast.19.grad_ref, bf16[2048,256]{1,0:T(8,128)(2,1)S(1)} %get-tuple-element.21.out_ref, ...), custom_call_target="tpu_custom_call" | custom-call | flops 21474836480 | bytes 4194304 | tf_op jit(solution)/shard_map/pallas_call | solution.py:203
  600.2 7.2 all-to-all-start.4
  607.4 2.2 reshape.289
  609.6 2.2 constant_dynamic-slice_fusion.6
  614.9 4.6 collective-permute-done.24
  619.5 6.6 collective-permute-done.25
  626.0 5.9 fusion.23
  634.7 9.7 all-to-all-done.4
  648.6 6.9 collective-permute-done.12
  656.9 9.1 fusion.37
  667.8 10.2 collective-permute-done.14
  678.0 8.6 collective-permute-done.15
  686.7 8.9 collective-permute-done.17
  695.6 7.4 fusion.20
  703.1 11.0 %convolution_convert_fusion.1 = bf16[2048,1408]{1,0:T(8,128)(2,1)} fusion(bf16[1024,1408]{1,0:T(8,128)(2,1)} %get-tuple-element.52, bf16[256,2048]{1,0:T(8,128)(2,1)} %collective-permute-done.8, bf16[256,2048]{1,0:T(8,128)(2,1)} %collective-permute-done.7, bf16[256,2048]{1,0:T(8,128)(2,1)} %collective-permute-done.6, bf16[256,2048]{1,0:T(8,128)(2,1)} %bitcast.17), kind=kOutput, calls=%fused_computation.5 | convolution fusion | flops 5925240832 | bytes 12845056 | tf_op jit(solution)/shard_map/dot_general | solution.py:59
  714.4 18.6 %convolution_convert_fusion = bf16[2048,2816]{1,0:T(8,128)(2,1)} fusion(bf16[1024,1408]{1,0:T(8,128)(2,1)} %get-tuple-element.51, bf16[1024,1408]{1,0:T(8,128)(2,1)} %copy-done.35, bf16[256,2048]{1,0:T(8,128)(2,1)} %collective-permute-done.2, bf16[256,2048]{1,0:T(8,128)(2,1)} %collective-permute-done.1, bf16[256,2048]{1,0:T(8,128)(2,1)} %collective-permute-done, ...), kind=kOutput, calls=%fused_computation | convolution fusion | flops 11845238784 | bytes 21495808 | tf_op jit(solution)/shard_map/dot_general | solution.py:59
  739.9 2.8 multiply_subtract_fusion.4
  742.8 1.9 fusion.34
  744.7 45.9 %reduce-scatter.16.cloned.1.call-done = f32[64,2]{1,0:T(8,128)} async-done(((f32[2048,2]{1,0:T(8,128)}), f32[64,2]{1,0:T(8,128)}) %reduce-scatter.16.cloned.1.call-update) | async-done | bytes 528
  791.4 47.2 %reduce-scatter.8.cloned.1.call-done = bf16[256,640]{1,0:T(8,128)(2,1)} async-done(((bf16[2048,640]{1,0:T(8,128)(2,1)}), bf16[256,640]{1,0:T(8,128)(2,1)}) %reduce-scatter.8.cloned.1.call-update) | async-done | bytes 327696 | tf_op jit(solution)/shard_map/reduce_scatter | solution.py:257
  844.5 1.9 collective-permute-done.20
  846.6 61.4 %reduce-scatter.14.cloned.1.call-done = bf16[256,1408]{1,0:T(8,128)(2,1)} async-done(((bf16[2048,1408]{1,0:T(8,128)(2,1)}), bf16[256,1408]{1,0:T(8,128)(2,1)}) %reduce-scatter.14.cloned.1.call-update) | async-done | bytes 720912 | tf_op jit(solution)/shard_map/reduce_scatter | solution.py:257
  913.5 2.3 collective-permute-done.33
  915.8 5.0 collective-permute-done.34
  921.7 106.3 %reduce-scatter.12.cloned.1.call-done = bf16[256,2816]{1,0:T(8,128)(2,1)} async-done(((bf16[2048,2816]{1,0:T(8,128)(2,1)}), bf16[256,2816]{1,0:T(8,128)(2,1)}) %reduce-scatter.12.cloned.1.call-update) | async-done | bytes 1441808 | tf_op jit(solution)/shard_map/reduce_scatter | solution.py:257
  1032.3 2.8 multiply_subtract_fusion.1
  1035.1 4.9 collective-permute-done.30
  1040.1 8.8 collective-permute-done.31
  1052.5 5.0 multiply_subtract_fusion
  (232 shorter events, 81.8 us)
Async XLA Ops:
  7.2 104.7 %all-gather.5.cloned.1.call-start = ((), (), s32[]{:S(2)}) async-start(), calls=%async_computation.10 | async-start | bytes 11354112 | tf_op jit(solution)/shard_map/all_gather | solution.py:309
  10.1 220.3 %all-gather.7.cloned.1.call-start = ((), (), s32[]{:S(2)}) async-start(), calls=%async_computation.11 | async-start | bytes 8650752 | tf_op jit(solution)/shard_map/all_gather | solution.py:315
  12.0 321.5 %all-gather.9.cloned.1.call-start = ((), (), s32[]{:S(2)}) async-start(), calls=%async_computation.12 | async-start | bytes 12976128 | tf_op jit(solution)/shard_map/all_gather | solution.py:330
  67.9 53.5 %copy-start.27 = (f32[256]{0:T(256)}, f32[256]{0:T(256)S(1)}, u32[]{:S(2)}) copy-start(f32[256]{0:T(256)S(1)} %get-tuple-element.112) | copy-start | bytes 3076
  68.7 58.2 %copy-start.18 = (f32[256,32]{0,1:T(8,128)}, f32[256,32]{0,1:T(8,128)S(1)}, u32[]{:S(2)}) copy-start(f32[256,32]{0,1:T(8,128)S(1)} %get-tuple-element.110) | copy-start | bytes 98308
  130.2 68.0 %all-to-all-start = ((bf16[8,256,384]{1,2,0:T(8,128)(2,1)}), bf16[8,256,384]{1,2,0:T(8,128)(2,1)}, u32[]{:S(2)}, u32[]{:S(2)}) async-start(bf16[8,256,384]{1,2,0:T(8,128)(2,1)} %maximum_bitcast_fusion.1), calls=%async_computation | async-start | bytes 3145728 | tf_op jit(solution)/shard_map/all_to_all | solution.py:349
  135.1 262.8 %all-gather.11.cloned.1.call-start = ((), (), s32[]{:S(2)}) async-start(), calls=%async_computation.13 | async-start | bytes 6488064 | tf_op jit(solution)/shard_map/all_gather | solution.py:331
  220.4 59.8 %all-to-all-start.1 = ((bf16[8,256,256]{1,2,0:T(8,128)(2,1)}), bf16[8,256,256]{1,2,0:T(8,128)(2,1)}, u32[]{:S(2)}, u32[]{:S(2)}) async-start(bf16[8,256,256]{1,2,0:T(8,128)(2,1)} %copy.62), calls=%async_computation.1 | async-start | bytes 2097152 | tf_op jit(solution)/shard_map/all_to_all | solution.py:354
  289.2 24.4 %collective-permute-start = (bf16[256,2048]{1,0:T(8,128)(2,1)}, bf16[256,2048]{1,0:T(8,128)(2,1)}, u32[]{:S(2)}, u32[]{:S(2)}) collective-permute-start(bf16[256,2048]{1,0:T(8,128)(2,1)} %multiply_convert_fusion.3), channel_id=1, source_target_pairs={{0,1},{1,0},{2,3},{3,2},{4,5},{5,4},{6,7},{7,6},{8,9},{9,8},{10,11... | collective-permute-start | bytes 3145736 | tf_op jit(solution)/shard_map/ppermute | solution.py:225
  290.4 43.1 %collective-permute-start.1 = (bf16[256,2048]{1,0:T(8,128)(2,1)}, bf16[256,2048]{1,0:T(8,128)(2,1)}, u32[]{:S(2)}, u32[]{:S(2)}) collective-permute-start(bf16[256,2048]{1,0:T(8,128)(2,1)} %multiply_convert_fusion.3), channel_id=1, source_target_pairs={{0,2},{1,3},{2,0},{3,1},{4,6},{5,7},{6,4},{7,5},{8,10},{9,11},{10,... | collective-permute-start | bytes 3145736 | tf_op jit(solution)/shard_map/ppermute | solution.py:225
  290.6 46.5 %collective-permute-start.2 = (bf16[256,2048]{1,0:T(8,128)(2,1)}, bf16[256,2048]{1,0:T(8,128)(2,1)}, u32[]{:S(2)}, u32[]{:S(2)}) collective-permute-start(bf16[256,2048]{1,0:T(8,128)(2,1)} %multiply_convert_fusion.3), channel_id=1, source_target_pairs={{0,3},{1,2},{2,1},{3,0},{4,7},{5,6},{6,5},{7,4},{8,11},{9,10},{10,... | collective-permute-start | bytes 3145736 | tf_op jit(solution)/shard_map/ppermute | solution.py:225
  291.9 66.7 %collective-permute-start.6 = (bf16[256,2048]{1,0:T(8,128)(2,1)}, bf16[256,2048]{1,0:T(8,128)(2,1)}, u32[]{:S(2)}, u32[]{:S(2)}) collective-permute-start(bf16[256,2048]{1,0:T(8,128)(2,1)} %bitcast.17), channel_id=1, source_target_pairs={{0,1},{1,0},{2,3},{3,2},{4,5},{5,4},{6,7},{7,6},{8,9},{9,8},{10,11... | collective-permute-start | bytes 3145736 | tf_op jit(solution)/shard_map/ppermute | solution.py:225
  293.1 66.4 %collective-permute-start.7 = (bf16[256,2048]{1,0:T(8,128)(2,1)}, bf16[256,2048]{1,0:T(8,128)(2,1)}, u32[]{:S(2)}, u32[]{:S(2)}) collective-permute-start(bf16[256,2048]{1,0:T(8,128)(2,1)} %bitcast.17), channel_id=1, source_target_pairs={{0,2},{1,3},{2,0},{3,1},{4,6},{5,7},{6,4},{7,5},{8,10},{9,11},{10,... | collective-permute-start | bytes 3145736 | tf_op jit(solution)/shard_map/ppermute | solution.py:225
  313.6 68.5 %collective-permute-start.8 = (bf16[256,2048]{1,0:T(8,128)(2,1)}, bf16[256,2048]{1,0:T(8,128)(2,1)}, u32[]{:S(2)}, u32[]{:S(2)}) collective-permute-start(bf16[256,2048]{1,0:T(8,128)(2,1)} %bitcast.17), channel_id=1, source_target_pairs={{0,3},{1,2},{2,1},{3,0},{4,7},{5,6},{6,5},{7,4},{8,11},{9,10},{10,... | collective-permute-start | bytes 3145736 | tf_op jit(solution)/shard_map/ppermute | solution.py:225
  432.2 47.0 %collective-permute-start.10 = (bf16[256,2048]{1,0:T(8,128)(2,1)S(1)}, bf16[256,2048]{1,0:T(8,128)(2,1)S(1)}, u32[]{:S(2)}, u32[]{:S(2)}) collective-permute-start(bf16[256,2048]{1,0:T(8,128)(2,1)S(1)} %get-tuple-element.55), channel_id=1, source_target_pairs={{0,2},{1,3},{2,0},{3,1},{4,6},{5,7},{6,4},{7,5},{8,10},{9,11},{10,... | collective-permute-start | bytes 3145736 | tf_op jit(solution)/shard_map/ppermute | solution.py:225
  433.5 47.8 %collective-permute-start.11 = (bf16[256,2048]{1,0:T(8,128)(2,1)S(1)}, bf16[256,2048]{1,0:T(8,128)(2,1)S(1)}, u32[]{:S(2)}, u32[]{:S(2)}) collective-permute-start(bf16[256,2048]{1,0:T(8,128)(2,1)S(1)} %get-tuple-element.54), channel_id=1, source_target_pairs={{0,3},{1,2},{2,1},{3,0},{4,7},{5,6},{6,5},{7,4},{8,11},{9,10},{10,... | collective-permute-start | bytes 3145736 | tf_op jit(solution)/shard_map/ppermute | solution.py:225
  434.7 46.7 %collective-permute-start.9 = (bf16[256,2048]{1,0:T(8,128)(2,1)S(1)}, bf16[256,2048]{1,0:T(8,128)(2,1)S(1)}, u32[]{:S(2)}, u32[]{:S(2)}) collective-permute-start(bf16[256,2048]{1,0:T(8,128)(2,1)S(1)} %get-tuple-element.53), channel_id=1, source_target_pairs={{0,1},{1,0},{2,3},{3,2},{4,5},{5,4},{6,7},{7,6},{8,9},{9,8},{10,11... | collective-permute-start | bytes 3145736 | tf_op jit(solution)/shard_map/ppermute | solution.py:225
  443.3 38.1 %copy-start.1 = (f32[256,2048]{1,0:T(8,128)S(1)}, f32[256,2048]{1,0:T(8,128)}, u32[]{:S(2)}) copy-start(f32[256,2048]{1,0:T(8,128)} %copy-done) | copy-start | bytes 6291460
  443.5 59.2 %collective-permute-start.3 = (bf16[256,2048]{1,0:T(8,128)(2,1)S(1)}, bf16[256,2048]{1,0:T(8,128)(2,1)S(1)}, u32[]{:S(2)}, u32[]{:S(2)}) collective-permute-start(bf16[256,2048]{1,0:T(8,128)(2,1)S(1)} %get-tuple-element.56), channel_id=1, source_target_pairs={{0,1},{1,0},{2,3},{3,2},{4,5},{5,4},{6,7},{7,6},{8,9},{9,8},{10,11... | collective-permute-start | bytes 3145736 | tf_op jit(solution)/shard_map/ppermute | solution.py:225
  444.8 57.9 %collective-permute-start.4 = (bf16[256,2048]{1,0:T(8,128)(2,1)S(1)}, bf16[256,2048]{1,0:T(8,128)(2,1)S(1)}, u32[]{:S(2)}, u32[]{:S(2)}) collective-permute-start(bf16[256,2048]{1,0:T(8,128)(2,1)S(1)} %get-tuple-element.58), channel_id=1, source_target_pairs={{0,2},{1,3},{2,0},{3,1},{4,6},{5,7},{6,4},{7,5},{8,10},{9,11},{10,... | collective-permute-start | bytes 3145736 | tf_op jit(solution)/shard_map/ppermute | solution.py:225
  479.3 46.8 %collective-permute-start.5 = (bf16[256,2048]{1,0:T(8,128)(2,1)S(1)}, bf16[256,2048]{1,0:T(8,128)(2,1)S(1)}, u32[]{:S(2)}, u32[]{:S(2)}) collective-permute-start(bf16[256,2048]{1,0:T(8,128)(2,1)S(1)} %get-tuple-element.57), channel_id=1, source_target_pairs={{0,3},{1,2},{2,1},{3,0},{4,7},{5,6},{6,5},{7,4},{8,11},{9,10},{10,... | collective-permute-start | bytes 3145736 | tf_op jit(solution)/shard_map/ppermute | solution.py:225
  481.4 49.6 %slice-start = ((s8[8388608]{0:T(1024)(128)(4,1)}), s8[4194304]{0:T(1024)(128)(4,1)S(1)}, s32[]{:S(2)}) async-start(s8[8388608]{0:T(1024)(128)(4,1)} %bitcast.170), calls=%async_computation.19 | async-start | bytes 8388608
  534.4 30.7 %all-to-all-start.3 = ((bf16[8,256,256]{2,1,0:T(8,128)(2,1)}), bf16[8,256,256]{2,1,0:T(8,128)(2,1)}, u32[]{:S(2)}, u32[]{:S(2)}) async-start(bf16[8,256,256]{2,1,0:T(8,128)(2,1)} %bitcast.181), calls=%async_computation.3 | async-start | bytes 2097152 | tf_op jit(solution)/shard_map/all_to_all | solution.py:390
  542.1 71.4 %collective-permute-start.21 = (bf16[256,2048]{0,1:T(8,128)(2,1)}, bf16[256,2048]{0,1:T(8,128)(2,1)}, u32[]{:S(2)}, u32[]{:S(2)}) collective-permute-start(bf16[256,2048]{0,1:T(8,128)(2,1)} %bitcast.13), channel_id=1, source_target_pairs={{0,1},{1,0},{2,3},{3,2},{4,5},{5,4},{6,7},{7,6},{8,9},{9,8},{10,11... | collective-permute-start | bytes 3145736 | tf_op jit(solution)/shard_map/ppermute | solution.py:225
  543.2 71.6 %collective-permute-start.22 = (bf16[256,2048]{0,1:T(8,128)(2,1)}, bf16[256,2048]{0,1:T(8,128)(2,1)}, u32[]{:S(2)}, u32[]{:S(2)}) collective-permute-start(bf16[256,2048]{0,1:T(8,128)(2,1)} %bitcast.13), channel_id=1, source_target_pairs={{0,2},{1,3},{2,0},{3,1},{4,6},{5,7},{6,4},{7,5},{8,10},{9,11},{10,... | collective-permute-start | bytes 3145736 | tf_op jit(solution)/shard_map/ppermute | solution.py:225
  543.5 71.3 %collective-permute-start.23 = (bf16[256,2048]{0,1:T(8,128)(2,1)}, bf16[256,2048]{0,1:T(8,128)(2,1)}, u32[]{:S(2)}, u32[]{:S(2)}) collective-permute-start(bf16[256,2048]{0,1:T(8,128)(2,1)} %bitcast.13), channel_id=1, source_target_pairs={{0,3},{1,2},{2,1},{3,0},{4,7},{5,6},{6,5},{7,4},{8,11},{9,10},{10,... | collective-permute-start | bytes 3145736 | tf_op jit(solution)/shard_map/ppermute | solution.py:225
  600.2 44.2 %all-to-all-start.4 = ((bf16[8,256,384]{1,2,0:T(8,128)(2,1)}), bf16[8,256,384]{1,2,0:T(8,128)(2,1)S(1)}, u32[]{:S(2)}, u32[]{:S(2)}) async-start(bf16[8,256,384]{1,2,0:T(8,128)(2,1)} %copy.66), calls=%async_computation.4 | async-start | bytes 3145728 | tf_op jit(solution)/shard_map/all_to_all | solution.py:394
  607.4 125.7 %reduce-scatter.10.cloned.1.call-start = ((), (), s32[]{:S(2)}) async-start(), calls=%async_computation.15 | async-start | bytes 2359296 | tf_op jit(solution)/shard_map/reduce_scatter | solution.py:257
  611.9 7.6 collective-permute-start.24
  613.1 12.9 %collective-permute-start.25 = (bf16[256,512]{1,0:T(8,128)(2,1)S(1)}, bf16[256,512]{1,0:T(8,128)(2,1)S(1)}, u32[]{:S(2)}, u32[]{:S(2)}) collective-permute-start(bf16[256,512]{1,0:T(8,128)(2,1)S(1)} %bitcast.203), channel_id=1, source_target_pairs={{0,2},{1,3},{2,0},{3,1},{4,6},{5,7},{6,4},{7,5},{8,10},{9,11},{10,... | collective-permute-start | bytes 786440 | tf_op jit(solution)/shard_map/ppermute | solution.py:225
  613.5 12.5 %collective-permute-start.26 = (bf16[256,512]{1,0:T(8,128)(2,1)S(1)}, bf16[256,512]{1,0:T(8,128)(2,1)S(1)}, u32[]{:S(2)}, u32[]{:S(2)}) collective-permute-start(bf16[256,512]{1,0:T(8,128)(2,1)S(1)} %bitcast.205), channel_id=1, source_target_pairs={{0,3},{1,2},{2,1},{3,0},{4,7},{5,6},{6,5},{7,4},{8,11},{9,10},{10,... | collective-permute-start | bytes 786440 | tf_op jit(solution)/shard_map/ppermute | solution.py:225
  631.9 158.6 %reduce-scatter.16.cloned.1.call-start = ((), (), s32[]{:S(2)}) async-start(), calls=%async_computation.18 | async-start | bytes 1081344
  632.0 23.5 %collective-permute-start.12 = (bf16[256,2048]{1,0:T(8,128)(2,1)}, bf16[256,2048]{1,0:T(8,128)(2,1)}, u32[]{:S(2)}, u32[]{:S(2)}) collective-permute-start(bf16[256,2048]{1,0:T(8,128)(2,1)} %fusion.30), channel_id=1, source_target_pairs={{0,1},{1,0},{2,3},{3,2},{4,5},{5,4},{6,7},{7,6},{8,9},{9,8},{10,11... | collective-permute-start | bytes 3145736 | tf_op jit(solution)/shard_map/ppermute | solution.py:225
  632.3 35.5 %collective-permute-start.13 = (bf16[256,2048]{1,0:T(8,128)(2,1)}, bf16[256,2048]{1,0:T(8,128)(2,1)}, u32[]{:S(2)}, u32[]{:S(2)}) collective-permute-start(bf16[256,2048]{1,0:T(8,128)(2,1)} %fusion.30), channel_id=1, source_target_pairs={{0,2},{1,3},{2,0},{3,1},{4,6},{5,7},{6,4},{7,5},{8,10},{9,11},{10,... | collective-permute-start | bytes 3145736 | tf_op jit(solution)/shard_map/ppermute | solution.py:225
  633.4 44.6 %collective-permute-start.14 = (bf16[256,2048]{1,0:T(8,128)(2,1)}, bf16[256,2048]{1,0:T(8,128)(2,1)}, u32[]{:S(2)}, u32[]{:S(2)}) collective-permute-start(bf16[256,2048]{1,0:T(8,128)(2,1)} %fusion.30), channel_id=1, source_target_pairs={{0,3},{1,2},{2,1},{3,0},{4,7},{5,6},{6,5},{7,4},{8,11},{9,10},{10,... | collective-permute-start | bytes 3145736 | tf_op jit(solution)/shard_map/ppermute | solution.py:225
  646.0 11.0 %copy-start.3 = (bf16[1,256,2048]{2,1,0:T(8,128)(2,1)S(1)}, bf16[1,256,2048]{2,1,0:T(8,128)(2,1)}, u32[]{:S(2)}) copy-start(bf16[1,256,2048]{2,1,0:T(8,128)(2,1)} %param.17) | copy-start | bytes 3145732
  646.0 11.0 %copy-start.26 = (f32[2048]{0:T(1024)S(1)}, f32[2048]{0:T(1024)}, u32[]{:S(2)}) copy-start(f32[2048]{0:T(1024)} %copy-done.25) | copy-start | bytes 24580
  647.0 39.7 %collective-permute-start.15 = (bf16[256,640]{1,0:T(8,128)(2,1)}, bf16[256,640]{1,0:T(8,128)(2,1)}, u32[]{:S(2)}, u32[]{:S(2)}) collective-permute-start(bf16[256,640]{1,0:T(8,128)(2,1)} %bitcast.198), channel_id=1, source_target_pairs={{0,1},{1,0},{2,3},{3,2},{4,5},{5,4},{6,7},{7,6},{8,9},{9,8},{10,11... | collective-permute-start | bytes 983048 | tf_op jit(solution)/shard_map/ppermute | solution.py:225
  648.3 38.3 %collective-permute-start.16 = (bf16[256,640]{1,0:T(8,128)(2,1)S(1)}, bf16[256,640]{1,0:T(8,128)(2,1)}, u32[]{:S(2)}, u32[]{:S(2)}) collective-permute-start(bf16[256,640]{1,0:T(8,128)(2,1)S(1)} %bitcast.199), channel_id=1, source_target_pairs={{0,2},{1,3},{2,0},{3,1},{4,6},{5,7},{6,4},{7,5},{8,10},{9,11},{10,... | collective-permute-start | bytes 983048 | tf_op jit(solution)/shard_map/ppermute | solution.py:225
  655.5 40.1 %collective-permute-start.17 = (bf16[256,640]{1,0:T(8,128)(2,1)S(1)}, bf16[256,640]{1,0:T(8,128)(2,1)}, u32[]{:S(2)}, u32[]{:S(2)}) collective-permute-start(bf16[256,640]{1,0:T(8,128)(2,1)S(1)} %bitcast.200), channel_id=1, source_target_pairs={{0,3},{1,2},{2,1},{3,0},{4,7},{5,6},{6,5},{7,4},{8,11},{9,10},{10,... | collective-permute-start | bytes 983048 | tf_op jit(solution)/shard_map/ppermute | solution.py:225
  667.6 171.0 %reduce-scatter.8.cloned.1.call-start = ((), (), s32[]{:S(2)}) async-start(), calls=%async_computation.14 | async-start | bytes 2949120 | tf_op jit(solution)/shard_map/reduce_scatter | solution.py:257
  703.0 204.9 %reduce-scatter.14.cloned.1.call-start = ((), (), s32[]{:S(2)}) async-start(), calls=%async_computation.17 | async-start | bytes 6488064 | tf_op jit(solution)/shard_map/reduce_scatter | solution.py:257
  714.2 313.9 %reduce-scatter.12.cloned.1.call-start = ((), (), s32[]{:S(2)}) async-start(), calls=%async_computation.16 | async-start | bytes 12976128 | tf_op jit(solution)/shard_map/reduce_scatter | solution.py:257
  733.0 9.7 copy-start.33
  734.2 3.7 collective-permute-start.27
  735.7 3.3 collective-permute-start.28
  735.8 4.1 collective-permute-start.29
  742.7 99.6 %copy-start.30 = (f32[2,64]{1,0:T(2,128)S(1)}, f32[2,64]{1,0:T(2,128)}, u32[]{:S(2)}) copy-start(f32[2,64]{1,0:T(2,128)} %param.23) | copy-start | bytes 1540
  742.7 99.6 %copy-start.31 = (f32[2,64]{1,0:T(2,128)S(1)}, f32[2,64]{1,0:T(2,128)}, u32[]{:S(2)}) copy-start(f32[2,64]{1,0:T(2,128)} %param.33) | copy-start | bytes 1540
  742.8 99.6 %copy-start.32 = (f32[2,64]{1,0:T(2,128)S(1)}, f32[2,64]{1,0:T(2,128)}, u32[]{:S(2)}) copy-start(f32[2,64]{1,0:T(2,128)} %param.28) | copy-start | bytes 1540
  744.7 167.2 %copy-start.13 = (f32[64,2560]{1,0:T(8,128)S(1)}, f32[64,2560]{1,0:T(8,128)}, u32[]{:S(2)}) copy-start(f32[64,2560]{1,0:T(8,128)} %param.19) | copy-start | bytes 1966084
  744.7 167.2 %copy-start.21 = (f32[64,2560]{1,0:T(8,128)S(1)}, f32[64,2560]{1,0:T(8,128)}, u32[]{:S(2)}) copy-start(f32[64,2560]{1,0:T(8,128)} %param.29) | copy-start | bytes 1966084
  744.7 167.2 %copy-start.22 = (f32[64,2560]{1,0:T(8,128)S(1)}, f32[64,2560]{1,0:T(8,128)}, u32[]{:S(2)}) copy-start(f32[64,2560]{1,0:T(8,128)} %param.24) | copy-start | bytes 1966084
  839.7 3.4 collective-permute-start.18
  841.0 3.6 collective-permute-start.19
  842.2 4.3 collective-permute-start.20
  909.2 6.6 collective-permute-start.33
  910.4 10.4 collective-permute-start.34
  911.6 9.2 collective-permute-start.35
  920.8 111.5 %copy-start.8 = (f32[64,5632]{1,0:T(8,128)S(1)}, f32[64,5632]{1,0:T(8,128)}, u32[]{:S(2)}) copy-start(f32[64,5632]{1,0:T(8,128)} %param.22) | copy-start | bytes 4325380
  920.8 111.5 %copy-start.16 = (f32[64,5632]{1,0:T(8,128)S(1)}, f32[64,5632]{1,0:T(8,128)}, u32[]{:S(2)}) copy-start(f32[64,5632]{1,0:T(8,128)} %param.32) | copy-start | bytes 4325380
  1029.6 10.5 collective-permute-start.30
  1030.9 18.0 %collective-permute-start.31 = (bf16[64,2816]{1,0:T(8,128)(2,1)S(1)}, bf16[64,2816]{1,0:T(8,128)(2,1)S(1)}, u32[]{:S(2)}, u32[]{:S(2)}) collective-permute-start(bf16[64,2816]{1,0:T(8,128)(2,1)S(1)} %get-tuple-element.70), channel_id=1, source_target_pairs={{0,2},{1,3},{2,0},{3,1},{4,6},{5,7},{6,4},{7,5},{8,10},{9,11},{10,... | collective-permute-start | bytes 1081352 | tf_op jit(solution)/shard_map/ppermute | solution.py:225
  1032.1 16.8 %collective-permute-start.32 = (bf16[64,2816]{1,0:T(8,128)(2,1)S(1)}, bf16[64,2816]{1,0:T(8,128)(2,1)S(1)}, u32[]{:S(2)}, u32[]{:S(2)}) collective-permute-start(bf16[64,2816]{1,0:T(8,128)(2,1)S(1)} %get-tuple-element.69), channel_id=1, source_target_pairs={{0,3},{1,2},{2,1},{3,0},{4,7},{5,6},{6,5},{7,4},{8,11},{9,10},{10,... | collective-permute-start | bytes 1081352 | tf_op jit(solution)/shard_map/ppermute | solution.py:225
  (24 other events, 89.7 us)
Sparse Core Ops, SparseCore 0:
  11.5 100.3 all-gather.4
  115.3 92.0 all-gather.6
  209.7 123.7 all-gather.8
  335.6 62.3 all-gather.10
  632.1 35.3 reduce-scatter.9
  670.2 120.3 reduce-scatter.15
  793.0 45.6 reduce-scatter.7
  841.0 66.8 reduce-scatter.13
  910.4 117.6 reduce-scatter.11

commit v2 on v1

v2 whole, which is shorter than its diff:
```python
import functools

import jax
import jax.numpy as jnp
from jax import lax
from jax.experimental import pallas as pl
from jax.experimental.pallas import tpu as pltpu
from jax.sharding import PartitionSpec as P

D = 2048
FF = 5632
HEADS = 32
KV_HEADS = 4
HEAD_DIM = 64
STEP = 10


epsilon = 1e-05
adam_epsilon = 1e-08
beta_first = 0.9
beta_second = 0.95
rope_base = 10000.0
weight_decay = 0.1
masked_value = -1e30


def rotate(field, position, sign):
    half = field.shape[-1] // 2
    exponent = jnp.arange(half).astype(jnp.float32) * (-2.0 / field.shape[-1])
    frequency = jnp.power(rope_base, exponent)
    angle = position[:, None] * frequency[None, :]
    cosine = jnp.cos(angle)[:, None, :]
    sine = sign * jnp.sin(angle)[:, None, :]
    first = field[..., :half]
    second = field[..., half:]
    return jnp.concatenate(
        [first * cosine - second * sine, second * cosine + first * sine], axis=-1
    )


def rms_scale(rows):
    return lax.rsqrt(jnp.mean(rows * rows, axis=-1, keepdims=True) + epsilon)


def norm_back(rows, scale_rows, gain, grad):
    weighted = grad * gain
    row_grad = scale_rows * weighted - rows * scale_rows**3 * jnp.mean(
        weighted * rows, axis=-1, keepdims=True
    )
    gain_grad = jnp.sum(grad * rows * scale_rows, axis=0)
    return (row_grad, gain_grad)


def dot(left, right):
    return jnp.dot(left, right, preferred_element_type=jnp.float32)


def outer(left, right):
    return lax.dot_general(
        left, right, (((0,), (0,)), ((), ())), preferred_element_type=jnp.float32
    )


def against(left, right):
    return lax.dot_general(
        left, right, (((1,), (1,)), ((), ())), preferred_element_type=jnp.float32
    )


def stack_heads(field, heads):
    return jnp.concatenate(
        [field[:, h * HEAD_DIM : (h + 1) * HEAD_DIM] for h in range(heads)], axis=0
    )


def unstack_heads(field, heads):
    rows = field.shape[0] // heads
    return jnp.concatenate([field[h * rows : (h + 1) * rows] for h in range(heads)], axis=1)


def masked_scores(keys, queries, block):
    scores = against(keys, queries)
    key_place = lax.broadcasted_iota(jnp.int32, scores.shape, 0)
    query_place = lax.rem(lax.broadcasted_iota(jnp.int32, scores.shape, 1), block)
    return jnp.where(key_place <= query_place, scores, masked_value)


def remote(source, target, send, arrive, axis, device):
    return pltpu.make_async_remote_copy(
        src_ref=source,
        dst_ref=target,
        send_sem=send,
        recv_sem=arrive,
        device_id={axis: device},
        device_id_type=pl.DeviceIdType.MESH,
    )


VMEM = pl.BlockSpec(memory_space=pltpu.VMEM)


def core_pair(index):
    return index // 2, lax.rem(index, 2)


def share_kernel(
    in_ref, gain_ref, out_ref, gate_up_ref, down_ref,
    feed_gate, feed_up, feed_down, in_rows, out_rows,
    low_gate, low_up, low_down,
    send_feed, come_feed, send_in, come_in, send_out, come_out,
    pass_in, passed_in, pass_out, passed_out,
):
    group, slices = lax.axis_size("seq"), lax.axis_size("fsdp")
    s, f = lax.axis_index("seq"), lax.axis_index("fsdp")
    pair, core = core_pair(s)
    depth, inward_cols = in_ref.shape
    ff_cols = FF // slices
    in_rows[pair, core, :, pl.ds(0, inward_cols)] = in_ref[...].astype(jnp.bfloat16)
    in_rows[pair, core, :, pl.ds(inward_cols, 128)] = gain_ref[...]
    out_rows[pair, core] = out_ref[...].astype(jnp.bfloat16)
    for t in range(slices):
        columns = pl.ds(t * ff_cols, ff_cols)
        low_gate[t] = gate_up_ref[:, columns].astype(jnp.bfloat16)
        low_up[t] = gate_up_ref[:, pl.ds(FF + t * ff_cols, ff_cols)].astype(jnp.bfloat16)
        low_down[t] = down_ref[:, columns].astype(jnp.bfloat16)

    barrier = pltpu.get_barrier_semaphore()
    near = [1] + list(range(2, group, 2))
    for d in near:
        pl.semaphore_signal(
            barrier, inc=1, device_id={"seq": s ^ d}, device_id_type=pl.DeviceIdType.MESH
        )
    for d in range(1, slices):
        pl.semaphore_signal(
            barrier, inc=1, device_id={"fsdp": f ^ d}, device_id_type=pl.DeviceIdType.MESH
        )
    pl.semaphore_wait(barrier, len(near) + slices - 1)

    feeds = ((low_gate, feed_gate), (low_up, feed_up), (low_down, feed_down))

    def feed_copy(k, d, owner, target):
        low, feed = feeds[k]
        return remote(
            low.at[target],
            feed.at[pl.ds(pl.multiple_of(owner * depth, depth), depth), :],
            send_feed.at[k, d], come_feed.at[k, d], "fsdp", target,
        )

    def row_copy(rows, send, come, d, owner, target):
        place, half = core_pair(owner)
        return remote(
            rows.at[place, half], rows.at[place, half], send.at[d], come.at[d], "seq", target
        )

    for d in near:
        row_copy(in_rows, send_in, come_in, d, s, s ^ d).start()
    for d in near:
        row_copy(out_rows, send_out, come_out, d, s, s ^ d).start()
    for d in range(1, slices):
        for k in range(3):
            feed_copy(k, d, f, f ^ d).start()
    mine = pl.ds(pl.multiple_of(f * depth, depth), depth)
    for low, feed in feeds:
        feed[mine, :] = low[f]
    for d in near[1:]:
        row_copy(in_rows, send_in, come_in, d, s ^ d, s ^ d).wait_recv()
        row_copy(in_rows, pass_in, passed_in, d, s ^ d, s ^ 1).start()
    for d in near[1:]:
        row_copy(out_rows, send_out, come_out, d, s ^ d, s ^ d).wait_recv()
        row_copy(out_rows, pass_out, passed_out, d, s ^ d, s ^ 1).start()
    for rows, send, come, forward, passed in (
        (in_rows, send_in, come_in, pass_in, passed_in),
        (out_rows, send_out, come_out, pass_out, passed_out),
    ):
        row_copy(rows, send, come, 1, s ^ 1, s ^ 1).wait()
        for d in near[1:]:
            row_copy(rows, send, come, d, s, s ^ d).wait_send()
            row_copy(rows, forward, passed, d, s ^ d, s ^ 1).wait_send()
            row_copy(rows, forward, passed, d, s ^ 1 ^ d, s ^ 1).wait_recv()
    for d in range(1, slices):
        for k in range(3):
            feed_copy(k, d, f ^ d, f ^ d).wait()


def share_weights(w_inward, gain_columns, w_outward, w_gate_up, w_down, group, slices):
    depth = w_inward.shape[0]
    ff_cols = FF // slices
    feed = jax.ShapeDtypeStruct((slices * depth, ff_cols), jnp.bfloat16)
    low = pltpu.VMEM((slices, depth, ff_cols), jnp.bfloat16)
    rows = lambda width: jax.ShapeDtypeStruct((group // 2, 2, depth, width), jnp.bfloat16)
    sems = [pltpu.SemaphoreType.DMA((3, slices))] * 2 + [pltpu.SemaphoreType.DMA((group,))] * 8
    return pl.pallas_call(
        share_kernel,
        in_specs=[VMEM] * 5,
        out_specs=[VMEM] * 5,
        out_shape=[feed, feed, feed, rows(w_inward.shape[1] + 128), rows(w_outward.shape[1])],
        scratch_shapes=[low, low, low] + sems,
        compiler_params=pltpu.CompilerParams(
            vmem_limit_bytes=48 << 20, collective_id=2, has_side_effects=True
        ),
    )(w_inward, gain_columns, w_outward, w_gate_up, w_down)


def spread_copies(rows, full, send, come, forward, passed):
    s, f = lax.axis_index("seq"), lax.axis_index("fsdp")
    core = lax.rem(s, 2)
    slices = lax.axis_size("fsdp")

    def first(d, owner, target):
        return remote(
            rows.at[:, core], full.at[:, core, owner], send.at[d], come.at[d], "fsdp", target
        )

    def second(d, half):
        block = full.at[:, half, f ^ d]
        return remote(block, block, forward.at[d], passed.at[d], "seq", s ^ 1)

    def start():
        for d in range(1, slices):
            first(d, f, f ^ d).start()

    def local():
        full[:, :, f] = rows[...]

    def finish():
        for d in range(1, slices):
            first(d, f ^ d, f ^ d).wait_recv()
            second(d, core).start()
        for d in range(1, slices):
            first(d, f, f ^ d).wait_send()
            second(d, core).wait_send()
            second(d, 1 - core).wait_recv()

    return start, local, finish


def meet_spread(extra=()):
    barrier = pltpu.get_barrier_semaphore()
    s, f = lax.axis_index("seq"), lax.axis_index("fsdp")
    near = sorted({1, *extra})
    slices = lax.axis_size("fsdp")
    for d in near:
        pl.semaphore_signal(
            barrier, inc=1, device_id={"seq": s ^ d}, device_id_type=pl.DeviceIdType.MESH
        )
    for d in range(1, slices):
        pl.semaphore_signal(
            barrier, inc=1, device_id={"fsdp": f ^ d}, device_id_type=pl.DeviceIdType.MESH
        )
    pl.semaphore_wait(barrier, len(near) + slices - 1)


def spread_kernel(rows, full, send, come, forward, passed):
    meet_spread()
    start, local, finish = spread_copies(rows, full, send, come, forward, passed)
    start()
    local()
    finish()


def spread_rows(rows, slices):
    pairs, two, depth, width = rows.shape
    full = pl.pallas_call(
        spread_kernel,
        in_specs=[VMEM],
        out_specs=VMEM,
        out_shape=jax.ShapeDtypeStruct((pairs, two, slices, depth, width), rows.dtype),
        scratch_shapes=[pltpu.SemaphoreType.DMA((slices,))] * 4,
        compiler_params=pltpu.CompilerParams(
            vmem_limit_bytes=48 << 20, collective_id=3, has_side_effects=True
        ),
    )(rows)
    return full.reshape(pairs * two * slices * depth, width)


def forward_kernel(
    query_ref, kv_ref, out_rows, query_here, kv_here, mixed_here, logs, attended, out_full,
    send_query, come_query, send_kv, come_kv, send_out, come_out, local_sem,
    send_rows, come_rows, pass_rows, passed_rows, *, heads, block
):
    group = lax.axis_size("seq")
    me = lax.axis_index("seq")
    local, width = query_ref.shape[0], heads * HEAD_DIM
    pair = 2 * HEAD_DIM
    copies = group // KV_HEADS
    length = group * local
    per_block = block // local
    meet_spread(range(1, group))
    spread_start, spread_local, spread_finish = spread_copies(
        out_rows, out_full, send_rows, come_rows, pass_rows, passed_rows
    )

    def query_copy(d, owner, target):
        return remote(
            query_ref.at[:, pl.ds(pl.multiple_of(target * width, 128), width)],
            query_here.at[pl.ds(pl.multiple_of(owner * local, local), local), :],
            send_query.at[d], come_query.at[d], "seq", target,
        )

    def kv_copy(d, owner, target):
        return remote(
            kv_ref.at[:, pl.ds(pl.multiple_of(target // copies * pair, 128), pair)],
            kv_here.at[pl.ds(pl.multiple_of(owner * local, local), local), :],
            send_kv.at[d], come_kv.at[d], "seq", target,
        )

    def out_copy(d, owner, target):
        return remote(
            mixed_here.at[pl.ds(pl.multiple_of(target * local, local), local), :],
            attended.at[:, pl.ds(pl.multiple_of(owner * width, 128), width)],
            send_out.at[d], come_out.at[d], "seq", target,
        )

    for d in range(1, group):
        kv_copy(d, me, me ^ d).start()
        query_copy(d, me, me ^ d).start()
    spread_start()
    mine = pl.ds(pl.multiple_of(me * local, local), local)
    own_columns = pl.ds(pl.multiple_of(me * width, 128), width)
    own_query = pltpu.make_async_copy(
        query_ref.at[:, own_columns], query_here.at[mine, :], local_sem.at[0]
    )
    own_kv = pltpu.make_async_copy(
        kv_ref.at[:, pl.ds(pl.multiple_of(me // copies * pair, 128), pair)],
        kv_here.at[mine, :],
        local_sem.at[1],
    )
    own_query.start()
    own_kv.start()
    spread_local()
    own_query.wait()
    own_kv.wait()

    def query_block(index, _):
        for part in range(per_block):
            source = index * per_block + part

            @pl.when(source != me)
            def _():
                kv_copy(source ^ me, source, source).wait_recv()
                query_copy(source ^ me, source, source).wait_recv()

        place = pl.ds(pl.multiple_of(index * block, block), block)
        queries = stack_heads(query_here[place, :], heads) * jnp.bfloat16(HEAD_DIM**-0.5)
        columns = heads * block

        def step(j, carry, masked):
            largest, total, mixed = carry
            start = pl.multiple_of(j * block, block)
            kv = kv_here[pl.ds(start, block), :]
            keys, values = kv[:, :HEAD_DIM], kv[:, HEAD_DIM:]
            if masked:
                scores = masked_scores(keys, queries, block)
            else:
                scores = against(keys, queries)
            new = jnp.maximum(largest, jnp.max(scores, axis=0, keepdims=True))
            fade = jnp.exp(largest - new)
            weights = jnp.exp(scores - new)
            total = total * fade + jnp.sum(weights, axis=0, keepdims=True)
            mixed = mixed * fade + outer(values, weights.astype(jnp.bfloat16))
            return new, total, mixed

        carry = (
            jnp.full((1, columns), masked_value, jnp.float32),
            jnp.zeros((1, columns), jnp.float32),
            jnp.zeros((HEAD_DIM, columns), jnp.float32),
        )
        carry = lax.fori_loop(0, index, lambda j, c: step(j, c, False), carry)
        largest, total, mixed = step(index, carry, True)
        logs[index] = largest + jnp.log(total)
        mixed_here[place, :] = unstack_heads((mixed / total).T, heads).astype(mixed_here.dtype)
        for part in range(per_block):
            target = index * per_block + part

            @pl.when(target != me)
            def _():
                out_copy(target ^ me, me, target).start()

        return 0

    lax.fori_loop(0, length // block, query_block, 0)
    own_out = pltpu.make_async_copy(
        mixed_here.at[mine, :], attended.at[:, own_columns], local_sem.at[0]
    )
    own_out.start()
    own_out.wait()
    spread_finish()
    for d in range(1, group):
        other = me ^ d
        kv_copy(d, me, other).wait_send()
        query_copy(d, me, other).wait_send()
        out_copy(d, other, other).wait()


def backward_kernel(
    grad_ref, query_here, kv_here, mixed_here, logs, query_back, kv_back,
    grad_here, query_grad, kv_grad, key_sum, value_sum,
    send_grad, come_grad, send_query, come_query, send_kv, come_kv, local_sem, *, heads, block
):
    group = lax.axis_size("seq")
    me = lax.axis_index("seq")
    local, width = grad_ref.shape[0], heads * HEAD_DIM
    length = group * local
    per_block = block // local
    blocks = length // block
    scale = HEAD_DIM**-0.5
    barrier = pltpu.get_barrier_semaphore()
    for d in range(1, group):
        pl.semaphore_signal(
            barrier, inc=1, device_id={"seq": me ^ d}, device_id_type=pl.DeviceIdType.MESH
        )
    pl.semaphore_wait(barrier, group - 1)

    def grad_copy(d, owner, target):
        return remote(
            grad_ref.at[:, pl.ds(pl.multiple_of(target * width, 128), width)],
            grad_here.at[pl.ds(pl.multiple_of(owner * local, local), local), :],
            send_grad.at[d], come_grad.at[d], "seq", target,
        )

    def query_copy(d, owner, target):
        return remote(
            query_grad.at[pl.ds(pl.multiple_of(target * local, local), local), :],
            query_back.at[:, pl.ds(pl.multiple_of(owner * width, 128), width)],
            send_query.at[d], come_query.at[d], "seq", target,
        )

    def kv_copy(d, owner, target):
        return remote(
            kv_grad.at[pl.ds(pl.multiple_of(target * local, local), local), :],
            kv_back.at[owner],
            send_kv.at[d], come_kv.at[d], "seq", target,
        )

    for d in range(1, group):
        grad_copy(d, me, me ^ d).start()
    mine = pl.ds(pl.multiple_of(me * local, local), local)
    own_columns = pl.ds(pl.multiple_of(me * width, 128), width)
    own_grad = pltpu.make_async_copy(
        grad_ref.at[:, own_columns], grad_here.at[mine, :], local_sem.at[0]
    )
    own_grad.start()
    own_grad.wait()
    key_sum[...] = jnp.zeros_like(key_sum)
    value_sum[...] = jnp.zeros_like(value_sum)

    def query_block(turn, _):
        index = blocks - 1 - turn
        for part in range(per_block):
            source = index * per_block + part

            @pl.when(source != me)
            def _():
                grad_copy(source ^ me, source, source).wait_recv()

        place = pl.ds(pl.multiple_of(index * block, block), block)
        queries = stack_heads(query_here[place, :], heads) * jnp.bfloat16(scale)
        grads = stack_heads(grad_here[place, :], heads)
        mixed = stack_heads(mixed_here[place, :], heads)
        inner = jnp.sum(
            (grads.astype(jnp.float32) * mixed.astype(jnp.float32)).T, axis=0, keepdims=True
        )
        log_total = logs[index]

        def step(j, total, masked):
            start = pl.multiple_of(j * block, block)
            rows = pl.ds(start, block)
            kv = kv_here[rows, :]
            keys, values = kv[:, :HEAD_DIM], kv[:, HEAD_DIM:]
            if masked:
                scores = masked_scores(keys, queries, block)
            else:
                scores = against(keys, queries)
            shares = jnp.exp(scores - log_total)
            share_grad = against(values, grads)
            score_grad = (shares * (share_grad - inner)).astype(jnp.bfloat16)
            value_sum[rows, :] += dot(shares.astype(jnp.bfloat16), grads)
            key_sum[rows, :] += dot(score_grad, queries)
            return total + outer(keys, score_grad)

        total = lax.fori_loop(
            0,
            index,
            lambda j, c: step(j, c, False),
            jnp.zeros((HEAD_DIM, heads * block), jnp.float32),
        )
        total = step(index, total, True)
        query_grad[place, :] = unstack_heads((total * scale).T, heads).astype(jnp.bfloat16)
        kv_grad[place, :] = jnp.concatenate(
            [key_sum[place, :], value_sum[place, :]], axis=1
        ).astype(jnp.bfloat16)
        for part in range(per_block):
            target = index * per_block + part

            @pl.when(target != me)
            def _():
                query_copy(target ^ me, me, target).start()
                kv_copy(target ^ me, me, target).start()

        return 0

    lax.fori_loop(0, blocks, query_block, 0)
    own_query = pltpu.make_async_copy(
        query_grad.at[mine, :], query_back.at[:, own_columns], local_sem.at[0]
    )
    own_kv = pltpu.make_async_copy(kv_grad.at[mine, :], kv_back.at[me], local_sem.at[1])
    own_query.start()
    own_kv.start()
    own_query.wait()
    own_kv.wait()
    for d in range(1, group):
        other = me ^ d
        grad_copy(d, me, other).wait_send()
        query_copy(d, other, other).wait()
        kv_copy(d, other, other).wait()


def attend_forward(query, kv, out_rows, group, slices, heads, block):
    local, width = query.shape[0], heads * HEAD_DIM
    length = group * local
    pairs = heads * length * length // 2
    sems = pltpu.SemaphoreType.DMA((group,))
    pairs_seq, _, depth, _ = out_rows.shape
    return pl.pallas_call(
        functools.partial(forward_kernel, heads=heads, block=block),
        in_specs=[VMEM] * 3,
        out_specs=[VMEM] * 6,
        out_shape=[
            jax.ShapeDtypeStruct((length, width), jnp.bfloat16),
            jax.ShapeDtypeStruct((length, 2 * HEAD_DIM), jnp.bfloat16),
            jax.ShapeDtypeStruct((length, width), jnp.bfloat16),
            jax.ShapeDtypeStruct((length // block, 1, heads * block), jnp.float32),
            jax.ShapeDtypeStruct((local, group * width), jnp.bfloat16),
            jax.ShapeDtypeStruct(
                (pairs_seq, 2, slices, depth, out_rows.shape[3]), jnp.bfloat16
            ),
        ],
        scratch_shapes=[sems] * 6
        + [pltpu.SemaphoreType.DMA((2,))]
        + [pltpu.SemaphoreType.DMA((slices,))] * 4,
        compiler_params=pltpu.CompilerParams(
            vmem_limit_bytes=48 << 20, collective_id=0, has_side_effects=True
        ),
        cost_estimate=pl.CostEstimate(
            flops=pairs * HEAD_DIM * 60, bytes_accessed=length * 4 * width, transcendentals=pairs
        ),
    )(query, kv, out_rows)


def attend_backward(grads, query_here, kv_here, mixed_here, logs, group, heads, block):
    local, width = grads.shape[0], heads * HEAD_DIM
    length = group * local
    pairs = heads * length * length // 2
    sems = pltpu.SemaphoreType.DMA((group,))
    return pl.pallas_call(
        functools.partial(backward_kernel, heads=heads, block=block),
        in_specs=[VMEM] * 5,
        out_specs=[VMEM] * 2,
        out_shape=[
            jax.ShapeDtypeStruct((local, group * width), jnp.bfloat16),
            jax.ShapeDtypeStruct((group, local, 2 * HEAD_DIM), jnp.bfloat16),
        ],
        scratch_shapes=[
            pltpu.VMEM((length, width), jnp.bfloat16),
            pltpu.VMEM((length, width), jnp.bfloat16),
            pltpu.VMEM((length, 2 * HEAD_DIM), jnp.bfloat16),
            pltpu.VMEM((length, HEAD_DIM), jnp.float32),
            pltpu.VMEM((length, HEAD_DIM), jnp.float32),
        ]
        + [sems] * 6
        + [pltpu.SemaphoreType.DMA((2,))],
        compiler_params=pltpu.CompilerParams(
            vmem_limit_bytes=48 << 20, collective_id=1, has_side_effects=True
        ),
        cost_estimate=pl.CostEstimate(
            flops=pairs * HEAD_DIM * 4, bytes_accessed=length * 8 * width, transcendentals=pairs
        ),
    )(grads, query_here, kv_here, mixed_here, logs)


def swap(piece, axis, offset):
    size = lax.axis_size(axis)
    return lax.ppermute(piece, axis, [(i, i ^ offset) for i in range(size)])


def gather_swap(piece, axis):
    return [piece] + [swap(piece, axis, d) for d in range(1, lax.axis_size(axis))]


def exchange_swap(stack, axis):
    me = lax.axis_index(axis)
    pieces = [
        lax.dynamic_index_in_dim(stack, me ^ d, 0, keepdims=False)
        for d in range(lax.axis_size(axis))
    ]
    return [pieces[0]] + [swap(p, axis, d) for d, p in enumerate(pieces) if d]


def reduce_swap(parts, axis):
    total = parts[0].astype(jnp.float32)
    for d in range(1, len(parts)):
        total = total + swap(parts[d], axis, d).astype(jnp.float32)
    return total


def in_order(pieces, axis):
    me = lax.axis_index(axis)
    stack = jnp.stack(pieces)
    return [
        lax.dynamic_index_in_dim(stack, j ^ me, 0, keepdims=False) for j in range(len(pieces))
    ]


def scatter_rows(partial, after=()):
    partial, *_ = lax.optimization_barrier((partial, *after))
    return lax.psum_scatter(partial, "seq", scatter_dimension=0, tiled=True)


def return_columns(mine):
    size = lax.axis_size("fsdp")
    stack = mine.reshape(size, mine.shape[0] // size, mine.shape[1])
    return in_order(exchange_swap(stack, "fsdp"), "fsdp")


def adam_update(weight, first, second, grad, rate, decay):
    first_new = beta_first * first + (1.0 - beta_first) * grad
    second_new = beta_second * second + (1.0 - beta_second) * grad * grad
    first_hat = first_new / (1.0 - beta_first**STEP)
    second_hat = second_new / (1.0 - beta_second**STEP)
    weight_new = weight - rate * (
        first_hat / (jnp.sqrt(second_hat) + adam_epsilon) + decay * weight
    )
    return (first_new, second_new, weight_new)


def body(
    inputs,
    cotangent,
    w_inward,
    w_outward,
    w_gate_up,
    w_down,
    gains,
    first_inward,
    first_outward,
    first_gate_up,
    first_down,
    first_gains,
    second_inward,
    second_outward,
    second_gate_up,
    second_down,
    second_gains,
):
    rows = inputs[0].astype(jnp.float32)
    upstream = cotangent[0]
    local = rows.shape[0]
    group = lax.axis_size("seq")
    slices = lax.axis_size("fsdp")
    heads_here = HEADS // group
    copies = group // KV_HEADS
    kv_width = KV_HEADS * HEAD_DIM
    head_cols = heads_here * HEAD_DIM
    inward_cols = D + 2 * kv_width
    ff_cols = FF // slices
    depth = w_inward.shape[0]
    position = (lax.axis_index("seq") * local + jnp.arange(local)).astype(jnp.float32)

    low_gains = jnp.pad(jnp.transpose(gains.astype(jnp.bfloat16)), ((0, 0), (0, 126)))
    feed_gate, feed_up, feed_down, in_rows, out_rows = share_weights(
        w_inward, low_gains, w_outward, w_gate_up, w_down, group, slices
    )
    gate_slice = lax.all_gather(feed_gate, "seq", axis=0, tiled=True)
    up_slice = lax.all_gather(feed_up, "seq", axis=0, tiled=True)
    down_slice = lax.all_gather(feed_down, "seq", axis=0, tiled=True)
    inward_gains = spread_rows(in_rows, slices)
    inward_full = inward_gains[:, :inward_cols]
    gain_first = inward_gains[:, inward_cols].astype(jnp.float32)
    gain_second = inward_gains[:, inward_cols + 1].astype(jnp.float32)

    scale_first = rms_scale(rows)
    normed = (rows * scale_first * gain_first).astype(jnp.bfloat16)
    mixed = dot(normed, inward_full)
    query = rotate(mixed[:, :D].reshape(local, HEADS, HEAD_DIM), position, 1.0).astype(jnp.bfloat16)
    key = rotate(
        mixed[:, D : D + kv_width].reshape(local, KV_HEADS, HEAD_DIM), position, 1.0
    ).astype(jnp.bfloat16)
    value = mixed[:, D + kv_width :].reshape(local, KV_HEADS, HEAD_DIM).astype(jnp.bfloat16)
    kv = jnp.concatenate([key, value], axis=-1).reshape(local, 2 * kv_width)
    length = group * local
    block = min(512, length)
    query_here, kv_here, mixed_here, logs, attended, outward_full = attend_forward(
        query.reshape(local, D), kv, out_rows, group, slices, heads_here, block
    )
    outward_full = outward_full.reshape(D, D)
    upstream_blocks = gather_swap(upstream, "fsdp")
    attended, upstream_blocks = lax.optimization_barrier((attended, upstream_blocks))
    upstream_all = jnp.concatenate(upstream_blocks, axis=0)
    middle = rows + dot(attended, outward_full)
    scale_second = rms_scale(middle)
    normed_second = (middle * scale_second * gain_second).astype(jnp.bfloat16)

    normed_all = jnp.concatenate(gather_swap(normed_second, "fsdp"), axis=0)
    gate = dot(normed_all, gate_slice)
    up_part = dot(normed_all, up_slice)
    sigmoid = jax.nn.sigmoid(gate)
    hidden = (gate * sigmoid * up_part).astype(jnp.bfloat16)
    down_partial = outer(upstream_all, hidden).astype(jnp.bfloat16)
    upstream_late, down_partial = lax.optimization_barrier((upstream_all, down_partial))
    hidden_grad = dot(upstream_late, down_slice)
    gate_grad = hidden_grad * up_part * sigmoid * (1.0 + gate * (1.0 - sigmoid))
    gate_grad = gate_grad.astype(jnp.bfloat16)
    up_grad = (hidden_grad * gate * sigmoid).astype(jnp.bfloat16)

    def send_back(part):
        part = part.astype(jnp.bfloat16)
        parts = [part[d * local : (d + 1) * local] for d in range(slices)]
        return [parts[0]] + [swap(p, "fsdp", d) for d, p in enumerate(parts) if d]

    def add_up(parts):
        return functools.reduce(jnp.add, [p.astype(jnp.float32) for p in parts])

    back_parts = send_back(against(gate_grad, gate_slice) + against(up_grad, up_slice))
    attended_blocks = gather_swap(attended, "fsdp")
    gate_grad, attended_blocks = lax.optimization_barrier((gate_grad, attended_blocks))
    gate_partial = outer(normed_all, gate_grad).astype(jnp.bfloat16)
    up_partial = outer(normed_all, up_grad).astype(jnp.bfloat16)
    back_parts, hidden, gate_partial, up_partial = lax.optimization_barrier(
        (back_parts, hidden, gate_partial, up_partial)
    )
    normed_second_grad = add_up(back_parts)
    down_mine = scatter_rows(down_partial)
    gate_mine = scatter_rows(gate_partial)
    up_mine = scatter_rows(up_partial)
    middle_back, gain_second_grad = norm_back(middle, scale_second, gain_second, normed_second_grad)
    middle_grad = upstream.astype(jnp.float32) + middle_back
    branch_low = middle_grad.astype(jnp.bfloat16)
    branch_low, down_mine = lax.optimization_barrier((branch_low, down_mine))
    attended_grad = against(branch_low, outward_full).astype(jnp.bfloat16)
    attended_grad, gate_mine = lax.optimization_barrier((attended_grad, gate_mine))
    query_back, kv_back = attend_backward(
        attended_grad, query_here, kv_here, mixed_here, logs, group, heads_here, block
    )
    first_blocks = gather_swap(normed, "fsdp")
    query_back, kv_back, up_mine, first_blocks = lax.optimization_barrier(
        (query_back, kv_back, up_mine, first_blocks)
    )
    query_grad = rotate(
        query_back.astype(jnp.float32).reshape(local, HEADS, HEAD_DIM), position, -1.0
    )
    kv_grad = kv_back.astype(jnp.float32).reshape(KV_HEADS, copies, local, 2 * HEAD_DIM)
    kv_grad = jnp.sum(kv_grad, axis=1).transpose(1, 0, 2)
    key_grad = rotate(kv_grad[:, :, :HEAD_DIM], position, -1.0)
    value_grad = kv_grad[:, :, HEAD_DIM:]
    inward_grad = jnp.concatenate(
        [
            query_grad.reshape(local, D),
            key_grad.reshape(local, kv_width),
            value_grad.reshape(local, kv_width),
        ],
        axis=-1,
    ).astype(jnp.bfloat16)
    normed_grad = against(inward_grad, inward_full)
    rows_back, gain_first_grad = norm_back(rows, scale_first, gain_first, normed_grad)
    input_grad = middle_grad + rows_back

    def column_slices(field):
        width = field.shape[1] // slices
        return field.reshape(local, slices, width).transpose(1, 0, 2)

    attended_all = jnp.concatenate(attended_blocks, axis=0)
    branch_all = jnp.concatenate(exchange_swap(column_slices(branch_low), "fsdp"), axis=0)
    outward_mine = scatter_rows(outer(attended_all, branch_all).astype(jnp.bfloat16))
    first_all = jnp.concatenate(first_blocks, axis=0)
    inward_grad_all = jnp.concatenate(exchange_swap(column_slices(inward_grad), "fsdp"), axis=0)
    gain_grads = jnp.stack([gain_first_grad, gain_second_grad], axis=1)
    gain_grads = jnp.pad(gain_grads.astype(jnp.bfloat16), ((0, 0), (0, 126)))
    inward_partial = outer(first_all, inward_grad_all).astype(jnp.bfloat16)
    slice_cols = inward_partial.shape[1]
    inward_mine = scatter_rows(
        jnp.concatenate([inward_partial, gain_grads], axis=1), (outward_mine,)
    )
    result = middle + add_up(send_back(against(hidden, down_slice)))
    down_back = return_columns(down_mine)
    gate_back = return_columns(gate_mine)
    up_back = return_columns(up_mine)
    outward_back = return_columns(outward_mine)
    inward_back = return_columns(inward_mine)

    gains_sum = add_up([piece[:, slice_cols : slice_cols + 2] for piece in inward_back])
    gains_sum = jnp.transpose(gains_sum)
    inward_back = [piece[:, :slice_cols] for piece in inward_back]
    inward_sum = jnp.concatenate(inward_back, axis=1).astype(jnp.float32)
    outward_sum = jnp.concatenate(outward_back, axis=1).astype(jnp.float32)
    gate_up_sum = jnp.concatenate(gate_back + up_back, axis=1).astype(jnp.float32)
    down_sum = jnp.concatenate(down_back, axis=1).astype(jnp.float32)
    first_inward_new, second_inward_new, inward_new = adam_update(
        w_inward, first_inward, second_inward, inward_sum, 0.02, weight_decay
    )
    first_outward_new, second_outward_new, outward_new = adam_update(
        w_outward, first_outward, second_outward, outward_sum, 0.15, weight_decay
    )
    first_gate_up_new, second_gate_up_new, gate_up_new = adam_update(
        w_gate_up, first_gate_up, second_gate_up, gate_up_sum, 0.02, weight_decay
    )
    first_down_new, second_down_new, down_new = adam_update(
        w_down, first_down, second_down, down_sum, 0.015, weight_decay
    )
    first_gains_new, second_gains_new, gains_new = adam_update(
        gains, first_gains, second_gains, gains_sum, 0.6, 0.0
    )
    return (
        result[None].astype(jnp.bfloat16),
        input_grad[None],
        first_inward_new,
        second_inward_new,
        inward_new,
        first_outward_new,
        second_outward_new,
        outward_new,
        first_gate_up_new,
        second_gate_up_new,
        gate_up_new,
        first_down_new,
        second_down_new,
        down_new,
        first_gains_new,
        second_gains_new,
        gains_new,
    )


def solution(mesh):
    in_specs = (
        P("fsdp", "seq", None),
        P("fsdp", "seq", None),
        P(("seq", "fsdp"), None),
        P(("seq", "fsdp"), None),
        P(("seq", "fsdp"), None),
        P(("seq", "fsdp"), None),
        P(None, ("seq", "fsdp")),
        P(("seq", "fsdp"), None),
        P(("seq", "fsdp"), None),
        P(("seq", "fsdp"), None),
        P(("seq", "fsdp"), None),
        P(None, ("seq", "fsdp")),
        P(("seq", "fsdp"), None),
        P(("seq", "fsdp"), None),
        P(("seq", "fsdp"), None),
        P(("seq", "fsdp"), None),
        P(None, ("seq", "fsdp")),
    )
    out_specs = (
        P("fsdp", "seq", None),
        P("fsdp", "seq", None),
        P(("seq", "fsdp"), None),
        P(("seq", "fsdp"), None),
        P(("seq", "fsdp"), None),
        P(("seq", "fsdp"), None),
        P(("seq", "fsdp"), None),
        P(("seq", "fsdp"), None),
        P(("seq", "fsdp"), None),
        P(("seq", "fsdp"), None),
        P(("seq", "fsdp"), None),
        P(("seq", "fsdp"), None),
        P(("seq", "fsdp"), None),
        P(("seq", "fsdp"), None),
        P(None, ("seq", "fsdp")),
        P(None, ("seq", "fsdp")),
        P(None, ("seq", "fsdp")),
    )
    return jax.shard_map(body, mesh=mesh, in_specs=in_specs, out_specs=out_specs, check_vma=False)
```

time: 1070 us -> 827 us (0.77)
  waiting for transfers between devices: 678 us -> 165 us
  Pallas kernels: 52.2 us -> 369 us
  blocking collectives: 39 us -> 0 us
  starting transfers between devices: 65 us -> 36 us
    reduce_scatter x4 -> x5, waiting for transfers between devices: 215 us -> 21.4 us  [scatter_rows(): return lax.psum_scatter(partial, 'seq', scatter_dimension=0, tiled=True)]
    pallas_call x0 -> x2, Pallas kernels: none -> 176 us  [the longest x1 112 us: spread_rows(): pl.pallas_call(spread_kernel, in_specs=[VMEM], out_specs=VMEM, out_shape=...]
    all_to_all x4 -> x0, waiting for transfers between devices: 142 us -> none  [the longest x1 62.2 us: body(): arrived = lax.all_to_all(packed, 'seq', 0, 0, tiled=True)]
    pallas_call x1, Pallas kernels: 18.9 us -> 106 us  [attend_forward(): pl.pallas_call(functools.partial(forward_kernel, heads=heads, block=block...]
    all_gather x4 -> x3, waiting for transfers between devices: 77.5 us -> 0.02 us  [the longest x1 0.02 us: body(): down_slice = lax.all_gather(feed_down, 'seq', axis=0, tiled=True)]
    ppermute x36 -> x39, waiting for transfers between devices: 197 us -> 142 us  [swap(): return lax.ppermute(piece, axis, [(i, i ^ offset) for i in range(size)])]
    pallas_call x1, Pallas kernels: 33.3 us -> 86.5 us  [attend_backward(): pl.pallas_call(functools.partial(backward_kernel, heads=heads, block=bloc...]
    unnamed x10 -> x8, waiting for transfers between devices: 46 us -> 1.32 us
  transfers between devices with their start and end apart: 49 -> 47, of which waited for: 34 -> 14; matrix products, arithmetic and copies ran while one was open for 15% -> 25% of each run, Pallas kernels for 5% -> 38%
where the time goes in v2:
time: 827 us; the launch traced here: 812 us
  Pallas kernels  369 us (45%)
  waiting for transfers between devices  165 us (20%)
  matrix products  137 us (17%)
  local copies, waits for them, and re-layouts  51.9 us (6%)
  other arithmetic  37.8 us (5%)
  starting transfers between devices  36 us (4%)
  between operations  15.5 us (2%)
    ppermute x39, waiting for transfers between devices, swap(): return lax.ppermute(piece, axis, [(i, i ^ offset) for i in range(size)])  142 us
    pallas_call x1, Pallas kernels, spread_rows(): pl.pallas_call(spread_kernel, in_specs=[VMEM], out_specs=VMEM, out_shape=...  112 us
    pallas_call x1, Pallas kernels, attend_forward(): pl.pallas_call(functools.partial(forward_kernel, heads=heads, block=block...  106 us
    pallas_call x1, Pallas kernels, attend_backward(): pl.pallas_call(functools.partial(backward_kernel, heads=heads, block=bloc...  86.5 us
    pallas_call x1, Pallas kernels, share_weights(): pl.pallas_call(share_kernel, in_specs=[VMEM] * 5, out_specs=[VMEM] * 5, o...  64 us
    dot_general x5, matrix products, dot(): return jnp.dot(left, right, preferred_element_type=jnp.float32)  53.2 us
    dot_general x5, matrix products, against(): lax.dot_general(left, right, (((1,), (1,)), ((), ())), preferred_element_...  42.8 us
    dot_general x5, matrix products, outer(): lax.dot_general(left, right, (((0,), (0,)), ((), ())), preferred_element_...  41.1 us
  transfers between devices with their start and end apart: 47, of which 14 were waited for; matrix products, arithmetic and copies ran while one was open for 25% of the time, Pallas kernels for 38%

profile of v2, /device:TPU:9, one launch (start us, length us, event | category | flops | bytes accessed | tf_op | source)
XLA Modules:
  0.0 812.0 jit_solution(11246327006273031309)
XLA Ops:
  8.1 1.4 copy-done
  11.5 64.0 %shard_map.296 = (bf16[256,1408]{1,0:T(8,128)(2,1)}, bf16[256,1408]{1,0:T(8,128)(2,1)}, bf16[256,1408]{1,0:T(8,128)(2,1)}, bf16[4,2,64,2688]{3,2,1,0:T(8,128)(2,1)}, bf16[4,2,64,2048]{3,2,1,0:T(8,128)(2,1)}) custom-call(f32[64,2560]{1,0:T(8,128)S(1)} %copy-done.3, bf16[64,128]{1,0:T(8,128)(2,1)S(1)} %pad.8.gain_ref, f32[64,2048]{1,0:T(8,128)S(1)} %copy-done.5, ...), custom_call_target="tpu_custom_call" | custom-call | tf_op jit(solution)/shard_map/pallas_call | solution.py:192
  79.1 1.8 copy-done.2
  80.9 112.1 %shard_map.297 = bf16[4,2,4,64,2688]{4,3,2,1,0:T(8,128)(2,1)} custom-call(bf16[4,2,64,2688]{3,2,1,0:T(8,128)(2,1)S(1)} %copy-done.2), custom_call_target="tpu_custom_call" | custom-call | tf_op jit(solution)/shard_map/pallas_call | solution.py:263
  193.0 2.5 slice_convert_fusion
  198.6 5.9 fusion.2
  204.5 1.6 slice.130
  206.8 1.9 copy.115
  212.3 106.4 %shard_map.298 = (bf16[2048,256]{1,0:T(8,128)(2,1)S(1)}, bf16[2048,128]{1,0:T(8,128)(2,1)S(1)}, bf16[2048,256]{1,0:T(8,128)(2,1)S(1)}, f32[4,1,2048]{2,1,0:T(1,1...) custom-call(bf16[256,2048]{1,0:T(8,128)(2,1)S(1)} %copy.125.query_ref, ...), custom_call_target="tpu_custom_call" | custom-call | flops 32212254720 | bytes 2097152 | tf_op jit(solution)/shard_map/pallas_call | solution.py:524
  321.4 1.6 copy.162
  323.0 6.1 multiply_reduce_fusion.2
  329.4 1.6 collective-permute-start.5
  334.0 1.3 constant_dynamic-update-slice_fusion.2
  335.3 1.3 constant_dynamic-update-slice_fusion.1
  336.6 1.3 constant_dynamic-update-slice_fusion
  337.9 16.6 %collective-permute-done.5 = bf16[256,2048]{1,0:T(8,128)(2,1)S(1)} collective-permute-done((bf16[256,2048]{1,0:T(8,128)(2,1)S(1)}, bf16[256,2048]{1,0:T(8,128)(2,1)S(1)}, u32[]{:S(2)}, u32[]{:S(2)}) %collective-permute-start.5) | collective-permute-done | bytes 1048608 | tf_op jit(solution)/shard_map/ppermute | solution.py:583
  355.7 22.3 %collective-permute-done.4 = bf16[256,2048]{1,0:T(8,128)(2,1)S(1)} collective-permute-done((bf16[256,2048]{1,0:T(8,128)(2,1)S(1)}, bf16[256,2048]{1,0:T(8,128)(2,1)S(1)}, u32[]{:S(2)}, u32[]{:S(2)}) %collective-permute-start.4) | collective-permute-done | bytes 1048608 | tf_op jit(solution)/shard_map/ppermute | solution.py:583
  379.0 12.9 %fusion.67 = f32[1024,1408]{1,0:T(8,128)} fusion(bf16[2048,1408]{1,0:T(8,128)(2,1)} %all-gather.4.cloned.1.call-done, bf16[256,2048]{1,0:T(8,128)(2,1)} %copy-done.54, bf16[256,2048]{1,0:T(8,128)(2,1)} %copy-done.56, bf16[256,2048]{1,0:T(8,128)(2,1)} %collective-permute-done.3, bf16[256,2048]{1,0:T(8,128)(2,1)} %copy-done.30), kind=kOutput, calls=%fused_computation.197 | convolution fusion | flops 5922357248 | bytes 15728640 | tf_op jit(solution)/shard_map/dot_general | solution.py:55
  391.9 14.0 %multiply_convert_fusion.2 = (bf16[1024,1408]{1,0:T(8,128)(2,1)S(1)}, f32[1024,1408]{1,0:T(8,128)}) fusion(f32[1024,1408]{1,0:T(8,128)} %fusion.67, bf16[2048,1408]{1,0:T(8,128)(2,1)} %all-gather.6.cloned.1.call-done, bf16[256,2048]{1,0:T(8,128)(2,1)} %copy-done.54, bf16[256,2048]{1,0:T(8,128)(2,1)} %copy-done.56, ...), kind=kOutput, calls=%fused_computation.10 | convolution fusion | flops 5931008000 | bytes 24379392 | tf_op jit(solution)/shard_map/dot_general | solution.py:55
  405.9 1.6 copy-done.59
  407.5 8.7 %convolution_convert_fusion.2 = bf16[2048,1408]{1,0:T(8,128)(2,1)} fusion(bf16[1024,2048]{1,0:T(8,128)(2,1)S(1)} %copy-done.44, bf16[1024,1408]{1,0:T(8,128)(2,1)S(1)} %get-tuple-element.75), kind=kOutput, calls=%fused_computation.7 | convolution fusion | flops 5908463616 | bytes 12845056 | tf_op jit(solution)/shard_map/dot_general | solution.py:59
  416.2 14.3 %multiply_convert_fusion = (bf16[1024,1408]{1,0:T(8,128)(2,1)S(1)}, bf16[1024,1408]{1,0:T(8,128)(2,1)S(1)}) fusion(f32[1024,1408]{1,0:T(8,128)} %fusion.67, f32[1024,1408]{1,0:T(8,128)} %get-tuple-element.249, bf16[1024,2048]{1,0:T(8,128)(2,1)} %copy-done.43, bf16[2048,1408]{1,0:T(8,128)(2,1)} %all-gather.8.cloned.1.call-done), kind=kOutput, calls=%fused_computation.8 | convolution fusion | flops 5924323328 | bytes 27262976 | tf_op jit(solution)/shard_map/dot_general | solution.py:55
  430.5 9.8 %fusion.82 = f32[1024,2048]{1,0:T(8,128)S(1)} fusion(bf16[1024,1408]{1,0:T(8,128)(2,1)S(1)} %get-tuple-element.74, bf16[2048,1408]{1,0:T(8,128)(2,1)} %all-gather.4.cloned.1.call-done), kind=kOutput, calls=%fused_computation.202 | convolution fusion | flops 5905580032 | bytes 17039360 | tf_op jit(solution)/shard_map/dot_general | solution.py:65
  440.3 8.8 %add_convert_fusion = bf16[1024,2048]{1,0:T(8,128)(2,1)S(1)} fusion(f32[1024,2048]{1,0:T(8,128)S(1)} %fusion.82, bf16[1024,1408]{1,0:T(8,128)(2,1)S(1)} %get-tuple-element.177, bf16[2048,1408]{1,0:T(8,128)(2,1)} %all-gather.6.cloned.1.call-done), kind=kOutput, calls=%fused_computation.4 | convolution fusion | flops 5909774336 | bytes 21233664 | tf_op jit(solution)/shard_map/dot_general | solution.py:65
  449.2 2.3 fusion.80
  454.1 10.2 %convolution_convert_fusion = bf16[2048,1408]{1,0:T(8,128)(2,1)} fusion(bf16[1024,1408]{1,0:T(8,128)(2,1)S(1)} %get-tuple-element.177, bf16[256,2048]{1,0:T(8,128)(2,1)S(1)} %copy-done.55, bf16[256,2048]{1,0:T(8,128)(2,1)S(1)} %copy-done.57, bf16[256,2048]{1,0:T(8,128)(2,1)} %collective-permute-done.3, bf16[256,2048]{1,0:T(8,128)(2,1)S(1)} %copy-done.31), kind=kOutput, calls=%fused_computation.5 | convolution fusion | flops 5925240832 | bytes 12845056 | tf_op jit(solution)/shard_map/dot_general | solution.py:59
  464.3 11.3 %convolution_convert_fusion.1 = bf16[2048,1408]{1,0:T(8,128)(2,1)} fusion(bf16[1024,1408]{1,0:T(8,128)(2,1)} %copy-done.58, bf16[256,2048]{1,0:T(8,128)(2,1)} %copy-done.54, bf16[256,2048]{1,0:T(8,128)(2,1)} %copy-done.56, bf16[256,2048]{1,0:T(8,128)(2,1)} %collective-permute-done.3, bf16[256,2048]{1,0:T(8,128)(2,1)} %copy-done.30), kind=kOutput, calls=%fused_computation.6 | convolution fusion | flops 5925240832 | bytes 12845056 | tf_op jit(solution)/shard_map/dot_general | solution.py:59
  476.3 22.5 %collective-permute-done.8 = bf16[256,2048]{1,0:T(8,128)(2,1)} collective-permute-done((bf16[256,2048]{1,0:T(8,128)(2,1)}, bf16[256,2048]{1,0:T(8,128)(2,1)}, u32[]{:S(2)}, u32[]{:S(2)}) %collective-permute-start.8) | collective-permute-done | bytes 1048608 | tf_op jit(solution)/shard_map/ppermute | solution.py:583
  499.5 9.6 %convolution_convert_fusion.3 = bf16[1024,2048]{1,0:T(8,128)(2,1)S(1)} fusion(bf16[1024,1408]{1,0:T(8,128)(2,1)} %copy-done.59, bf16[2048,1408]{1,0:T(8,128)(2,1)} %all-gather.8.cloned.1.call-done), kind=kOutput, calls=%fused_computation.36 | convolution fusion | flops 5907677184 | bytes 12845056 | tf_op jit(solution)/shard_map/dot_general | solution.py:65
  509.2 1.8 fusion.79
  516.3 3.4 multiply_reduce_fusion
  519.8 16.5 %collective-permute-done.14 = bf16[256,2048]{1,0:T(8,128)(2,1)} collective-permute-done((bf16[256,2048]{1,0:T(8,128)(2,1)}, bf16[256,2048]{1,0:T(8,128)(2,1)}, u32[]{:S(2)}, u32[]{:S(2)}) %collective-permute-start.14) | collective-permute-done | bytes 1048608 | tf_op jit(solution)/shard_map/ppermute | solution.py:583
  536.3 24.6 %collective-permute-done.13 = bf16[256,2048]{1,0:T(8,128)(2,1)} collective-permute-done((bf16[256,2048]{1,0:T(8,128)(2,1)}, bf16[256,2048]{1,0:T(8,128)(2,1)}, u32[]{:S(2)}, u32[]{:S(2)}) %collective-permute-start.13) | collective-permute-done | bytes 1048608 | tf_op jit(solution)/shard_map/ppermute | solution.py:583
  560.9 5.3 fusion.78
  566.2 2.0 constant_dynamic-slice_fusion
  570.8 6.1 convolution_convert_fusion.4.grad_ref
  576.9 2.4 reshape.259
  579.4 2.2 constant_dynamic-slice_fusion.8
  581.7 3.0 collective-permute-done.38
  584.8 1.4 collective-permute-start.17
  586.1 7.1 collective-permute-done.37
  596.3 19.6 %collective-permute-done.23 = bf16[256,512]{1,0:T(8,128)(2,1)S(1)} collective-permute-done((bf16[256,512]{1,0:T(8,128)(2,1)S(1)}, bf16[256,512]{1,0:T(8,128)(2,1)S(1)}, u32[]{:S(2)}, u32[]{:S(2)}) %collective-permute-start.23) | collective-permute-done | bytes 262176 | tf_op jit(solution)/shard_map/ppermute | solution.py:583
  617.0 2.8 multiply_subtract_fusion.1
  619.9 5.0 collective-permute-done.22
  624.9 5.6 fusion.23
  634.1 86.5 %shard_map.299 = (bf16[256,2048]{1,0:T(8,128)(2,1)S(1)}, bf16[8,256,128]{2,1,0:T(8,128)(2,1)S(1)}) custom-call(bf16[256,2048]{1,0:T(8,128)(2,1)S(1)} %convolution_convert_fusion.4.grad_ref, bf16[2048,256]{1,0:T(8,128)(2,1)S(1)} %copy-done.8, bf16[2048,128]{1,0:T(8,128)(2,1)S(1)} %copy-done.12, bf16[2048,256]{1,0:T(8,128)(2,1)S(1)} %copy-done.10, ...), custom_call_target="tpu_custom_call" | custom-call | flops 2147483648 | bytes 4194304 | tf_op jit(solution)/shard_map/pallas_call | solution.py:555
  725.2 2.0 copy.152
  730.3 1.3 collective-permute-start.18
  731.6 2.0 constant_dynamic-slice_fusion.2
  733.6 8.5 %fusion.37 = (bf16[2048]{0:T(1024)(128)(2,1)S(1)}, f32[256]{0:T(256)S(1)}, f32[256,2048]{1,0:T(8,128)}) fusion(bf16[1,256,2048]{2,1,0:T(8,128)(2,1)S(1)} %copy-done.15, f32[256]{0:T(256)S(1)} %copy-done.49, f32[2048]{0:T(1024)S(1)} %bitcast.210, bf16[2048,2688]{1,0:T(8,128)(2,1)} %bitcast.168, bf16[256,256]{0,1:T(8,128)(2,1)S(1)} %bitcast.188, ...), kind=kOutput, calls=%fused_computation.56 | convolution fusion | flops 2691954432 | bytes 14956544 | tf_op jit(solution)/shard_map/dot_general | solution.py:65
  743.8 1.4 collective-permute-start.30
  745.2 5.4 fusion.20
  750.5 2.0 pad_maximum_fusion.1
  752.5 1.4 constant_dynamic-slice_fusion.1
  755.4 3.6 fusion.34
  759.0 1.3 collective-permute-start.33
  760.3 1.4 pad_maximum_fusion.4
  761.8 2.8 collective-permute-done.34
  767.6 5.2 multiply_subtract_fusion
  772.9 21.4 %reduce-scatter.14.cloned.1.call-done = bf16[256,768]{0,1:T(8,128)(2,1)} async-done(((bf16[2048,768]{0,1:T(8,128)(2,1)}), bf16[256,768]{0,1:T(8,128)(2,1)}) %reduce-scatter.14.cloned.1.call-update) | async-done | bytes 393232 | tf_op jit(solution)/shard_map/reduce_scatter | solution.py:616
  795.5 2.2 collective-permute-start.26
  798.2 2.6 multiply_subtract_fusion.4
  800.8 1.3 collective-permute-done.25
  802.8 1.6 multiply_subtract_fusion.3
  (287 shorter events, 58.9 us)
Async XLA Ops:
  7.2 371.8 %all-gather.4.cloned.1.call-start = ((), (), s32[]{:S(2)}) async-start(), calls=%async_computation.5 | async-start | bytes 6488064 | tf_op jit(solution)/shard_map/all_gather | solution.py:673
  75.5 316.4 %all-gather.6.cloned.1.call-start = ((), (), s32[]{:S(2)}) async-start(), calls=%async_computation.6 | async-start | bytes 6488064 | tf_op jit(solution)/shard_map/all_gather | solution.py:674
  76.3 339.9 %all-gather.8.cloned.1.call-start = ((), (), s32[]{:S(2)}) async-start(), calls=%async_computation.7 | async-start | bytes 6488064 | tf_op jit(solution)/shard_map/all_gather | solution.py:675
  76.3 246.7 %collective-permute-start = (bf16[256,2048]{1,0:T(8,128)(2,1)}, bf16[256,2048]{1,0:T(8,128)(2,1)}, u32[]{:S(2)}, u32[]{:S(2)}) collective-permute-start(bf16[256,2048]{1,0:T(8,128)(2,1)} %bitcast.177), channel_id=1, source_target_pairs={{0,1},{1,0},{2,3},{3,2},{4,5},{5,4},{6,7},{7,6},{8,9},{9,8},{10,11... | collective-permute-start | bytes 3145736 | tf_op jit(solution)/shard_map/ppermute | solution.py:583
  76.7 246.3 %collective-permute-start.1 = (bf16[256,2048]{1,0:T(8,128)(2,1)}, bf16[256,2048]{1,0:T(8,128)(2,1)}, u32[]{:S(2)}, u32[]{:S(2)}) collective-permute-start(bf16[256,2048]{1,0:T(8,128)(2,1)} %bitcast.178), channel_id=1, source_target_pairs={{0,2},{1,3},{2,0},{3,1},{4,6},{5,7},{6,4},{7,5},{8,10},{9,11},{10,... | collective-permute-start | bytes 3145736 | tf_op jit(solution)/shard_map/ppermute | solution.py:583
  77.9 245.1 %collective-permute-start.2 = (bf16[256,2048]{1,0:T(8,128)(2,1)}, bf16[256,2048]{1,0:T(8,128)(2,1)}, u32[]{:S(2)}, u32[]{:S(2)}) collective-permute-start(bf16[256,2048]{1,0:T(8,128)(2,1)} %bitcast.179), channel_id=1, source_target_pairs={{0,3},{1,2},{2,1},{3,0},{4,7},{5,6},{6,5},{7,4},{8,11},{9,10},{10,... | collective-permute-start | bytes 3145736 | tf_op jit(solution)/shard_map/ppermute | solution.py:583
  79.1 487.1 %reduce-scatter.6.cloned.1.call-start = ((), (), s32[]{:S(2)}) async-start(), calls=%async_computation.8 | async-start | bytes 6488064 | tf_op jit(solution)/shard_map/reduce_scatter | solution.py:616
  329.4 25.1 %collective-permute-start.5 = (bf16[256,2048]{1,0:T(8,128)(2,1)S(1)}, bf16[256,2048]{1,0:T(8,128)(2,1)S(1)}, u32[]{:S(2)}, u32[]{:S(2)}) collective-permute-start(bf16[256,2048]{1,0:T(8,128)(2,1)S(1)} %multiply_convert_fusion.3), channel_id=1, source_target_pairs={{0,3},{1,2},{2,1},{3,0},{4,7},{5,6},{6,5},{7,4},{8,11},{9,10},{10,... | collective-permute-start | bytes 3145736 | tf_op jit(solution)/shard_map/ppermute | solution.py:583
  331.0 47.0 %collective-permute-start.4 = (bf16[256,2048]{1,0:T(8,128)(2,1)S(1)}, bf16[256,2048]{1,0:T(8,128)(2,1)S(1)}, u32[]{:S(2)}, u32[]{:S(2)}) collective-permute-start(bf16[256,2048]{1,0:T(8,128)(2,1)S(1)} %multiply_convert_fusion.3), channel_id=1, source_target_pairs={{0,2},{1,3},{2,0},{3,1},{4,6},{5,7},{6,4},{7,5},{8,10},{9,11},{10,... | collective-permute-start | bytes 3145736 | tf_op jit(solution)/shard_map/ppermute | solution.py:583
  331.6 47.4 %collective-permute-start.3 = (bf16[256,2048]{1,0:T(8,128)(2,1)S(1)}, bf16[256,2048]{1,0:T(8,128)(2,1)}, u32[]{:S(2)}, u32[]{:S(2)}) collective-permute-start(bf16[256,2048]{1,0:T(8,128)(2,1)S(1)} %multiply_convert_fusion.3), channel_id=1, source_target_pairs={{0,1},{1,0},{2,3},{3,2},{4,5},{5,4},{6,7},{7,6},{8,9},{9,8},{10,11... | collective-permute-start | bytes 3145736 | tf_op jit(solution)/shard_map/ppermute | solution.py:583
  332.1 121.0 %collective-permute-start.9 = (bf16[256,2048]{1,0:T(8,128)(2,1)S(1)}, bf16[256,2048]{1,0:T(8,128)(2,1)}, u32[]{:S(2)}, u32[]{:S(2)}) collective-permute-start(bf16[256,2048]{1,0:T(8,128)(2,1)S(1)} %get-tuple-element.97), channel_id=1, source_target_pairs={{0,1},{1,0},{2,3},{3,2},{4,5},{5,4},{6,7},{7,6},{8,9},{9,8},{10,11... | collective-permute-start | bytes 3145736 | tf_op jit(solution)/shard_map/ppermute | solution.py:583
  333.0 121.0 %collective-permute-start.10 = (bf16[256,2048]{1,0:T(8,128)(2,1)S(1)}, bf16[256,2048]{1,0:T(8,128)(2,1)}, u32[]{:S(2)}, u32[]{:S(2)}) collective-permute-start(bf16[256,2048]{1,0:T(8,128)(2,1)S(1)} %get-tuple-element.97), channel_id=1, source_target_pairs={{0,2},{1,3},{2,0},{3,1},{4,6},{5,7},{6,4},{7,5},{8,10},{9,11},{10,... | collective-permute-start | bytes 3145736 | tf_op jit(solution)/shard_map/ppermute | solution.py:583
  337.9 40.1 %copy-start.43 = (bf16[1024,2048]{1,0:T(8,128)(2,1)}, bf16[1024,2048]{1,0:T(8,128)(2,1)S(1)}, u32[]{:S(2)}) copy-start(bf16[1024,2048]{1,0:T(8,128)(2,1)S(1)} %constant_dynamic-update-slice_fusion) | copy-start | bytes 12582916
  354.5 23.5 %copy-start.54 = (bf16[256,2048]{1,0:T(8,128)(2,1)}, bf16[256,2048]{1,0:T(8,128)(2,1)S(1)}, u32[]{:S(2)}) copy-start(bf16[256,2048]{1,0:T(8,128)(2,1)S(1)} %collective-permute-done.5) | copy-start | bytes 3145732
  354.5 99.6 %collective-permute-start.11 = (bf16[256,2048]{1,0:T(8,128)(2,1)S(1)}, bf16[256,2048]{1,0:T(8,128)(2,1)}, u32[]{:S(2)}, u32[]{:S(2)}) collective-permute-start(bf16[256,2048]{1,0:T(8,128)(2,1)S(1)} %get-tuple-element.97), channel_id=1, source_target_pairs={{0,3},{1,2},{2,1},{3,0},{4,7},{5,6},{6,5},{7,4},{8,11},{9,10},{10,... | collective-permute-start | bytes 3145736 | tf_op jit(solution)/shard_map/ppermute | solution.py:583
  391.9 15.6 %copy-start.44 = (bf16[1024,2048]{1,0:T(8,128)(2,1)S(1)}, bf16[1024,2048]{1,0:T(8,128)(2,1)}, u32[]{:S(2)}) copy-start(bf16[1024,2048]{1,0:T(8,128)(2,1)} %copy-done.43) | copy-start | bytes 12582916
  416.1 214.4 %reduce-scatter.8.cloned.1.call-start = ((), (), s32[]{:S(2)}) async-start(), calls=%async_computation.9 | async-start | bytes 6488064 | tf_op jit(solution)/shard_map/reduce_scatter | solution.py:616
  430.5 9.8 %copy-start.58 = (bf16[1024,1408]{1,0:T(8,128)(2,1)}, bf16[1024,1408]{1,0:T(8,128)(2,1)S(1)}, u32[]{:S(2)}) copy-start(bf16[1024,1408]{1,0:T(8,128)(2,1)S(1)} %get-tuple-element.74) | copy-start | bytes 8650756
  451.4 24.5 %collective-permute-start.6 = (bf16[256,2048]{1,0:T(8,128)(2,1)}, bf16[256,2048]{1,0:T(8,128)(2,1)}, u32[]{:S(2)}, u32[]{:S(2)}) collective-permute-start(bf16[256,2048]{1,0:T(8,128)(2,1)} %get-tuple-element.186), channel_id=1, source_target_pairs={{0,1},{1,0},{2,3},{3,2},{4,5},{5,4},{6,7},{7,6},{8,9},{9,8},{10,11... | collective-permute-start | bytes 3145736 | tf_op jit(solution)/shard_map/ppermute | solution.py:583
  452.3 24.0 %collective-permute-start.7 = (bf16[256,2048]{1,0:T(8,128)(2,1)}, bf16[256,2048]{1,0:T(8,128)(2,1)}, u32[]{:S(2)}, u32[]{:S(2)}) collective-permute-start(bf16[256,2048]{1,0:T(8,128)(2,1)} %get-tuple-element.185), channel_id=1, source_target_pairs={{0,2},{1,3},{2,0},{3,1},{4,6},{5,7},{6,4},{7,5},{8,10},{9,11},{10,... | collective-permute-start | bytes 3145736 | tf_op jit(solution)/shard_map/ppermute | solution.py:583
  453.1 45.8 %collective-permute-start.8 = (bf16[256,2048]{1,0:T(8,128)(2,1)}, bf16[256,2048]{1,0:T(8,128)(2,1)}, u32[]{:S(2)}, u32[]{:S(2)}) collective-permute-start(bf16[256,2048]{1,0:T(8,128)(2,1)} %get-tuple-element.184), channel_id=1, source_target_pairs={{0,3},{1,2},{2,1},{3,0},{4,7},{5,6},{6,5},{7,4},{8,11},{9,10},{10,... | collective-permute-start | bytes 3145736 | tf_op jit(solution)/shard_map/ppermute | solution.py:583
  498.9 221.8 %reduce-scatter.10.cloned.1.call-start = ((), (), s32[]{:S(2)}) async-start(), calls=%async_computation.10 | async-start | bytes 6488064 | tf_op jit(solution)/shard_map/reduce_scatter | solution.py:616
  499.5 253.0 %reduce-scatter.12.cloned.1.call-start = ((), (), s32[]{:S(2)}) async-start(), calls=%async_computation.11 | async-start | bytes 2359296 | tf_op jit(solution)/shard_map/reduce_scatter | solution.py:616
  512.1 24.1 %collective-permute-start.14 = (bf16[256,2048]{1,0:T(8,128)(2,1)}, bf16[256,2048]{1,0:T(8,128)(2,1)}, u32[]{:S(2)}, u32[]{:S(2)}) collective-permute-start(bf16[256,2048]{1,0:T(8,128)(2,1)} %get-tuple-element.182), channel_id=1, source_target_pairs={{0,3},{1,2},{2,1},{3,0},{4,7},{5,6},{6,5},{7,4},{8,11},{9,10},{10,... | collective-permute-start | bytes 3145736 | tf_op jit(solution)/shard_map/ppermute | solution.py:583
  513.3 47.6 %collective-permute-start.13 = (bf16[256,2048]{1,0:T(8,128)(2,1)}, bf16[256,2048]{1,0:T(8,128)(2,1)}, u32[]{:S(2)}, u32[]{:S(2)}) collective-permute-start(bf16[256,2048]{1,0:T(8,128)(2,1)} %get-tuple-element.183), channel_id=1, source_target_pairs={{0,2},{1,3},{2,0},{3,1},{4,6},{5,7},{6,4},{7,5},{8,10},{9,11},{10,... | collective-permute-start | bytes 3145736 | tf_op jit(solution)/shard_map/ppermute | solution.py:583
  514.2 46.7 %collective-permute-start.12 = (bf16[256,2048]{1,0:T(8,128)(2,1)}, bf16[256,2048]{1,0:T(8,128)(2,1)}, u32[]{:S(2)}, u32[]{:S(2)}) collective-permute-start(bf16[256,2048]{1,0:T(8,128)(2,1)} %get-tuple-element.181), channel_id=1, source_target_pairs={{0,1},{1,0},{2,3},{3,2},{4,5},{5,4},{6,7},{7,6},{8,9},{9,8},{10,11... | collective-permute-start | bytes 3145736 | tf_op jit(solution)/shard_map/ppermute | solution.py:583
  514.8 205.8 %collective-permute-start.15 = (bf16[256,2048]{1,0:T(8,128)(2,1)}, bf16[256,2048]{1,0:T(8,128)(2,1)}, u32[]{:S(2)}, u32[]{:S(2)}) collective-permute-start(bf16[256,2048]{1,0:T(8,128)(2,1)} %fusion.30), channel_id=1, source_target_pairs={{0,1},{1,0},{2,3},{3,2},{4,5},{5,4},{6,7},{7,6},{8,9},{9,8},{10,11... | collective-permute-start | bytes 3145736 | tf_op jit(solution)/shard_map/ppermute | solution.py:583
  515.6 205.0 %collective-permute-start.16 = (bf16[256,2048]{1,0:T(8,128)(2,1)}, bf16[256,2048]{1,0:T(8,128)(2,1)}, u32[]{:S(2)}, u32[]{:S(2)}) collective-permute-start(bf16[256,2048]{1,0:T(8,128)(2,1)} %fusion.30), channel_id=1, source_target_pairs={{0,2},{1,3},{2,0},{3,1},{4,6},{5,7},{6,4},{7,5},{8,10},{9,11},{10,... | collective-permute-start | bytes 3145736 | tf_op jit(solution)/shard_map/ppermute | solution.py:583
  516.3 44.6 %copy-start.16 = (bf16[256,2048]{1,0:T(8,128)(2,1)S(1)}, bf16[256,2048]{1,0:T(8,128)(2,1)}, u32[]{:S(2)}) copy-start(bf16[256,2048]{1,0:T(8,128)(2,1)} %get-tuple-element.76) | copy-start | bytes 3145732
  516.3 44.6 %copy-start.22 = (bf16[1,256,2048]{2,1,0:T(8,128)(2,1)S(1)}, bf16[1,256,2048]{2,1,0:T(8,128)(2,1)}, u32[]{:S(2)}) copy-start(bf16[1,256,2048]{2,1,0:T(8,128)(2,1)} %param.18) | copy-start | bytes 3145732
  568.2 16.6 %collective-permute-start.38 = (bf16[64,1408]{1,0:T(8,128)(2,1)}, bf16[64,1408]{1,0:T(8,128)(2,1)}, u32[]{:S(2)}, u32[]{:S(2)}) collective-permute-start(bf16[64,1408]{1,0:T(8,128)(2,1)} %get-tuple-element.210), channel_id=1, source_target_pairs={{0,3},{1,2},{2,1},{3,0},{4,7},{5,6},{6,5},{7,4},{8,11},{9,10},{10,... | collective-permute-start | bytes 540680 | tf_op jit(solution)/shard_map/ppermute | solution.py:583
  569.3 23.9 %collective-permute-start.37 = (bf16[64,1408]{1,0:T(8,128)(2,1)}, bf16[64,1408]{1,0:T(8,128)(2,1)}, u32[]{:S(2)}, u32[]{:S(2)}) collective-permute-start(bf16[64,1408]{1,0:T(8,128)(2,1)} %get-tuple-element.211), channel_id=1, source_target_pairs={{0,2},{1,3},{2,0},{3,1},{4,6},{5,7},{6,4},{7,5},{8,10},{9,11},{10,... | collective-permute-start | bytes 540680 | tf_op jit(solution)/shard_map/ppermute | solution.py:583
  570.2 24.0 %collective-permute-start.36 = (bf16[64,1408]{1,0:T(8,128)(2,1)}, bf16[64,1408]{1,0:T(8,128)(2,1)}, u32[]{:S(2)}, u32[]{:S(2)}) collective-permute-start(bf16[64,1408]{1,0:T(8,128)(2,1)} %get-tuple-element.212), channel_id=1, source_target_pairs={{0,1},{1,0},{2,3},{3,2},{4,5},{5,4},{6,7},{7,6},{8,9},{9,8},{10,11... | collective-permute-start | bytes 540680 | tf_op jit(solution)/shard_map/ppermute | solution.py:583
  581.5 35.5 %copy-start.1 = (f32[64,5632]{1,0:T(8,128)S(1)}, f32[64,5632]{1,0:T(8,128)}, u32[]{:S(2)}) copy-start(f32[64,5632]{1,0:T(8,128)} %down_ref.1) | copy-start | bytes 4325380
  581.5 35.5 %copy-start.26 = (f32[64,5632]{1,0:T(8,128)S(1)}, f32[64,5632]{1,0:T(8,128)}, u32[]{:S(2)}) copy-start(f32[64,5632]{1,0:T(8,128)} %param.32) | copy-start | bytes 4325380
  581.6 35.5 %copy-start.27 = (f32[64,5632]{1,0:T(8,128)S(1)}, f32[64,5632]{1,0:T(8,128)}, u32[]{:S(2)}) copy-start(f32[64,5632]{1,0:T(8,128)} %param.27) | copy-start | bytes 4325380
  584.8 135.9 %collective-permute-start.17 = (bf16[256,2048]{1,0:T(8,128)(2,1)}, bf16[256,2048]{1,0:T(8,128)(2,1)}, u32[]{:S(2)}, u32[]{:S(2)}) collective-permute-start(bf16[256,2048]{1,0:T(8,128)(2,1)} %fusion.30), channel_id=1, source_target_pairs={{0,3},{1,2},{2,1},{3,0},{4,7},{5,6},{6,5},{7,4},{8,11},{9,10},{10,... | collective-permute-start | bytes 3145736 | tf_op jit(solution)/shard_map/ppermute | solution.py:583
  593.2 22.7 %collective-permute-start.23 = (bf16[256,512]{1,0:T(8,128)(2,1)S(1)}, bf16[256,512]{1,0:T(8,128)(2,1)S(1)}, u32[]{:S(2)}, u32[]{:S(2)}) collective-permute-start(bf16[256,512]{1,0:T(8,128)(2,1)S(1)} %bitcast.198), channel_id=1, source_target_pairs={{0,3},{1,2},{2,1},{3,0},{4,7},{5,6},{6,5},{7,4},{8,11},{9,10},{10,... | collective-permute-start | bytes 786440 | tf_op jit(solution)/shard_map/ppermute | solution.py:583
  594.2 30.7 %collective-permute-start.22 = (bf16[256,512]{1,0:T(8,128)(2,1)S(1)}, bf16[256,512]{1,0:T(8,128)(2,1)S(1)}, u32[]{:S(2)}, u32[]{:S(2)}) collective-permute-start(bf16[256,512]{1,0:T(8,128)(2,1)S(1)} %bitcast.197), channel_id=1, source_target_pairs={{0,2},{1,3},{2,0},{3,1},{4,6},{5,7},{6,4},{7,5},{8,10},{9,11},{10,... | collective-permute-start | bytes 786440 | tf_op jit(solution)/shard_map/ppermute | solution.py:583
  615.9 8.9 %collective-permute-start.21 = (bf16[256,512]{1,0:T(8,128)(2,1)S(1)}, bf16[256,512]{1,0:T(8,128)(2,1)S(1)}, u32[]{:S(2)}, u32[]{:S(2)}) collective-permute-start(bf16[256,512]{1,0:T(8,128)(2,1)S(1)} %bitcast.196), channel_id=1, source_target_pairs={{0,1},{1,0},{2,3},{3,2},{4,5},{5,4},{6,7},{7,6},{8,9},{9,8},{10,11... | collective-permute-start | bytes 786440 | tf_op jit(solution)/shard_map/ppermute | solution.py:583
  630.5 163.8 %reduce-scatter.14.cloned.1.call-start = ((), (), s32[]{:S(2)}) async-start(), calls=%async_computation.12 | async-start | bytes 3538944 | tf_op jit(solution)/shard_map/reduce_scatter | solution.py:616
  634.1 87.6 %copy-start.29 = (f32[256,32]{1,0:T(8,128)S(1)}, f32[256,32]{1,0:T(8,128)}, u32[]{:S(2)}) copy-start(f32[256,32]{1,0:T(8,128)} %copy-done.28) | copy-start | bytes 98308
  724.4 9.2 %copy-start.15 = (bf16[1,256,2048]{2,1,0:T(8,128)(2,1)S(1)}, bf16[1,256,2048]{2,1,0:T(8,128)(2,1)}, u32[]{:S(2)}) copy-start(bf16[1,256,2048]{2,1,0:T(8,128)(2,1)} %param.17) | copy-start | bytes 3145732
  724.4 9.2 %copy-start.37 = (bf16[256,4,64]{0,2,1:T(8,128)(2,1)S(1)}, bf16[256,4,64]{0,2,1:T(8,128)(2,1)}, u32[]{:S(2)}) copy-start(bf16[256,4,64]{0,2,1:T(8,128)(2,1)} %copy.130) | copy-start | bytes 393220
  724.4 9.2 %copy-start.47 = (f32[2048,1]{0,1:T(1,128)S(1)}, f32[2048,1]{0,1:T(1,128)}, u32[]{:S(2)}) copy-start(f32[2048,1]{0,1:T(1,128)} %copy-done.46) | copy-start | bytes 24580
  724.4 9.2 %copy-start.49 = (f32[256]{0:T(256)S(1)}, f32[256]{0:T(256)}, u32[]{:S(2)}) copy-start(f32[256]{0:T(256)} %copy-done.48) | copy-start | bytes 3076
  727.2 16.6 %collective-permute-start.20 = (bf16[256,640]{1,0:T(8,128)(2,1)}, bf16[256,640]{1,0:T(8,128)(2,1)}, u32[]{:S(2)}, u32[]{:S(2)}) collective-permute-start(bf16[256,640]{1,0:T(8,128)(2,1)} %bitcast.193), channel_id=1, source_target_pairs={{0,3},{1,2},{2,1},{3,0},{4,7},{5,6},{6,5},{7,4},{8,11},{9,10},{10,... | collective-permute-start | bytes 983048 | tf_op jit(solution)/shard_map/ppermute | solution.py:583
  729.2 16.0 %collective-permute-start.19 = (bf16[256,640]{1,0:T(8,128)(2,1)}, bf16[256,640]{1,0:T(8,128)(2,1)}, u32[]{:S(2)}, u32[]{:S(2)}) collective-permute-start(bf16[256,640]{1,0:T(8,128)(2,1)} %bitcast.192), channel_id=1, source_target_pairs={{0,2},{1,3},{2,0},{3,1},{4,6},{5,7},{6,4},{7,5},{8,10},{9,11},{10,... | collective-permute-start | bytes 983048 | tf_op jit(solution)/shard_map/ppermute | solution.py:583
  730.3 14.8 %collective-permute-start.18 = (bf16[256,640]{1,0:T(8,128)(2,1)}, bf16[256,640]{1,0:T(8,128)(2,1)}, u32[]{:S(2)}, u32[]{:S(2)}) collective-permute-start(bf16[256,640]{1,0:T(8,128)(2,1)} %bitcast.23), channel_id=1, source_target_pairs={{0,1},{1,0},{2,3},{3,2},{4,5},{5,4},{6,7},{7,6},{8,9},{9,8},{10,11... | collective-permute-start | bytes 983048 | tf_op jit(solution)/shard_map/ppermute | solution.py:583
  742.3 16.7 %collective-permute-start.32 = (bf16[64,1408]{1,0:T(8,128)(2,1)}, bf16[64,1408]{1,0:T(8,128)(2,1)}, u32[]{:S(2)}, u32[]{:S(2)}) collective-permute-start(bf16[64,1408]{1,0:T(8,128)(2,1)} %get-tuple-element.218), channel_id=1, source_target_pairs={{0,3},{1,2},{2,1},{3,0},{4,7},{5,6},{6,5},{7,4},{8,11},{9,10},{10,... | collective-permute-start | bytes 540680 | tf_op jit(solution)/shard_map/ppermute | solution.py:583
  743.5 16.8 %collective-permute-start.31 = (bf16[64,1408]{1,0:T(8,128)(2,1)}, bf16[64,1408]{1,0:T(8,128)(2,1)}, u32[]{:S(2)}, u32[]{:S(2)}) collective-permute-start(bf16[64,1408]{1,0:T(8,128)(2,1)} %get-tuple-element.219), channel_id=1, source_target_pairs={{0,2},{1,3},{2,0},{3,1},{4,6},{5,7},{6,4},{7,5},{8,10},{9,11},{10,... | collective-permute-start | bytes 540680 | tf_op jit(solution)/shard_map/ppermute | solution.py:583
  743.8 16.5 %collective-permute-start.30 = (bf16[64,1408]{1,0:T(8,128)(2,1)S(1)}, bf16[64,1408]{1,0:T(8,128)(2,1)}, u32[]{:S(2)}, u32[]{:S(2)}) collective-permute-start(bf16[64,1408]{1,0:T(8,128)(2,1)S(1)} %get-tuple-element.220), channel_id=1, source_target_pairs={{0,1},{1,0},{2,3},{3,2},{4,5},{5,4},{6,7},{7,6},{8,9},{9,8},{10,11... | collective-permute-start | bytes 540680 | tf_op jit(solution)/shard_map/ppermute | solution.py:583
  753.9 7.9 collective-permute-start.35
  755.1 9.5 %collective-permute-start.34 = (bf16[64,1408]{1,0:T(8,128)(2,1)S(1)}, bf16[64,1408]{1,0:T(8,128)(2,1)S(1)}, u32[]{:S(2)}, u32[]{:S(2)}) collective-permute-start(bf16[64,1408]{1,0:T(8,128)(2,1)S(1)} %get-tuple-element.215), channel_id=1, source_target_pairs={{0,2},{1,3},{2,0},{3,1},{4,6},{5,7},{6,4},{7,5},{8,10},{9,11},{10,... | collective-permute-start | bytes 540680 | tf_op jit(solution)/shard_map/ppermute | solution.py:583
  755.4 12.3 %copy-start.24 = (f32[64,11264]{1,0:T(8,128)S(1)}, f32[64,11264]{1,0:T(8,128)}, u32[]{:S(2)}) copy-start(f32[64,11264]{1,0:T(8,128)} %param.26) | copy-start | bytes 8650756
  759.0 5.6 collective-permute-start.33
  764.9 7.9 collective-permute-start.29
  765.6 7.2 collective-permute-start.28
  766.6 6.2 collective-permute-start.27
  772.8 25.4 %copy-start.6 = (f32[64,2048]{1,0:T(8,128)S(1)}, f32[64,2048]{1,0:T(8,128)}, u32[]{:S(2)}) copy-start(f32[64,2048]{1,0:T(8,128)} %out_ref.1) | copy-start | bytes 1572868
  772.8 25.4 %copy-start.41 = (f32[64,2048]{1,0:T(8,128)S(1)}, f32[64,2048]{1,0:T(8,128)}, u32[]{:S(2)}) copy-start(f32[64,2048]{1,0:T(8,128)} %param.30) | copy-start | bytes 1572868
  795.5 5.3 collective-permute-start.26
  797.7 4.5 collective-permute-start.25
  797.9 4.2 collective-permute-start.24
  (44 other events, 128.5 us)
Sparse Core Ops, SparseCore 0:
  75.6 57.4 all-gather.3
  134.8 59.0 all-gather.5
  195.6 100.4 all-gather.7
  416.3 68.9 reduce-scatter.5
  499.0 70.1 reduce-scatter.7
  571.4 62.9 reduce-scatter.9
  637.2 76.2 reduce-scatter.11
  752.6 41.5 reduce-scatter.13

commit v3 on v2

--- a/solution.py
+++ b/solution.py
@@ -103,40 +103,52 @@
     return index // 2, lax.rem(index, 2)
 
 
+def pass_rows_start(rows, send, come, near):
+    s = lax.axis_index("seq")
+    for d in [1] + near:
+        rows_copy(rows, send, come, d, s, s ^ d).start()
+
+
+def pass_rows_finish(rows, send, come, forward, passed, near):
+    s = lax.axis_index("seq")
+    for d in near:
+        rows_copy(rows, send, come, d, s ^ d, s ^ d).wait_recv()
+        rows_copy(rows, forward, passed, d, s ^ d, s ^ 1).start()
+    rows_copy(rows, send, come, 1, s ^ 1, s ^ 1).wait()
+    for d in near:
+        rows_copy(rows, send, come, d, s, s ^ d).wait_send()
+        rows_copy(rows, forward, passed, d, s ^ d, s ^ 1).wait_send()
+        rows_copy(rows, forward, passed, d, s ^ 1 ^ d, s ^ 1).wait_recv()
+
+
+def rows_copy(rows, send, come, d, owner, target):
+    place, half = core_pair(owner)
+    return remote(rows.at[place, half], rows.at[place, half], send.at[d], come.at[d], "seq", target)
+
+
 def share_kernel(
-    in_ref, gain_ref, out_ref, gate_up_ref, down_ref,
-    feed_gate, feed_up, feed_down, in_rows, out_rows,
-    low_gate, low_up, low_down,
-    send_feed, come_feed, send_in, come_in, send_out, come_out,
-    pass_in, passed_in, pass_out, passed_out,
+    in_ref, gain_ref, gate_up_ref, down_ref, feed_gate_up, feed_down, in_rows,
+    low_gate_up, low_down, send_feed, come_feed, send_in, come_in, pass_in, passed_in,
 ):
     group, slices = lax.axis_size("seq"), lax.axis_size("fsdp")
     s, f = lax.axis_index("seq"), lax.axis_index("fsdp")
     pair, core = core_pair(s)
     depth, inward_cols = in_ref.shape
     ff_cols = FF // slices
+    near = list(range(2, group, 2))
     in_rows[pair, core, :, pl.ds(0, inward_cols)] = in_ref[...].astype(jnp.bfloat16)
     in_rows[pair, core, :, pl.ds(inward_cols, 128)] = gain_ref[...]
-    out_rows[pair, core] = out_ref[...].astype(jnp.bfloat16)
+    meet_spread(near)
+    pass_rows_start(in_rows, send_in, come_in, near)
     for t in range(slices):
         columns = pl.ds(t * ff_cols, ff_cols)
-        low_gate[t] = gate_up_ref[:, columns].astype(jnp.bfloat16)
-        low_up[t] = gate_up_ref[:, pl.ds(FF + t * ff_cols, ff_cols)].astype(jnp.bfloat16)
+        low_gate_up[t, :, pl.ds(0, ff_cols)] = gate_up_ref[:, columns].astype(jnp.bfloat16)
+        low_gate_up[t, :, pl.ds(ff_cols, ff_cols)] = gate_up_ref[
+            :, pl.ds(FF + t * ff_cols, ff_cols)
+        ].astype(jnp.bfloat16)
         low_down[t] = down_ref[:, columns].astype(jnp.bfloat16)
 
-    barrier = pltpu.get_barrier_semaphore()
-    near = [1] + list(range(2, group, 2))
-    for d in near:
-        pl.semaphore_signal(
-            barrier, inc=1, device_id={"seq": s ^ d}, device_id_type=pl.DeviceIdType.MESH
-        )
-    for d in range(1, slices):
-        pl.semaphore_signal(
-            barrier, inc=1, device_id={"fsdp": f ^ d}, device_id_type=pl.DeviceIdType.MESH
-        )
-    pl.semaphore_wait(barrier, len(near) + slices - 1)
-
-    feeds = ((low_gate, feed_gate), (low_up, feed_up), (low_down, feed_down))
+    feeds = ((low_gate_up, feed_gate_up), (low_down, feed_down))
 
     def feed_copy(k, d, owner, target):
         low, feed = feeds[k]
@@ -146,59 +158,41 @@
             send_feed.at[k, d], come_feed.at[k, d], "fsdp", target,
         )
 
-    def row_copy(rows, send, come, d, owner, target):
-        place, half = core_pair(owner)
-        return remote(
-            rows.at[place, half], rows.at[place, half], send.at[d], come.at[d], "seq", target
-        )
-
-    for d in near:
-        row_copy(in_rows, send_in, come_in, d, s, s ^ d).start()
-    for d in near:
-        row_copy(out_rows, send_out, come_out, d, s, s ^ d).start()
     for d in range(1, slices):
-        for k in range(3):
+        for k in range(2):
             feed_copy(k, d, f, f ^ d).start()
     mine = pl.ds(pl.multiple_of(f * depth, depth), depth)
     for low, feed in feeds:
         feed[mine, :] = low[f]
-    for d in near[1:]:
-        row_copy(in_rows, send_in, come_in, d, s ^ d, s ^ d).wait_recv()
-        row_copy(in_rows, pass_in, passed_in, d, s ^ d, s ^ 1).start()
-    for d in near[1:]:
-        row_copy(out_rows, send_out, come_out, d, s ^ d, s ^ d).wait_recv()
-        row_copy(out_rows, pass_out, passed_out, d, s ^ d, s ^ 1).start()
-    for rows, send, come, forward, passed in (
-        (in_rows, send_in, come_in, pass_in, passed_in),
-        (out_rows, send_out, come_out, pass_out, passed_out),
-    ):
-        row_copy(rows, send, come, 1, s ^ 1, s ^ 1).wait()
-        for d in near[1:]:
-            row_copy(rows, send, come, d, s, s ^ d).wait_send()
-            row_copy(rows, forward, passed, d, s ^ d, s ^ 1).wait_send()
-            row_copy(rows, forward, passed, d, s ^ 1 ^ d, s ^ 1).wait_recv()
+    pass_rows_finish(in_rows, send_in, come_in, pass_in, passed_in, near)
     for d in range(1, slices):
-        for k in range(3):
+        for k in range(2):
             feed_copy(k, d, f ^ d, f ^ d).wait()
 
 
-def share_weights(w_inward, gain_columns, w_outward, w_gate_up, w_down, group, slices):
+def share_weights(w_inward, gain_columns, w_gate_up, w_down, group, slices):
     depth = w_inward.shape[0]
     ff_cols = FF // slices
-    feed = jax.ShapeDtypeStruct((slices * depth, ff_cols), jnp.bfloat16)
-    low = pltpu.VMEM((slices, depth, ff_cols), jnp.bfloat16)
-    rows = lambda width: jax.ShapeDtypeStruct((group // 2, 2, depth, width), jnp.bfloat16)
-    sems = [pltpu.SemaphoreType.DMA((3, slices))] * 2 + [pltpu.SemaphoreType.DMA((group,))] * 8
+    width = w_inward.shape[1] + 128
+    sems = [pltpu.SemaphoreType.DMA((2, slices))] * 2 + [pltpu.SemaphoreType.DMA((group,))] * 4
     return pl.pallas_call(
         share_kernel,
-        in_specs=[VMEM] * 5,
-        out_specs=[VMEM] * 5,
-        out_shape=[feed, feed, feed, rows(w_inward.shape[1] + 128), rows(w_outward.shape[1])],
-        scratch_shapes=[low, low, low] + sems,
+        in_specs=[VMEM] * 4,
+        out_specs=[VMEM] * 3,
+        out_shape=[
+            jax.ShapeDtypeStruct((slices * depth, 2 * ff_cols), jnp.bfloat16),
+            jax.ShapeDtypeStruct((slices * depth, ff_cols), jnp.bfloat16),
+            jax.ShapeDtypeStruct((group // 2, 2, depth, width), jnp.bfloat16),
+        ],
+        scratch_shapes=[
+            pltpu.VMEM((slices, depth, 2 * ff_cols), jnp.bfloat16),
+            pltpu.VMEM((slices, depth, ff_cols), jnp.bfloat16),
+        ]
+        + sems,
         compiler_params=pltpu.CompilerParams(
             vmem_limit_bytes=48 << 20, collective_id=2, has_side_effects=True
         ),
-    )(w_inward, gain_columns, w_outward, w_gate_up, w_down)
+    )(w_inward, gain_columns, w_gate_up, w_down)
 
 
 def spread_copies(rows, full, send, come, forward, passed):
@@ -250,27 +244,39 @@
     pl.semaphore_wait(barrier, len(near) + slices - 1)
 
 
-def spread_kernel(rows, full, send, come, forward, passed):
-    meet_spread()
+def spread_kernel(
+    rows, out_ref, full, out_rows, send, come, forward, passed,
+    send_out, come_out, pass_out, passed_out,
+):
+    near = list(range(2, lax.axis_size("seq"), 2))
+    pair, core = core_pair(lax.axis_index("seq"))
+    meet_spread(near)
     start, local, finish = spread_copies(rows, full, send, come, forward, passed)
     start()
+    out_rows[pair, core] = out_ref[...].astype(jnp.bfloat16)
+    pass_rows_start(out_rows, send_out, come_out, near)
     local()
+    pass_rows_finish(out_rows, send_out, come_out, pass_out, passed_out, near)
     finish()
 
 
-def spread_rows(rows, slices):
+def spread_rows(rows, w_outward, slices):
     pairs, two, depth, width = rows.shape
-    full = pl.pallas_call(
+    full, out_rows = pl.pallas_call(
         spread_kernel,
-        in_specs=[VMEM],
-        out_specs=VMEM,
-        out_shape=jax.ShapeDtypeStruct((pairs, two, slices, depth, width), rows.dtype),
-        scratch_shapes=[pltpu.SemaphoreType.DMA((slices,))] * 4,
+        in_specs=[VMEM] * 2,
+        out_specs=[VMEM] * 2,
+        out_shape=[
+            jax.ShapeDtypeStruct((pairs, two, slices, depth, width), rows.dtype),
+            jax.ShapeDtypeStruct((pairs, two, depth, w_outward.shape[1]), rows.dtype),
+        ],
+        scratch_shapes=[pltpu.SemaphoreType.DMA((slices,))] * 4
+        + [pltpu.SemaphoreType.DMA((2 * pairs,))] * 4,
         compiler_params=pltpu.CompilerParams(
             vmem_limit_bytes=48 << 20, collective_id=3, has_side_effects=True
         ),
-    )(rows)
-    return full.reshape(pairs * two * slices * depth, width)
+    )(rows, w_outward)
+    return full.reshape(pairs * two * slices * depth, width), out_rows
 
 
 def forward_kernel(
@@ -393,9 +399,11 @@
 
 
 def backward_kernel(
-    grad_ref, query_here, kv_here, mixed_here, logs, query_back, kv_back,
+    grad_ref, query_here, kv_here, mixed_here, logs, normed_ref, attended_ref, branch_ref,
+    query_back, kv_back, normed_all, attended_all, branch_all,
     grad_here, query_grad, kv_grad, key_sum, value_sum,
-    send_grad, come_grad, send_query, come_query, send_kv, come_kv, local_sem, *, heads, block
+    send_grad, come_grad, send_query, come_query, send_kv, come_kv, local_sem,
+    send_slice, come_slice, *, heads, block
 ):
     group = lax.axis_size("seq")
     me = lax.axis_index("seq")
@@ -404,12 +412,17 @@
     per_block = block // local
     blocks = length // block
     scale = HEAD_DIM**-0.5
-    barrier = pltpu.get_barrier_semaphore()
-    for d in range(1, group):
-        pl.semaphore_signal(
-            barrier, inc=1, device_id={"seq": me ^ d}, device_id_type=pl.DeviceIdType.MESH
-        )
-    pl.semaphore_wait(barrier, group - 1)
+    slices, f = lax.axis_size("fsdp"), lax.axis_index("fsdp")
+    share = branch_all.shape[2]
+    meet_spread(range(1, group))
+
+    def slice_copy(k, d, target):
+        columns = pl.ds(pl.multiple_of(target * share, 128), share)
+        source = (branch_ref.at[:, columns], attended_ref, normed_ref)[k]
+        into = (branch_all, attended_all, normed_all)[k]
+        return remote(
+            source, into.at[d], send_slice.at[k, d], come_slice.at[k, d], "fsdp", target
+        )
 
     def grad_copy(d, owner, target):
         return remote(
@@ -434,6 +447,12 @@
 
     for d in range(1, group):
         grad_copy(d, me, me ^ d).start()
+    for k in range(3):
+        for d in range(1, slices):
+            slice_copy(k, d, f ^ d).start()
+    normed_all[0] = normed_ref[...]
+    attended_all[0] = attended_ref[...]
+    branch_all[0] = branch_ref[:, pl.ds(pl.multiple_of(f * share, 128), share)]
     mine = pl.ds(pl.multiple_of(me * local, local), local)
     own_columns = pl.ds(pl.multiple_of(me * width, 128), width)
     own_grad = pltpu.make_async_copy(
@@ -513,6 +532,9 @@
         grad_copy(d, me, other).wait_send()
         query_copy(d, other, other).wait()
         kv_copy(d, other, other).wait()
+    for k in range(3):
+        for d in range(1, slices):
+            slice_copy(k, d, f ^ d).wait()
 
 
 def attend_forward(query, kv, out_rows, group, slices, heads, block):
@@ -542,23 +564,30 @@
             vmem_limit_bytes=48 << 20, collective_id=0, has_side_effects=True
         ),
         cost_estimate=pl.CostEstimate(
-            flops=pairs * HEAD_DIM * 60, bytes_accessed=length * 4 * width, transcendentals=pairs
+            flops=pairs * HEAD_DIM * 160, bytes_accessed=length * 4 * width, transcendentals=pairs
         ),
     )(query, kv, out_rows)
 
 
-def attend_backward(grads, query_here, kv_here, mixed_here, logs, group, heads, block):
+def attend_backward(
+    grads, query_here, kv_here, mixed_here, logs, normed, attended, branch, group, slices, heads, block
+):
     local, width = grads.shape[0], heads * HEAD_DIM
     length = group * local
     pairs = heads * length * length // 2
+    features = normed.shape[1]
+    gathered = jax.ShapeDtypeStruct((slices, local, features), jnp.bfloat16)
     sems = pltpu.SemaphoreType.DMA((group,))
     return pl.pallas_call(
         functools.partial(backward_kernel, heads=heads, block=block),
-        in_specs=[VMEM] * 5,
-        out_specs=[VMEM] * 2,
+        in_specs=[VMEM] * 8,
+        out_specs=[VMEM] * 5,
         out_shape=[
             jax.ShapeDtypeStruct((local, group * width), jnp.bfloat16),
             jax.ShapeDtypeStruct((group, local, 2 * HEAD_DIM), jnp.bfloat16),
+            gathered,
+            gathered,
+            jax.ShapeDtypeStruct((slices, local, features // slices), jnp.bfloat16),
         ],
         scratch_shapes=[
             pltpu.VMEM((length, width), jnp.bfloat16),
@@ -568,14 +597,231 @@
             pltpu.VMEM((length, HEAD_DIM), jnp.float32),
         ]
         + [sems] * 6
-        + [pltpu.SemaphoreType.DMA((2,))],
+        + [pltpu.SemaphoreType.DMA((2,))]
+        + [pltpu.SemaphoreType.DMA((3, slices))] * 2,
         compiler_params=pltpu.CompilerParams(
             vmem_limit_bytes=48 << 20, collective_id=1, has_side_effects=True
         ),
         cost_estimate=pl.CostEstimate(
-            flops=pairs * HEAD_DIM * 4, bytes_accessed=length * 8 * width, transcendentals=pairs
+            flops=pairs * HEAD_DIM * 160, bytes_accessed=length * 8 * width, transcendentals=pairs
         ),
-    )(grads, query_here, kv_here, mixed_here, logs)
+    )(grads, query_here, kv_here, mixed_here, logs, normed, attended, branch)
+
+
+def meet_slices():
+    slices, f = lax.axis_size("fsdp"), lax.axis_index("fsdp")
+    barrier = pltpu.get_barrier_semaphore()
+    for d in range(1, slices):
+        pl.semaphore_signal(
+            barrier, inc=1, device_id={"fsdp": f ^ d}, device_id_type=pl.DeviceIdType.MESH
+        )
+    pl.semaphore_wait(barrier, slices - 1)
+
+
+def row_copy(stage, target, sem, r):
+    width = stage.shape[0]
+    rows = pl.ds(pl.multiple_of(r * width, width), width)
+    return pltpu.make_async_copy(stage, target.at[rows, :], sem)
+
+
+def grad_rows(field, grads, target, stage, sems):
+    width = stage.shape[1]
+    steps = target.shape[0] // width
+
+    def step(r, _):
+        columns = pl.ds(pl.multiple_of(r * width, width), width)
+        slot = lax.rem(r, 2)
+        left = field[:, :, columns].reshape(grads[0].shape[0], width)
+
+        @pl.when(r > 1)
+        def _():
+            row_copy(stage.at[slot], target, sems.at[slot], r - 2).wait()
+
+        for k, grad in enumerate(grads):
+            units = grad.shape[1]
+            stage[slot, :, pl.ds(k * units, units)] = outer(left, grad[...]).astype(jnp.bfloat16)
+        row_copy(stage.at[slot], target, sems.at[slot], r).start()
+        return 0
+
+    lax.fori_loop(0, steps, step, 0)
+    for r in (steps - 2, steps - 1):
+        row_copy(stage.at[r % 2], target, sems.at[r % 2], r).wait()
+
+
+def feed_first_kernel(
+    x_ref, dy_ref, gate_up_ref, x_all, gate_all, up_all, hidden, down_grad_out,
+    gate_sum, up_sum, grad_stage, send_x, come_x, grad_sem, *, strip
+):
+    slices, f = lax.axis_size("fsdp"), lax.axis_index("fsdp")
+    local = x_ref.shape[0]
+    meet_slices()
+
+    def x_copy(d):
+        return remote(x_ref, x_all.at[d], send_x.at[d], come_x.at[d], "fsdp", f ^ d)
+
+    for d in range(1, slices):
+        x_copy(d).start()
+    x_all[0] = x_ref[...]
+
+    def token_block(d, _):
+        @pl.when(d > 0)
+        def _():
+            x_copy(d).wait_recv()
+
+        x = x_all[d]
+        units = hidden.shape[1]
+        gate_sum[...] = dot(x, gate_up_ref[:, pl.ds(0, units)])
+        up_sum[...] = dot(x, gate_up_ref[:, pl.ds(units, units)])
+
+        def part(i, _):
+            rows = pl.ds(pl.multiple_of(i * strip, strip), strip)
+            place = pl.ds(pl.multiple_of(d * local + i * strip, strip), strip)
+            gate, up = gate_sum[rows, :], up_sum[rows, :]
+            hidden[place, :] = (gate / (1.0 + jnp.exp(-gate)) * up).astype(jnp.bfloat16)
+            gate_all[place, :] = gate.astype(jnp.bfloat16)
+            up_all[place, :] = up.astype(jnp.bfloat16)
+            return 0
+
+        lax.fori_loop(0, local // strip, part, 0)
+        return 0
+
+    lax.fori_loop(0, slices, token_block, 0)
+    grad_rows(dy_ref, [hidden], down_grad_out, grad_stage, grad_sem)
+    for d in range(1, slices):
+        x_copy(d).wait_send()
+
+
+def feed_second_kernel(
+    x_ref, dy_ref, gate_all, up_all, hidden, gate_up_ref, down_ref,
+    back_ref, out_parts, gate_up_grad_out,
+    gate_grad, up_grad, hidden_sum, back_send, back_come, out_stage, grad_stage,
+    send_back, come_back, out_sem, grad_sem, *, strip
+):
+    slices, f = lax.axis_size("fsdp"), lax.axis_index("fsdp")
+    local = back_ref.shape[0]
+    meet_slices()
+
+    def back_copy(d):
+        return remote(
+            back_send.at[d], back_come.at[d - 1], send_back.at[d], come_back.at[d], "fsdp", f ^ d
+        )
+
+    def out_copy(d):
+        slot = lax.rem(d, 2)
+        return pltpu.make_async_copy(out_stage.at[slot], out_parts.at[d], out_sem.at[slot])
+
+    def token_block(turn, _):
+        d = slices - 1 - turn
+        place = pl.ds(pl.multiple_of(d * local, local), local)
+        hidden_sum[...] = dot(dy_ref[d], down_ref[...])
+
+        def part(i, _):
+            rows = pl.ds(pl.multiple_of(i * strip, strip), strip)
+            here = pl.ds(pl.multiple_of(d * local + i * strip, strip), strip)
+            gate = gate_all[here, :].astype(jnp.float32)
+            up = up_all[here, :].astype(jnp.float32)
+            sigmoid = 1.0 / (1.0 + jnp.exp(-gate))
+            grad = hidden_sum[rows, :]
+            gate_grad[here, :] = (
+                grad * up * sigmoid * (1.0 + gate * (1.0 - sigmoid))
+            ).astype(jnp.bfloat16)
+            up_grad[here, :] = (grad * gate * sigmoid).astype(jnp.bfloat16)
+            return 0
+
+        lax.fori_loop(0, local // strip, part, 0)
+        units = hidden.shape[1]
+        back = against(gate_grad[place, :], gate_up_ref[:, pl.ds(0, units)])
+        back = back + against(up_grad[place, :], gate_up_ref[:, pl.ds(units, units)])
+        back_send[d] = back.astype(jnp.bfloat16)
+
+        @pl.when(d > 0)
+        def _():
+            back_copy(d).start()
+
+        @pl.when(turn > 1)
+        def _():
+            out_copy(d + 2).wait()
+
+        out_stage[lax.rem(d, 2)] = against(hidden[place, :], down_ref[...]).astype(jnp.bfloat16)
+        out_copy(d).start()
+        return 0
+
+    lax.fori_loop(0, slices, token_block, 0)
+    out_copy(1).wait()
+    out_copy(0).wait()
+    grad_rows(x_ref, [gate_grad, up_grad], gate_up_grad_out, grad_stage, grad_sem)
+    for d in range(1, slices):
+        back_copy(d).wait()
+    back_ref[...] = functools.reduce(
+        jnp.add, [back_send[0].astype(jnp.float32)]
+        + [back_come[d - 1].astype(jnp.float32) for d in range(1, slices)],
+    )
+
+
+ANY = pl.BlockSpec(memory_space=pl.ANY)
+
+
+def feed_first(x, upstream_all, gate_up_slice):
+    slices, local, width = upstream_all.shape
+    ff_cols = gate_up_slice.shape[1] // 2
+    tokens = slices * local
+    units = jax.ShapeDtypeStruct((tokens, ff_cols), jnp.bfloat16)
+    high = pltpu.VMEM((local, ff_cols), jnp.float32)
+    sems = pltpu.SemaphoreType.DMA((slices,))
+    return pl.pallas_call(
+        functools.partial(feed_first_kernel, strip=32),
+        in_specs=[VMEM] * 3,
+        out_specs=[VMEM] * 4 + [ANY],
+        out_shape=[
+            jax.ShapeDtypeStruct((slices, local, width), jnp.bfloat16),
+            units,
+            units,
+            units,
+            jax.ShapeDtypeStruct((width, ff_cols), jnp.bfloat16),
+        ],
+        scratch_shapes=[high, high, pltpu.VMEM((2, 256, ff_cols), jnp.bfloat16)]
+        + [sems] * 2
+        + [pltpu.SemaphoreType.DMA((2,))],
+        compiler_params=pltpu.CompilerParams(
+            vmem_limit_bytes=60 << 20, collective_id=4, has_side_effects=True
+        ),
+        cost_estimate=pl.CostEstimate(
+            flops=10 * tokens * width * ff_cols, bytes_accessed=30 << 20, transcendentals=0
+        ),
+    )(x, upstream_all, gate_up_slice)
+
+
+def feed_second(x_all, upstream_all, gate_all, up_all, hidden, gate_up_slice, down_slice):
+    slices, local, width = upstream_all.shape
+    ff_cols = gate_up_slice.shape[1] // 2
+    tokens = slices * local
+    blocks = pltpu.VMEM((slices, local, width), jnp.bfloat16)
+    low = pltpu.VMEM((tokens, ff_cols), jnp.bfloat16)
+    sems = pltpu.SemaphoreType.DMA((slices,))
+    return pl.pallas_call(
+        functools.partial(feed_second_kernel, strip=32),
+        in_specs=[VMEM] * 7,
+        out_specs=[VMEM] + [ANY] * 2,
+        out_shape=[
+            jax.ShapeDtypeStruct((local, width), jnp.float32),
+            jax.ShapeDtypeStruct((slices, local, width), jnp.bfloat16),
+            jax.ShapeDtypeStruct((width, 2 * ff_cols), jnp.bfloat16),
+        ],
+        scratch_shapes=[low, low, pltpu.VMEM((local, ff_cols), jnp.float32), blocks]
+        + [
+            pltpu.VMEM((slices - 1, local, width), jnp.bfloat16),
+            pltpu.VMEM((2, local, width), jnp.bfloat16),
+            pltpu.VMEM((2, 256, 2 * ff_cols), jnp.bfloat16),
+        ]
+        + [sems] * 2
+        + [pltpu.SemaphoreType.DMA((2,)), pltpu.SemaphoreType.DMA((2,))],
+        compiler_params=pltpu.CompilerParams(
+            vmem_limit_bytes=62 << 20, collective_id=5, has_side_effects=True
+        ),
+        cost_estimate=pl.CostEstimate(
+            flops=20 * tokens * width * ff_cols, bytes_accessed=40 << 20, transcendentals=0
+        ),
+    )(x_all, upstream_all, gate_all, up_all, hidden, gate_up_slice, down_slice)
 
 
 def swap(piece, axis, offset):
@@ -667,13 +913,11 @@
     position = (lax.axis_index("seq") * local + jnp.arange(local)).astype(jnp.float32)
 
     low_gains = jnp.pad(jnp.transpose(gains.astype(jnp.bfloat16)), ((0, 0), (0, 126)))
-    feed_gate, feed_up, feed_down, in_rows, out_rows = share_weights(
-        w_inward, low_gains, w_outward, w_gate_up, w_down, group, slices
-    )
-    gate_slice = lax.all_gather(feed_gate, "seq", axis=0, tiled=True)
-    up_slice = lax.all_gather(feed_up, "seq", axis=0, tiled=True)
-    down_slice = lax.all_gather(feed_down, "seq", axis=0, tiled=True)
-    inward_gains = spread_rows(in_rows, slices)
+    feed_gate_up, feed_down, in_rows = share_weights(
+        w_inward, low_gains, w_gate_up, w_down, group, slices
+    )
+    gate_up_slice = lax.all_gather(feed_gate_up, "seq", axis=0, tiled=True)
+    inward_gains, out_rows = spread_rows(in_rows, w_outward, slices)
     inward_full = inward_gains[:, :inward_cols]
     gain_first = inward_gains[:, inward_cols].astype(jnp.float32)
     gain_second = inward_gains[:, inward_cols + 1].astype(jnp.float32)
@@ -693,58 +937,49 @@
         query.reshape(local, D), kv, out_rows, group, slices, heads_here, block
     )
     outward_full = outward_full.reshape(D, D)
-    upstream_blocks = gather_swap(upstream, "fsdp")
-    attended, upstream_blocks = lax.optimization_barrier((attended, upstream_blocks))
-    upstream_all = jnp.concatenate(upstream_blocks, axis=0)
+    upstream_late, _ = lax.optimization_barrier((upstream, inward_gains))
+    upstream_blocks = gather_swap(upstream_late, "fsdp")
+    attended, upstream_blocks, feed_down = lax.optimization_barrier(
+        (attended, upstream_blocks, feed_down)
+    )
+    down_slice = lax.all_gather(feed_down, "seq", axis=0, tiled=True)
+    upstream_all = jnp.stack(upstream_blocks)
     middle = rows + dot(attended, outward_full)
     scale_second = rms_scale(middle)
     normed_second = (middle * scale_second * gain_second).astype(jnp.bfloat16)
 
-    normed_all = jnp.concatenate(gather_swap(normed_second, "fsdp"), axis=0)
-    gate = dot(normed_all, gate_slice)
-    up_part = dot(normed_all, up_slice)
-    sigmoid = jax.nn.sigmoid(gate)
-    hidden = (gate * sigmoid * up_part).astype(jnp.bfloat16)
-    down_partial = outer(upstream_all, hidden).astype(jnp.bfloat16)
-    upstream_late, down_partial = lax.optimization_barrier((upstream_all, down_partial))
-    hidden_grad = dot(upstream_late, down_slice)
-    gate_grad = hidden_grad * up_part * sigmoid * (1.0 + gate * (1.0 - sigmoid))
-    gate_grad = gate_grad.astype(jnp.bfloat16)
-    up_grad = (hidden_grad * gate * sigmoid).astype(jnp.bfloat16)
-
-    def send_back(part):
-        part = part.astype(jnp.bfloat16)
-        parts = [part[d * local : (d + 1) * local] for d in range(slices)]
-        return [parts[0]] + [swap(p, "fsdp", d) for d, p in enumerate(parts) if d]
-
     def add_up(parts):
         return functools.reduce(jnp.add, [p.astype(jnp.float32) for p in parts])
 
-    back_parts = send_back(against(gate_grad, gate_slice) + against(up_grad, up_slice))
-    attended_blocks = gather_swap(attended, "fsdp")
-    gate_grad, attended_blocks = lax.optimization_barrier((gate_grad, attended_blocks))
-    gate_partial = outer(normed_all, gate_grad).astype(jnp.bfloat16)
-    up_partial = outer(normed_all, up_grad).astype(jnp.bfloat16)
-    back_parts, hidden, gate_partial, up_partial = lax.optimization_barrier(
-        (back_parts, hidden, gate_partial, up_partial)
-    )
-    normed_second_grad = add_up(back_parts)
+    normed_all, gate_all, up_all, hidden, down_partial = feed_first(
+        normed_second, upstream_all, gate_up_slice
+    )
+    normed_second_grad, out_parts, gate_up_partial = feed_second(
+        normed_all, upstream_all, gate_all, up_all, hidden, gate_up_slice, down_slice
+    )
     down_mine = scatter_rows(down_partial)
-    gate_mine = scatter_rows(gate_partial)
-    up_mine = scatter_rows(up_partial)
+    gate_up_mine = scatter_rows(gate_up_partial)
     middle_back, gain_second_grad = norm_back(middle, scale_second, gain_second, normed_second_grad)
     middle_grad = upstream.astype(jnp.float32) + middle_back
     branch_low = middle_grad.astype(jnp.bfloat16)
-    branch_low, down_mine = lax.optimization_barrier((branch_low, down_mine))
     attended_grad = against(branch_low, outward_full).astype(jnp.bfloat16)
-    attended_grad, gate_mine = lax.optimization_barrier((attended_grad, gate_mine))
-    query_back, kv_back = attend_backward(
-        attended_grad, query_here, kv_here, mixed_here, logs, group, heads_here, block
-    )
-    first_blocks = gather_swap(normed, "fsdp")
-    query_back, kv_back, up_mine, first_blocks = lax.optimization_barrier(
-        (query_back, kv_back, up_mine, first_blocks)
-    )
+    query_back, kv_back, normed_all, attended_all, branch_all = attend_backward(
+        attended_grad, query_here, kv_here, mixed_here, logs, normed, attended, branch_low,
+        group, slices, heads_here, block,
+    )
+    query_back, kv_back, normed_all, attended_all, branch_all, down_mine, gate_up_mine = (
+        lax.optimization_barrier(
+            (query_back, kv_back, normed_all, attended_all, branch_all, down_mine, gate_up_mine)
+        )
+    )
+    outward_mine = scatter_rows(
+        outer(attended_all.reshape(-1, D), branch_all.reshape(-1, D // slices)).astype(jnp.bfloat16)
+    )
+
+    def column_slices(field):
+        width = field.shape[1] // slices
+        return field.reshape(local, slices, width).transpose(1, 0, 2)
+
     query_grad = rotate(
         query_back.astype(jnp.float32).reshape(local, HEADS, HEAD_DIM), position, -1.0
     )
@@ -760,33 +995,30 @@
         ],
         axis=-1,
     ).astype(jnp.bfloat16)
+    inward_grad_blocks = exchange_swap(column_slices(inward_grad), "fsdp")
     normed_grad = against(inward_grad, inward_full)
     rows_back, gain_first_grad = norm_back(rows, scale_first, gain_first, normed_grad)
     input_grad = middle_grad + rows_back
 
-    def column_slices(field):
-        width = field.shape[1] // slices
-        return field.reshape(local, slices, width).transpose(1, 0, 2)
-
-    attended_all = jnp.concatenate(attended_blocks, axis=0)
-    branch_all = jnp.concatenate(exchange_swap(column_slices(branch_low), "fsdp"), axis=0)
-    outward_mine = scatter_rows(outer(attended_all, branch_all).astype(jnp.bfloat16))
-    first_all = jnp.concatenate(first_blocks, axis=0)
-    inward_grad_all = jnp.concatenate(exchange_swap(column_slices(inward_grad), "fsdp"), axis=0)
+    inward_grad_blocks, gain_first_grad, out_parts, down_mine, gate_up_mine = (
+        lax.optimization_barrier(
+            (inward_grad_blocks, gain_first_grad, out_parts, down_mine, gate_up_mine)
+        )
+    )
     gain_grads = jnp.stack([gain_first_grad, gain_second_grad], axis=1)
     gain_grads = jnp.pad(gain_grads.astype(jnp.bfloat16), ((0, 0), (0, 126)))
-    inward_partial = outer(first_all, inward_grad_all).astype(jnp.bfloat16)
+    inward_partial = outer(normed_all.reshape(-1, D), jnp.concatenate(inward_grad_blocks, axis=0))
+    inward_partial = inward_partial.astype(jnp.bfloat16)
     slice_cols = inward_partial.shape[1]
-    inward_mine = scatter_rows(
-        jnp.concatenate([inward_partial, gain_grads], axis=1), (outward_mine,)
-    )
-    result = middle + add_up(send_back(against(hidden, down_slice)))
-    down_back = return_columns(down_mine)
-    gate_back = return_columns(gate_mine)
-    up_back = return_columns(up_mine)
-    outward_back = return_columns(outward_mine)
-    inward_back = return_columns(inward_mine)
-
+    inward_mine = scatter_rows(jnp.concatenate([inward_partial, gain_grads], axis=1))
+    out_parts = [out_parts[0]] + [swap(out_parts[d], "fsdp", d) for d in range(1, slices)]
+    result = middle + add_up(out_parts)
+    back = return_columns(jnp.concatenate([gate_up_mine, down_mine], axis=1))
+    gate_back = [piece[:, :ff_cols] for piece in back]
+    up_back = [piece[:, ff_cols : 2 * ff_cols] for piece in back]
+    down_back = [piece[:, 2 * ff_cols :] for piece in back]
+    inward_back = return_columns(jnp.concatenate([inward_mine, outward_mine], axis=1))
+    outward_back = [piece[:, slice_cols + 128 :] for piece in inward_back]
     gains_sum = add_up([piece[:, slice_cols : slice_cols + 2] for piece in inward_back])
     gains_sum = jnp.transpose(gains_sum)
     inward_back = [piece[:, :slice_cols] for piece in inward_back]

time: 827 us -> 712 us (0.86)
  matrix products: 137 us -> 37.4 us
  Pallas kernels: 369 us -> 459 us
  waiting for transfers between devices: 165 us -> 98.2 us
  starting transfers between devices: 36 us -> 15.2 us
  local copies, waits for them, and re-layouts: 51.9 us -> 31.7 us
  other arithmetic: 37.8 us -> 46.5 us
    ppermute x39 -> x15, waiting for transfers between devices: 142 us -> 44.4 us  [swap(): return lax.ppermute(piece, axis, [(i, i ^ offset) for i in range(size)])]
    pallas_call x2 -> x4, Pallas kernels: 176 us -> 250 us  [the longest x1 71.8 us: feed_first(): pl.pallas_call(functools.partial(feed_first_kernel, strip=32), in_specs=[...]
    dot_general x5 -> x2, matrix products: 53.2 us -> 12.3 us  [dot(): return jnp.dot(left, right, preferred_element_type=jnp.float32)]
    reduce_scatter x5 -> x4, waiting for transfers between devices: 21.4 us -> 53.7 us  [scatter_rows(): return lax.psum_scatter(partial, 'seq', scatter_dimension=0, tiled=True)]
    pallas_call x1, Pallas kernels: 86.5 us -> 118 us  [attend_backward(): pl.pallas_call(functools.partial(backward_kernel, heads=heads, block=bloc...]
    dot_general x5 -> x2, matrix products: 41.1 us -> 10.4 us  [outer(): lax.dot_general(left, right, (((0,), (0,)), ((), ())), preferred_element_...]
    dot_general x5 -> x2, matrix products: 42.8 us -> 14.7 us  [against(): lax.dot_general(left, right, (((1,), (1,)), ((), ())), preferred_element_...]
    ppermute x39 -> x15, starting transfers between devices: 35.6 us -> 14.3 us  [swap(): return lax.ppermute(piece, axis, [(i, i ^ offset) for i in range(size)])]
  transfers between devices with their start and end apart: 47 -> 21, of which waited for: 14 -> 8; matrix products, arithmetic and copies ran while one was open for 25% -> 12% of each run, Pallas kernels for 38% -> 60%
where the time goes in v3:
time: 712 us; the launch traced here: 704 us
  Pallas kernels  459 us (64%)
  waiting for transfers between devices  98.2 us (14%)
  other arithmetic  46.5 us (7%)
  matrix products  37.4 us (5%)
  local copies, waits for them, and re-layouts  31.7 us (4%)
  between operations  15.4 us (2%)
  starting transfers between devices  15.2 us (2%)
    pallas_call x1, Pallas kernels, attend_backward(): pl.pallas_call(functools.partial(backward_kernel, heads=heads, block=bloc...  118 us
    pallas_call x1, Pallas kernels, attend_forward(): pl.pallas_call(functools.partial(forward_kernel, heads=heads, block=block...  91.7 us
    pallas_call x1, Pallas kernels, feed_first(): pl.pallas_call(functools.partial(feed_first_kernel, strip=32), in_specs=[...  71.8 us
    pallas_call x1, Pallas kernels, spread_rows(): pl.pallas_call(spread_kernel, in_specs=[VMEM] * 2, out_specs=[VMEM] * 2,...  70.1 us
    pallas_call x1, Pallas kernels, feed_second(): pl.pallas_call(functools.partial(feed_second_kernel, strip=32), in_specs=...  67.5 us
    reduce_scatter x4, waiting for transfers between devices, scatter_rows(): return lax.psum_scatter(partial, 'seq', scatter_dimension=0, tiled=True)  53.7 us
    ppermute x15, waiting for transfers between devices, swap(): return lax.ppermute(piece, axis, [(i, i ^ offset) for i in range(size)])  44.4 us
    pallas_call x1, Pallas kernels, share_weights(): pl.pallas_call(share_kernel, in_specs=[VMEM] * 4, out_specs=[VMEM] * 3, o...  40.4 us
  transfers between devices with their start and end apart: 21, of which 8 were waited for; matrix products, arithmetic and copies ran while one was open for 12% of the time, Pallas kernels for 60%

profile of v3, /device:TPU:9, one launch (start us, length us, event | category | flops | bytes accessed | tf_op | source)
XLA Modules:
  0.0 703.6 jit_solution(4563193226707647448)
XLA Ops:
  8.1 1.4 copy-done
  9.4 1.1 copy-done.3
  10.5 40.4 %shard_map.296 = (bf16[256,2816]{1,0:T(8,128)(2,1)}, bf16[256,1408]{1,0:T(8,128)(2,1)}, bf16[4,2,64,2688]{3,2,1,0:T(8,128)(2,1)}) custom-call(f32[64,2560]{1,0:T(8,128)S(1)} %copy-done.3, bf16[64,128]{1,0:T(8,128)(2,1)S(1)} %pad.8.gain_ref, f32[64,11264]{1,0:T(8,128)} %gate_up_ref.1, f32[64,5632]{1,0:T(8,128)S(1)} %copy-done), custom_call_target="tpu_custom_call" | custom-call | tf_op jit(solution)/shard_map/pallas_call | solution.py:178
  51.0 1.8 copy-done.2
  52.8 70.1 %shard_map.297 = (bf16[4,2,4,64,2688]{4,3,2,1,0:T(8,128)(2,1)}, bf16[4,2,64,2048]{3,2,1,0:T(8,128)(2,1)S(1)}) custom-call(bf16[4,2,64,2688]{3,2,1,0:T(8,128)(2,1)S(1)} %copy-done.2, f32[64,2048]{1,0:T(8,128)S(1)} %copy-done.5), custom_call_target="tpu_custom_call" | custom-call | tf_op jit(solution)/shard_map/pallas_call | solution.py:265
  122.9 1.3 copy-done.7
  124.5 1.2 collective-permute-start.1
  125.7 1.2 collective-permute-start.2
  126.9 2.6 slice_convert_fusion
  131.2 6.1 fusion.2
  137.5 1.5 slice.178
  139.5 0.8 broadcast_multiply_fusion
  141.2 2.9 copy.120
  144.1 1.9 subtract_convert_fusion
  146.7 91.7 %shard_map.298 = (bf16[2048,256]{1,0:T(8,128)(2,1)S(1)}, bf16[2048,128]{1,0:T(8,128)(2,1)S(1)}, bf16[2048,256]{1,0:T(8,128)(2,1)S(1)}, f32[4,1,2048]{2,1,0:T(1,1...) custom-call(bf16[256,2048]{1,0:T(8,128)(2,1)S(1)} %copy.130.query_ref, ...), custom_call_target="tpu_custom_call" | custom-call | flops 85899345920 | bytes 2097152 | tf_op jit(solution)/shard_map/pallas_call | solution.py:546
  238.5 1.0 copy-done.9
  239.4 1.0 copy-done.11
  240.7 1.6 copy.164
  242.3 6.1 multiply_reduce_fusion.2
  248.5 4.5 pad_maximum_fusion.dy_ref
  253.0 1.2 multiply_convert_fusion.x_ref
  254.2 71.8 %shard_map.299 = (bf16[4,256,2048]{2,1,0:T(8,128)(2,1)}, bf16[1024,1408]{1,0:T(8,128)(2,1)}, bf16[1024,1408]{1,0:T(8,128)(2,1)}, bf16[1024,1408]{1,0:T(8,128)(2,1)}, bf16[2048,1408]{1,0:T(8,128)(2,1)}) custom-call(bf16[256,2048]{1,0:T(8,128)(2,1)} %multiply_convert_fusion.x_ref, bf16[4,256,2048]{2,1,0:T(8,128)(2,1)} %pad_maximum_fusion.dy_ref, ...), custom_call_target="tpu_custom_call" | custom-call | flops 29527900160 | bytes 31457280 | tf_op jit(solution)/shard_map/pallas_call | solution.py:771
  326.5 67.5 %shard_map.300 = (f32[256,2048]{1,0:T(8,128)}, bf16[4,256,2048]{2,1,0:T(8,128)(2,1)}, bf16[2048,2816]{1,0:T(8,128)(2,1)}) custom-call(bf16[4,256,2048]{2,1,0:T(8,128)(2,1)} %get-tuple-element.76.x_ref, bf16[4,256,2048]{2,1,0:T(8,128)(2,1)} %pad_maximum_fusion.dy_ref, bf16[1024,1408]{1,0:T(8,128)(2,1)} %get-tuple-element.77.gate_all, ...), custom_call_target="tpu_custom_call" | custom-call | flops 59055800320 | bytes 41943040 | tf_op jit(solution)/shard_map/pallas_call | solution.py:801
  394.8 0.8 copy.133
  395.7 2.3 multiply_reduce_fusion
  398.1 3.2 fusion.50
  401.3 6.2 convolution_convert_fusion.1.grad_ref
  407.5 117.6 %shard_map.301 = (bf16[256,2048]{1,0:T(8,128)(2,1)S(1)}, bf16[8,256,128]{2,1,0:T(8,128)(2,1)S(1)}, bf16[4,256,2048]{2,1,0:T(8,128)(2,1)}, bf16[4,256,2048]{2,1,0:T(8,128)(2,1)}, bf16[4,256,512]{2,1,0:T(8,128)(2,1)S(1)}) custom-call(bf16[256,2048]{1,0:T(8,128)(2,1)S(1)} %convolution_convert_fusion.1.grad_ref, bf16[2048,256]{1,0:T(8,128)(2,1)S(1)} %copy-done.10, ...), custom_call_target="tpu_custom_call" | custom-call | flops 85899345920 | bytes 4194304 | tf_op jit(solution)/shard_map/pallas_call | solution.py:581
  525.1 49.2 %reduce-scatter.7.cloned.1.call-done = bf16[256,2816]{1,0:T(8,128)(2,1)} async-done(((bf16[2048,2816]{1,0:T(8,128)(2,1)}), bf16[256,2816]{1,0:T(8,128)(2,1)}) %reduce-scatter.7.cloned.1.call-update) | async-done | bytes 1441808 | tf_op jit(solution)/shard_map/reduce_scatter | solution.py:862
  574.4 1.6 copy.132
  576.0 1.9 multiply_subtract_fusion.2
  578.8 5.9 bitcast_convert_fusion
  584.9 1.1 copy-done.17
  586.0 8.6 %fusion.15 = (f32[256]{0:T(256)S(1)}, bf16[2048]{0:T(1024)(128)(2,1)S(1)}, f32[256,2048]{1,0:T(8,128)}) fusion(bf16[1,256,2048]{2,1,0:T(8,128)(2,1)S(1)} %copy-done.17, f32[2048]{0:T(1024)S(1)} %bitcast.139, f32[256]{0:T(256)S(1)} %copy-done.40, bf16[2048,2688]{1,0:T(8,128)(2,1)} %bitcast.137, bf16[256,256]{0,1:T(8,128)(2,1)S(1)} %bitcast.122, ...), kind=kOutput, calls=%fused_computation.33 | convolution fusion | flops 2691954432 | bytes 14956544 | tf_op jit(solution)/shard_map/dot_general | solution.py:65
  595.8 1.2 collective-permute-start.4
  597.3 0.9 collective-permute-start.5
  598.4 4.3 fusion.14
  602.8 4.9 collective-permute-done.4
  607.7 4.5 convolution_convert_fusion
  612.2 1.9 pad_maximum_fusion.1
  614.8 1.0 constant_dynamic-slice_fusion
  615.8 0.8 collective-permute-start.12
  617.2 1.2 collective-permute-start.14
  618.4 1.9 slice_bitcast_fusion.2
  620.3 0.8 collective-permute-start.6
  621.8 8.7 %collective-permute-done.12 = bf16[64,4224]{1,0:T(8,128)(2,1)S(1)} collective-permute-done((bf16[64,4224]{1,0:T(8,128)(2,1)}, bf16[64,4224]{1,0:T(8,128)(2,1)S(1)}, u32[]{:S(2)}, u32[]{:S(2)}) %collective-permute-start.12) | collective-permute-done | bytes 540704 | tf_op jit(solution)/shard_map/ppermute | solution.py:829
  630.4 1.2 collective-permute-start.8
  631.6 10.6 %collective-permute-done.13 = bf16[64,4224]{1,0:T(8,128)(2,1)S(1)} collective-permute-done((bf16[64,4224]{1,0:T(8,128)(2,1)S(1)}, bf16[64,4224]{1,0:T(8,128)(2,1)S(1)}, u32[]{:S(2)}, u32[]{:S(2)}) %collective-permute-start.13) | collective-permute-done | bytes 540704 | tf_op jit(solution)/shard_map/ppermute | solution.py:829
  643.3 1.4 copy-done.20
  644.7 0.9 copy-done.21
  645.6 0.9 copy-done.15
  646.5 5.0 multiply_subtract_fusion
  651.5 2.8 multiply_subtract_fusion.1
  654.3 4.5 reduce-scatter.9.cloned.1.call-done
  658.8 2.0 pad_maximum_fusion.7
  660.8 1.3 copy.142
  662.1 1.3 collective-permute-start.9
  663.4 1.2 collective-permute-start.10
  664.6 1.1 collective-permute-start.11
  665.7 13.0 %collective-permute-done.7 = bf16[256,2048]{1,0:T(8,128)(2,1)} collective-permute-done((bf16[256,2048]{1,0:T(8,128)(2,1)}, bf16[256,2048]{1,0:T(8,128)(2,1)}, u32[]{:S(2)}, u32[]{:S(2)}) %collective-permute-start.7) | collective-permute-done | bytes 1048608 | tf_op jit(solution)/shard_map/ppermute | solution.py:829
  678.7 7.0 collective-permute-done.8
  685.7 4.0 fusion.29
  692.3 2.5 multiply_subtract_fusion.4
  694.8 1.6 multiply_subtract_fusion.3
  (187 shorter events, 15.2 us)
Async XLA Ops:
  7.2 247.1 %all-gather.3.cloned.1.call-start = ((), (), s32[]{:S(2)}) async-start(), calls=%async_computation.4 | async-start | bytes 12976128 | tf_op jit(solution)/shard_map/all_gather | solution.py:919
  8.0 1.4 copy-start
  9.4 1.1 copy-start.3
  10.5 40.5 %copy-start.5 = (f32[64,2048]{1,0:T(8,128)S(1)}, f32[64,2048]{1,0:T(8,128)}, u32[]{:S(2)}) copy-start(f32[64,2048]{1,0:T(8,128)} %out_ref.1) | copy-start | bytes 1572868
  50.9 275.6 %all-gather.5.cloned.1.call-start = ((), (), s32[]{:S(2)}) async-start(), calls=%async_computation.5 | async-start | bytes 6488064 | tf_op jit(solution)/shard_map/all_gather | solution.py:945
  51.0 1.8 copy-start.2
  122.9 1.3 copy-start.7
  124.2 116.2 %collective-permute-start = (bf16[256,2048]{1,0:T(8,128)(2,1)}, bf16[256,2048]{1,0:T(8,128)(2,1)}, u32[]{:S(2)}, u32[]{:S(2)}) collective-permute-start(bf16[256,2048]{1,0:T(8,128)(2,1)} %bitcast.10), channel_id=1, source_target_pairs={{0,1},{1,0},{2,3},{3,2},{4,5},{5,4},{6,7},{7,6},{8,9},{9,8},{10,11... | collective-permute-start | bytes 3145736 | tf_op jit(solution)/shard_map/ppermute | solution.py:829
  124.5 115.9 %collective-permute-start.1 = (bf16[256,2048]{1,0:T(8,128)(2,1)}, bf16[256,2048]{1,0:T(8,128)(2,1)}, u32[]{:S(2)}, u32[]{:S(2)}) collective-permute-start(bf16[256,2048]{1,0:T(8,128)(2,1)} %bitcast.10), channel_id=1, source_target_pairs={{0,2},{1,3},{2,0},{3,1},{4,6},{5,7},{6,4},{7,5},{8,10},{9,11},{10,... | collective-permute-start | bytes 3145736 | tf_op jit(solution)/shard_map/ppermute | solution.py:829
  125.7 114.7 %collective-permute-start.2 = (bf16[256,2048]{1,0:T(8,128)(2,1)}, bf16[256,2048]{1,0:T(8,128)(2,1)}, u32[]{:S(2)}, u32[]{:S(2)}) collective-permute-start(bf16[256,2048]{1,0:T(8,128)(2,1)} %bitcast.10), channel_id=1, source_target_pairs={{0,3},{1,2},{2,1},{3,0},{4,7},{5,6},{6,5},{7,4},{8,11},{9,10},{10,... | collective-permute-start | bytes 3145736 | tf_op jit(solution)/shard_map/ppermute | solution.py:829
  126.9 2.9 copy-start.16
  129.8 1.2 copy-start.37
  131.2 6.2 copy-start.27
  140.3 3.8 copy-start.32
  140.4 3.7 copy-start.25
  238.5 1.0 copy-start.9
  240.4 8.1 %copy-start.8 = (bf16[256,2048]{1,0:T(8,128)(2,1)}, bf16[256,2048]{1,0:T(8,128)(2,1)S(1)}, u32[]{:S(2)}) copy-start(bf16[256,2048]{1,0:T(8,128)(2,1)S(1)} %get-tuple-element.69.attended_ref) | copy-start | bytes 3145732
  240.5 284.7 %reduce-scatter.5.cloned.1.call-start = ((), (), s32[]{:S(2)}) async-start(), calls=%async_computation.6 | async-start | bytes 6488064 | tf_op jit(solution)/shard_map/reduce_scatter | solution.py:862
  248.5 4.5 copy-start.12
  326.0 248.3 %reduce-scatter.7.cloned.1.call-start = ((), (), s32[]{:S(2)}) async-start(), calls=%async_computation.7 | async-start | bytes 12976128 | tf_op jit(solution)/shard_map/reduce_scatter | solution.py:862
  394.1 1.7 copy-start.13
  394.1 260.2 %reduce-scatter.11.cloned.1.call-start = ((), (), s32[]{:S(2)}) async-start(), calls=%async_computation.9 | async-start | bytes 2359296 | tf_op jit(solution)/shard_map/reduce_scatter | solution.py:862
  395.7 2.3 copy-start.18
  401.3 6.2 copy-start.28
  401.3 6.2 copy-start.10
  525.1 50.9 %copy-start.33 = (f32[256,32]{0,1:T(8,128)S(1)}, f32[256,32]{0,1:T(8,128)}, u32[]{:S(2)}) copy-start(f32[256,32]{0,1:T(8,128)} %copy-done.32) | copy-start | bytes 98308
  576.0 2.2 copy-start.26
  576.0 2.2 copy-start.34
  584.7 1.2 copy-start.17
  584.7 1.2 copy-start.38
  584.7 1.2 copy-start.40
  584.8 74.0 %reduce-scatter.9.cloned.1.call-start = ((), (), s32[]{:S(2)}) async-start(), calls=%async_computation.8 | async-start | bytes 3538944 | tf_op jit(solution)/shard_map/reduce_scatter | solution.py:862
  594.6 3.8 copy-start.41
  594.9 7.8 %collective-permute-start.3 = (bf16[256,640]{1,0:T(8,128)(2,1)S(1)}, bf16[256,640]{1,0:T(8,128)(2,1)S(1)}, u32[]{:S(2)}, u32[]{:S(2)}) collective-permute-start(bf16[256,640]{1,0:T(8,128)(2,1)S(1)} %bitcast.126), channel_id=1, source_target_pairs={{0,1},{1,0},{2,3},{3,2},{4,5},{5,4},{6,7},{7,6},{8,9},{9,8},{10,11... | collective-permute-start | bytes 983048 | tf_op jit(solution)/shard_map/ppermute | solution.py:829
  595.8 11.8 %collective-permute-start.4 = (bf16[256,640]{1,0:T(8,128)(2,1)S(1)}, bf16[256,640]{1,0:T(8,128)(2,1)}, u32[]{:S(2)}, u32[]{:S(2)}) collective-permute-start(bf16[256,640]{1,0:T(8,128)(2,1)S(1)} %bitcast.127), channel_id=1, source_target_pairs={{0,2},{1,3},{2,0},{3,1},{4,6},{5,7},{6,4},{7,5},{8,10},{9,11},{10,... | collective-permute-start | bytes 983048 | tf_op jit(solution)/shard_map/ppermute | solution.py:829
  597.3 10.4 %collective-permute-start.5 = (bf16[256,640]{1,0:T(8,128)(2,1)S(1)}, bf16[256,640]{1,0:T(8,128)(2,1)}, u32[]{:S(2)}, u32[]{:S(2)}) collective-permute-start(bf16[256,640]{1,0:T(8,128)(2,1)S(1)} %bitcast.128), channel_id=1, source_target_pairs={{0,3},{1,2},{2,1},{3,0},{4,7},{5,6},{6,5},{7,4},{8,11},{9,10},{10,... | collective-permute-start | bytes 983048 | tf_op jit(solution)/shard_map/ppermute | solution.py:829
  598.4 9.3 %copy-start.45 = (bf16[4,256,2048]{2,1,0:T(8,128)(2,1)S(1)}, bf16[4,256,2048]{2,1,0:T(8,128)(2,1)}, u32[]{:S(2)}) copy-start(bf16[4,256,2048]{2,1,0:T(8,128)(2,1)} %get-tuple-element.99) | copy-start | bytes 12582916
  612.2 2.0 copy-start.24
  612.2 2.4 copy-start.29
  614.8 3.6 copy-start.19
  615.8 14.7 %collective-permute-start.12 = (bf16[64,4224]{1,0:T(8,128)(2,1)}, bf16[64,4224]{1,0:T(8,128)(2,1)S(1)}, u32[]{:S(2)}, u32[]{:S(2)}) collective-permute-start(bf16[64,4224]{1,0:T(8,128)(2,1)} %get-tuple-element.193), channel_id=1, source_target_pairs={{0,1},{1,0},{2,3},{3,2},{4,5},{5,4},{6,7},{7,6},{8,9},{9,8},{10,11... | collective-permute-start | bytes 1622024 | tf_op jit(solution)/shard_map/ppermute | solution.py:829
  616.5 25.7 %collective-permute-start.13 = (bf16[64,4224]{1,0:T(8,128)(2,1)S(1)}, bf16[64,4224]{1,0:T(8,128)(2,1)S(1)}, u32[]{:S(2)}, u32[]{:S(2)}) collective-permute-start(bf16[64,4224]{1,0:T(8,128)(2,1)S(1)} %get-tuple-element.192), channel_id=1, source_target_pairs={{0,2},{1,3},{2,0},{3,1},{4,6},{5,7},{6,4},{7,5},{8,10},{9,11},{10,... | collective-permute-start | bytes 1622024 | tf_op jit(solution)/shard_map/ppermute | solution.py:829
  617.2 25.2 %collective-permute-start.14 = (bf16[64,4224]{1,0:T(8,128)(2,1)S(1)}, bf16[64,4224]{1,0:T(8,128)(2,1)S(1)}, u32[]{:S(2)}, u32[]{:S(2)}) collective-permute-start(bf16[64,4224]{1,0:T(8,128)(2,1)S(1)} %get-tuple-element.191), channel_id=1, source_target_pairs={{0,3},{1,2},{2,1},{3,0},{4,7},{5,6},{6,5},{7,4},{8,11},{9,10},{10,... | collective-permute-start | bytes 1622024 | tf_op jit(solution)/shard_map/ppermute | solution.py:829
  620.3 44.3 %collective-permute-start.6 = (bf16[256,2048]{1,0:T(8,128)(2,1)}, bf16[256,2048]{1,0:T(8,128)(2,1)}, u32[]{:S(2)}, u32[]{:S(2)}) collective-permute-start(bf16[256,2048]{1,0:T(8,128)(2,1)} %get-tuple-element.183), channel_id=1, source_target_pairs={{0,1},{1,0},{2,3},{3,2},{4,5},{5,4},{6,7},{7,6},{8,9},{9,8},{10,11... | collective-permute-start | bytes 3145736 | tf_op jit(solution)/shard_map/ppermute | solution.py:829
  621.0 57.6 %collective-permute-start.7 = (bf16[256,2048]{1,0:T(8,128)(2,1)}, bf16[256,2048]{1,0:T(8,128)(2,1)}, u32[]{:S(2)}, u32[]{:S(2)}) collective-permute-start(bf16[256,2048]{1,0:T(8,128)(2,1)} %get-tuple-element.185), channel_id=1, source_target_pairs={{0,2},{1,3},{2,0},{3,1},{4,6},{5,7},{6,4},{7,5},{8,10},{9,11},{10,... | collective-permute-start | bytes 3145736 | tf_op jit(solution)/shard_map/ppermute | solution.py:829
  630.4 55.2 %collective-permute-start.8 = (bf16[256,2048]{1,0:T(8,128)(2,1)}, bf16[256,2048]{1,0:T(8,128)(2,1)}, u32[]{:S(2)}, u32[]{:S(2)}) collective-permute-start(bf16[256,2048]{1,0:T(8,128)(2,1)} %get-tuple-element.184), channel_id=1, source_target_pairs={{0,3},{1,2},{2,1},{3,0},{4,7},{5,6},{6,5},{7,4},{8,11},{9,10},{10,... | collective-permute-start | bytes 3145736 | tf_op jit(solution)/shard_map/ppermute | solution.py:829
  642.8 1.9 copy-start.20
  642.8 2.7 copy-start.21
  643.0 3.5 copy-start.15
  646.5 5.0 copy-start.1
  646.5 5.0 copy-start.22
  646.5 5.0 copy-start.23
  654.3 31.3 %copy-start.14 = (f32[256,2048]{1,0:T(8,128)S(1)}, f32[256,2048]{1,0:T(8,128)}, u32[]{:S(2)}) copy-start(f32[256,2048]{1,0:T(8,128)} %copy-done.12) | copy-start | bytes 6291460
  662.1 27.5 %collective-permute-start.9 = (bf16[64,1280]{1,0:T(8,128)(2,1)S(1)}, bf16[64,1280]{1,0:T(8,128)(2,1)S(1)}, u32[]{:S(2)}, u32[]{:S(2)}) collective-permute-start(bf16[64,1280]{1,0:T(8,128)(2,1)S(1)} %get-tuple-element.213), channel_id=1, source_target_pairs={{0,1},{1,0},{2,3},{3,2},{4,5},{5,4},{6,7},{7,6},{8,9},{9,8},{10,11... | collective-permute-start | bytes 491528 | tf_op jit(solution)/shard_map/ppermute | solution.py:829
  663.4 26.3 %collective-permute-start.10 = (bf16[64,1280]{1,0:T(8,128)(2,1)S(1)}, bf16[64,1280]{1,0:T(8,128)(2,1)S(1)}, u32[]{:S(2)}, u32[]{:S(2)}) collective-permute-start(bf16[64,1280]{1,0:T(8,128)(2,1)S(1)} %get-tuple-element.212), channel_id=1, source_target_pairs={{0,2},{1,3},{2,0},{3,1},{4,6},{5,7},{6,4},{7,5},{8,10},{9,11},{10,... | collective-permute-start | bytes 491528 | tf_op jit(solution)/shard_map/ppermute | solution.py:829
  664.6 25.1 %collective-permute-start.11 = (bf16[64,1280]{1,0:T(8,128)(2,1)S(1)}, bf16[64,1280]{1,0:T(8,128)(2,1)S(1)}, u32[]{:S(2)}, u32[]{:S(2)}) collective-permute-start(bf16[64,1280]{1,0:T(8,128)(2,1)S(1)} %get-tuple-element.211), channel_id=1, source_target_pairs={{0,3},{1,2},{2,1},{3,0},{4,7},{5,6},{6,5},{7,4},{8,11},{9,10},{10,... | collective-permute-start | bytes 491528 | tf_op jit(solution)/shard_map/ppermute | solution.py:829
  689.7 2.0 copy-start.42
  689.7 2.0 copy-start.43
  689.7 2.0 copy-start.44
  689.7 2.6 copy-start.6
  689.7 2.6 copy-start.35
  691.2 3.6 copy-start.4
  691.2 3.6 copy-start.30
  691.2 3.6 copy-start.31
  (3 other events, 2.3 us)
Sparse Core Ops, SparseCore 0:
  51.1 154.3 all-gather.2
  240.6 64.2 all-gather.4
  326.2 68.6 reduce-scatter.4
  397.0 177.3 reduce-scatter.6
  584.9 29.1 reduce-scatter.10
  621.9 36.8 reduce-scatter.8

commit v4 on v3

v4 whole, which is shorter than its diff:
```python
import functools

import jax
import jax.numpy as jnp
from jax import lax
from jax.experimental import pallas as pl
from jax.experimental.pallas import tpu as pltpu
from jax.sharding import PartitionSpec as P

D = 2048
FF = 5632
HEADS = 32
KV_HEADS = 4
HEAD_DIM = 64
STEP = 10


epsilon = 1e-05
adam_epsilon = 1e-08
beta_first = 0.9
beta_second = 0.95
rope_base = 10000.0
weight_decay = 0.1
masked_value = -1e30


def rotate(field, position, sign):
    half = field.shape[-1] // 2
    exponent = jnp.arange(half).astype(jnp.float32) * (-2.0 / field.shape[-1])
    frequency = jnp.power(rope_base, exponent)
    angle = position[:, None] * frequency[None, :]
    cosine = jnp.cos(angle)[:, None, :]
    sine = sign * jnp.sin(angle)[:, None, :]
    first = field[..., :half]
    second = field[..., half:]
    return jnp.concatenate(
        [first * cosine - second * sine, second * cosine + first * sine], axis=-1
    )


def rms_scale(rows):
    return lax.rsqrt(jnp.mean(rows * rows, axis=-1, keepdims=True) + epsilon)


def norm_back(rows, scale_rows, gain, grad):
    weighted = grad * gain
    row_grad = scale_rows * weighted - rows * scale_rows**3 * jnp.mean(
        weighted * rows, axis=-1, keepdims=True
    )
    gain_grad = jnp.sum(grad * rows * scale_rows, axis=0)
    return (row_grad, gain_grad)


def dot(left, right):
    return jnp.dot(left, right, preferred_element_type=jnp.float32)


def outer(left, right):
    return lax.dot_general(
        left, right, (((0,), (0,)), ((), ())), preferred_element_type=jnp.float32
    )


def against(left, right):
    return lax.dot_general(
        left, right, (((1,), (1,)), ((), ())), preferred_element_type=jnp.float32
    )


def stack_heads(field, heads):
    return jnp.concatenate(
        [field[:, h * HEAD_DIM : (h + 1) * HEAD_DIM] for h in range(heads)], axis=0
    )


def unstack_heads(field, heads):
    rows = field.shape[0] // heads
    return jnp.concatenate([field[h * rows : (h + 1) * rows] for h in range(heads)], axis=1)


def masked_scores(keys, queries, block, first):
    scores = against(keys, queries)
    key_place = lax.broadcasted_iota(jnp.int32, scores.shape, 0)
    query_place = first + lax.rem(lax.broadcasted_iota(jnp.int32, scores.shape, 1), block)
    return jnp.where(key_place <= query_place, scores, masked_value)


def remote(source, target, send, arrive, axis, device):
    return pltpu.make_async_remote_copy(
        src_ref=source,
        dst_ref=target,
        send_sem=send,
        recv_sem=arrive,
        device_id={axis: device},
        device_id_type=pl.DeviceIdType.MESH,
    )


VMEM = pl.BlockSpec(memory_space=pltpu.VMEM)


def core_pair(index):
    return index // 2, lax.rem(index, 2)


def pass_rows_start(rows, send, come, near):
    s = lax.axis_index("seq")
    for d in [1] + near:
        rows_copy(rows, send, come, d, s, s ^ d).start()


def pass_rows_finish(rows, send, come, forward, passed, near):
    s = lax.axis_index("seq")
    for d in near:
        rows_copy(rows, send, come, d, s ^ d, s ^ d).wait_recv()
        rows_copy(rows, forward, passed, d, s ^ d, s ^ 1).start()
    rows_copy(rows, send, come, 1, s ^ 1, s ^ 1).wait()
    for d in near:
        rows_copy(rows, send, come, d, s, s ^ d).wait_send()
        rows_copy(rows, forward, passed, d, s ^ d, s ^ 1).wait_send()
        rows_copy(rows, forward, passed, d, s ^ 1 ^ d, s ^ 1).wait_recv()


def rows_copy(rows, send, come, d, owner, target):
    place, half = core_pair(owner)
    return remote(rows.at[place, half], rows.at[place, half], send.at[d], come.at[d], "seq", target)


def share_kernel(
    in_ref, gain_ref, gate_up_ref, down_ref, feed_gate_up, feed_down, in_rows,
    low_gate_up, low_down, send_feed, come_feed, send_in, come_in, pass_in, passed_in,
):
    group, slices = lax.axis_size("seq"), lax.axis_size("fsdp")
    s, f = lax.axis_index("seq"), lax.axis_index("fsdp")
    pair, core = core_pair(s)
    depth, inward_cols = in_ref.shape
    ff_cols = FF // slices
    near = list(range(2, group, 2))
    in_rows[pair, core, :, pl.ds(0, inward_cols)] = in_ref[...].astype(jnp.bfloat16)
    in_rows[pair, core, :, pl.ds(inward_cols, 128)] = gain_ref[...]
    meet_spread(near)
    pass_rows_start(in_rows, send_in, come_in, near)
    for t in range(slices):
        columns = pl.ds(t * ff_cols, ff_cols)
        low_gate_up[t, :, pl.ds(0, ff_cols)] = gate_up_ref[:, columns].astype(jnp.bfloat16)
        low_gate_up[t, :, pl.ds(ff_cols, ff_cols)] = gate_up_ref[
            :, pl.ds(FF + t * ff_cols, ff_cols)
        ].astype(jnp.bfloat16)
        low_down[t] = down_ref[:, columns].astype(jnp.bfloat16)

    feeds = ((low_gate_up, feed_gate_up), (low_down, feed_down))

    def feed_copy(k, d, owner, target):
        low, feed = feeds[k]
        return remote(
            low.at[target],
            feed.at[pl.ds(pl.multiple_of(owner * depth, depth), depth), :],
            send_feed.at[k, d], come_feed.at[k, d], "fsdp", target,
        )

    for d in range(1, slices):
        for k in range(2):
            feed_copy(k, d, f, f ^ d).start()
    mine = pl.ds(pl.multiple_of(f * depth, depth), depth)
    for low, feed in feeds:
        feed[mine, :] = low[f]
    pass_rows_finish(in_rows, send_in, come_in, pass_in, passed_in, near)
    for d in range(1, slices):
        for k in range(2):
            feed_copy(k, d, f ^ d, f ^ d).wait()


def share_weights(w_inward, gain_columns, w_gate_up, w_down, group, slices):
    depth = w_inward.shape[0]
    ff_cols = FF // slices
    width = w_inward.shape[1] + 128
    sems = [pltpu.SemaphoreType.DMA((2, slices))] * 2 + [pltpu.SemaphoreType.DMA((group,))] * 4
    return pl.pallas_call(
        share_kernel,
        in_specs=[VMEM] * 4,
        out_specs=[VMEM] * 3,
        out_shape=[
            jax.ShapeDtypeStruct((slices * depth, 2 * ff_cols), jnp.bfloat16),
            jax.ShapeDtypeStruct((slices * depth, ff_cols), jnp.bfloat16),
            jax.ShapeDtypeStruct((group // 2, 2, depth, width), jnp.bfloat16),
        ],
        scratch_shapes=[
            pltpu.VMEM((slices, depth, 2 * ff_cols), jnp.bfloat16),
            pltpu.VMEM((slices, depth, ff_cols), jnp.bfloat16),
        ]
        + sems,
        compiler_params=pltpu.CompilerParams(
            vmem_limit_bytes=48 << 20, collective_id=2, has_side_effects=True
        ),
    )(w_inward, gain_columns, w_gate_up, w_down)


def block_order():
    slices = lax.axis_size("fsdp")
    if slices != 4:
        return list(range(1, slices))
    core = lax.rem(lax.axis_index("seq"), 2)
    return [2 - core, 1 + core, 3]


def gather_blocks(source, place, send, come):
    f, slices = lax.axis_index("fsdp"), lax.axis_size("fsdp")
    order = block_order()
    square = slices == 4
    near = [1, 2] if square else order

    def direct(d, owner, holder):
        return remote(source, place(owner, holder), send.at[d], come.at[d], "fsdp", f ^ d)

    def relay(owner, holder):
        return remote(
            place(order[0], 0), place(owner, holder), send.at[3], come.at[3], "fsdp", f ^ order[1]
        )

    def start():
        for d in near:
            direct(d, 0, d).start()

    def take(turn):
        if square and turn == 2:
            relay(3, 0).wait_recv()
        else:
            direct(order[turn], order[turn], 0).wait_recv()
        if square and turn == 0:
            relay(order[0], order[1]).start()

    def finish():
        for d in near:
            direct(d, 0, d).wait_send()
        if square:
            relay(order[0], order[1]).wait_send()

    return order, start, take, finish


def spread_copies(rows, full, send, come, forward, passed):
    s, f = lax.axis_index("seq"), lax.axis_index("fsdp")
    core = lax.rem(s, 2)
    order, begin, take, sent = gather_blocks(
        rows.at[:, core], lambda owner, holder: full.at[:, core, f ^ owner], send, come
    )

    def second(d, half):
        block = full.at[:, half, f ^ d]
        return remote(block, block, forward.at[d], passed.at[d], "seq", s ^ 1)

    def local():
        full[:, :, f] = rows[...]

    def early():
        take(0)
        second(order[0], core).start()

    def finish():
        for turn, d in enumerate(order[1:]):
            take(turn + 1)
            second(d, core).start()
        sent()
        for d in range(1, lax.axis_size("fsdp")):
            second(d, core).wait_send()
            second(d, 1 - core).wait_recv()

    return begin, local, early, finish


def meet_spread(extra=()):
    barrier = pltpu.get_barrier_semaphore()
    s, f = lax.axis_index("seq"), lax.axis_index("fsdp")
    near = sorted({1, *extra})
    slices = lax.axis_size("fsdp")
    for d in near:
        pl.semaphore_signal(
            barrier, inc=1, device_id={"seq": s ^ d}, device_id_type=pl.DeviceIdType.MESH
        )
    for d in range(1, slices):
        pl.semaphore_signal(
            barrier, inc=1, device_id={"fsdp": f ^ d}, device_id_type=pl.DeviceIdType.MESH
        )
    pl.semaphore_wait(barrier, len(near) + slices - 1)


def spread_kernel(
    rows, out_ref, full, out_rows, send, come, forward, passed,
    send_out, come_out, pass_out, passed_out,
):
    near = list(range(2, lax.axis_size("seq"), 2))
    pair, core = core_pair(lax.axis_index("seq"))
    meet_spread(near)
    start, local, early, finish = spread_copies(rows, full, send, come, forward, passed)
    start()
    out_rows[pair, core] = out_ref[...].astype(jnp.bfloat16)
    pass_rows_start(out_rows, send_out, come_out, near)
    local()
    early()
    pass_rows_finish(out_rows, send_out, come_out, pass_out, passed_out, near)
    finish()


def spread_rows(rows, w_outward, slices):
    pairs, two, depth, width = rows.shape
    full, out_rows = pl.pallas_call(
        spread_kernel,
        in_specs=[VMEM] * 2,
        out_specs=[VMEM] * 2,
        out_shape=[
            jax.ShapeDtypeStruct((pairs, two, slices, depth, width), rows.dtype),
            jax.ShapeDtypeStruct((pairs, two, depth, w_outward.shape[1]), rows.dtype),
        ],
        scratch_shapes=[pltpu.SemaphoreType.DMA((slices,))] * 4
        + [pltpu.SemaphoreType.DMA((2 * pairs,))] * 4,
        compiler_params=pltpu.CompilerParams(
            vmem_limit_bytes=48 << 20, collective_id=3, has_side_effects=True
        ),
    )(rows, w_outward)
    return full.reshape(pairs * two * slices * depth, width), out_rows


def forward_kernel(
    query_ref, kv_ref, out_rows, kv_all, mixed_ref, logs, out_full,
    queries, largest, total, mixed,
    send_kv, come_kv, pass_kv, passed_kv, send_rows, come_rows, pass_rows, passed_rows,
):
    group, s = lax.axis_size("seq"), lax.axis_index("seq")
    place, core = core_pair(s)
    local = query_ref.shape[0]
    per_head = HEADS // KV_HEADS
    width, pair = per_head * HEAD_DIM, 2 * HEAD_DIM
    near = list(range(2, group, 2))
    meet_spread(range(1, group))
    spread_start, spread_local, spread_early, spread_finish = spread_copies(
        out_rows, out_full, send_rows, come_rows, pass_rows, passed_rows
    )

    def kv_copy(d, owner, target):
        chip, half = core_pair(owner)
        return remote(kv_ref, kv_all.at[chip, half], send_kv.at[d], come_kv.at[d], "seq", target)

    def hand_on(chip, half):
        block = kv_all.at[chip, half]
        return remote(block, block, pass_kv.at[chip, half], passed_kv.at[chip, half], "seq", s ^ 1)

    kv_copy(1, s, s ^ 1).start()
    for d in near:

        @pl.when((s ^ d) > s)
        def _():
            kv_copy(d, s, s ^ d).start()

    spread_start()
    kv_all[place, core] = kv_ref[...]
    for h in range(KV_HEADS):
        field = query_ref[:, pl.ds(h * width, width)]
        queries[h] = stack_heads(field, per_head) * jnp.bfloat16(HEAD_DIM**-0.5)
    spread_local()

    def scores_of(h, chip, masked):
        kv = kv_all[chip, :, :, pl.ds(pl.multiple_of(h * pair, pair), pair)]
        kv = kv.reshape(2 * local, pair)
        keys, values = kv[:, :HEAD_DIM], kv[:, HEAD_DIM:]
        if masked:
            return masked_scores(keys, queries[h], local, core * local), values
        return against(keys, queries[h]), values

    def own_chip(h, _):
        scores, values = scores_of(h, place, True)
        new = jnp.max(scores, axis=0, keepdims=True)
        weights = jnp.exp(scores - new)
        largest[h] = new
        total[h] = jnp.sum(weights, axis=0, keepdims=True)
        mixed[h] = outer(values, weights.astype(jnp.bfloat16))
        return 0

    kv_copy(1, s ^ 1, s ^ 1).wait_recv()
    lax.fori_loop(0, KV_HEADS, own_chip, 0)

    def earlier_chip(turn, _):
        chip = place - 1 - turn

        @pl.when(chip == 0)
        def _():
            spread_early()

        owner = 2 * chip + core
        kv_copy(owner ^ s, owner, owner).wait_recv()
        hand_on(chip, core).start()
        hand_on(chip, 1 - core).wait_recv()

        def head(h, _):
            scores, values = scores_of(h, chip, False)
            new = jnp.maximum(largest[h], jnp.max(scores, axis=0, keepdims=True))
            fade = jnp.exp(largest[h] - new)
            weights = jnp.exp(scores - new)
            largest[h] = new
            total[h] = total[h] * fade + jnp.sum(weights, axis=0, keepdims=True)
            mixed[h] = mixed[h] * fade + outer(values, weights.astype(jnp.bfloat16))
            return 0

        lax.fori_loop(0, KV_HEADS, head, 0)
        return 0

    lax.fori_loop(0, place, earlier_chip, 0)

    @pl.when(place == 0)
    def _():
        spread_early()

    for h in range(KV_HEADS):
        logs[h] = largest[h] + jnp.log(total[h])
        mixed_ref[:, pl.ds(h * width, width)] = unstack_heads(
            (mixed[h] / total[h]).T, per_head
        ).astype(mixed_ref.dtype)
    kv_copy(1, s, s ^ 1).wait_send()
    for d in near:

        @pl.when((s ^ d) > s)
        def _():
            kv_copy(d, s, s ^ d).wait_send()

    def handed(chip, _):
        hand_on(chip, core).wait_send()
        return 0

    lax.fori_loop(0, place, handed, 0)
    spread_finish()


def backward_kernel(
    grad_ref, query_ref, mixed_ref, logs, kv_all, branch_ref, normed_ref,
    cosine_ref, sine_ref, cosine_rows, sine_rows,
    inward_grad, inward_slices, attended_all, branch_all, normed_all, kv_grad,
    queries, grads, inner, query_sum, parts, part_come, final_come,
    send_part, come_part, send_final, come_final, send_slice, come_slice,
    send_mixed, come_mixed, send_normed, come_normed,
):
    group, s = lax.axis_size("seq"), lax.axis_index("seq")
    place, core = core_pair(s)
    local = query_ref.shape[0]
    per_head = HEADS // KV_HEADS
    width, pair = per_head * HEAD_DIM, 2 * HEAD_DIM
    scale = HEAD_DIM**-0.5
    slices, f = lax.axis_size("fsdp"), lax.axis_index("fsdp")
    share = branch_all.shape[2]
    meet_spread(range(1, group))

    def slice_copy(d, target):
        columns = pl.ds(pl.multiple_of(target * share, 128), share)
        return remote(
            branch_ref.at[:, columns], branch_all.at[d], send_slice.at[d], come_slice.at[d],
            "fsdp", target,
        )

    gathers = [
        gather_blocks(mixed_ref, lambda owner, holder: attended_all.at[owner ^ holder],
                      send_mixed, come_mixed),
        gather_blocks(normed_ref, lambda owner, holder: normed_all.at[owner ^ holder],
                      send_normed, come_normed),
    ]

    def gathers_early():
        for _, _, take, _ in gathers:
            take(0)

    def part_copy(chip, half):
        return remote(
            parts.at[chip, half], part_come.at[chip], send_part.at[chip], come_part.at[chip],
            "seq", s ^ 1,
        )

    def final_copy(chip, sender):
        return remote(
            parts.at[chip, core], final_come.at[sender], send_final.at[chip], come_final.at[sender],
            "seq", 2 * chip + core,
        )

    for d in range(1, slices):
        slice_copy(d, f ^ d).start()
    for _, begin, _, _ in gathers:
        begin()
    normed_all[0] = normed_ref[...]
    attended_all[0] = mixed_ref[...]
    branch_all[0] = branch_ref[:, pl.ds(pl.multiple_of(f * share, 128), share)]
    for h in range(KV_HEADS):
        columns = pl.ds(h * width, width)
        queries[h] = stack_heads(query_ref[:, columns], per_head) * jnp.bfloat16(scale)
        grad = stack_heads(grad_ref[:, columns], per_head)
        grads[h] = grad
        product = grad.astype(jnp.float32) * stack_heads(mixed_ref[:, columns], per_head).astype(
            jnp.float32
        )
        inner[h] = jnp.sum(product.T, axis=0, keepdims=True)
    query_sum[...] = jnp.zeros_like(query_sum)

    def head_grads(h, chip, masked):
        columns = pl.ds(pl.multiple_of(h * pair, pair), pair)
        kv = kv_all[chip, :, :, columns].reshape(2 * local, pair)
        keys, values = kv[:, :HEAD_DIM], kv[:, HEAD_DIM:]
        if masked:
            scores = masked_scores(keys, queries[h], local, core * local)
        else:
            scores = against(keys, queries[h])
        shares = jnp.exp(scores - logs[h])
        share_grad = against(values, grads[h])
        score_grad = (shares * (share_grad - inner[h])).astype(jnp.bfloat16)
        value_grad = dot(shares.astype(jnp.bfloat16), grads[h])
        key_grad = dot(score_grad, queries[h])
        part = jnp.concatenate([key_grad, value_grad], axis=1).astype(jnp.bfloat16)
        parts[chip, :, :, columns] = part.reshape(2, local, pair)
        query_sum[h] += outer(keys, score_grad)
        return 0

    def finish_chip(chip):
        part_copy(chip, core).wait_recv()
        parts[chip, core] = (
            parts[chip, core].astype(jnp.float32) + part_come[chip].astype(jnp.float32)
        ).astype(jnp.bfloat16)
        final_copy(chip, place).start()

    def earlier_chip(chip, _):
        @pl.when(chip == place - 1)
        def _():
            gathers_early()

        lax.fori_loop(0, KV_HEADS, lambda h, c: head_grads(h, chip, False), 0)
        part_copy(chip, 1 - core).start()

        @pl.when(chip > 0)
        def _():
            finish_chip(chip - 1)

        return 0

    lax.fori_loop(0, place, earlier_chip, 0)
    lax.fori_loop(0, KV_HEADS, lambda h, c: head_grads(h, place, True), 0)

    @pl.when(core == 1)
    def _():
        part_copy(place, 0).start()

    @pl.when(place == 0)
    def _():
        gathers_early()

    @pl.when(place > 0)
    def _():
        finish_chip(place - 1)

    half = HEAD_DIM // 2
    for h in range(KV_HEADS):
        total = query_sum[h] * scale
        one, two = total[:half], total[half:]
        turned = jnp.concatenate(
            [
                one * cosine_ref[...] + two * sine_ref[...],
                two * cosine_ref[...] - one * sine_ref[...],
            ],
            axis=0,
        )
        inward_grad[:, pl.ds(h * width, width)] = unstack_heads(turned.T, per_head).astype(
            jnp.bfloat16
        )
    kv_grad[...] = parts[place, core].astype(jnp.float32)

    @pl.when(core == 0)
    def _():
        part_copy(place, 0).wait_recv()
        kv_grad[...] += part_come[place].astype(jnp.float32)

    def later_chip(chip, _):
        final_copy(place, chip).wait_recv()
        kv_grad[...] += final_come[chip].astype(jnp.float32)
        return 0

    lax.fori_loop(place + 1, group // 2, later_chip, 0)
    key_grads, value_grads = [], []
    for h in range(KV_HEADS):
        field = kv_grad[:, pl.ds(h * pair, pair)]
        one, two = field[:, :half], field[:, half:HEAD_DIM]
        key_grads.append(one * cosine_rows[...] + two * sine_rows[...])
        key_grads.append(two * cosine_rows[...] - one * sine_rows[...])
        value_grads.append(field[:, HEAD_DIM:])
    inward_grad[:, pl.ds(HEADS * HEAD_DIM, 2 * KV_HEADS * HEAD_DIM)] = jnp.concatenate(
        key_grads + value_grads, axis=1
    ).astype(jnp.bfloat16)
    part_cols = inward_slices.shape[2]
    for t in range(slices):
        inward_slices[t] = inward_grad[:, pl.ds(t * part_cols, part_cols)]

    def sent(chip, _):
        part_copy(chip, 1 - core).wait_send()
        final_copy(chip, place).wait_send()
        return 0

    lax.fori_loop(0, place, sent, 0)

    @pl.when(core == 1)
    def _():
        part_copy(place, 0).wait_send()

    for d in range(1, slices):
        slice_copy(d, f ^ d).wait()
    for order, _, take, finish in gathers:
        for turn in range(1, len(order)):
            take(turn)
        finish()


def attend_forward(query, kv, out_rows, group, slices):
    local, width = query.shape
    per_head = HEADS // KV_HEADS
    columns = per_head * local
    pairs_seq, _, depth, _ = out_rows.shape
    tiles = KV_HEADS * group * columns * local
    return pl.pallas_call(
        forward_kernel,
        in_specs=[VMEM] * 3,
        out_specs=[VMEM] * 4,
        out_shape=[
            jax.ShapeDtypeStruct((group // 2, 2, local, kv.shape[1]), jnp.bfloat16),
            jax.ShapeDtypeStruct((local, width), jnp.bfloat16),
            jax.ShapeDtypeStruct((KV_HEADS, 1, columns), jnp.float32),
            jax.ShapeDtypeStruct(
                (pairs_seq, 2, slices, depth, out_rows.shape[3]), jnp.bfloat16
            ),
        ],
        scratch_shapes=[
            pltpu.VMEM((KV_HEADS, columns, HEAD_DIM), jnp.bfloat16),
            pltpu.VMEM((KV_HEADS, 1, columns), jnp.float32),
            pltpu.VMEM((KV_HEADS, 1, columns), jnp.float32),
            pltpu.VMEM((KV_HEADS, HEAD_DIM, columns), jnp.float32),
        ]
        + [pltpu.SemaphoreType.DMA((group,))] * 2
        + [pltpu.SemaphoreType.DMA((group // 2, 2))] * 2
        + [pltpu.SemaphoreType.DMA((slices,))] * 4,
        compiler_params=pltpu.CompilerParams(
            vmem_limit_bytes=56 << 20, collective_id=0, has_side_effects=True
        ),
        cost_estimate=pl.CostEstimate(
            flops=tiles * HEAD_DIM * 80, bytes_accessed=20 << 20, transcendentals=tiles
        ),
    )(query, kv, out_rows)


def attend_backward(
    grads, query, mixed, logs, kv_all, branch, normed, cosine, sine, group, slices
):
    local, features = branch.shape
    per_head = HEADS // KV_HEADS
    columns = per_head * local
    kv_cols = kv_all.shape[3]
    inward_cols = features + kv_cols
    tiles = KV_HEADS * group * columns * local
    gathered = jax.ShapeDtypeStruct((slices, local, features), jnp.bfloat16)
    stacked = pltpu.VMEM((KV_HEADS, columns, HEAD_DIM), jnp.bfloat16)
    one_half = pltpu.VMEM((group // 2, local, kv_cols), jnp.bfloat16)
    return pl.pallas_call(
        backward_kernel,
        in_specs=[VMEM] * 11,
        out_specs=[VMEM] * 5,
        out_shape=[
            jax.ShapeDtypeStruct((local, inward_cols), jnp.bfloat16),
            jax.ShapeDtypeStruct((slices, local, inward_cols // slices), jnp.bfloat16),
            gathered,
            jax.ShapeDtypeStruct((slices, local, features // slices), jnp.bfloat16),
            gathered,
        ],
        scratch_shapes=[
            pltpu.VMEM((local, kv_cols), jnp.float32),
            stacked,
            stacked,
            pltpu.VMEM((KV_HEADS, 1, columns), jnp.float32),
            pltpu.VMEM((KV_HEADS, HEAD_DIM, columns), jnp.float32),
            pltpu.VMEM((group // 2, 2, local, kv_cols), jnp.bfloat16),
            one_half,
            one_half,
        ]
        + [pltpu.SemaphoreType.DMA((group // 2,))] * 4
        + [pltpu.SemaphoreType.DMA((slices,))] * 6,
        compiler_params=pltpu.CompilerParams(
            vmem_limit_bytes=60 << 20, collective_id=1, has_side_effects=True
        ),
        cost_estimate=pl.CostEstimate(
            flops=tiles * HEAD_DIM * 80, bytes_accessed=20 << 20, transcendentals=tiles
        ),
    )(
        grads, query, mixed, logs, kv_all, branch, normed,
        jnp.tile(cosine.T, (1, per_head)), jnp.tile(sine.T, (1, per_head)), cosine, sine,
    )


def meet_slices():
    slices, f = lax.axis_size("fsdp"), lax.axis_index("fsdp")
    barrier = pltpu.get_barrier_semaphore()
    for d in range(1, slices):
        pl.semaphore_signal(
            barrier, inc=1, device_id={"fsdp": f ^ d}, device_id_type=pl.DeviceIdType.MESH
        )
    pl.semaphore_wait(barrier, slices - 1)


def row_copy(stage, target, sem, r):
    width = stage.shape[0]
    rows = pl.ds(pl.multiple_of(r * width, width), width)
    return pltpu.make_async_copy(stage, target.at[rows, :], sem)


def grad_rows(field, grads, target, stage, sems):
    width = stage.shape[1]
    steps = target.shape[0] // width

    def step(r, _):
        columns = pl.ds(pl.multiple_of(r * width, width), width)
        slot = lax.rem(r, 2)
        left = field[:, :, columns].reshape(grads[0].shape[0], width)

        @pl.when(r > 1)
        def _():
            row_copy(stage.at[slot], target, sems.at[slot], r - 2).wait()

        for k, grad in enumerate(grads):
            units = grad.shape[1]
            stage[slot, :, pl.ds(k * units, units)] = outer(left, grad[...]).astype(jnp.bfloat16)
        row_copy(stage.at[slot], target, sems.at[slot], r).start()
        return 0

    lax.fori_loop(0, steps, step, 0)
    for r in (steps - 2, steps - 1):
        row_copy(stage.at[r % 2], target, sems.at[r % 2], r).wait()


def feed_first_kernel(
    x_ref, dy_ref, gate_up_ref, x_all, gate_all, up_all, hidden, down_grad_out,
    gate_sum, up_sum, grad_stage, send_x, come_x, grad_sem, *, strip
):
    slices, f = lax.axis_size("fsdp"), lax.axis_index("fsdp")
    local = x_ref.shape[0]
    meet_slices()

    order, begin, take, sent = gather_blocks(
        x_ref, lambda owner, holder: x_all.at[owner ^ holder], send_x, come_x
    )
    begin()
    x_all[0] = x_ref[...]

    def token_block(turn, d):
        for i in range(slices - 1):

            @pl.when(turn == i + 1)
            def _():
                take(i)

        x = x_all[d]
        units = hidden.shape[1]
        gate_sum[...] = dot(x, gate_up_ref[:, pl.ds(0, units)])
        up_sum[...] = dot(x, gate_up_ref[:, pl.ds(units, units)])

        def part(i, _):
            rows = pl.ds(pl.multiple_of(i * strip, strip), strip)
            place = pl.ds(pl.multiple_of(d * local + i * strip, strip), strip)
            gate, up = gate_sum[rows, :], up_sum[rows, :]
            hidden[place, :] = (gate / (1.0 + jnp.exp(-gate)) * up).astype(jnp.bfloat16)
            gate_all[place, :] = gate.astype(jnp.bfloat16)
            up_all[place, :] = up.astype(jnp.bfloat16)
            return 0

        lax.fori_loop(0, local // strip, part, 0)
        following = 0
        for i in reversed(range(slices - 1)):
            following = jnp.where(turn == i, order[i], following)
        return following

    lax.fori_loop(0, slices, token_block, jnp.int32(0))
    grad_rows(dy_ref, [hidden], down_grad_out, grad_stage, grad_sem)
    sent()


def feed_second_kernel(
    x_ref, dy_ref, gate_all, up_all, hidden, gate_up_ref, down_ref,
    back_ref, out_parts, gate_up_grad_out,
    gate_grad, up_grad, hidden_sum, back_send, back_come, out_stage, grad_stage,
    send_back, come_back, out_sem, grad_sem, *, strip
):
    slices, f = lax.axis_size("fsdp"), lax.axis_index("fsdp")
    local = back_ref.shape[0]
    meet_slices()

    square = slices == 4
    order = block_order()
    first, second = (order[1], order[0]) if square else (None, None)
    turns = [3, second, first, 0] if square else list(range(slices - 1, -1, -1))

    def back_copy(d, target, landing):
        return remote(
            back_send.at[d], back_come.at[landing - 1], send_back.at[d], come_back.at[landing],
            "fsdp", f ^ target,
        )

    def out_copy(slot, d):
        return pltpu.make_async_copy(out_stage.at[slot], out_parts.at[d], out_sem.at[slot])

    def token_block(turn, carry):
        d, before = carry
        place = pl.ds(pl.multiple_of(d * local, local), local)
        hidden_sum[...] = dot(dy_ref[d], down_ref[...])

        def part(i, _):
            rows = pl.ds(pl.multiple_of(i * strip, strip), strip)
            here = pl.ds(pl.multiple_of(d * local + i * strip, strip), strip)
            gate = gate_all[here, :].astype(jnp.float32)
            up = up_all[here, :].astype(jnp.float32)
            sigmoid = 1.0 / (1.0 + jnp.exp(-gate))
            grad = hidden_sum[rows, :]
            gate_grad[here, :] = (
                grad * up * sigmoid * (1.0 + gate * (1.0 - sigmoid))
            ).astype(jnp.bfloat16)
            up_grad[here, :] = (grad * gate * sigmoid).astype(jnp.bfloat16)
            return 0

        lax.fori_loop(0, local // strip, part, 0)
        units = hidden.shape[1]
        back = against(gate_grad[place, :], gate_up_ref[:, pl.ds(0, units)])
        back = back + against(up_grad[place, :], gate_up_ref[:, pl.ds(units, units)])
        back_send[d] = back.astype(jnp.bfloat16)
        if square:

            @pl.when(turn == 0)
            def _():
                back_copy(3, first, 3).start()

            @pl.when(turn == 2)
            def _():
                back_copy(3, first, 3).wait_recv()
                back_send[second] = (
                    back_send[second].astype(jnp.float32) + back_come[2].astype(jnp.float32)
                ).astype(jnp.bfloat16)
                back_copy(second, second, second).start()
                back_copy(first, first, first).start()

        else:

            @pl.when(d > 0)
            def _():
                back_copy(d, d, d).start()

        @pl.when(turn > 1)
        def _():
            out_copy(lax.rem(turn, 2), before).wait()

        out_stage[lax.rem(turn, 2)] = against(hidden[place, :], down_ref[...]).astype(jnp.bfloat16)
        out_copy(lax.rem(turn, 2), d).start()
        following = 0
        for i in reversed(range(slices - 1)):
            following = jnp.where(turn == i, turns[i + 1], following)
        return following, d

    lax.fori_loop(0, slices, token_block, (jnp.int32(turns[0]), jnp.int32(0)))
    out_copy(0, 0).wait()
    out_copy(1, 0).wait()
    grad_rows(x_ref, [gate_grad, up_grad], gate_up_grad_out, grad_stage, grad_sem)
    if square:
        back_copy(3, first, 3).wait_send()
    for d in (1, 2) if square else range(1, slices):
        back_copy(d, d, d).wait()
    home = [back_send[0]] + [back_come[d - 1] for d in ((1, 2) if square else range(1, slices))]
    back_ref[...] = functools.reduce(jnp.add, [p.astype(jnp.float32) for p in home])


ANY = pl.BlockSpec(memory_space=pl.ANY)


def feed_first(x, upstream_all, gate_up_slice):
    slices, local, width = upstream_all.shape
    ff_cols = gate_up_slice.shape[1] // 2
    tokens = slices * local
    units = jax.ShapeDtypeStruct((tokens, ff_cols), jnp.bfloat16)
    high = pltpu.VMEM((local, ff_cols), jnp.float32)
    sems = pltpu.SemaphoreType.DMA((slices,))
    return pl.pallas_call(
        functools.partial(feed_first_kernel, strip=32),
        in_specs=[VMEM] * 3,
        out_specs=[VMEM] * 4 + [ANY],
        out_shape=[
            jax.ShapeDtypeStruct((slices, local, width), jnp.bfloat16),
            units,
            units,
            units,
            jax.ShapeDtypeStruct((width, ff_cols), jnp.bfloat16),
        ],
        scratch_shapes=[high, high, pltpu.VMEM((2, 256, ff_cols), jnp.bfloat16)]
        + [sems] * 2
        + [pltpu.SemaphoreType.DMA((2,))],
        compiler_params=pltpu.CompilerParams(
            vmem_limit_bytes=60 << 20, collective_id=4, has_side_effects=True
        ),
        cost_estimate=pl.CostEstimate(
            flops=10 * tokens * width * ff_cols, bytes_accessed=30 << 20, transcendentals=0
        ),
    )(x, upstream_all, gate_up_slice)


def feed_second(
    x_all, upstream_all, gate_all, up_all, hidden, gate_up_slice, down_slice
):
    slices, local, width = upstream_all.shape
    ff_cols = gate_up_slice.shape[1] // 2
    tokens = slices * local
    blocks = pltpu.VMEM((slices, local, width), jnp.bfloat16)
    low = pltpu.VMEM((tokens, ff_cols), jnp.bfloat16)
    sems = pltpu.SemaphoreType.DMA((slices,))
    return pl.pallas_call(
        functools.partial(feed_second_kernel, strip=32),
        in_specs=[VMEM] * 7,
        out_specs=[VMEM] + [ANY] * 2,
        out_shape=[
            jax.ShapeDtypeStruct((local, width), jnp.float32),
            jax.ShapeDtypeStruct((slices, local, width), jnp.bfloat16),
            jax.ShapeDtypeStruct((width, 2 * ff_cols), jnp.bfloat16),
        ],
        scratch_shapes=[low, low, pltpu.VMEM((local, ff_cols), jnp.float32), blocks]
        + [
            pltpu.VMEM((slices - 1, local, width), jnp.bfloat16),
            pltpu.VMEM((2, local, width), jnp.bfloat16),
            pltpu.VMEM((2, 256, 2 * ff_cols), jnp.bfloat16),
        ]
        + [sems] * 2
        + [pltpu.SemaphoreType.DMA((2,)), pltpu.SemaphoreType.DMA((2,))],
        compiler_params=pltpu.CompilerParams(
            vmem_limit_bytes=62 << 20, collective_id=5, has_side_effects=True
        ),
        cost_estimate=pl.CostEstimate(
            flops=20 * tokens * width * ff_cols, bytes_accessed=40 << 20, transcendentals=0
        ),
    )(x_all, upstream_all, gate_all, up_all, hidden, gate_up_slice, down_slice)


def home_kernel(*refs, count, moves, summed):
    slices, f = lax.axis_size("fsdp"), lax.axis_index("fsdp")
    sources, rest = refs[:count], refs[count:]
    results, rest = rest[: -(count + 2)], rest[-(count + 2) :]
    landed, (send, come) = rest[:count], rest[count:]
    depth = sources[0].shape[0] // slices
    meet_slices()

    def copy(k, d):
        rows = pl.ds(pl.multiple_of((f ^ d) * depth, depth), depth)
        return remote(
            sources[k].at[rows, :], landed[k].at[d], send.at[k, d], come.at[k, d], "fsdp", f ^ d
        )

    for k in range(count):
        for d in range(1, slices):
            copy(k, d).start()
    for k in range(count):
        landed[k][0] = sources[k][pl.ds(pl.multiple_of(f * depth, depth), depth), :]
    for k in range(count):
        for d in range(1, slices):
            copy(k, d).wait()
    for t in range(slices):
        for source, first, width, result, base in moves:
            results[result][:, pl.ds(base + t * width, width)] = landed[source][
                f ^ t, :, pl.ds(first, width)
            ]
    if summed:
        source, first = summed
        results[-1][...] = functools.reduce(
            jnp.add,
            [landed[source][d, :, pl.ds(first, 128)].astype(jnp.float32) for d in range(slices)],
        )


def bring_home(sources, moves, widths, summed, slices, number):
    depth = sources[0].shape[0] // slices
    shapes = [jax.ShapeDtypeStruct((depth, width), jnp.bfloat16) for width in widths]
    if summed:
        shapes.append(jax.ShapeDtypeStruct((depth, 128), jnp.float32))
    return pl.pallas_call(
        functools.partial(home_kernel, count=len(sources), moves=moves, summed=summed),
        in_specs=[VMEM] * len(sources),
        out_specs=[VMEM] * len(shapes),
        out_shape=shapes,
        scratch_shapes=[pltpu.VMEM((slices, depth, s.shape[1]), jnp.bfloat16) for s in sources]
        + [pltpu.SemaphoreType.DMA((len(sources), slices))] * 2,
        compiler_params=pltpu.CompilerParams(
            vmem_limit_bytes=32 << 20, collective_id=number, has_side_effects=True
        ),
        cost_estimate=pl.CostEstimate(flops=10 << 30, bytes_accessed=4 << 20, transcendentals=0),
    )(*sources)


def swap(piece, axis, offset):
    size = lax.axis_size(axis)
    return lax.ppermute(piece, axis, [(i, i ^ offset) for i in range(size)])


def gather_swap(piece, axis):
    return [piece] + [swap(piece, axis, d) for d in range(1, lax.axis_size(axis))]


def exchange_swap(stack, axis):
    me = lax.axis_index(axis)
    pieces = [
        lax.dynamic_index_in_dim(stack, me ^ d, 0, keepdims=False)
        for d in range(lax.axis_size(axis))
    ]
    return [pieces[0]] + [swap(p, axis, d) for d, p in enumerate(pieces) if d]


def reduce_swap(parts, axis):
    total = parts[0].astype(jnp.float32)
    for d in range(1, len(parts)):
        total = total + swap(parts[d], axis, d).astype(jnp.float32)
    return total


def scatter_rows(partial, after=()):
    partial, *_ = lax.optimization_barrier((partial, *after))
    return lax.psum_scatter(partial, "seq", scatter_dimension=0, tiled=True)


def adam_update(weight, first, second, grad, rate, decay):
    first_new = beta_first * first + (1.0 - beta_first) * grad
    second_new = beta_second * second + (1.0 - beta_second) * grad * grad
    first_hat = first_new / (1.0 - beta_first**STEP)
    second_hat = second_new / (1.0 - beta_second**STEP)
    weight_new = weight - rate * (
        first_hat / (jnp.sqrt(second_hat) + adam_epsilon) + decay * weight
    )
    return (first_new, second_new, weight_new)


def body(
    inputs,
    cotangent,
    w_inward,
    w_outward,
    w_gate_up,
    w_down,
    gains,
    first_inward,
    first_outward,
    first_gate_up,
    first_down,
    first_gains,
    second_inward,
    second_outward,
    second_gate_up,
    second_down,
    second_gains,
):
    rows = inputs[0].astype(jnp.float32)
    upstream = cotangent[0]
    local = rows.shape[0]
    group = lax.axis_size("seq")
    slices = lax.axis_size("fsdp")
    kv_width = KV_HEADS * HEAD_DIM
    inward_cols = D + 2 * kv_width
    ff_cols = FF // slices
    depth = w_inward.shape[0]
    position = (lax.axis_index("seq") * local + jnp.arange(local)).astype(jnp.float32)

    low_gains = jnp.pad(jnp.transpose(gains.astype(jnp.bfloat16)), ((0, 0), (0, 126)))
    feed_gate_up, feed_down, in_rows = share_weights(
        w_inward, low_gains, w_gate_up, w_down, group, slices
    )
    gate_up_slice = lax.all_gather(feed_gate_up, "seq", axis=0, tiled=True)
    inward_gains, out_rows = spread_rows(in_rows, w_outward, slices)
    inward_full = inward_gains[:, :inward_cols]
    gain_first = inward_gains[:, inward_cols].astype(jnp.float32)
    gain_second = inward_gains[:, inward_cols + 1].astype(jnp.float32)

    scale_first = rms_scale(rows)
    normed = (rows * scale_first * gain_first).astype(jnp.bfloat16)
    mixed = dot(normed, inward_full)
    query = rotate(mixed[:, :D].reshape(local, HEADS, HEAD_DIM), position, 1.0).astype(jnp.bfloat16)
    key = rotate(
        mixed[:, D : D + kv_width].reshape(local, KV_HEADS, HEAD_DIM), position, 1.0
    ).astype(jnp.bfloat16)
    value = mixed[:, D + kv_width :].reshape(local, KV_HEADS, HEAD_DIM).astype(jnp.bfloat16)
    kv = jnp.concatenate([key, value], axis=-1).reshape(local, 2 * kv_width)
    query = query.reshape(local, D)
    kv_all, attended, logs, outward_full = attend_forward(query, kv, out_rows, group, slices)
    outward_full = outward_full.reshape(D, D)
    upstream_late, _ = lax.optimization_barrier((upstream, inward_gains))
    upstream_blocks = gather_swap(upstream_late, "fsdp")
    attended, upstream_blocks = lax.optimization_barrier((attended, upstream_blocks))
    down_slice = lax.all_gather(feed_down, "seq", axis=0, tiled=True)
    upstream_all = jnp.stack(upstream_blocks)
    middle = rows + dot(attended, outward_full)
    scale_second = rms_scale(middle)
    normed_second = (middle * scale_second * gain_second).astype(jnp.bfloat16)

    def add_up(parts):
        return functools.reduce(jnp.add, [p.astype(jnp.float32) for p in parts])

    normed_all, gate_all, up_all, hidden, down_partial = feed_first(
        normed_second, upstream_all, gate_up_slice
    )
    normed_second_grad, out_parts, gate_up_partial = feed_second(
        normed_all, upstream_all, gate_all, up_all, hidden, gate_up_slice, down_slice
    )
    down_mine = scatter_rows(down_partial)
    gate_up_mine = scatter_rows(gate_up_partial)
    middle_back, gain_second_grad = norm_back(middle, scale_second, gain_second, normed_second_grad)
    middle_grad = upstream.astype(jnp.float32) + middle_back
    branch_low = middle_grad.astype(jnp.bfloat16)
    attended_grad = against(branch_low, outward_full).astype(jnp.bfloat16)
    exponent = jnp.arange(HEAD_DIM // 2).astype(jnp.float32) * (-2.0 / HEAD_DIM)
    angle = position[:, None] * jnp.power(rope_base, exponent)[None, :]
    inward_grad, inward_slices, attended_all, branch_all, first_all = attend_backward(
        attended_grad, query, attended, logs, kv_all, branch_low, normed,
        jnp.cos(angle), jnp.sin(angle), group, slices,
    )
    out_parts = [out_parts[0]] + [swap(out_parts[d], "fsdp", d) for d in range(1, slices)]
    inward_grad, inward_slices, attended_all, branch_all, first_all, down_mine, out_parts = (
        lax.optimization_barrier(
            (inward_grad, inward_slices, attended_all, branch_all, first_all, down_mine, out_parts)
        )
    )
    result = middle + add_up(out_parts)
    inward_grad_blocks = exchange_swap(inward_slices, "fsdp")
    outward_mine = scatter_rows(
        outer(attended_all.reshape(-1, D), branch_all.reshape(-1, D // slices)).astype(jnp.bfloat16)
    )

    normed_grad = against(inward_grad, inward_full)
    rows_back, gain_first_grad = norm_back(rows, scale_first, gain_first, normed_grad)
    input_grad = middle_grad + rows_back

    inward_grad_blocks, gain_first_grad, down_mine, gate_up_mine = lax.optimization_barrier(
        (inward_grad_blocks, gain_first_grad, down_mine, gate_up_mine)
    )
    gain_grads = jnp.stack([gain_first_grad, gain_second_grad], axis=1)
    gain_grads = jnp.pad(gain_grads.astype(jnp.bfloat16), ((0, 0), (0, 126)))
    inward_partial = outer(first_all.reshape(-1, D), jnp.concatenate(inward_grad_blocks, axis=0))
    inward_partial = inward_partial.astype(jnp.bfloat16)
    slice_cols = inward_partial.shape[1]
    inward_mine = scatter_rows(jnp.concatenate([inward_partial, gain_grads], axis=1))
    gate_up_sum, down_sum = bring_home(
        [gate_up_mine, down_mine],
        [(0, 0, ff_cols, 0, 0), (0, ff_cols, ff_cols, 0, FF), (1, 0, ff_cols, 1, 0)],
        [2 * FF, FF], None, slices, 6,
    )
    inward_sum, outward_sum, gains_sum = bring_home(
        [inward_mine, outward_mine],
        [(0, 0, slice_cols, 0, 0), (1, 0, D // slices, 1, 0)],
        [inward_cols, D], (0, slice_cols), slices, 7,
    )
    gate_up_sum, down_sum, inward_sum, outward_sum = [
        field.astype(jnp.float32) for field in (gate_up_sum, down_sum, inward_sum, outward_sum)
    ]
    gains_sum = jnp.transpose(gains_sum[:, :2])
    first_inward_new, second_inward_new, inward_new = adam_update(
        w_inward, first_inward, second_inward, inward_sum, 0.02, weight_decay
    )
    first_outward_new, second_outward_new, outward_new = adam_update(
        w_outward, first_outward, second_outward, outward_sum, 0.15, weight_decay
    )
    first_gate_up_new, second_gate_up_new, gate_up_new = adam_update(
        w_gate_up, first_gate_up, second_gate_up, gate_up_sum, 0.02, weight_decay
    )
    first_down_new, second_down_new, down_new = adam_update(
        w_down, first_down, second_down, down_sum, 0.015, weight_decay
    )
    first_gains_new, second_gains_new, gains_new = adam_update(
        gains, first_gains, second_gains, gains_sum, 0.6, 0.0
    )
    return (
        result[None].astype(jnp.bfloat16),
        input_grad[None],
        first_inward_new,
        second_inward_new,
        inward_new,
        first_outward_new,
        second_outward_new,
        outward_new,
        first_gate_up_new,
        second_gate_up_new,
        gate_up_new,
        first_down_new,
        second_down_new,
        down_new,
        first_gains_new,
        second_gains_new,
        gains_new,
    )


def solution(mesh):
    in_specs = (
        P("fsdp", "seq", None),
        P("fsdp", "seq", None),
        P(("seq", "fsdp"), None),
        P(("seq", "fsdp"), None),
        P(("seq", "fsdp"), None),
        P(("seq", "fsdp"), None),
        P(None, ("seq", "fsdp")),
        P(("seq", "fsdp"), None),
        P(("seq", "fsdp"), None),
        P(("seq", "fsdp"), None),
        P(("seq", "fsdp"), None),
        P(None, ("seq", "fsdp")),
        P(("seq", "fsdp"), None),
        P(("seq", "fsdp"), None),
        P(("seq", "fsdp"), None),
        P(("seq", "fsdp"), None),
        P(None, ("seq", "fsdp")),
    )
    out_specs = (
        P("fsdp", "seq", None),
        P("fsdp", "seq", None),
        P(("seq", "fsdp"), None),
        P(("seq", "fsdp"), None),
        P(("seq", "fsdp"), None),
        P(("seq", "fsdp"), None),
        P(("seq", "fsdp"), None),
        P(("seq", "fsdp"), None),
        P(("seq", "fsdp"), None),
        P(("seq", "fsdp"), None),
        P(("seq", "fsdp"), None),
        P(("seq", "fsdp"), None),
        P(("seq", "fsdp"), None),
        P(("seq", "fsdp"), None),
        P(None, ("seq", "fsdp")),
        P(None, ("seq", "fsdp")),
        P(None, ("seq", "fsdp")),
    )
    return jax.shard_map(body, mesh=mesh, in_specs=in_specs, out_specs=out_specs, check_vma=False)
```

time: 712 us -> 631 us (0.89)
  waiting for transfers between devices: 98.2 us -> 18.2 us
    ppermute x15 -> x9, waiting for transfers between devices: 44.4 us -> 0.03 us  [swap(): return lax.ppermute(piece, axis, [(i, i ^ offset) for i in range(size)])]
    reduce_scatter x4, waiting for transfers between devices: 53.7 us -> 18 us  [scatter_rows(): return lax.psum_scatter(partial, 'seq', scatter_dimension=0, tiled=True)]
    pallas_call x2 -> x4, Pallas kernels: 209 us -> 228 us  [the longest x1 136 us: attend_backward(): pl.pallas_call(backward_kernel, in_specs=[VMEM] * 11, out_specs=[VMEM] *...]
    pallas_call x1, Pallas kernels: 70.1 us -> 58.9 us  [spread_rows(): pl.pallas_call(spread_kernel, in_specs=[VMEM] * 2, out_specs=[VMEM] * 2,...]
    reduce_scatter x4, starting transfers between devices: 0.78 us -> 11.7 us  [scatter_rows(): return lax.psum_scatter(partial, 'seq', scatter_dimension=0, tiled=True)]
    pallas_call x1, Pallas kernels: 71.8 us -> 62.7 us  [feed_first(): pl.pallas_call(functools.partial(feed_first_kernel, strip=32), in_specs=[...]
    ppermute x15 -> x9, starting transfers between devices: 14.3 us -> 8.01 us  [swap(): return lax.ppermute(piece, axis, [(i, i ^ offset) for i in range(size)])]
    unnamed x108 -> x120, local copies, waits for them, and re-layouts: 17 us -> 18.5 us
  transfers between devices with their start and end apart: 21 -> 15, of which waited for: 8 -> 1; matrix products, arithmetic and copies ran while one was open for 12% -> 15% of each run, Pallas kernels for 60% -> 65%
where the time goes in v4:
time: 631 us; the launch traced here: 620 us
  Pallas kernels  452 us (72%)
  other arithmetic  40.4 us (6%)
  matrix products  37.5 us (6%)
  local copies, waits for them, and re-layouts  37.4 us (6%)
  starting transfers between devices  19.8 us (3%)
  waiting for transfers between devices  18.2 us (3%)
  between operations  15.2 us (2%)
    pallas_call x1, Pallas kernels, attend_backward(): pl.pallas_call(backward_kernel, in_specs=[VMEM] * 11, out_specs=[VMEM] *...  136 us
    pallas_call x1, Pallas kernels, attend_forward(): pl.pallas_call(forward_kernel, in_specs=[VMEM] * 3, out_specs=[VMEM] * 4,...  63.6 us
    pallas_call x1, Pallas kernels, feed_first(): pl.pallas_call(functools.partial(feed_first_kernel, strip=32), in_specs=[...  62.7 us
    pallas_call x1, Pallas kernels, feed_second(): pl.pallas_call(functools.partial(feed_second_kernel, strip=32), in_specs=...  62.3 us
    pallas_call x1, Pallas kernels, spread_rows(): pl.pallas_call(spread_kernel, in_specs=[VMEM] * 2, out_specs=[VMEM] * 2,...  58.9 us
    pallas_call x1, Pallas kernels, share_weights(): pl.pallas_call(share_kernel, in_specs=[VMEM] * 4, out_specs=[VMEM] * 3, o...  40.4 us
    pallas_call x2, Pallas kernels, bring_home(): pl.pallas_call(functools.partial(home_kernel, count=len(sources), moves=m...  27.6 us
    unnamed x120, local copies, waits for them, and re-layouts  18.5 us
  transfers between devices with their start and end apart: 15, of which 1 were waited for; matrix products, arithmetic and copies ran while one was open for 15% of the time, Pallas kernels for 65%

profile of v4, /device:TPU:9, one launch (start us, length us, event | category | flops | bytes accessed | tf_op | source)
XLA Modules:
  0.0 620.2 jit_solution(15872371181432317797)
XLA Ops:
  7.2 0.7 convert_element_type.115
  8.1 1.4 copy-done
  9.4 1.1 copy-done.3
  10.5 40.4 %shard_map.296 = (bf16[256,2816]{1,0:T(8,128)(2,1)}, bf16[256,1408]{1,0:T(8,128)(2,1)}, bf16[4,2,64,2688]{3,2,1,0:T(8,128)(2,1)}) custom-call(f32[64,2560]{1,0:T(8,128)S(1)} %copy-done.3, bf16[64,128]{1,0:T(8,128)(2,1)S(1)} %pad.8.gain_ref, f32[64,11264]{1,0:T(8,128)} %gate_up_ref.1, f32[64,5632]{1,0:T(8,128)S(1)} %copy-done), custom_call_target="tpu_custom_call" | custom-call | tf_op jit(solution)/shard_map/pallas_call | solution.py:178
  51.0 1.8 copy-done.2
  52.7 58.9 %shard_map.297 = (bf16[4,2,4,64,2688]{4,3,2,1,0:T(8,128)(2,1)}, bf16[4,2,64,2048]{3,2,1,0:T(8,128)(2,1)S(1)}) custom-call(bf16[4,2,64,2688]{3,2,1,0:T(8,128)(2,1)S(1)} %copy-done.2, f32[64,2048]{1,0:T(8,128)S(1)} %copy-done.5), custom_call_target="tpu_custom_call" | custom-call | tf_op jit(solution)/shard_map/pallas_call | solution.py:306
  111.6 1.3 copy-done.7
  113.0 2.6 collective-permute-start.2
  115.7 2.5 slice_convert_fusion
  119.7 6.0 fusion.2
  125.8 0.7 slice.66
  126.5 0.7 slice.92
  127.3 1.1 copy.115
  129.0 1.2 multiply_cosine_fusion
  130.2 0.7 copy.113
  130.9 1.6 copy.114
  132.5 1.7 copy.118
  134.1 0.8 subtract_convert_fusion.1
  135.0 0.9 pad_maximum_fusion.2
  135.9 0.8 copy.138.kv_ref
  136.7 1.8 copy.111
  138.6 1.9 subtract_convert_fusion
  140.5 1.4 copy.120.query_ref
  142.0 63.6 %shard_map.298 = (bf16[4,2,256,512]{3,2,1,0:T(8,128)(2,1)}, bf16[256,2048]{1,0:T(8,128)(2,1)}, f32[4,1,2048]{2,1,0:T(1,128)}, bf16[4,2,4,64,2048]{4,3,2,1,0:T(8,128)(2,1)}) custom-call(bf16[256,2048]{1,0:T(8,128)(2,1)} %copy.120.query_ref, bf16[256,512]{1,0:T(8,128)(2,1)} %copy.138.kv_ref, bf16[4,2,64,2048]{3,2,1,0:T(8,128)(2,1)} %copy-done.7), custom_call_target="tpu_custom_call" | custom-call | flops 85899345920 | bytes 20971520 | tf_op jit(solution)/shard_map/pallas_call | solution.py:618
  206.0 6.7 %multiply_reduce_fusion.2 = (f32[256]{0:T(256)S(1)}, f32[256,2048]{1,0:T(8,128)S(1)}) fusion(bf16[256,2048]{1,0:T(8,128)(2,1)} %get-tuple-element.72.mixed_ref, bf16[2048,2048]{1,0:T(8,128)(2,1)} %bitcast.87, bf16[1,256,2048]{2,1,0:T(8,128)(2,1)S(1)} %copy-done.15), kind=kOutput, calls=%fused_computation.38 | convolution fusion | flops 2149580544 | bytes 12583936 | tf_op jit(solution)/shard_map/dot_general | solution.py:55
  212.7 4.6 pad_maximum_fusion.dy_ref
  217.2 1.2 multiply_convert_fusion.x_ref
  218.5 62.7 %shard_map.299 = (bf16[4,256,2048]{2,1,0:T(8,128)(2,1)}, bf16[1024,1408]{1,0:T(8,128)(2,1)}, bf16[1024,1408]{1,0:T(8,128)(2,1)}, bf16[1024,1408]{1,0:T(8,128)(2,1)}, bf16[2048,1408]{1,0:T(8,128)(2,1)}) custom-call(bf16[256,2048]{1,0:T(8,128)(2,1)} %multiply_convert_fusion.x_ref, bf16[4,256,2048]{2,1,0:T(8,128)(2,1)} %pad_maximum_fusion.dy_ref, ...), custom_call_target="tpu_custom_call" | custom-call | flops 29527900160 | bytes 31457280 | tf_op jit(solution)/shard_map/pallas_call | solution.py:882
  281.3 62.3 %shard_map.300 = (f32[256,2048]{1,0:T(8,128)}, bf16[4,256,2048]{2,1,0:T(8,128)(2,1)}, bf16[2048,2816]{1,0:T(8,128)(2,1)}) custom-call(bf16[4,256,2048]{2,1,0:T(8,128)(2,1)} %get-tuple-element.79.x_ref, bf16[4,256,2048]{2,1,0:T(8,128)(2,1)} %pad_maximum_fusion.dy_ref, bf16[1024,1408]{1,0:T(8,128)(2,1)} %get-tuple-element.80.gate_all, ...), custom_call_target="tpu_custom_call" | custom-call | flops 59055800320 | bytes 41943040 | tf_op jit(solution)/shard_map/pallas_call | solution.py:914
  343.6 11.3 %reduce-scatter.11.cloned.1.call-start = ((), (), s32[]{:S(2)}) async-start(), calls=%async_computation.9 | async-start | bytes 2359296 | tf_op jit(solution)/shard_map/reduce_scatter | solution.py:1021
  355.2 0.8 copy.141
  356.0 0.8 copy.142
  356.8 4.6 slice_bitcast_fusion
  361.4 1.1 collective-permute-start.3
  362.5 1.2 collective-permute-start.4
  364.6 4.5 fusion.45
  369.1 3.3 convolution_convert_fusion.1.grad_ref
  372.4 136.3 %shard_map.301 = (bf16[256,2560]{1,0:T(8,128)(2,1)}, bf16[4,256,640]{2,1,0:T(8,128)(2,1)}, bf16[4,256,2048]{2,1,0:T(8,128)(2,1)}, bf16[4,256,512]{2,1,0:T(8,128)(2,1)}, bf16[4,256,2048]{2,1,0:T(8,128)(2,1)}) custom-call(bf16[256,2048]{1,0:T(8,128)(2,1)} %convolution_convert_fusion.1.grad_ref, bf16[256,2048]{1,0:T(8,128)(2,1)} %copy.120.query_ref, ...), custom_call_target="tpu_custom_call" | custom-call | flops 85899345920 | bytes 20971520 | tf_op jit(solution)/shard_map/pallas_call | solution.py:660
  508.8 6.5 %bitcast_convert_fusion = bf16[2048,512]{1,0:T(8,128)(2,1)} fusion(bf16[4,256,2048]{2,1,0:T(8,128)(2,1)} %get-tuple-element.108, bf16[4,256,512]{2,1,0:T(8,128)(2,1)} %get-tuple-element.109), kind=kOutput, calls=%fused_computation.14 | convolution fusion | flops 2148532224 | bytes 7340032 | tf_op jit(solution)/shard_map/dot_general | solution.py:59
  516.2 0.7 copy.128
  517.0 1.5 dynamic-slice_bitcast_fusion
  518.5 1.1 collective-permute-start.6
  520.0 1.2 collective-permute-start.8
  521.2 8.9 %fusion.17 = (bf16[2048]{0:T(1024)(128)(2,1)}, f32[256]{0:T(256)}, f32[256,2048]{1,0:T(8,128)}) fusion(bf16[1,256,2048]{2,1,0:T(8,128)(2,1)S(1)} %copy-done.16, f32[256]{0:T(256)} %copy-done.39, f32[2048]{0:T(1024)S(1)} %bitcast.84, bf16[256,2560]{1,0:T(8,128)(2,1)S(1)} %copy-done.53, bf16[2048,2688]{1,0:T(8,128)(2,1)} %bitcast.82), kind=kOutput, calls=%fused_computation.32 | convolution fusion | flops 2688022272 | bytes 14956544 | tf_op jit(solution)/shard_map/dot_general | solution.py:65
  530.1 3.4 fusion.27
  533.5 0.7 copy-done.51
  534.2 0.7 copy-done.52
  534.9 0.7 stack.32
  536.0 6.0 convolution_convert_fusion
  542.0 2.0 fusion.5
  544.0 0.6 copy-done.50
  544.6 1.0 copy-done.17
  545.6 3.7 fusion.14
  549.3 18.2 %shard_map.303 = (bf16[64,11264]{1,0:T(8,128)(2,1)S(1)}, bf16[64,5632]{1,0:T(8,128)(2,1)S(1)}) custom-call(bf16[256,2816]{1,0:T(8,128)(2,1)S(1)} %copy-done.8, bf16[256,1408]{1,0:T(8,128)(2,1)S(1)} %copy-done.9), custom_call_target="tpu_custom_call" | custom-call | flops 10737418240 | bytes 4194304 | tf_op jit(solution)/shard_map/pallas_call | solution.py:980
  567.5 2.8 multiply_subtract_fusion.1
  570.3 1.5 copy-done.21
  571.8 0.9 copy-done.22
  572.7 5.2 multiply_subtract_fusion
  577.9 18.0 %reduce-scatter.9.cloned.1.call-done.refs_0_ = bf16[256,768]{1,0:T(8,128)(2,1)} async-done(((bf16[2048,768]{1,0:T(8,128)(2,1)}), bf16[256,768]{1,0:T(8,128)(2,1)}) %reduce-scatter.9.cloned.1.call-update) | async-done | bytes 393232 | tf_op jit(solution)/shard_map/reduce_scatter | solution.py:1021
  596.0 1.0 copy-done.10
  597.0 0.9 copy-done.11
  597.9 9.5 %shard_map.302 = (bf16[64,2560]{1,0:T(8,128)(2,1)S(1)}, bf16[64,2048]{1,0:T(8,128)(2,1)S(1)}, f32[64,128]{1,0:T(8,128)S(1)}) custom-call(bf16[256,768]{1,0:T(8,128)(2,1)S(1)} %copy-done.10, bf16[256,512]{1,0:T(8,128)(2,1)S(1)} %copy-done.11), custom_call_target="tpu_custom_call" | custom-call | flops 10737418240 | bytes 4194304 | tf_op jit(solution)/shard_map/pallas_call | solution.py:980
  609.6 1.6 multiply_subtract_fusion.2
  611.5 1.4 multiply_subtract_fusion.3
  (164 shorter events, 8.5 us)
Async XLA Ops:
  7.2 211.3 %all-gather.3.cloned.1.call-start = ((), (), s32[]{:S(2)}) async-start(), calls=%async_computation.4 | async-start | bytes 12976128 | tf_op jit(solution)/shard_map/all_gather | solution.py:1069
  8.0 1.4 copy-start
  9.4 1.1 copy-start.3
  10.5 40.5 %copy-start.5 = (f32[64,2048]{1,0:T(8,128)S(1)}, f32[64,2048]{1,0:T(8,128)}, u32[]{:S(2)}) copy-start(f32[64,2048]{1,0:T(8,128)} %out_ref.1) | copy-start | bytes 1572868
  50.9 230.4 %all-gather.5.cloned.1.call-start = ((), (), s32[]{:S(2)}) async-start(), calls=%async_computation.5 | async-start | bytes 6488064 | tf_op jit(solution)/shard_map/all_gather | solution.py:1090
  51.0 1.8 copy-start.2
  111.6 1.3 copy-start.7
  112.9 93.0 %collective-permute-start = (bf16[256,2048]{1,0:T(8,128)(2,1)}, bf16[256,2048]{1,0:T(8,128)(2,1)}, u32[]{:S(2)}, u32[]{:S(2)}) collective-permute-start(bf16[256,2048]{1,0:T(8,128)(2,1)} %bitcast.10), channel_id=1, source_target_pairs={{0,1},{1,0},{2,3},{3,2},{4,5},{5,4},{6,7},{7,6},{8,9},{9,8},{10,11... | collective-permute-start | bytes 3145736 | tf_op jit(solution)/shard_map/ppermute | solution.py:996
  112.9 93.0 %collective-permute-start.1 = (bf16[256,2048]{1,0:T(8,128)(2,1)}, bf16[256,2048]{1,0:T(8,128)(2,1)}, u32[]{:S(2)}, u32[]{:S(2)}) collective-permute-start(bf16[256,2048]{1,0:T(8,128)(2,1)} %bitcast.10), channel_id=1, source_target_pairs={{0,2},{1,3},{2,0},{3,1},{4,6},{5,7},{6,4},{7,5},{8,10},{9,11},{10,... | collective-permute-start | bytes 3145736 | tf_op jit(solution)/shard_map/ppermute | solution.py:996
  113.0 93.0 %collective-permute-start.2 = (bf16[256,2048]{1,0:T(8,128)(2,1)}, bf16[256,2048]{1,0:T(8,128)(2,1)}, u32[]{:S(2)}, u32[]{:S(2)}) collective-permute-start(bf16[256,2048]{1,0:T(8,128)(2,1)} %bitcast.10), channel_id=1, source_target_pairs={{0,3},{1,2},{2,1},{3,0},{4,7},{5,6},{6,5},{7,4},{8,11},{9,10},{10,... | collective-permute-start | bytes 3145736 | tf_op jit(solution)/shard_map/ppermute | solution.py:996
  115.6 2.9 copy-start.15
  115.6 393.2 %reduce-scatter.5.cloned.1.call-start = ((), (), s32[]{:S(2)}) async-start(), calls=%async_computation.6 | async-start | bytes 6488064 | tf_op jit(solution)/shard_map/reduce_scatter | solution.py:1021
  118.2 10.3 %copy-start.46 = (f32[32]{0:T(128)}, f32[32]{0:T(128)S(1)}, u32[]{:S(2)}) copy-start(f32[32]{0:T(128)S(1)} %multiply_power_fusion) | copy-start | bytes 388
  118.5 7.3 %copy-start.37 = (f32[2048,1]{0,1:T(1,128)}, f32[2048,1]{0,1:T(1,128)S(1)}, u32[]{:S(2)}) copy-start(f32[2048,1]{0,1:T(1,128)S(1)} %copy.143) | copy-start | bytes 24580
  119.4 6.4 %copy-start.39 = (f32[256]{0:T(256)}, f32[256]{0:T(256)S(1)}, u32[]{:S(2)}) copy-start(f32[256]{0:T(256)S(1)} %get-tuple-element.228) | copy-start | bytes 3076
  119.7 6.1 copy-start.27
  130.2 8.4 %copy-start.31 = (f32[256,32]{1,0:T(8,128)}, f32[256,32]{1,0:T(8,128)S(1)}, u32[]{:S(2)}) copy-start(f32[256,32]{1,0:T(8,128)S(1)} %get-tuple-element.225.cosine_rows) | copy-start | bytes 98308
  136.7 1.8 copy-start.34
  136.7 1.8 copy-start.35
  142.0 63.6 %copy-start.19 = (f32[2048,1]{1,0:T(8,128)S(1)}, f32[2048,1]{1,0:T(8,128)}, u32[]{:S(2)}) copy-start(f32[2048,1]{1,0:T(8,128)} %get-tuple-element.207) | copy-start | bytes 24580
  212.6 4.6 copy-start.12
  281.2 253.7 %reduce-scatter.7.cloned.1.call-start = ((), (), s32[]{:S(2)}) async-start(), calls=%async_computation.7 | async-start | bytes 12976128 | tf_op jit(solution)/shard_map/reduce_scatter | solution.py:1021
  343.6 11.4 %copy-start.42 = (f32[256]{0:T(256)S(1)}, f32[256]{0:T(256)}, u32[]{:S(2)}) copy-start(f32[256]{0:T(256)} %copy-done.41) | copy-start | bytes 3076
  343.6 11.4 %copy-start.47 = (f32[32]{0:T(128)S(1)}, f32[32]{0:T(128)}, u32[]{:S(2)}) copy-start(f32[32]{0:T(128)} %copy-done.46) | copy-start | bytes 388
  343.6 234.3 %reduce-scatter.11.cloned.1.call-start = ((), (), s32[]{:S(2)}) async-start(), calls=%async_computation.9 | async-start | bytes 2359296 | tf_op jit(solution)/shard_map/reduce_scatter | solution.py:1021
  356.8 7.2 %copy-start.13 = (f32[256,2048]{1,0:T(8,128)S(1)}, f32[256,2048]{1,0:T(8,128)}, u32[]{:S(2)}) copy-start(f32[256,2048]{1,0:T(8,128)} %copy-done.12) | copy-start | bytes 6291460
  356.8 7.2 %copy-start.18 = (f32[256,2048]{1,0:T(8,128)S(1)}, f32[256,2048]{1,0:T(8,128)}, u32[]{:S(2)}) copy-start(f32[256,2048]{1,0:T(8,128)} %get-tuple-element.84) | copy-start | bytes 6291460
  356.8 12.3 %slice-start = ((s8[8388608]{0:T(1024)(128)(4,1)}), s8[4194304]{0:T(1024)(128)(4,1)S(1)}, s32[]{:S(2)}) async-start(s8[8388608]{0:T(1024)(128)(4,1)} %bitcast.88), calls=%async_computation.10 | async-start | bytes 8388608
  361.4 147.3 %collective-permute-start.3 = (bf16[256,2048]{1,0:T(8,128)(2,1)}, bf16[256,2048]{1,0:T(8,128)(2,1)S(1)}, u32[]{:S(2)}, u32[]{:S(2)}) collective-permute-start(bf16[256,2048]{1,0:T(8,128)(2,1)} %get-tuple-element.211), channel_id=1, source_target_pairs={{0,1},{1,0},{2,3},{3,2},{4,5},{5,4},{6,7},{7,6},{8,9},{9,8},{10,11... | collective-permute-start | bytes 3145736 | tf_op jit(solution)/shard_map/ppermute | solution.py:996
  362.5 146.2 %collective-permute-start.4 = (bf16[256,2048]{1,0:T(8,128)(2,1)}, bf16[256,2048]{1,0:T(8,128)(2,1)}, u32[]{:S(2)}, u32[]{:S(2)}) collective-permute-start(bf16[256,2048]{1,0:T(8,128)(2,1)} %get-tuple-element.210), channel_id=1, source_target_pairs={{0,2},{1,3},{2,0},{3,1},{4,6},{5,7},{6,4},{7,5},{8,10},{9,11},{10,... | collective-permute-start | bytes 3145736 | tf_op jit(solution)/shard_map/ppermute | solution.py:996
  363.7 145.1 %collective-permute-start.5 = (bf16[256,2048]{1,0:T(8,128)(2,1)}, bf16[256,2048]{1,0:T(8,128)(2,1)}, u32[]{:S(2)}, u32[]{:S(2)}) collective-permute-start(bf16[256,2048]{1,0:T(8,128)(2,1)} %get-tuple-element.209), channel_id=1, source_target_pairs={{0,3},{1,2},{2,1},{3,0},{4,7},{5,6},{6,5},{7,4},{8,11},{9,10},{10,... | collective-permute-start | bytes 3145736 | tf_op jit(solution)/shard_map/ppermute | solution.py:996
  364.0 5.1 slice-start.1
  369.1 3.3 copy-start.28
  508.7 6.6 %copy-start.25 = (bf16[256,2048]{1,0:T(8,128)(2,1)}, bf16[256,2048]{1,0:T(8,128)(2,1)S(1)}, u32[]{:S(2)}) copy-start(bf16[256,2048]{1,0:T(8,128)(2,1)S(1)} %collective-permute-done.3) | copy-start | bytes 3145732
  515.3 5.8 copy-start.16
  515.4 5.8 copy-start.38
  515.4 80.6 %reduce-scatter.9.cloned.1.call-start = ((), (), s32[]{:S(2)}) async-start(), calls=%async_computation.8 | async-start | bytes 3538944 | tf_op jit(solution)/shard_map/reduce_scatter | solution.py:1021
  516.9 4.2 copy-start.53
  518.5 15.0 %collective-permute-start.6 = (bf16[256,640]{1,0:T(8,128)(2,1)S(1)}, bf16[256,640]{1,0:T(8,128)(2,1)S(1)}, u32[]{:S(2)}, u32[]{:S(2)}) collective-permute-start(bf16[256,640]{1,0:T(8,128)(2,1)S(1)} %get-tuple-element.217), channel_id=1, source_target_pairs={{0,1},{1,0},{2,3},{3,2},{4,5},{5,4},{6,7},{7,6},{8,9},{9,8},{10,11... | collective-permute-start | bytes 983048 | tf_op jit(solution)/shard_map/ppermute | solution.py:996
  519.5 13.9 %collective-permute-start.7 = (bf16[256,640]{1,0:T(8,128)(2,1)S(1)}, bf16[256,640]{1,0:T(8,128)(2,1)S(1)}, u32[]{:S(2)}, u32[]{:S(2)}) collective-permute-start(bf16[256,640]{1,0:T(8,128)(2,1)S(1)} %get-tuple-element.216), channel_id=1, source_target_pairs={{0,2},{1,3},{2,0},{3,1},{4,6},{5,7},{6,4},{7,5},{8,10},{9,11},{10,... | collective-permute-start | bytes 983048 | tf_op jit(solution)/shard_map/ppermute | solution.py:996
  520.0 10.1 %copy-start.20 = (bf16[256,2048]{1,0:T(8,128)(2,1)S(1)}, bf16[256,2048]{1,0:T(8,128)(2,1)}, u32[]{:S(2)}) copy-start(bf16[256,2048]{1,0:T(8,128)(2,1)} %get-tuple-element.94) | copy-start | bytes 3145732
  520.0 10.1 %copy-start.26 = (bf16[256,2048]{1,0:T(8,128)(2,1)S(1)}, bf16[256,2048]{1,0:T(8,128)(2,1)}, u32[]{:S(2)}) copy-start(bf16[256,2048]{1,0:T(8,128)(2,1)} %copy-done.25) | copy-start | bytes 3145732
  520.0 14.9 %collective-permute-start.8 = (bf16[256,640]{1,0:T(8,128)(2,1)S(1)}, bf16[256,640]{1,0:T(8,128)(2,1)}, u32[]{:S(2)}, u32[]{:S(2)}) collective-permute-start(bf16[256,640]{1,0:T(8,128)(2,1)S(1)} %get-tuple-element.215), channel_id=1, source_target_pairs={{0,3},{1,2},{2,1},{3,0},{4,7},{5,6},{6,5},{7,4},{8,11},{9,10},{10,... | collective-permute-start | bytes 983048 | tf_op jit(solution)/shard_map/ppermute | solution.py:996
  544.0 1.7 copy-start.17
  544.0 1.7 copy-start.40
  544.0 1.7 copy-start.43
  545.6 3.7 copy-start.8
  545.6 3.7 copy-start.9
  549.3 18.2 %copy-start.1 = (f32[64,5632]{1,0:T(8,128)S(1)}, f32[64,5632]{1,0:T(8,128)}, u32[]{:S(2)}) copy-start(f32[64,5632]{1,0:T(8,128)} %down_ref.1) | copy-start | bytes 4325380
  549.3 18.2 %copy-start.23 = (f32[64,5632]{1,0:T(8,128)S(1)}, f32[64,5632]{1,0:T(8,128)}, u32[]{:S(2)}) copy-start(f32[64,5632]{1,0:T(8,128)} %param.32) | copy-start | bytes 4325380
  549.3 18.2 %copy-start.24 = (f32[64,5632]{1,0:T(8,128)S(1)}, f32[64,5632]{1,0:T(8,128)}, u32[]{:S(2)}) copy-start(f32[64,5632]{1,0:T(8,128)} %param.27) | copy-start | bytes 4325380
  567.5 2.8 copy-start.14
  567.5 4.3 copy-start.21
  567.5 5.2 copy-start.22
  572.7 34.7 %copy-start.36 = (f32[2,64]{0,1:T(8,128)S(1)}, f32[2,64]{0,1:T(8,128)}, u32[]{:S(2)}) copy-start(f32[2,64]{0,1:T(8,128)} %copy.128) | copy-start | bytes 1540
  572.7 34.9 %copy-start.45 = (f32[2,64]{1,0:T(2,128)S(1)}, f32[2,64]{1,0:T(2,128)}, u32[]{:S(2)}) copy-start(f32[2,64]{1,0:T(2,128)} %param.23) | copy-start | bytes 1540
  572.7 36.9 %copy-start.29 = (f32[64,2560]{1,0:T(8,128)S(1)}, f32[64,2560]{1,0:T(8,128)}, u32[]{:S(2)}) copy-start(f32[64,2560]{1,0:T(8,128)} %param.29) | copy-start | bytes 1966084
  572.7 36.9 %copy-start.30 = (f32[64,2560]{1,0:T(8,128)S(1)}, f32[64,2560]{1,0:T(8,128)}, u32[]{:S(2)}) copy-start(f32[64,2560]{1,0:T(8,128)} %param.24) | copy-start | bytes 1966084
  577.9 31.7 %copy-start.4 = (f32[64,2560]{1,0:T(8,128)S(1)}, f32[64,2560]{1,0:T(8,128)}, u32[]{:S(2)}) copy-start(f32[64,2560]{1,0:T(8,128)} %in_ref.1) | copy-start | bytes 1966084
  596.0 1.0 copy-start.10
  597.0 0.9 copy-start.11
  609.6 1.6 copy-start.6
  609.6 1.6 copy-start.32
  609.6 1.9 copy-start.33
  (7 other events, 5.0 us)
Sparse Core Ops, SparseCore 0:
  51.0 141.4 all-gather.2
  194.2 62.0 all-gather.4
  281.3 74.9 reduce-scatter.4
  358.5 125.9 reduce-scatter.6
  515.5 36.6 reduce-scatter.10
  554.3 41.5 reduce-scatter.8

commit v5 on v4

--- a/solution.py
+++ b/solution.py
@@ -284,13 +284,12 @@
     pl.semaphore_wait(barrier, len(near) + slices - 1)
 
 
-def spread_kernel(
+def spread_part(
     rows, out_ref, full, out_rows, send, come, forward, passed,
-    send_out, come_out, pass_out, passed_out,
+    send_out, come_out, pass_out, passed_out, follow,
 ):
     near = list(range(2, lax.axis_size("seq"), 2))
     pair, core = core_pair(lax.axis_index("seq"))
-    meet_spread(near)
     start, local, early, finish = spread_copies(rows, full, send, come, forward, passed)
     start()
     out_rows[pair, core] = out_ref[...].astype(jnp.bfloat16)
@@ -298,32 +297,65 @@
     local()
     early()
     pass_rows_finish(out_rows, send_out, come_out, pass_out, passed_out, near)
+    follow()
     finish()
 
 
-def spread_rows(rows, w_outward, slices):
-    pairs, two, depth, width = rows.shape
-    full, out_rows = pl.pallas_call(
-        spread_kernel,
-        in_specs=[VMEM] * 2,
-        out_specs=[VMEM] * 2,
-        out_shape=[
-            jax.ShapeDtypeStruct((pairs, two, slices, depth, width), rows.dtype),
-            jax.ShapeDtypeStruct((pairs, two, depth, w_outward.shape[1]), rows.dtype),
-        ],
-        scratch_shapes=[pltpu.SemaphoreType.DMA((slices,))] * 4
-        + [pltpu.SemaphoreType.DMA((2 * pairs,))] * 4,
-        compiler_params=pltpu.CompilerParams(
-            vmem_limit_bytes=48 << 20, collective_id=3, has_side_effects=True
-        ),
-    )(rows, w_outward)
-    return full.reshape(pairs * two * slices * depth, width), out_rows
+def projections(x_ref, cosine_ref, sine_ref, full, normed, query, kv, gains):
+    depth = full.shape[0] * 2 * full.shape[2] * full.shape[3]
+    width, kv_width = HEADS * HEAD_DIM, KV_HEADS * HEAD_DIM
+
+    def weights(first, count):
+        return full[:, :, :, :, pl.ds(first, count)].reshape(depth, count)
+
+    def turn(field):
+        parts = []
+        for i in range(field.shape[1] // 128):
+            part = field[:, i * 128 : (i + 1) * 128]
+            lane = lax.rem(lax.broadcasted_iota(jnp.int32, part.shape, 1), HEAD_DIM)
+            other = jnp.where(
+                lane < HEAD_DIM // 2,
+                pltpu.roll(part, 128 - HEAD_DIM // 2, 1),
+                pltpu.roll(part, HEAD_DIM // 2, 1),
+            )
+            parts.append(part * cosine_ref[...] + other * sine_ref[...])
+        return jnp.concatenate(parts, axis=1)
+
+    def keys_and_values():
+        gains[...] = weights(width + 2 * kv_width, 128).astype(jnp.float32).T[:2]
+        x = x_ref[...].astype(jnp.float32)
+        normed[...] = (x * rms_scale(x) * gains[0:1, :]).astype(jnp.bfloat16)
+        mixed = dot(normed[...], weights(width, 2 * kv_width))
+        keys, values = turn(mixed[:, :kv_width]), mixed[:, kv_width:]
+        kv[...] = jnp.concatenate(
+            [
+                field[:, h * HEAD_DIM : (h + 1) * HEAD_DIM]
+                for h in range(KV_HEADS)
+                for field in (keys, values)
+            ],
+            axis=1,
+        ).astype(jnp.bfloat16)
+
+    def queries():
+        def query_part(i, _):
+            first = pl.multiple_of(i * 512, 512)
+            query[:, pl.ds(first, 512)] = turn(dot(normed[...], weights(first, 512))).astype(
+                jnp.bfloat16
+            )
+            return 0
+
+        lax.fori_loop(0, width // 512, query_part, 0)
+
+    return keys_and_values, queries
 
 
 def forward_kernel(
-    query_ref, kv_ref, out_rows, kv_all, mixed_ref, logs, out_full,
-    queries, largest, total, mixed,
+    in_rows, out_ref, x_ref, cosine_ref, sine_ref, dy_ref,
+    in_full, normed, query_ref, gains, kv_all, mixed_ref, logs, out_full, middle, normed_second, dy_all,
+    kv_ref, out_rows, queries, largest, total, mixed,
+    send_in, come_in, pass_in, passed_in, send_z, come_z, pass_z, passed_z,
     send_kv, come_kv, pass_kv, passed_kv, send_rows, come_rows, pass_rows, passed_rows,
+    send_dy, come_dy, own_sem,
 ):
     group, s = lax.axis_size("seq"), lax.axis_index("seq")
     place, core = core_pair(s)
@@ -332,9 +364,25 @@
     width, pair = per_head * HEAD_DIM, 2 * HEAD_DIM
     near = list(range(2, group, 2))
     meet_spread(range(1, group))
+    find_keys, find_queries = projections(
+        x_ref, cosine_ref, sine_ref, in_full, normed, query_ref, kv_ref, gains
+    )
     spread_start, spread_local, spread_early, spread_finish = spread_copies(
         out_rows, out_full, send_rows, come_rows, pass_rows, passed_rows
     )
+
+    dy_order, dy_start, dy_take, dy_sent = gather_blocks(
+        dy_ref, lambda owner, holder: dy_all.at[owner ^ holder], send_dy, come_dy
+    )
+    own_dy = pltpu.make_async_copy(dy_ref, dy_all.at[0], own_sem)
+    own_dy.start()
+
+    def links_early():
+        spread_early()
+        dy_start()
+
+    def links_late():
+        dy_take(0)
 
     def kv_copy(d, owner, target):
         chip, half = core_pair(owner)
@@ -344,6 +392,11 @@
         block = kv_all.at[chip, half]
         return remote(block, block, pass_kv.at[chip, half], passed_kv.at[chip, half], "seq", s ^ 1)
 
+    spread_part(
+        in_rows, out_ref, in_full, out_rows, send_in, come_in, pass_in, passed_in,
+        send_z, come_z, pass_z, passed_z, spread_start,
+    )
+    find_keys()
     kv_copy(1, s, s ^ 1).start()
     for d in near:
 
@@ -351,12 +404,13 @@
         def _():
             kv_copy(d, s, s ^ d).start()
 
-    spread_start()
+    spread_local()
+    find_queries()
     kv_all[place, core] = kv_ref[...]
     for h in range(KV_HEADS):
         field = query_ref[:, pl.ds(h * width, width)]
         queries[h] = stack_heads(field, per_head) * jnp.bfloat16(HEAD_DIM**-0.5)
-    spread_local()
+    links_early()
 
     def scores_of(h, chip, masked):
         kv = kv_all[chip, :, :, pl.ds(pl.multiple_of(h * pair, pair), pair)]
@@ -378,12 +432,16 @@
     kv_copy(1, s ^ 1, s ^ 1).wait_recv()
     lax.fori_loop(0, KV_HEADS, own_chip, 0)
 
+    @pl.when(place == 0)
+    def _():
+        links_late()
+
     def earlier_chip(turn, _):
         chip = place - 1 - turn
 
-        @pl.when(chip == 0)
+        @pl.when(turn == jnp.minimum(place - 1, 1))
         def _():
-            spread_early()
+            links_late()
 
         owner = 2 * chip + core
         kv_copy(owner ^ s, owner, owner).wait_recv()
@@ -405,10 +463,6 @@
 
     lax.fori_loop(0, place, earlier_chip, 0)
 
-    @pl.when(place == 0)
-    def _():
-        spread_early()
-
     for h in range(KV_HEADS):
         logs[h] = largest[h] + jnp.log(total[h])
         mixed_ref[:, pl.ds(h * width, width)] = unstack_heads(
@@ -428,14 +482,30 @@
     lax.fori_loop(0, place, handed, 0)
     spread_finish()
 
+    depth = out_full.shape[0] * 2 * out_full.shape[2] * out_full.shape[3]
+
+    def middle_part(i, _):
+        columns = pl.ds(pl.multiple_of(i * 512, 512), 512)
+        weights = out_full[:, :, :, :, columns].reshape(depth, 512)
+        middle[:, columns] = x_ref[:, columns].astype(jnp.float32) + dot(mixed_ref[...], weights)
+        return 0
+
+    lax.fori_loop(0, middle.shape[1] // 512, middle_part, 0)
+    field = middle[...]
+    normed_second[...] = (field * rms_scale(field) * gains[1:2, :]).astype(jnp.bfloat16)
+    for turn in range(1, len(dy_order)):
+        dy_take(turn)
+    dy_sent()
+    own_dy.wait()
+
 
 def backward_kernel(
-    grad_ref, query_ref, mixed_ref, logs, kv_all, branch_ref, normed_ref,
-    cosine_ref, sine_ref, cosine_rows, sine_rows,
-    inward_grad, inward_slices, attended_all, branch_all, normed_all, kv_grad,
+    grad_ref, query_ref, mixed_ref, logs, kv_all, branch_ref,
+    cosine_ref, sine_ref, cosine_rows, sine_rows, out_parts,
+    inward_grad, inward_slices, attended_all, branch_all, out_come, kv_grad,
     queries, grads, inner, query_sum, parts, part_come, final_come,
     send_part, come_part, send_final, come_final, send_slice, come_slice,
-    send_mixed, come_mixed, send_normed, come_normed,
+    send_mixed, come_mixed, send_out, come_out,
 ):
     group, s = lax.axis_size("seq"), lax.axis_index("seq")
     place, core = core_pair(s)
@@ -457,13 +527,18 @@
     gathers = [
         gather_blocks(mixed_ref, lambda owner, holder: attended_all.at[owner ^ holder],
                       send_mixed, come_mixed),
-        gather_blocks(normed_ref, lambda owner, holder: normed_all.at[owner ^ holder],
-                      send_normed, come_normed),
     ]
+
+    def out_copy(d):
+        return remote(
+            out_parts.at[d], out_come.at[d - 1], send_out.at[d], come_out.at[d], "fsdp", f ^ d
+        )
 
     def gathers_early():
         for _, _, take, _ in gathers:
             take(0)
+        for d in range(1, slices):
+            out_copy(d).start()
 
     def part_copy(chip, half):
         return remote(
@@ -481,7 +556,6 @@
         slice_copy(d, f ^ d).start()
     for _, begin, _, _ in gathers:
         begin()
-    normed_all[0] = normed_ref[...]
     attended_all[0] = mixed_ref[...]
     branch_all[0] = branch_ref[:, pl.ds(pl.multiple_of(f * share, 128), share)]
     for h in range(KV_HEADS):
@@ -586,6 +660,8 @@
     inward_grad[:, pl.ds(HEADS * HEAD_DIM, 2 * KV_HEADS * HEAD_DIM)] = jnp.concatenate(
         key_grads + value_grads, axis=1
     ).astype(jnp.bfloat16)
+    rest = inward_grad.shape[1] - slices * inward_slices.shape[2]
+    inward_grad[:, pl.ds(inward_grad.shape[1] - rest, rest)] = jnp.zeros((local, rest), jnp.bfloat16)
     part_cols = inward_slices.shape[2]
     for t in range(slices):
         inward_slices[t] = inward_grad[:, pl.ds(t * part_cols, part_cols)]
@@ -602,6 +678,7 @@
         part_copy(place, 0).wait_send()
 
     for d in range(1, slices):
+        out_copy(d).wait()
         slice_copy(d, f ^ d).wait()
     for order, _, take, finish in gathers:
         for turn in range(1, len(order)):
@@ -609,44 +686,61 @@
         finish()
 
 
-def attend_forward(query, kv, out_rows, group, slices):
-    local, width = query.shape
-    per_head = HEADS // KV_HEADS
-    columns = per_head * local
-    pairs_seq, _, depth, _ = out_rows.shape
+def attend_forward(rows, w_outward, x, cosine, sine, upstream, group, slices):
+    local, width = x.shape
+    pairs, two, depth, inward_width = rows.shape
+    outward_width = w_outward.shape[1]
+    kv_cols = 2 * KV_HEADS * HEAD_DIM
+    columns = HEADS // KV_HEADS * local
+    low = jax.ShapeDtypeStruct((local, width), jnp.bfloat16)
     tiles = KV_HEADS * group * columns * local
-    return pl.pallas_call(
+    four_slices = [pltpu.SemaphoreType.DMA((slices,))] * 4
+    in_full, *results = pl.pallas_call(
         forward_kernel,
-        in_specs=[VMEM] * 3,
-        out_specs=[VMEM] * 4,
+        in_specs=[VMEM] * 5 + [ANY],
+        out_specs=[VMEM] * 10 + [ANY],
         out_shape=[
-            jax.ShapeDtypeStruct((group // 2, 2, local, kv.shape[1]), jnp.bfloat16),
-            jax.ShapeDtypeStruct((local, width), jnp.bfloat16),
+            jax.ShapeDtypeStruct((pairs, two, slices, depth, inward_width), jnp.bfloat16),
+            low,
+            low,
+            jax.ShapeDtypeStruct((2, width), jnp.float32),
+            jax.ShapeDtypeStruct((pairs, two, local, kv_cols), jnp.bfloat16),
+            low,
             jax.ShapeDtypeStruct((KV_HEADS, 1, columns), jnp.float32),
-            jax.ShapeDtypeStruct(
-                (pairs_seq, 2, slices, depth, out_rows.shape[3]), jnp.bfloat16
-            ),
+            jax.ShapeDtypeStruct((pairs, two, slices, depth, outward_width), jnp.bfloat16),
+            jax.ShapeDtypeStruct((local, width), jnp.float32),
+            low,
+            jax.ShapeDtypeStruct((slices, local, width), jnp.bfloat16),
         ],
         scratch_shapes=[
+            pltpu.VMEM((local, kv_cols), jnp.bfloat16),
+            pltpu.VMEM((pairs, two, depth, outward_width), jnp.bfloat16),
             pltpu.VMEM((KV_HEADS, columns, HEAD_DIM), jnp.bfloat16),
             pltpu.VMEM((KV_HEADS, 1, columns), jnp.float32),
             pltpu.VMEM((KV_HEADS, 1, columns), jnp.float32),
             pltpu.VMEM((KV_HEADS, HEAD_DIM, columns), jnp.float32),
         ]
-        + [pltpu.SemaphoreType.DMA((group,))] * 2
-        + [pltpu.SemaphoreType.DMA((group // 2, 2))] * 2
-        + [pltpu.SemaphoreType.DMA((slices,))] * 4,
+        + four_slices
+        + [pltpu.SemaphoreType.DMA((group,))] * 6
+        + [pltpu.SemaphoreType.DMA((pairs, 2))] * 2
+        + four_slices
+        + [pltpu.SemaphoreType.DMA((slices,))] * 2
+        + [pltpu.SemaphoreType.DMA],
         compiler_params=pltpu.CompilerParams(
-            vmem_limit_bytes=56 << 20, collective_id=0, has_side_effects=True
+            vmem_limit_bytes=60 << 20, collective_id=0, has_side_effects=True
         ),
         cost_estimate=pl.CostEstimate(
-            flops=tiles * HEAD_DIM * 80, bytes_accessed=20 << 20, transcendentals=tiles
+            flops=tiles * HEAD_DIM * 160, bytes_accessed=20 << 20, transcendentals=tiles
         ),
-    )(query, kv, out_rows)
+    )(
+        rows, w_outward, x, jnp.tile(cosine, (1, 4)),
+        jnp.tile(jnp.concatenate([-sine, sine], axis=1), (1, 2)), upstream,
+    )
+    return in_full.reshape(-1, inward_width), *results
 
 
 def attend_backward(
-    grads, query, mixed, logs, kv_all, branch, normed, cosine, sine, group, slices
+    grads, query, mixed, logs, kv_all, branch, cosine, sine, out_parts, group, slices
 ):
     local, features = branch.shape
     per_head = HEADS // KV_HEADS
@@ -659,14 +753,14 @@
     one_half = pltpu.VMEM((group // 2, local, kv_cols), jnp.bfloat16)
     return pl.pallas_call(
         backward_kernel,
-        in_specs=[VMEM] * 11,
-        out_specs=[VMEM] * 5,
+        in_specs=[VMEM] * 10 + [ANY],
+        out_specs=[VMEM] * 4 + [ANY],
         out_shape=[
-            jax.ShapeDtypeStruct((local, inward_cols), jnp.bfloat16),
+            jax.ShapeDtypeStruct((local, inward_cols + 128), jnp.bfloat16),
             jax.ShapeDtypeStruct((slices, local, inward_cols // slices), jnp.bfloat16),
             gathered,
             jax.ShapeDtypeStruct((slices, local, features // slices), jnp.bfloat16),
-            gathered,
+            jax.ShapeDtypeStruct((slices - 1, local, features), jnp.bfloat16),
         ],
         scratch_shapes=[
             pltpu.VMEM((local, kv_cols), jnp.float32),
@@ -679,7 +773,8 @@
             one_half,
         ]
         + [pltpu.SemaphoreType.DMA((group // 2,))] * 4
-        + [pltpu.SemaphoreType.DMA((slices,))] * 6,
+        + [pltpu.SemaphoreType.DMA((slices,))] * 4
+        + [pltpu.SemaphoreType.DMA((slices,))] * 2,
         compiler_params=pltpu.CompilerParams(
             vmem_limit_bytes=60 << 20, collective_id=1, has_side_effects=True
         ),
@@ -687,8 +782,9 @@
             flops=tiles * HEAD_DIM * 80, bytes_accessed=20 << 20, transcendentals=tiles
         ),
     )(
-        grads, query, mixed, logs, kv_all, branch, normed,
+        grads, query, mixed, logs, kv_all, branch,
         jnp.tile(cosine.T, (1, per_head)), jnp.tile(sine.T, (1, per_head)), cosine, sine,
+        out_parts,
     )
 
 
@@ -733,11 +829,18 @@
 
 
 def feed_first_kernel(
-    x_ref, dy_ref, gate_up_ref, x_all, gate_all, up_all, hidden, down_grad_out,
-    gate_sum, up_sum, grad_stage, send_x, come_x, grad_sem, *, strip
+    *refs, slices, strip
 ):
-    slices, f = lax.axis_size("fsdp"), lax.axis_index("fsdp")
+    (
+        dy_ref, x_ref, gate_up_ref, normed_ref,
+        x_all, gate_all, up_all, hidden, down_grad_out, normed_near,
+        gate_sum, up_sum, grad_stage, dy_all, send_x, come_x, grad_sem, dy_sem,
+        send_normed, come_normed, own_sem,
+    ) = refs
+    f = lax.axis_index("fsdp")
     local = x_ref.shape[0]
+    for d in range(slices):
+        pltpu.make_async_copy(dy_ref.at[d], dy_all.at[d], dy_sem.at[d]).start()
     meet_slices()
 
     order, begin, take, sent = gather_blocks(
@@ -745,6 +848,15 @@
     )
     begin()
     x_all[0] = x_ref[...]
+
+    def normed_copy(d):
+        return remote(
+            normed_ref, normed_near.at[d], send_normed.at[d], come_normed.at[d], "fsdp", f ^ d
+        )
+
+    near = (1, 2) if slices == 4 else range(1, slices)
+    own_normed = pltpu.make_async_copy(normed_ref, normed_near.at[0], own_sem)
+    own_normed.start()
 
     def token_block(turn, d):
         for i in range(slices - 1):
@@ -752,6 +864,9 @@
             @pl.when(turn == i + 1)
             def _():
                 take(i)
+                if i == slices - 2:
+                    for k in near:
+                        normed_copy(k).start()
 
         x = x_all[d]
         units = hidden.shape[1]
@@ -774,25 +889,50 @@
         return following
 
     lax.fori_loop(0, slices, token_block, jnp.int32(0))
-    grad_rows(dy_ref, [hidden], down_grad_out, grad_stage, grad_sem)
+    for d in range(slices):
+        pltpu.make_async_copy(dy_ref.at[d], dy_all.at[d], dy_sem.at[d]).wait()
+    grad_rows(dy_all, [hidden], down_grad_out, grad_stage, grad_sem)
     sent()
+    own_normed.wait()
+    for d in near:
+        normed_copy(d).wait()
 
 
 def feed_second_kernel(
-    x_ref, dy_ref, gate_all, up_all, hidden, gate_up_ref, down_ref,
-    back_ref, out_parts, gate_up_grad_out,
-    gate_grad, up_grad, hidden_sum, back_send, back_come, out_stage, grad_stage,
-    send_back, come_back, out_sem, grad_sem, *, strip
+    *refs, slices, strip
 ):
-    slices, f = lax.axis_size("fsdp"), lax.axis_index("fsdp")
+    (
+        dy_ref, x_ref, gate_all, up_all, hidden, gate_up_ref, down_ref, normed_near,
+        back_ref, out_parts, gate_up_grad_out, normed_far,
+        dy_all,
+        gate_grad, up_grad, hidden_sum, back_send, back_come, out_stage, grad_stage,
+        send_back, come_back, out_sem, grad_sem, dy_sem,
+        send_normed, come_normed,
+    ) = refs
+    f = lax.axis_index("fsdp")
     local = back_ref.shape[0]
+
+    def dy_copy(d):
+        return pltpu.make_async_copy(dy_ref.at[d], dy_all.at[d], dy_sem.at[d])
+
+    for d in range(slices):
+        dy_copy(d).start()
     meet_slices()
-
     square = slices == 4
     order = block_order()
     first, second = (order[1], order[0]) if square else (None, None)
     turns = [3, second, first, 0] if square else list(range(slices - 1, -1, -1))
 
+    def relay():
+        return remote(
+            normed_near.at[order[0]], normed_far, send_normed, come_normed, "fsdp", f ^ order[1]
+        )
+
+    if square:
+        relay().start()
+    for d in range(slices):
+        dy_copy(d).wait()
+
     def back_copy(d, target, landing):
         return remote(
             back_send.at[d], back_come.at[landing - 1], send_back.at[d], come_back.at[landing],
@@ -805,7 +945,7 @@
     def token_block(turn, carry):
         d, before = carry
         place = pl.ds(pl.multiple_of(d * local, local), local)
-        hidden_sum[...] = dot(dy_ref[d], down_ref[...])
+        hidden_sum[...] = dot(dy_all[d], down_ref[...])
 
         def part(i, _):
             rows = pl.ds(pl.multiple_of(i * strip, strip), strip)
@@ -862,6 +1002,7 @@
     out_copy(1, 0).wait()
     grad_rows(x_ref, [gate_grad, up_grad], gate_up_grad_out, grad_stage, grad_sem)
     if square:
+        relay().wait()
         back_copy(3, first, 3).wait_send()
     for d in (1, 2) if square else range(1, slices):
         back_copy(d, d, d).wait()
@@ -872,7 +1013,7 @@
 ANY = pl.BlockSpec(memory_space=pl.ANY)
 
 
-def feed_first(x, upstream_all, gate_up_slice):
+def feed_first(x, upstream_all, gate_up_slice, normed):
     slices, local, width = upstream_all.shape
     ff_cols = gate_up_slice.shape[1] // 2
     tokens = slices * local
@@ -880,61 +1021,86 @@
     high = pltpu.VMEM((local, ff_cols), jnp.float32)
     sems = pltpu.SemaphoreType.DMA((slices,))
     return pl.pallas_call(
-        functools.partial(feed_first_kernel, strip=32),
-        in_specs=[VMEM] * 3,
-        out_specs=[VMEM] * 4 + [ANY],
+        functools.partial(feed_first_kernel, slices=slices, strip=32),
+        in_specs=[ANY] + [VMEM] * 3,
+        out_specs=[VMEM] * 4 + [ANY] * 2,
         out_shape=[
             jax.ShapeDtypeStruct((slices, local, width), jnp.bfloat16),
             units,
             units,
             units,
             jax.ShapeDtypeStruct((width, ff_cols), jnp.bfloat16),
+            jax.ShapeDtypeStruct((slices, local, width), jnp.bfloat16),
         ],
-        scratch_shapes=[high, high, pltpu.VMEM((2, 256, ff_cols), jnp.bfloat16)]
-        + [sems] * 2
-        + [pltpu.SemaphoreType.DMA((2,))],
+        scratch_shapes=[
+            high,
+            high,
+            pltpu.VMEM((2, 256, ff_cols), jnp.bfloat16),
+            pltpu.VMEM((slices, local, width), jnp.bfloat16),
+            sems,
+            sems,
+            pltpu.SemaphoreType.DMA((2,)),
+            sems,
+            sems,
+            sems,
+            pltpu.SemaphoreType.DMA,
+        ],
         compiler_params=pltpu.CompilerParams(
             vmem_limit_bytes=60 << 20, collective_id=4, has_side_effects=True
         ),
         cost_estimate=pl.CostEstimate(
             flops=10 * tokens * width * ff_cols, bytes_accessed=30 << 20, transcendentals=0
         ),
-    )(x, upstream_all, gate_up_slice)
+    )(upstream_all, x, gate_up_slice, normed)
 
 
 def feed_second(
-    x_all, upstream_all, gate_all, up_all, hidden, gate_up_slice, down_slice
+    x_all, upstream_all, gate_all, up_all, hidden, gate_up_slice, down_slice, normed_near
 ):
-    slices, local, width = upstream_all.shape
+    slices, local, width = x_all.shape
     ff_cols = gate_up_slice.shape[1] // 2
     tokens = slices * local
     blocks = pltpu.VMEM((slices, local, width), jnp.bfloat16)
     low = pltpu.VMEM((tokens, ff_cols), jnp.bfloat16)
     sems = pltpu.SemaphoreType.DMA((slices,))
+    pair = pltpu.SemaphoreType.DMA((2,))
     return pl.pallas_call(
-        functools.partial(feed_second_kernel, strip=32),
-        in_specs=[VMEM] * 7,
-        out_specs=[VMEM] + [ANY] * 2,
+        functools.partial(feed_second_kernel, slices=slices, strip=32),
+        in_specs=[ANY] + [VMEM] * 6 + [ANY],
+        out_specs=[VMEM] + [ANY] * 3,
         out_shape=[
             jax.ShapeDtypeStruct((local, width), jnp.float32),
             jax.ShapeDtypeStruct((slices, local, width), jnp.bfloat16),
             jax.ShapeDtypeStruct((width, 2 * ff_cols), jnp.bfloat16),
+            jax.ShapeDtypeStruct((local, width), jnp.bfloat16),
         ],
-        scratch_shapes=[low, low, pltpu.VMEM((local, ff_cols), jnp.float32), blocks]
-        + [
+        scratch_shapes=[
+            blocks,
+            low,
+            low,
+            pltpu.VMEM((local, ff_cols), jnp.float32),
+            blocks,
             pltpu.VMEM((slices - 1, local, width), jnp.bfloat16),
             pltpu.VMEM((2, local, width), jnp.bfloat16),
             pltpu.VMEM((2, 256, 2 * ff_cols), jnp.bfloat16),
-        ]
-        + [sems] * 2
-        + [pltpu.SemaphoreType.DMA((2,)), pltpu.SemaphoreType.DMA((2,))],
+            sems,
+            sems,
+            pair,
+            pair,
+            sems,
+            pltpu.SemaphoreType.DMA,
+            pltpu.SemaphoreType.DMA,
+        ],
         compiler_params=pltpu.CompilerParams(
             vmem_limit_bytes=62 << 20, collective_id=5, has_side_effects=True
         ),
         cost_estimate=pl.CostEstimate(
             flops=20 * tokens * width * ff_cols, bytes_accessed=40 << 20, transcendentals=0
         ),
-    )(x_all, upstream_all, gate_all, up_all, hidden, gate_up_slice, down_slice)
+    )(
+        upstream_all, x_all, gate_all, up_all, hidden, gate_up_slice, down_slice,
+        normed_near,
+    )
 
 
 def home_kernel(*refs, count, moves, summed):
@@ -1067,40 +1233,24 @@
         w_inward, low_gains, w_gate_up, w_down, group, slices
     )
     gate_up_slice = lax.all_gather(feed_gate_up, "seq", axis=0, tiled=True)
-    inward_gains, out_rows = spread_rows(in_rows, w_outward, slices)
-    inward_full = inward_gains[:, :inward_cols]
-    gain_first = inward_gains[:, inward_cols].astype(jnp.float32)
-    gain_second = inward_gains[:, inward_cols + 1].astype(jnp.float32)
-
+    exponent = jnp.arange(HEAD_DIM // 2).astype(jnp.float32) * (-2.0 / HEAD_DIM)
+    angle = position[:, None] * jnp.power(rope_base, exponent)[None, :]
+    cosine, sine = jnp.cos(angle), jnp.sin(angle)
+    (
+        inward_gains, normed, query, gains_full, kv_all, attended, logs, outward_full,
+        middle, normed_second, upstream_all,
+    ) = attend_forward(in_rows, w_outward, inputs[0], cosine, sine, upstream, group, slices)
+    gain_first, gain_second = gains_full[0], gains_full[1]
     scale_first = rms_scale(rows)
-    normed = (rows * scale_first * gain_first).astype(jnp.bfloat16)
-    mixed = dot(normed, inward_full)
-    query = rotate(mixed[:, :D].reshape(local, HEADS, HEAD_DIM), position, 1.0).astype(jnp.bfloat16)
-    key = rotate(
-        mixed[:, D : D + kv_width].reshape(local, KV_HEADS, HEAD_DIM), position, 1.0
-    ).astype(jnp.bfloat16)
-    value = mixed[:, D + kv_width :].reshape(local, KV_HEADS, HEAD_DIM).astype(jnp.bfloat16)
-    kv = jnp.concatenate([key, value], axis=-1).reshape(local, 2 * kv_width)
-    query = query.reshape(local, D)
-    kv_all, attended, logs, outward_full = attend_forward(query, kv, out_rows, group, slices)
+    scale_second = rms_scale(middle)
+    down_slice = lax.all_gather(feed_down, "seq", axis=0, tiled=True)
     outward_full = outward_full.reshape(D, D)
-    upstream_late, _ = lax.optimization_barrier((upstream, inward_gains))
-    upstream_blocks = gather_swap(upstream_late, "fsdp")
-    attended, upstream_blocks = lax.optimization_barrier((attended, upstream_blocks))
-    down_slice = lax.all_gather(feed_down, "seq", axis=0, tiled=True)
-    upstream_all = jnp.stack(upstream_blocks)
-    middle = rows + dot(attended, outward_full)
-    scale_second = rms_scale(middle)
-    normed_second = (middle * scale_second * gain_second).astype(jnp.bfloat16)
-
-    def add_up(parts):
-        return functools.reduce(jnp.add, [p.astype(jnp.float32) for p in parts])
-
-    normed_all, gate_all, up_all, hidden, down_partial = feed_first(
-        normed_second, upstream_all, gate_up_slice
-    )
-    normed_second_grad, out_parts, gate_up_partial = feed_second(
-        normed_all, upstream_all, gate_all, up_all, hidden, gate_up_slice, down_slice
+    normed_all, gate_all, up_all, hidden, down_partial, normed_near = feed_first(
+        normed_second, upstream_all, gate_up_slice, normed
+    )
+    normed_second_grad, out_parts, gate_up_partial, normed_far = feed_second(
+        normed_all, upstream_all, gate_all, up_all, hidden, gate_up_slice, down_slice,
+        normed_near,
     )
     down_mine = scatter_rows(down_partial)
     gate_up_mine = scatter_rows(gate_up_partial)
@@ -1108,45 +1258,56 @@
     middle_grad = upstream.astype(jnp.float32) + middle_back
     branch_low = middle_grad.astype(jnp.bfloat16)
     attended_grad = against(branch_low, outward_full).astype(jnp.bfloat16)
-    exponent = jnp.arange(HEAD_DIM // 2).astype(jnp.float32) * (-2.0 / HEAD_DIM)
-    angle = position[:, None] * jnp.power(rope_base, exponent)[None, :]
-    inward_grad, inward_slices, attended_all, branch_all, first_all = attend_backward(
-        attended_grad, query, attended, logs, kv_all, branch_low, normed,
-        jnp.cos(angle), jnp.sin(angle), group, slices,
-    )
-    out_parts = [out_parts[0]] + [swap(out_parts[d], "fsdp", d) for d in range(1, slices)]
-    inward_grad, inward_slices, attended_all, branch_all, first_all, down_mine, out_parts = (
+    inward_grad, inward_slices, attended_all, branch_all, out_come = attend_backward(
+        attended_grad, query, attended, logs, kv_all, branch_low,
+        cosine, sine, out_parts, group, slices,
+    )
+    inward_grad, inward_slices, attended_all, branch_all, down_mine, normed_far = (
         lax.optimization_barrier(
-            (inward_grad, inward_slices, attended_all, branch_all, first_all, down_mine, out_parts)
-        )
-    )
-    result = middle + add_up(out_parts)
+            (inward_grad, inward_slices, attended_all, branch_all, down_mine, normed_far)
+        )
+    )
     inward_grad_blocks = exchange_swap(inward_slices, "fsdp")
-    outward_mine = scatter_rows(
-        outer(attended_all.reshape(-1, D), branch_all.reshape(-1, D // slices)).astype(jnp.bfloat16)
-    )
-
-    normed_grad = against(inward_grad, inward_full)
+    outward_partial = outer(attended_all.reshape(-1, D), branch_all.reshape(-1, D // slices))
+    outward_partial = outward_partial.astype(jnp.bfloat16)
+    normed_grad = against(inward_grad, inward_gains)
     rows_back, gain_first_grad = norm_back(rows, scale_first, gain_first, normed_grad)
     input_grad = middle_grad + rows_back
 
-    inward_grad_blocks, gain_first_grad, down_mine, gate_up_mine = lax.optimization_barrier(
-        (inward_grad_blocks, gain_first_grad, down_mine, gate_up_mine)
+    inward_grad_blocks, gain_first_grad = lax.optimization_barrier(
+        (inward_grad_blocks, gain_first_grad)
     )
     gain_grads = jnp.stack([gain_first_grad, gain_second_grad], axis=1)
     gain_grads = jnp.pad(gain_grads.astype(jnp.bfloat16), ((0, 0), (0, 126)))
-    inward_partial = outer(first_all.reshape(-1, D), jnp.concatenate(inward_grad_blocks, axis=0))
+    if slices == 4:
+        inward_partial = outer(
+            normed_near[:3].reshape(-1, D), jnp.concatenate(inward_grad_blocks[:3], axis=0)
+        ) + outer(normed_far, inward_grad_blocks[3])
+    else:
+        inward_partial = outer(
+            normed_near.reshape(-1, D), jnp.concatenate(inward_grad_blocks, axis=0)
+        )
     inward_partial = inward_partial.astype(jnp.bfloat16)
     slice_cols = inward_partial.shape[1]
-    inward_mine = scatter_rows(jnp.concatenate([inward_partial, gain_grads], axis=1))
+    inward_partial, gate_up_mine = lax.optimization_barrier(
+        (
+            jnp.concatenate([inward_partial, gain_grads, outward_partial], axis=1),
+            gate_up_mine,
+        )
+    )
+    inward_mine = scatter_rows(inward_partial)
+    result = middle + functools.reduce(
+        jnp.add,
+        [p.astype(jnp.float32) for p in [out_parts[0]] + [out_come[d] for d in range(slices - 1)]],
+    )
     gate_up_sum, down_sum = bring_home(
         [gate_up_mine, down_mine],
         [(0, 0, ff_cols, 0, 0), (0, ff_cols, ff_cols, 0, FF), (1, 0, ff_cols, 1, 0)],
         [2 * FF, FF], None, slices, 6,
     )
     inward_sum, outward_sum, gains_sum = bring_home(
-        [inward_mine, outward_mine],
-        [(0, 0, slice_cols, 0, 0), (1, 0, D // slices, 1, 0)],
+        [inward_mine],
+        [(0, 0, slice_cols, 0, 0), (0, slice_cols + 128, D // slices, 1, 0)],
         [inward_cols, D], (0, slice_cols), slices, 7,
     )
     gate_up_sum, down_sum, inward_sum, outward_sum = [

time: 631 us -> 586 us (0.929)
  waiting for transfers between devices: 18.2 us -> 48.9 us
  starting transfers between devices: 19.8 us -> 3.02 us
  local copies, waits for them, and re-layouts: 37.4 us -> 22 us
  other arithmetic: 40.4 us -> 25.3 us
  Pallas kernels: 452 us -> 438 us
  matrix products: 37.5 us -> 25.9 us
    reduce_scatter x4 -> x3, waiting for transfers between devices: 18 us -> 40.2 us  [scatter_rows(): return lax.psum_scatter(partial, 'seq', scatter_dimension=0, tiled=True)]
    dot_general x2 -> x0, matrix products: 12.7 us -> none  [dot(): return jnp.dot(left, right, preferred_element_type=jnp.float32)]
    pallas_call x5 -> x4, Pallas kernels: 384 us -> 372 us  [the longest x1 134 us: attend_forward(): pl.pallas_call(forward_kernel, in_specs=[VMEM] * 5 + [ANY], out_specs=[VM...]
    reduce_scatter x4 -> x3, starting transfers between devices: 11.7 us -> 0.29 us  [scatter_rows(): return lax.psum_scatter(partial, 'seq', scatter_dimension=0, tiled=True)]
    all_gather x1, waiting for transfers between devices: 0.01 us -> 7.95 us  [body(): gate_up_slice = lax.all_gather(feed_gate_up, 'seq', axis=0, tiled=True)]
    convert_element_type x4 -> x0, other arithmetic: 7.38 us -> none  [the longest x1 3.36 us: body(): result[None].astype(jnp.bfloat16)]
    another operation x3 -> x0, other arithmetic: 7.26 us -> none  [the longest x1 4.57 us: body(): upstream_all = jnp.stack(upstream_blocks)]
    unnamed x120 -> x86, local copies, waits for them, and re-layouts: 18.5 us -> 12.3 us
  transfers between devices with their start and end apart: 15 -> 8, of which waited for: 1 -> 3; matrix products, arithmetic and copies ran while one was open for 15% -> 10% of each run, Pallas kernels for 65% -> 67%
where the time goes in v5:
time: 586 us; the launch traced here: 578 us
  Pallas kernels  438 us (75%)
  waiting for transfers between devices  48.9 us (8%)
  matrix products  25.9 us (4%)
  other arithmetic  25.3 us (4%)
  local copies, waits for them, and re-layouts  22 us (4%)
  between operations  14.8 us (3%)
    pallas_call x1, Pallas kernels, attend_forward(): pl.pallas_call(forward_kernel, in_specs=[VMEM] * 5 + [ANY], out_specs=[VM...  134 us
    pallas_call x1, Pallas kernels, attend_backward(): pl.pallas_call(backward_kernel, in_specs=[VMEM] * 10 + [ANY], out_specs=[...  103 us
    pallas_call x1, Pallas kernels, feed_first(): pl.pallas_call(functools.partial(feed_first_kernel, slices=slices, strip=...  70 us
    pallas_call x1, Pallas kernels, feed_second(): pl.pallas_call(functools.partial(feed_second_kernel, slices=slices, strip...  65.2 us
    pallas_call x1, Pallas kernels, share_weights(): pl.pallas_call(share_kernel, in_specs=[VMEM] * 4, out_specs=[VMEM] * 3, o...  40.3 us
    reduce_scatter x3, waiting for transfers between devices, scatter_rows(): return lax.psum_scatter(partial, 'seq', scatter_dimension=0, tiled=True)  40.2 us
    pallas_call x2, Pallas kernels, bring_home(): pl.pallas_call(functools.partial(home_kernel, count=len(sources), moves=m...  25.8 us
    dot_general x2, matrix products, against(): lax.dot_general(left, right, (((1,), (1,)), ((), ())), preferred_element_...  16.1 us
  transfers between devices with their start and end apart: 8, of which 3 were waited for; matrix products, arithmetic and copies ran while one was open for 10% of the time, Pallas kernels for 67%

profile of v5, /device:TPU:9, one launch (start us, length us, event | category | flops | bytes accessed | tf_op | source)
XLA Modules:
  0.0 578.3 jit_solution(16389986153365255241)
XLA Ops:
  7.2 0.7 convert_element_type.76
  7.9 0.1 copy.99
  8.1 1.4 copy-done
  9.4 1.1 copy-done.2
  10.5 40.3 %shard_map.296 = (bf16[256,2816]{1,0:T(8,128)(2,1)}, bf16[256,1408]{1,0:T(8,128)(2,1)}, bf16[4,2,64,2688]{3,2,1,0:T(8,128)(2,1)}) custom-call(f32[64,2560]{1,0:T(8,128)S(1)} %copy-done.2, bf16[64,128]{1,0:T(8,128)(2,1)S(1)} %pad.8.gain_ref, f32[64,11264]{1,0:T(8,128)} %gate_up_ref.1, f32[64,5632]{1,0:T(8,128)S(1)} %copy-done), custom_call_target="tpu_custom_call" | custom-call | tf_op jit(solution)/shard_map/pallas_call | solution.py:178
  50.9 0.7 all-gather.5.cloned.1.call-update
  51.7 0.5 fusion.28
  52.3 0.1 pad_maximum_fusion
  52.4 0.1 copy.102
  52.5 0.8 copy.104.sine_ref
  53.3 0.8 copy.103.cosine_ref
  54.1 133.9 %shard_map.297 = (bf16[4,2,4,64,2688]{4,3,2,1,0:T(8,128)(2,1)}, bf16[256,2048]{1,0:T(8,128)(2,1)}, bf16[256,2048]{1,0:T(8,128)(2,1)}, f32[2,2048]{1,0:T(2,128)},...) custom-call(bf16[4,2,64,2688]{3,2,1,0:T(8,128)(2,1)} %get-tuple-elem, ...), custom_call_target="tpu_custom_call" | custom-call | flops 171798691840 | bytes 20971520 | tf_op jit(solution)/shard_map/pallas_call | solution.py:698
  188.0 8.0 %all-gather.3.cloned.1.call-done.refs_2_.refs_5_ = bf16[2048,2816]{1,0:T(8,128)(2,1)} async-done(((bf16[256,2816]{1,0:T(8,128)(2,1)}), bf16[2048,2816]{1,0:T(8,128)(2,1)}) %all-gather.3.cloned.1.call-update) | async-done | bytes 11534352 | tf_op jit(solution)/shard_map/all_gather | solution.py:1235
  196.0 70.0 %shard_map.298 = (bf16[4,256,2048]{2,1,0:T(8,128)(2,1)}, bf16[1024,1408]{1,0:T(8,128)(2,1)}, bf16[1024,1408]{1,0:T(8,128)(2,1)}, bf16[1024,1408]{1,0:T(8,128)(2,...) custom-call(bf16[4,256,2048]{2,1,0:T(8,128)(2,1)} %get-tuple-element.66.refs_0_, ...), custom_call_target="tpu_custom_call" | custom-call | flops 29527900160 | bytes 31457280 | tf_op jit(solution)/shard_map/pallas_call | solution.py:1023
  266.0 65.2 %shard_map.299 = (f32[256,2048]{1,0:T(8,128)}, bf16[4,256,2048]{2,1,0:T(8,128)(2,1)}, bf16[2048,2816]{1,0:T(8,128)(2,1)}, bf16[256,2048]{1,0:T(8,128)(2,1)}) custom-call(bf16[4,256,2048]{2,1,0:T(8,128)(2,1)} %get-tuple-element.66.refs_0_, bf16[4,256,2048]{2,1,0:T(8,128)(2,1)} %get-tuple-element.70.refs_1_, bf16[1024,1408]{1,0:T(8,128)(2,1)} %get-tuple-element.71.refs_2_, ...), custom_call_target="tpu_custom_call" | custom-call | flops 59055800320 | bytes 41943040 | tf_op jit(solution)/shard_map/pallas_call | solution.py:1067
  331.3 0.2 reduce-scatter.8.cloned.1.call-start
  331.6 0.4 copy-done.29
  331.9 0.2 multiply_sine_fusion.1
  332.2 0.8 copy.125
  333.0 0.8 copy.126
  333.8 0.3 fusion.6
  334.0 0.2 multiply_reduce_fusion.2
  334.3 4.1 slice.30
  338.5 0.5 multiply_reduce_fusion
  339.0 0.7 copy-done.18
  339.7 2.0 fusion.42
  341.7 7.1 %convolution_convert_fusion.grad_ref = bf16[256,2048]{1,0:T(8,128)(2,1)} fusion(bf16[256,2048]{1,0:T(8,128)(2,1)S(1)} %get-tuple-element.199.branch_ref, bf16[2048,2048]{1,0:T(8,128)(2,1)} %bitcast.71), kind=kOutput, calls=%fused_computation.17 | convolution fusion | flops 2148007936 | bytes 10485760 | tf_op jit(solution)/shard_map/dot_general | solution.py:65
  348.8 103.1 %shard_map.300 = (bf16[256,2688]{1,0:T(8,128)(2,1)}, bf16[4,256,640]{2,1,0:T(8,128)(2,1)}, bf16[4,256,2048]{2,1,0:T(8,128)(2,1)}, bf16[4,256,512]{2,1,0:T(8,128)(2,1)}, bf16[3,256,2048]{2,1,0:T(8,128)(2,1)}) custom-call(bf16[256,2048]{1,0:T(8,128)(2,1)} %convolution_convert_fusion.grad_ref, bf16[256,2048]{1,0:T(8,128)(2,1)} %get-tuple-element.80.query_ref, ...), custom_call_target="tpu_custom_call" | custom-call | flops 85899345920 | bytes 20971520 | tf_op jit(solution)/shard_map/pallas_call | solution.py:754
  452.0 2.2 dynamic-slice_bitcast_fusion
  454.2 0.9 collective-permute-start
  455.1 0.3 collective-permute-start.1
  455.4 1.5 collective-permute-start.2
  456.9 9.0 %fusion.13 = (bf16[2048]{0:T(1024)(128)(2,1)S(1)}, f32[256]{0:T(256)S(1)}, f32[256,2048]{1,0:T(8,128)}) fusion(f32[256]{0:T(256)S(1)} %get-tuple-element.215, bf16[1,256,2048]{2,1,0:T(8,128)(2,1)S(1)} %copy-done.10, f32[2048]{0:T(1024)S(1)} %bitcast.68, bf16[256,2688]{1,0:T(8,128)(2,1)S(1)} %copy-done.38, bf16[2048,2688]{1,0:T(8,128)(2,1)} %bitcast.70), kind=kOutput, calls=%fused_computation.26 | convolution fusion | flops 2822240000 | bytes 15546368 | tf_op jit(solution)/shard_map/dot_general | solution.py:65
  465.9 3.8 bitcast_convert_fusion
  469.7 0.7 copy-done.35
  470.4 0.1 copy-done.36
  470.5 1.1 copy.107
  471.6 4.9 fusion.18
  476.6 1.1 add_convert_fusion
  477.7 0.5 copy-done.13
  478.2 0.1 copy-done.14
  478.3 3.0 fusion.3
  481.3 1.8 reduce-scatter.6.cloned.1.call-done.refs_0_
  483.1 0.1 copy.115
  483.2 0.1 copy.110
  483.3 0.1 copy.112
  483.4 6.9 %fusion.10 = (f32[1,256,2048]{2,1,0:T(8,128)}, bf16[1,256,2048]{2,1,0:T(8,128)(2,1)}) fusion(f32[256,2048]{1,0:T(8,128)} %get-tuple-element.200, f32[256,2048]{1,0:T(8,128)} %get-tuple-element.218, f32[256]{0:T(256)S(1)} %broadcast_multiply_fusion.3, f32[256]{0:T(256)S(1)} %get-tuple-element.214, f32[2048]{0:T(1024)S(1)} %bitcast.69, ...), kind=kLoop, calls=%fused_computation.23 | loop fusion | flops 8388608 | bytes 14691328 | tf_op jit(solution)/shard_map/broadcast_in_dim | solution.py:1334
  490.3 15.3 %shard_map.302 = (bf16[64,11264]{1,0:T(8,128)(2,1)S(1)}, bf16[64,5632]{1,0:T(8,128)(2,1)S(1)}) custom-call(bf16[256,2816]{1,0:T(8,128)(2,1)S(1)} %copy-done.4, bf16[256,1408]{1,0:T(8,128)(2,1)S(1)} %copy-done.5), custom_call_target="tpu_custom_call" | custom-call | flops 10737418240 | bytes 4194304 | tf_op jit(solution)/shard_map/pallas_call | solution.py:1146
  505.7 2.8 multiply_subtract_fusion.1
  508.5 1.5 copy-done.11
  510.0 0.9 copy-done.12
  510.8 5.0 multiply_subtract_fusion
  515.8 38.4 %reduce-scatter.8.cloned.1.call-done.refs_0_ = bf16[256,1280]{1,0:T(8,128)(2,1)} async-done(((bf16[2048,1280]{1,0:T(8,128)(2,1)}), bf16[256,1280]{1,0:T(8,128)(2,1)}) %reduce-scatter.8.cloned.1.call-update) | async-done | bytes 655376 | tf_op jit(solution)/shard_map/reduce_scatter | solution.py:1187
  554.2 1.1 copy-done.6
  555.3 10.5 %shard_map.301 = (bf16[64,2560]{1,0:T(8,128)(2,1)S(1)}, bf16[64,2048]{1,0:T(8,128)(2,1)S(1)}, f32[64,128]{1,0:T(8,128)S(1)}) custom-call(bf16[256,1280]{1,0:T(8,128)(2,1)S(1)} %copy-done.6), custom_call_target="tpu_custom_call" | custom-call | flops 10737418240 | bytes 4194304 | tf_op jit(solution)/shard_map/pallas_call | solution.py:1146
  565.8 0.1 copy.113
  565.9 0.1 copy.114
  566.0 0.1 copy.116
  566.1 0.6 copy.119
  566.8 0.6 copy.117
  567.4 0.6 copy.118
  568.1 1.6 multiply_subtract_fusion.2
  569.7 0.3 copy-done.26
  569.9 1.4 multiply_subtract_fusion.3
  (102 shorter events, 0.7 us)
Async XLA Ops:
  7.2 188.8 %all-gather.3.cloned.1.call-start = ((), (), s32[]{:S(2)}) async-start(), calls=%async_computation.3 | async-start | bytes 12976128 | tf_op jit(solution)/shard_map/all_gather | solution.py:1235
  8.0 1.4 copy-start
  9.4 1.1 copy-start.2
  50.8 215.2 %all-gather.5.cloned.1.call-start = ((), (), s32[]{:S(2)}) async-start(), calls=%async_computation.4 | async-start | bytes 6488064 | tf_op jit(solution)/shard_map/all_gather | solution.py:1246
  51.6 400.4 %reduce-scatter.4.cloned.1.call-start = ((), (), s32[]{:S(2)}) async-start(), calls=%async_computation.5 | async-start | bytes 6488064 | tf_op jit(solution)/shard_map/reduce_scatter | solution.py:1187
  51.7 0.6 copy-start.31
  51.7 0.6 copy-start.28
  52.2 135.8 %copy-start.22 = (f32[256,32]{1,0:T(8,128)}, f32[256,32]{1,0:T(8,128)S(1)}, u32[]{:S(2)}) copy-start(f32[256,32]{1,0:T(8,128)S(1)} %get-tuple-element.212.sine_rows) | copy-start | bytes 98308
  52.2 135.8 %copy-start.23 = (f32[256,32]{1,0:T(8,128)}, f32[256,32]{1,0:T(8,128)S(1)}, u32[]{:S(2)}) copy-start(f32[256,32]{1,0:T(8,128)S(1)} %get-tuple-element.213.cosine_rows) | copy-start | bytes 98308
  266.0 217.1 %reduce-scatter.6.cloned.1.call-start = ((), (), s32[]{:S(2)}) async-start(), calls=%async_computation.6 | async-start | bytes 12976128 | tf_op jit(solution)/shard_map/reduce_scatter | solution.py:1187
  331.2 0.7 copy-start.29
  331.3 0.7 copy-start.32
  331.3 2.5 copy-start.10
  331.3 2.7 copy-start.7
  331.3 222.9 %reduce-scatter.8.cloned.1.call-start = ((), (), s32[]{:S(2)}) async-start(), calls=%async_computation.7 | async-start | bytes 5898240 | tf_op jit(solution)/shard_map/reduce_scatter | solution.py:1187
  332.9 1.4 copy-start.27
  334.3 4.1 copy-start.9
  338.5 1.2 copy-start.18
  341.7 7.1 %copy-start.19 = (bf16[256,2048]{1,0:T(8,128)(2,1)}, bf16[256,2048]{1,0:T(8,128)(2,1)S(1)}, u32[]{:S(2)}) copy-start(bf16[256,2048]{1,0:T(8,128)(2,1)S(1)} %get-tuple-element.199.branch_ref) | copy-start | bytes 3145732
  452.0 4.9 copy-start.38
  454.2 15.5 %collective-permute-start = (bf16[256,640]{1,0:T(8,128)(2,1)S(1)}, bf16[256,640]{1,0:T(8,128)(2,1)S(1)}, u32[]{:S(2)}, u32[]{:S(2)}) collective-permute-start(bf16[256,640]{1,0:T(8,128)(2,1)S(1)} %get-tuple-element.203), channel_id=1, source_target_pairs={{0,1},{1,0},{2,3},{3,2},{4,5},{5,4},{6,7},{7,6},{8,9},{9,8},{10,11... | collective-permute-start | bytes 983048 | tf_op jit(solution)/shard_map/ppermute | solution.py:1162
  455.1 14.6 %collective-permute-start.1 = (bf16[256,640]{1,0:T(8,128)(2,1)S(1)}, bf16[256,640]{1,0:T(8,128)(2,1)S(1)}, u32[]{:S(2)}, u32[]{:S(2)}) collective-permute-start(bf16[256,640]{1,0:T(8,128)(2,1)S(1)} %get-tuple-element.202), channel_id=1, source_target_pairs={{0,2},{1,3},{2,0},{3,1},{4,6},{5,7},{6,4},{7,5},{8,10},{9,11},{10,... | collective-permute-start | bytes 983048 | tf_op jit(solution)/shard_map/ppermute | solution.py:1162
  455.4 14.3 %collective-permute-start.2 = (bf16[256,640]{1,0:T(8,128)(2,1)S(1)}, bf16[256,640]{1,0:T(8,128)(2,1)S(1)}, u32[]{:S(2)}, u32[]{:S(2)}) collective-permute-start(bf16[256,640]{1,0:T(8,128)(2,1)S(1)} %get-tuple-element.201), channel_id=1, source_target_pairs={{0,3},{1,2},{2,1},{3,0},{4,7},{5,6},{6,5},{7,4},{8,11},{9,10},{10,... | collective-permute-start | bytes 983048 | tf_op jit(solution)/shard_map/ppermute | solution.py:1162
  456.9 9.1 %copy-start.37 = (bf16[4,256,2048]{2,1,0:T(8,128)(2,1)S(1)}, bf16[4,256,2048]{2,1,0:T(8,128)(2,1)}, u32[]{:S(2)}) copy-start(bf16[4,256,2048]{2,1,0:T(8,128)(2,1)} %get-tuple-element.100) | copy-start | bytes 12582916
  456.9 9.1 %copy-start.39 = (bf16[4,256,512]{2,1,0:T(8,128)(2,1)S(1)}, bf16[4,256,512]{2,1,0:T(8,128)(2,1)}, u32[]{:S(2)}) copy-start(bf16[4,256,512]{2,1,0:T(8,128)(2,1)} %get-tuple-element.101) | copy-start | bytes 3145732
  469.7 0.7 copy-start.35
  469.7 0.8 copy-start.36
  471.6 5.0 copy-start.17
  476.5 1.6 copy-start.13
  476.6 1.7 copy-start.14
  481.3 1.8 copy-start.30
  481.3 1.9 copy-start.33
  481.3 2.0 copy-start.34
  483.4 6.9 %copy-start.4 = (bf16[256,2816]{1,0:T(8,128)(2,1)S(1)}, bf16[256,2816]{1,0:T(8,128)(2,1)}, u32[]{:S(2)}) copy-start(bf16[256,2816]{1,0:T(8,128)(2,1)} %reduce-scatter.6.cloned.1.call-done.refs_0_) | copy-start | bytes 4325380
  483.4 6.9 %copy-start.5 = (bf16[256,1408]{1,0:T(8,128)(2,1)S(1)}, bf16[256,1408]{1,0:T(8,128)(2,1)}, u32[]{:S(2)}) copy-start(bf16[256,1408]{1,0:T(8,128)(2,1)} %reduce-scatter.4.cloned.1.call-done.refs_1_) | copy-start | bytes 2162692
  490.3 15.3 %copy-start.1 = (f32[64,5632]{1,0:T(8,128)S(1)}, f32[64,5632]{1,0:T(8,128)}, u32[]{:S(2)}) copy-start(f32[64,5632]{1,0:T(8,128)} %down_ref.1) | copy-start | bytes 4325380
  490.3 15.3 %copy-start.15 = (f32[64,5632]{1,0:T(8,128)S(1)}, f32[64,5632]{1,0:T(8,128)}, u32[]{:S(2)}) copy-start(f32[64,5632]{1,0:T(8,128)} %param.32) | copy-start | bytes 4325380
  490.3 15.3 %copy-start.16 = (f32[64,5632]{1,0:T(8,128)S(1)}, f32[64,5632]{1,0:T(8,128)}, u32[]{:S(2)}) copy-start(f32[64,5632]{1,0:T(8,128)} %param.27) | copy-start | bytes 4325380
  505.6 2.8 copy-start.8
  505.7 4.3 copy-start.11
  505.7 5.1 copy-start.12
  515.8 52.2 %copy-start.3 = (f32[64,2560]{1,0:T(8,128)S(1)}, f32[64,2560]{1,0:T(8,128)}, u32[]{:S(2)}) copy-start(f32[64,2560]{1,0:T(8,128)} %in_ref.1) | copy-start | bytes 1966084
  554.2 1.1 copy-start.6
  555.3 12.8 %copy-start.20 = (f32[64,2560]{1,0:T(8,128)S(1)}, f32[64,2560]{1,0:T(8,128)}, u32[]{:S(2)}) copy-start(f32[64,2560]{1,0:T(8,128)} %param.29) | copy-start | bytes 1966084
  555.3 12.8 %copy-start.21 = (f32[64,2560]{1,0:T(8,128)S(1)}, f32[64,2560]{1,0:T(8,128)}, u32[]{:S(2)}) copy-start(f32[64,2560]{1,0:T(8,128)} %param.24) | copy-start | bytes 1966084
  568.0 1.6 copy-start.24
  568.0 1.6 copy-start.25
  568.1 1.9 copy-start.26
Sparse Core Ops, SparseCore 0:
  51.0 144.9 all-gather.2
  197.6 61.2 all-gather.4
  266.1 73.5 reduce-scatter.3
  341.8 141.1 reduce-scatter.5
  485.2 68.9 reduce-scatter.7

commit v6 on v5

--- a/solution.py
+++ b/solution.py
@@ -351,11 +351,11 @@
 
 def forward_kernel(
     in_rows, out_ref, x_ref, cosine_ref, sine_ref, dy_ref,
-    in_full, normed, query_ref, gains, kv_all, mixed_ref, logs, out_full, middle, normed_second, dy_all,
+    in_full, normed, query_ref, gains, kv_all, mixed_ref, logs, out_full, middle, normed_second, dy_all, normed_near,
     kv_ref, out_rows, queries, largest, total, mixed,
     send_in, come_in, pass_in, passed_in, send_z, come_z, pass_z, passed_z,
     send_kv, come_kv, pass_kv, passed_kv, send_rows, come_rows, pass_rows, passed_rows,
-    send_dy, come_dy, own_sem,
+    send_dy, come_dy, send_normed, come_normed, own_sem,
 ):
     group, s = lax.axis_size("seq"), lax.axis_index("seq")
     place, core = core_pair(s)
@@ -374,7 +374,17 @@
     dy_order, dy_start, dy_take, dy_sent = gather_blocks(
         dy_ref, lambda owner, holder: dy_all.at[owner ^ holder], send_dy, come_dy
     )
-    own_dy = pltpu.make_async_copy(dy_ref, dy_all.at[0], own_sem)
+    slices, f = lax.axis_size("fsdp"), lax.axis_index("fsdp")
+    square = slices == 4
+
+    def normed_copy(d):
+        slot = 1 if square else d
+        return remote(
+            normed, normed_near.at[slot], send_normed.at[slot], come_normed.at[slot], "fsdp", f ^ d
+        )
+
+    near_normed = dy_order[:1] if square else range(1, slices)
+    own_dy = pltpu.make_async_copy(dy_ref, dy_all.at[0], own_sem.at[0])
     own_dy.start()
 
     def links_early():
@@ -383,6 +393,8 @@
 
     def links_late():
         dy_take(0)
+        for d in near_normed:
+            normed_copy(d).start()
 
     def kv_copy(d, owner, target):
         chip, half = core_pair(owner)
@@ -493,10 +505,15 @@
     lax.fori_loop(0, middle.shape[1] // 512, middle_part, 0)
     field = middle[...]
     normed_second[...] = (field * rms_scale(field) * gains[1:2, :]).astype(jnp.bfloat16)
+    own_normed = pltpu.make_async_copy(normed, normed_near.at[0], own_sem.at[1])
+    own_normed.start()
     for turn in range(1, len(dy_order)):
         dy_take(turn)
     dy_sent()
+    for d in near_normed:
+        normed_copy(d).wait()
     own_dy.wait()
+    own_normed.wait()
 
 
 def backward_kernel(
@@ -537,8 +554,6 @@
     def gathers_early():
         for _, _, take, _ in gathers:
             take(0)
-        for d in range(1, slices):
-            out_copy(d).start()
 
     def part_copy(chip, half):
         return remote(
@@ -556,6 +571,8 @@
         slice_copy(d, f ^ d).start()
     for _, begin, _, _ in gathers:
         begin()
+    for d in range(1, slices):
+        out_copy(d).start()
     attended_all[0] = mixed_ref[...]
     branch_all[0] = branch_ref[:, pl.ds(pl.multiple_of(f * share, 128), share)]
     for h in range(KV_HEADS):
@@ -609,6 +626,11 @@
         return 0
 
     lax.fori_loop(0, place, earlier_chip, 0)
+
+    @pl.when(place > 0)
+    def _():
+        finish_chip(place - 1)
+
     lax.fori_loop(0, KV_HEADS, lambda h, c: head_grads(h, place, True), 0)
 
     @pl.when(core == 1)
@@ -618,10 +640,6 @@
     @pl.when(place == 0)
     def _():
         gathers_early()
-
-    @pl.when(place > 0)
-    def _():
-        finish_chip(place - 1)
 
     half = HEAD_DIM // 2
     for h in range(KV_HEADS):
@@ -698,7 +716,7 @@
     in_full, *results = pl.pallas_call(
         forward_kernel,
         in_specs=[VMEM] * 5 + [ANY],
-        out_specs=[VMEM] * 10 + [ANY],
+        out_specs=[VMEM] * 10 + [ANY] * 2,
         out_shape=[
             jax.ShapeDtypeStruct((pairs, two, slices, depth, inward_width), jnp.bfloat16),
             low,
@@ -711,6 +729,7 @@
             jax.ShapeDtypeStruct((local, width), jnp.float32),
             low,
             jax.ShapeDtypeStruct((slices, local, width), jnp.bfloat16),
+            jax.ShapeDtypeStruct((2 if slices == 4 else slices, local, width), jnp.bfloat16),
         ],
         scratch_shapes=[
             pltpu.VMEM((local, kv_cols), jnp.bfloat16),
@@ -724,8 +743,8 @@
         + [pltpu.SemaphoreType.DMA((group,))] * 6
         + [pltpu.SemaphoreType.DMA((pairs, 2))] * 2
         + four_slices
-        + [pltpu.SemaphoreType.DMA((slices,))] * 2
-        + [pltpu.SemaphoreType.DMA],
+        + four_slices
+        + [pltpu.SemaphoreType.DMA((2,))],
         compiler_params=pltpu.CompilerParams(
             vmem_limit_bytes=60 << 20, collective_id=0, has_side_effects=True
         ),
@@ -833,9 +852,9 @@
 ):
     (
         dy_ref, x_ref, gate_up_ref, normed_ref,
-        x_all, gate_all, up_all, hidden, down_grad_out, normed_near,
+        x_all, gate_all, up_all, hidden, down_grad_out, normed_other,
         gate_sum, up_sum, grad_stage, dy_all, send_x, come_x, grad_sem, dy_sem,
-        send_normed, come_normed, own_sem,
+        send_normed, come_normed,
     ) = refs
     f = lax.axis_index("fsdp")
     local = x_ref.shape[0]
@@ -849,14 +868,10 @@
     begin()
     x_all[0] = x_ref[...]
 
-    def normed_copy(d):
-        return remote(
-            normed_ref, normed_near.at[d], send_normed.at[d], come_normed.at[d], "fsdp", f ^ d
-        )
-
-    near = (1, 2) if slices == 4 else range(1, slices)
-    own_normed = pltpu.make_async_copy(normed_ref, normed_near.at[0], own_sem)
-    own_normed.start()
+    square = slices == 4
+
+    def normed_copy():
+        return remote(normed_ref, normed_other, send_normed, come_normed, "fsdp", f ^ order[1])
 
     def token_block(turn, d):
         for i in range(slices - 1):
@@ -864,9 +879,8 @@
             @pl.when(turn == i + 1)
             def _():
                 take(i)
-                if i == slices - 2:
-                    for k in near:
-                        normed_copy(k).start()
+                if square and i == 2:
+                    normed_copy().start()
 
         x = x_all[d]
         units = hidden.shape[1]
@@ -893,9 +907,8 @@
         pltpu.make_async_copy(dy_ref.at[d], dy_all.at[d], dy_sem.at[d]).wait()
     grad_rows(dy_all, [hidden], down_grad_out, grad_stage, grad_sem)
     sent()
-    own_normed.wait()
-    for d in near:
-        normed_copy(d).wait()
+    if square:
+        normed_copy().wait()
 
 
 def feed_second_kernel(
@@ -925,7 +938,7 @@
 
     def relay():
         return remote(
-            normed_near.at[order[0]], normed_far, send_normed, come_normed, "fsdp", f ^ order[1]
+            normed_near.at[1], normed_far, send_normed, come_normed, "fsdp", f ^ order[1]
         )
 
     if square:
@@ -1030,7 +1043,7 @@
             units,
             units,
             jax.ShapeDtypeStruct((width, ff_cols), jnp.bfloat16),
-            jax.ShapeDtypeStruct((slices, local, width), jnp.bfloat16),
+            jax.ShapeDtypeStruct((local, width), jnp.bfloat16),
         ],
         scratch_shapes=[
             high,
@@ -1041,8 +1054,7 @@
             sems,
             pltpu.SemaphoreType.DMA((2,)),
             sems,
-            sems,
-            sems,
+            pltpu.SemaphoreType.DMA,
             pltpu.SemaphoreType.DMA,
         ],
         compiler_params=pltpu.CompilerParams(
@@ -1103,58 +1115,100 @@
     )
 
 
-def home_kernel(*refs, count, moves, summed):
+def home_kernel(*refs, count, results, moves, gains):
     slices, f = lax.axis_size("fsdp"), lax.axis_index("fsdp")
-    sources, rest = refs[:count], refs[count:]
-    results, rest = rest[: -(count + 2)], rest[-(count + 2) :]
-    landed, (send, come) = rest[:count], rest[count:]
-    depth = sources[0].shape[0] // slices
-    meet_slices()
+    group, s = lax.axis_size("seq"), lax.axis_index("seq")
+    inputs, refs = refs[: count + gains], refs[count + gains :]
+    outputs, refs = refs[: results + gains], refs[results + gains :]
+    landed, refs = refs[:count], refs[count:]
+    send, come = refs[:2]
+    depth = inputs[0].shape[0] // slices
+    if gains:
+        meet_spread(range(1, group))
+    else:
+        meet_slices()
 
     def copy(k, d):
         rows = pl.ds(pl.multiple_of((f ^ d) * depth, depth), depth)
         return remote(
-            sources[k].at[rows, :], landed[k].at[d], send.at[k, d], come.at[k, d], "fsdp", f ^ d
-        )
-
+            inputs[k].at[rows, :], landed[k].at[d], send.at[k, d], come.at[k, d], "fsdp", f ^ d
+        )
+
+    if gains:
+        seq_come, tiles, tile_come, seq_send, seq_sem, tile_send, tile_sem = refs[2:]
+
+        def seq_copy(d):
+            return remote(
+                inputs[count].at[s ^ d], seq_come.at[d], seq_send.at[d], seq_sem.at[d], "seq", s ^ d
+            )
+
+        def tile_copy(d):
+            return remote(
+                tiles.at[f ^ d], tile_come.at[d], tile_send.at[d], tile_sem.at[d], "fsdp", f ^ d
+            )
+
+        for d in range(1, group):
+            seq_copy(d).start()
     for k in range(count):
         for d in range(1, slices):
             copy(k, d).start()
     for k in range(count):
-        landed[k][0] = sources[k][pl.ds(pl.multiple_of(f * depth, depth), depth), :]
+        landed[k][0] = inputs[k][pl.ds(pl.multiple_of(f * depth, depth), depth), :]
+    if gains:
+        seq_come[0] = inputs[count][s]
+        for d in range(1, group):
+            seq_copy(d).wait()
+        total = functools.reduce(jnp.add, [seq_come[d] for d in range(group)])
+        part = total.shape[1] // slices
+        tiles[...] = jnp.zeros_like(tiles)
+        for t in range(slices):
+            tiles[t, :, pl.ds(0, part)] = total[:, t * part : (t + 1) * part]
+        for d in range(1, slices):
+            tile_copy(d).start()
+        tile_come[0] = tiles[f]
     for k in range(count):
         for d in range(1, slices):
             copy(k, d).wait()
     for t in range(slices):
         for source, first, width, result, base in moves:
-            results[result][:, pl.ds(base + t * width, width)] = landed[source][
+            outputs[result][:, pl.ds(base + t * width, width)] = landed[source][
                 f ^ t, :, pl.ds(first, width)
             ]
-    if summed:
-        source, first = summed
-        results[-1][...] = functools.reduce(
-            jnp.add,
-            [landed[source][d, :, pl.ds(first, 128)].astype(jnp.float32) for d in range(slices)],
-        )
-
-
-def bring_home(sources, moves, widths, summed, slices, number):
+    if gains:
+        for d in range(1, slices):
+            tile_copy(d).wait()
+        outputs[results][...] = functools.reduce(jnp.add, [tile_come[d] for d in range(slices)])
+
+
+def bring_home(sources, moves, widths, gains, group, slices, number):
     depth = sources[0].shape[0] // slices
     shapes = [jax.ShapeDtypeStruct((depth, width), jnp.bfloat16) for width in widths]
-    if summed:
-        shapes.append(jax.ShapeDtypeStruct((depth, 128), jnp.float32))
+    scratch = [pltpu.VMEM((slices, depth, s.shape[1]), jnp.bfloat16) for s in sources]
+    scratch += [pltpu.SemaphoreType.DMA((len(sources), slices))] * 2
+    extra = []
+    if gains is not None:
+        extra = [gains]
+        shapes.append(jax.ShapeDtypeStruct((8, 128), jnp.float32))
+        scratch += [
+            pltpu.VMEM(gains.shape, jnp.float32),
+            pltpu.VMEM((slices, 8, 128), jnp.float32),
+            pltpu.VMEM((slices, 8, 128), jnp.float32),
+        ]
+        scratch += [pltpu.SemaphoreType.DMA((group,))] * 2
+        scratch += [pltpu.SemaphoreType.DMA((slices,))] * 2
     return pl.pallas_call(
-        functools.partial(home_kernel, count=len(sources), moves=moves, summed=summed),
-        in_specs=[VMEM] * len(sources),
+        functools.partial(
+            home_kernel, count=len(sources), results=len(widths), moves=moves, gains=len(extra)
+        ),
+        in_specs=[VMEM] * (len(sources) + len(extra)),
         out_specs=[VMEM] * len(shapes),
         out_shape=shapes,
-        scratch_shapes=[pltpu.VMEM((slices, depth, s.shape[1]), jnp.bfloat16) for s in sources]
-        + [pltpu.SemaphoreType.DMA((len(sources), slices))] * 2,
+        scratch_shapes=scratch,
         compiler_params=pltpu.CompilerParams(
             vmem_limit_bytes=32 << 20, collective_id=number, has_side_effects=True
         ),
         cost_estimate=pl.CostEstimate(flops=10 << 30, bytes_accessed=4 << 20, transcendentals=0),
-    )(*sources)
+    )(*sources, *extra)
 
 
 def swap(piece, axis, offset):
@@ -1238,14 +1292,14 @@
     cosine, sine = jnp.cos(angle), jnp.sin(angle)
     (
         inward_gains, normed, query, gains_full, kv_all, attended, logs, outward_full,
-        middle, normed_second, upstream_all,
+        middle, normed_second, upstream_all, normed_near,
     ) = attend_forward(in_rows, w_outward, inputs[0], cosine, sine, upstream, group, slices)
     gain_first, gain_second = gains_full[0], gains_full[1]
     scale_first = rms_scale(rows)
     scale_second = rms_scale(middle)
     down_slice = lax.all_gather(feed_down, "seq", axis=0, tiled=True)
     outward_full = outward_full.reshape(D, D)
-    normed_all, gate_all, up_all, hidden, down_partial, normed_near = feed_first(
+    normed_all, gate_all, up_all, hidden, down_partial, normed_other = feed_first(
         normed_second, upstream_all, gate_up_slice, normed
     )
     normed_second_grad, out_parts, gate_up_partial, normed_far = feed_second(
@@ -1270,50 +1324,49 @@
     inward_grad_blocks = exchange_swap(inward_slices, "fsdp")
     outward_partial = outer(attended_all.reshape(-1, D), branch_all.reshape(-1, D // slices))
     outward_partial = outward_partial.astype(jnp.bfloat16)
+
+    if slices == 4:
+        own, one, two, far = inward_grad_blocks
+        even = lax.rem(lax.axis_index("seq"), 2) == 0
+        near_blocks = jnp.concatenate([own, jnp.where(even, two, one)], axis=0)
+        inward_partial = (
+            outer(normed_near.reshape(-1, D), near_blocks)
+            + outer(normed_other, jnp.where(even, one, two))
+            + outer(normed_far, far)
+        )
+    else:
+        inward_partial = outer(
+            normed_near.reshape(-1, D), jnp.concatenate(inward_grad_blocks, axis=0)
+        )
+    inward_partial = inward_partial.astype(jnp.bfloat16)
+    slice_cols = inward_partial.shape[1]
+    inward_partial, gate_up_mine, inward_grad = lax.optimization_barrier(
+        (jnp.concatenate([inward_partial, outward_partial], axis=1), gate_up_mine, inward_grad)
+    )
+    inward_mine = scatter_rows(inward_partial)
     normed_grad = against(inward_grad, inward_gains)
     rows_back, gain_first_grad = norm_back(rows, scale_first, gain_first, normed_grad)
     input_grad = middle_grad + rows_back
-
-    inward_grad_blocks, gain_first_grad = lax.optimization_barrier(
-        (inward_grad_blocks, gain_first_grad)
-    )
-    gain_grads = jnp.stack([gain_first_grad, gain_second_grad], axis=1)
-    gain_grads = jnp.pad(gain_grads.astype(jnp.bfloat16), ((0, 0), (0, 126)))
-    if slices == 4:
-        inward_partial = outer(
-            normed_near[:3].reshape(-1, D), jnp.concatenate(inward_grad_blocks[:3], axis=0)
-        ) + outer(normed_far, inward_grad_blocks[3])
-    else:
-        inward_partial = outer(
-            normed_near.reshape(-1, D), jnp.concatenate(inward_grad_blocks, axis=0)
-        )
-    inward_partial = inward_partial.astype(jnp.bfloat16)
-    slice_cols = inward_partial.shape[1]
-    inward_partial, gate_up_mine = lax.optimization_barrier(
-        (
-            jnp.concatenate([inward_partial, gain_grads, outward_partial], axis=1),
-            gate_up_mine,
-        )
-    )
-    inward_mine = scatter_rows(inward_partial)
+    gain_grads = jnp.stack([gain_first_grad, gain_second_grad]).reshape(2, group, D // group)
+    gain_grads = jnp.pad(gain_grads.transpose(1, 0, 2), ((0, 0), (0, 6), (0, 0)))
     result = middle + functools.reduce(
         jnp.add,
         [p.astype(jnp.float32) for p in [out_parts[0]] + [out_come[d] for d in range(slices - 1)]],
     )
-    gate_up_sum, down_sum = bring_home(
+    gate_up_sum, down_sum, gains_sum = bring_home(
         [gate_up_mine, down_mine],
         [(0, 0, ff_cols, 0, 0), (0, ff_cols, ff_cols, 0, FF), (1, 0, ff_cols, 1, 0)],
-        [2 * FF, FF], None, slices, 6,
-    )
-    inward_sum, outward_sum, gains_sum = bring_home(
+        [2 * FF, FF], gain_grads, group, slices, 6,
+    )
+    inward_sum, outward_sum = bring_home(
         [inward_mine],
-        [(0, 0, slice_cols, 0, 0), (0, slice_cols + 128, D // slices, 1, 0)],
-        [inward_cols, D], (0, slice_cols), slices, 7,
+        [(0, 0, slice_cols, 0, 0), (0, slice_cols, D // slices, 1, 0)],
+        [inward_cols, D], None, group, slices, 7,
     )
     gate_up_sum, down_sum, inward_sum, outward_sum = [
         field.astype(jnp.float32) for field in (gate_up_sum, down_sum, inward_sum, outward_sum)
     ]
-    gains_sum = jnp.transpose(gains_sum[:, :2])
+    gains_sum = gains_sum[:2, :depth]
     first_inward_new, second_inward_new, inward_new = adam_update(
         w_inward, first_inward, second_inward, inward_sum, 0.02, weight_decay
     )

time: 586 us -> 573 us (0.978)
  waiting for transfers between devices: 48.9 us -> 15.2 us
  Pallas kernels: 438 us -> 471 us
  local copies, waits for them, and re-layouts: 22 us -> 14.1 us
    reduce_scatter x3, waiting for transfers between devices: 40.2 us -> 7.01 us  [scatter_rows(): return lax.psum_scatter(partial, 'seq', scatter_dimension=0, tiled=True)]
    pallas_call x1, Pallas kernels: 134 us -> 149 us  [attend_forward(): pl.pallas_call(forward_kernel, in_specs=[VMEM] * 5 + [ANY], out_specs=[VM...]
    pallas_call x1, Pallas kernels: 103 us -> 117 us  [attend_backward(): pl.pallas_call(backward_kernel, in_specs=[VMEM] * 10 + [ANY], out_specs=[...]
    pallas_call x2, Pallas kernels: 25.8 us -> 36.3 us  [bring_home(): pl.pallas_call(functools.partial(home_kernel, count=len(sources), results...]
    all_gather x1, waiting for transfers between devices: 7.95 us -> 0.02 us  [body(): gate_up_slice = lax.all_gather(feed_gate_up, 'seq', axis=0, tiled=True)]
    ppermute x3, waiting for transfers between devices: 0.01 us -> 7.37 us  [swap(): return lax.ppermute(piece, axis, [(i, i ^ offset) for i in range(size)])]
    pallas_call x1, Pallas kernels: 70 us -> 63.3 us  [feed_first(): pl.pallas_call(functools.partial(feed_first_kernel, slices=slices, strip=...]
    unnamed x86 -> x78, local copies, waits for them, and re-layouts: 12.3 us -> 10.8 us
  transfers between devices with their start and end apart: 8 -> 8, of which waited for: 3 -> 4; matrix products, arithmetic and copies ran while one was open for 10% -> 8% of each run, Pallas kernels for 67% -> 75%
where the time goes in v6:
time: 573 us; the launch traced here: 565 us
  Pallas kernels  471 us (82%)
  other arithmetic  23.4 us (4%)
  matrix products  22.9 us (4%)
  waiting for transfers between devices  15.2 us (3%)
  between operations  14.9 us (3%)
  local copies, waits for them, and re-layouts  14.1 us (2%)
    pallas_call x1, Pallas kernels, attend_forward(): pl.pallas_call(forward_kernel, in_specs=[VMEM] * 5 + [ANY], out_specs=[VM...  149 us
    pallas_call x1, Pallas kernels, attend_backward(): pl.pallas_call(backward_kernel, in_specs=[VMEM] * 10 + [ANY], out_specs=[...  117 us
    pallas_call x1, Pallas kernels, feed_second(): pl.pallas_call(functools.partial(feed_second_kernel, slices=slices, strip...  64.2 us
    pallas_call x1, Pallas kernels, feed_first(): pl.pallas_call(functools.partial(feed_first_kernel, slices=slices, strip=...  63.3 us
    pallas_call x1, Pallas kernels, share_weights(): pl.pallas_call(share_kernel, in_specs=[VMEM] * 4, out_specs=[VMEM] * 3, o...  40.3 us
    pallas_call x2, Pallas kernels, bring_home(): pl.pallas_call(functools.partial(home_kernel, count=len(sources), results...  36.3 us
    dot_general x2, matrix products, against(): lax.dot_general(left, right, (((1,), (1,)), ((), ())), preferred_element_...  14.3 us
  transfers between devices with their start and end apart: 8, of which 4 were waited for; matrix products, arithmetic and copies ran while one was open for 8% of the time, Pallas kernels for 75%

profile of v6, /device:TPU:9, one launch (start us, length us, event | category | flops | bytes accessed | tf_op | source)
XLA Modules:
  0.0 565.1 jit_solution(4253927586981496403)
XLA Ops:
  7.2 0.0 all-gather.3.cloned.1.call-start
  7.2 0.7 convert_element_type.75
  7.9 0.1 copy.50
  8.1 1.4 copy-done
  9.4 1.1 copy-done.2
  10.5 40.3 %shard_map.296 = (bf16[256,2816]{1,0:T(8,128)(2,1)}, bf16[256,1408]{1,0:T(8,128)(2,1)}, bf16[4,2,64,2688]{3,2,1,0:T(8,128)(2,1)}) custom-call(f32[64,2560]{1,0:T(8,128)S(1)} %copy-done.2, bf16[64,128]{1,0:T(8,128)(2,1)S(1)} %pad.8.gain_ref, f32[64,11264]{1,0:T(8,128)} %gate_up_ref.1, f32[64,5632]{1,0:T(8,128)S(1)} %copy-done), custom_call_target="tpu_custom_call" | custom-call | tf_op jit(solution)/shard_map/pallas_call | solution.py:178
  50.8 0.0 all-gather.3.cloned.1.call-update
  50.8 0.0 all-gather.5.cloned.1.call-start
  50.9 0.7 all-gather.5.cloned.1.call-update
  51.6 0.0 reduce-scatter.4.cloned.1.call-start
  51.7 0.5 fusion.25
  52.3 0.6 copy-done.24
  52.9 0.1 pad_maximum_fusion.1
  53.0 0.1 copy.53
  53.1 0.8 copy.55.sine_ref
  53.9 0.1 copy.52
  54.0 0.8 copy.54.cosine_ref
  54.7 149.4 %shard_map.297 = (bf16[4,2,4,64,2688]{4,3,2,1,0:T(8,128)(2,1)}, bf16[256,2048]{1,0:T(8,128)(2,1)}, bf16[256,2048]{1,0:T(8,128)(2,1)}, f32[2,2048]{1,0:T(2,128)},...) custom-call(bf16[4,2,64,2688]{3,2,1,0:T(8,128)(2,1)} %get-tuple-elem, ...), custom_call_target="tpu_custom_call" | custom-call | flops 171798691840 | bytes 20971520 | tf_op jit(solution)/shard_map/pallas_call | solution.py:716
  204.2 0.0 all-gather.3.cloned.1.call-done.refs_2_.refs_5_
  204.2 63.3 %shard_map.298 = (bf16[4,256,2048]{2,1,0:T(8,128)(2,1)}, bf16[1024,1408]{1,0:T(8,128)(2,1)}, bf16[1024,1408]{1,0:T(8,128)(2,1)}, bf16[1024,1408]{1,0:T(8,128)(2,...) custom-call(bf16[4,256,2048]{2,1,0:T(8,128)(2,1)} %get-tuple-element.63.refs_0_, ...), custom_call_target="tpu_custom_call" | custom-call | flops 29527900160 | bytes 31457280 | tf_op jit(solution)/shard_map/pallas_call | solution.py:1036
  267.5 0.0 reduce-scatter.4.cloned.1.call-update
  267.6 0.6 reduce-scatter.6.cloned.1.call-start
  268.1 0.0 all-gather.5.cloned.1.call-done.refs_6_
  268.2 64.2 %shard_map.299 = (f32[256,2048]{1,0:T(8,128)}, bf16[4,256,2048]{2,1,0:T(8,128)(2,1)}, bf16[2048,2816]{1,0:T(8,128)(2,1)}, bf16[256,2048]{1,0:T(8,128)(2,1)}) custom-call(bf16[4,256,2048]{2,1,0:T(8,128)(2,1)} %get-tuple-element.63.refs_0_, bf16[4,256,2048]{2,1,0:T(8,128)(2,1)} %get-tuple-element.67.refs_1_, bf16[1024,1408]{1,0:T(8,128)(2,1)} %get-tuple-element.68.refs_2_, ...), custom_call_target="tpu_custom_call" | custom-call | flops 59055800320 | bytes 41943040 | tf_op jit(solution)/shard_map/pallas_call | solution.py:1079
  332.5 0.2 reduce-scatter.8.cloned.1.call-start
  332.7 0.4 copy-done.31
  333.1 0.2 multiply_sine_fusion.1
  333.3 0.8 copy.67
  334.1 0.8 copy.68
  334.9 0.2 multiply_reduce_fusion.2
  335.2 1.4 copy-done.10
  336.5 0.6 multiply_reduce_fusion
  337.1 0.6 copy-done.20
  337.8 2.0 fusion.37
  339.7 7.2 %convolution_convert_fusion.grad_ref = bf16[256,2048]{1,0:T(8,128)(2,1)} fusion(bf16[256,2048]{1,0:T(8,128)(2,1)S(1)} %get-tuple-element.124.branch_ref, bf16[2048,2048]{1,0:T(8,128)(2,1)} %bitcast.71), kind=kOutput, calls=%fused_computation.12 | convolution fusion | flops 2148007936 | bytes 10485760 | tf_op jit(solution)/shard_map/dot_general | solution.py:65
  347.0 117.4 %shard_map.300 = (bf16[256,2688]{1,0:T(8,128)(2,1)}, bf16[4,256,640]{2,1,0:T(8,128)(2,1)}, bf16[4,256,2048]{2,1,0:T(8,128)(2,1)}, bf16[4,256,512]{2,1,0:T(8,128)(2,1)}, bf16[3,256,2048]{2,1,0:T(8,128)(2,1)}) custom-call(bf16[256,2048]{1,0:T(8,128)(2,1)} %convolution_convert_fusion.grad_ref, bf16[256,2048]{1,0:T(8,128)(2,1)} %get-tuple-element.77.query_ref, ...), custom_call_target="tpu_custom_call" | custom-call | flops 85899345920 | bytes 20971520 | tf_op jit(solution)/shard_map/pallas_call | solution.py:773
  464.4 0.0 reduce-scatter.4.cloned.1.call-done.refs_1_
  464.4 1.5 dynamic-slice_bitcast_fusion.3
  465.9 0.1 collective-permute-start
  466.0 0.6 collective-permute-start.1
  466.6 2.0 collective-permute-start.2
  468.6 4.6 bitcast_convert_fusion
  473.2 2.4 collective-permute-done
  475.7 1.9 fusion.16
  477.6 1.1 fusion.22
  478.7 5.0 collective-permute-done.2
  483.6 1.1 add_convert_fusion
  484.7 2.5 pad_maximum_fusion
  487.2 1.6 reduce-scatter.6.cloned.1.call-done.refs_0_
  488.9 0.3 fusion.2
  489.2 7.1 %fusion.9 = (f32[2048]{0:T(1024)S(1)}, f32[256]{0:T(256)S(1)}, f32[256,2048]{1,0:T(8,128)S(1)}) fusion(f32[256]{0:T(256)S(1)} %get-tuple-element.138, bf16[1,256,2048]{2,1,0:T(8,128)(2,1)S(1)} %copy-done.11, f32[2048]{0:T(1024)S(1)} %bitcast.66, bf16[256,2688]{1,0:T(8,128)(2,1)} %get-tuple-element.95, bf16[2048,2688]{1,0:T(8,128)(2,1)} %bitcast.70), kind=kOutput, calls=%fused_computation.21 | convolution fusion | flops 2822240000 | bytes 15550464 | tf_op jit(solution)/shard_map/dot_general | solution.py:65
  496.4 27.3 %shard_map.302 = (bf16[64,11264]{1,0:T(8,128)(2,1)S(1)}, bf16[64,5632]{1,0:T(8,128)(2,1)S(1)}, f32[8,128]{1,0:T(8,128)S(1)}) custom-call(bf16[256,2816]{1,0:T(8,128)(2,1)S(1)} %copy-done.4, bf16[256,1408]{1,0:T(8,128)(2,1)S(1)} %copy-done.5, f32[8,8,256]{2,1,0:T(8,128)S(1)} %pad.9.refs_2_), custom_call_target="tpu_custom_call" | custom-call | flops 10737418240 | bytes 4194304 | tf_op jit(solution)/shard_map/pallas_call | solution.py:1199
  523.8 0.6 multiply_subtract_fusion.4
  524.4 4.8 fusion.6
  529.2 2.8 multiply_subtract_fusion.1
  532.0 1.5 copy-done.13
  533.5 0.9 copy-done.14
  534.4 5.0 multiply_subtract_fusion
  539.4 5.4 reduce-scatter.8.cloned.1.call-done.refs_0_
  544.7 1.1 copy-done.6
  545.8 9.0 %shard_map.301 = (bf16[64,2560]{1,0:T(8,128)(2,1)S(1)}, bf16[64,2048]{1,0:T(8,128)(2,1)S(1)}) custom-call(bf16[256,1152]{1,0:T(8,128)(2,1)S(1)} %copy-done.6), custom_call_target="tpu_custom_call" | custom-call | flops 10737418240 | bytes 4194304 | tf_op jit(solution)/shard_map/pallas_call | solution.py:1199
  554.9 1.6 multiply_subtract_fusion.2
  556.5 0.3 copy-done.28
  556.7 1.4 multiply_subtract_fusion.3
  (84 shorter events, 0.4 us)
Async XLA Ops:
  7.2 197.0 %all-gather.3.cloned.1.call-start = ((), (), s32[]{:S(2)}) async-start(), calls=%async_computation.3 | async-start | bytes 12976128 | tf_op jit(solution)/shard_map/all_gather | solution.py:1289
  8.0 1.4 copy-start
  9.4 1.1 copy-start.2
  50.8 217.3 %all-gather.5.cloned.1.call-start = ((), (), s32[]{:S(2)}) async-start(), calls=%async_computation.4 | async-start | bytes 6488064 | tf_op jit(solution)/shard_map/all_gather | solution.py:1300
  51.6 412.8 %reduce-scatter.4.cloned.1.call-start = ((), (), s32[]{:S(2)}) async-start(), calls=%async_computation.5 | async-start | bytes 6488064 | tf_op jit(solution)/shard_map/reduce_scatter | solution.py:1241
  51.7 0.6 copy-start.32
  51.7 0.6 copy-start.30
  52.2 0.7 copy-start.24
  52.3 151.9 %copy-start.25 = (f32[256,32]{1,0:T(8,128)}, f32[256,32]{1,0:T(8,128)S(1)}, u32[]{:S(2)}) copy-start(f32[256,32]{1,0:T(8,128)S(1)} %get-tuple-element.136.cosine_rows) | copy-start | bytes 98308
  267.6 221.3 %reduce-scatter.6.cloned.1.call-start = ((), (), s32[]{:S(2)}) async-start(), calls=%async_computation.6 | async-start | bytes 12976128 | tf_op jit(solution)/shard_map/reduce_scatter | solution.py:1241
  332.4 0.7 copy-start.31
  332.4 0.7 copy-start.33
  332.4 2.5 copy-start.7
  332.5 2.7 copy-start.29
  332.5 212.3 %reduce-scatter.8.cloned.1.call-start = ((), (), s32[]{:S(2)}) async-start(), calls=%async_computation.7 | async-start | bytes 5308416 | tf_op jit(solution)/shard_map/reduce_scatter | solution.py:1241
  334.9 1.6 copy-start.10
  336.5 1.2 copy-start.20
  339.7 7.2 %copy-start.21 = (bf16[256,2048]{1,0:T(8,128)(2,1)}, bf16[256,2048]{1,0:T(8,128)(2,1)S(1)}, u32[]{:S(2)}) copy-start(bf16[256,2048]{1,0:T(8,128)(2,1)S(1)} %get-tuple-element.124.branch_ref) | copy-start | bytes 3145732
  464.4 4.2 copy-start.37
  465.9 9.7 %collective-permute-start = (bf16[256,640]{1,0:T(8,128)(2,1)S(1)}, bf16[256,640]{1,0:T(8,128)(2,1)S(1)}, u32[]{:S(2)}, u32[]{:S(2)}) collective-permute-start(bf16[256,640]{1,0:T(8,128)(2,1)S(1)} %get-tuple-element.129), channel_id=1, source_target_pairs={{0,2},{1,3},{2,0},{3,1},{4,6},{5,7},{6,4},{7,5},{8,10},{9,11},{10,... | collective-permute-start | bytes 983048 | tf_op jit(solution)/shard_map/ppermute | solution.py:1216
  466.0 9.6 %collective-permute-start.1 = (bf16[256,640]{1,0:T(8,128)(2,1)S(1)}, bf16[256,640]{1,0:T(8,128)(2,1)S(1)}, u32[]{:S(2)}, u32[]{:S(2)}) collective-permute-start(bf16[256,640]{1,0:T(8,128)(2,1)S(1)} %get-tuple-element.128), channel_id=1, source_target_pairs={{0,1},{1,0},{2,3},{3,2},{4,5},{5,4},{6,7},{7,6},{8,9},{9,8},{10,11... | collective-permute-start | bytes 983048 | tf_op jit(solution)/shard_map/ppermute | solution.py:1216
  466.6 9.1 %copy-start.16 = (bf16[2,256,2048]{2,1,0:T(8,128)(2,1)S(1)}, bf16[2,256,2048]{2,1,0:T(8,128)(2,1)}, u32[]{:S(2)}) copy-start(bf16[2,256,2048]{2,1,0:T(8,128)(2,1)} %get-tuple-element.72.refs_7_) | copy-start | bytes 6291460
  466.6 17.0 %collective-permute-start.2 = (bf16[256,640]{1,0:T(8,128)(2,1)S(1)}, bf16[256,640]{1,0:T(8,128)(2,1)S(1)}, u32[]{:S(2)}, u32[]{:S(2)}) collective-permute-start(bf16[256,640]{1,0:T(8,128)(2,1)S(1)} %get-tuple-element.127), channel_id=1, source_target_pairs={{0,3},{1,2},{2,1},{3,0},{4,7},{5,6},{6,5},{7,4},{8,11},{9,10},{10,... | collective-permute-start | bytes 983048 | tf_op jit(solution)/shard_map/ppermute | solution.py:1216
  475.7 1.9 copy-start.15
  477.6 6.0 %copy-start.19 = (bf16[256,2048]{1,0:T(8,128)(2,1)S(1)}, bf16[256,2048]{1,0:T(8,128)(2,1)}, u32[]{:S(2)}) copy-start(bf16[256,2048]{1,0:T(8,128)(2,1)} %get-tuple-element.90) | copy-start | bytes 3145732
  487.2 1.7 copy-start.11
  489.2 7.2 %copy-start.4 = (bf16[256,2816]{1,0:T(8,128)(2,1)S(1)}, bf16[256,2816]{1,0:T(8,128)(2,1)}, u32[]{:S(2)}) copy-start(bf16[256,2816]{1,0:T(8,128)(2,1)} %reduce-scatter.6.cloned.1.call-done.refs_0_) | copy-start | bytes 4325380
  489.2 7.2 %copy-start.5 = (bf16[256,1408]{1,0:T(8,128)(2,1)S(1)}, bf16[256,1408]{1,0:T(8,128)(2,1)}, u32[]{:S(2)}) copy-start(bf16[256,1408]{1,0:T(8,128)(2,1)} %reduce-scatter.4.cloned.1.call-done.refs_1_) | copy-start | bytes 2162692
  496.4 27.4 %copy-start.34 = (f32[2,64]{1,0:T(2,128)S(1)}, f32[2,64]{1,0:T(2,128)}, u32[]{:S(2)}) copy-start(f32[2,64]{1,0:T(2,128)} %param.23) | copy-start | bytes 1540
  496.4 27.4 %copy-start.35 = (f32[2,64]{1,0:T(2,128)S(1)}, f32[2,64]{1,0:T(2,128)}, u32[]{:S(2)}) copy-start(f32[2,64]{1,0:T(2,128)} %param.33) | copy-start | bytes 1540
  496.4 27.4 %copy-start.36 = (f32[2,64]{1,0:T(2,128)S(1)}, f32[2,64]{1,0:T(2,128)}, u32[]{:S(2)}) copy-start(f32[2,64]{1,0:T(2,128)} %param.28) | copy-start | bytes 1540
  496.4 28.0 %copy-start.9 = (f32[256,2048]{1,0:T(8,128)S(1)}, f32[256,2048]{1,0:T(8,128)}, u32[]{:S(2)}) copy-start(f32[256,2048]{1,0:T(8,128)} %get-tuple-element.125) | copy-start | bytes 6291460
  496.4 28.0 %copy-start.12 = (bf16[3,256,2048]{2,1,0:T(8,128)(2,1)S(1)}, bf16[3,256,2048]{2,1,0:T(8,128)(2,1)}, u32[]{:S(2)}) copy-start(bf16[3,256,2048]{2,1,0:T(8,128)(2,1)} %get-tuple-element.81) | copy-start | bytes 9437188
  524.4 4.8 copy-start.1
  524.4 4.8 copy-start.17
  524.4 4.8 copy-start.18
  529.2 2.8 copy-start.8
  529.2 4.3 copy-start.13
  529.2 5.2 copy-start.14
  539.4 15.4 %copy-start.3 = (f32[64,2560]{1,0:T(8,128)S(1)}, f32[64,2560]{1,0:T(8,128)}, u32[]{:S(2)}) copy-start(f32[64,2560]{1,0:T(8,128)} %in_ref.1) | copy-start | bytes 1966084
  544.7 1.1 copy-start.6
  545.8 9.0 %copy-start.22 = (f32[64,2560]{1,0:T(8,128)S(1)}, f32[64,2560]{1,0:T(8,128)}, u32[]{:S(2)}) copy-start(f32[64,2560]{1,0:T(8,128)} %param.29) | copy-start | bytes 1966084
  545.8 9.0 %copy-start.23 = (f32[64,2560]{1,0:T(8,128)S(1)}, f32[64,2560]{1,0:T(8,128)}, u32[]{:S(2)}) copy-start(f32[64,2560]{1,0:T(8,128)} %param.24) | copy-start | bytes 1966084
  554.8 1.6 copy-start.26
  554.8 1.6 copy-start.27
  554.8 1.9 copy-start.28
Sparse Core Ops, SparseCore 0:
  51.0 145.5 all-gather.2
  198.2 61.2 all-gather.4
  267.7 76.7 reduce-scatter.3
  346.7 142.1 reduce-scatter.5
  491.0 53.6 reduce-scatter.7

commit v7 on v6

--- a/solution.py
+++ b/solution.py
@@ -140,6 +140,16 @@
     in_rows[pair, core, :, pl.ds(inward_cols, 128)] = gain_ref[...]
     meet_spread(near)
     pass_rows_start(in_rows, send_in, come_in, near)
+    feeds = ((low_gate_up, feed_gate_up), (low_down, feed_down))
+
+    def feed_copy(k, d, owner, target):
+        low, feed = feeds[k]
+        return remote(
+            low.at[target],
+            feed.at[pl.ds(pl.multiple_of(owner * depth, depth), depth), :],
+            send_feed.at[k, d], come_feed.at[k, d], "fsdp", target,
+        )
+
     for t in range(slices):
         columns = pl.ds(t * ff_cols, ff_cols)
         low_gate_up[t, :, pl.ds(0, ff_cols)] = gate_up_ref[:, columns].astype(jnp.bfloat16)
@@ -148,19 +158,11 @@
         ].astype(jnp.bfloat16)
         low_down[t] = down_ref[:, columns].astype(jnp.bfloat16)
 
-    feeds = ((low_gate_up, feed_gate_up), (low_down, feed_down))
-
-    def feed_copy(k, d, owner, target):
-        low, feed = feeds[k]
-        return remote(
-            low.at[target],
-            feed.at[pl.ds(pl.multiple_of(owner * depth, depth), depth), :],
-            send_feed.at[k, d], come_feed.at[k, d], "fsdp", target,
-        )
-
-    for d in range(1, slices):
-        for k in range(2):
-            feed_copy(k, d, f, f ^ d).start()
+        @pl.when(f != t)
+        def _():
+            for k in range(2):
+                feed_copy(k, f ^ t, f, t).start()
+
     mine = pl.ds(pl.multiple_of(f * depth, depth), depth)
     for low, feed in feeds:
         feed[mine, :] = low[f]
@@ -432,17 +434,27 @@
             return masked_scores(keys, queries[h], local, core * local), values
         return against(keys, queries[h]), values
 
-    def own_chip(h, _):
+    def keep(heads, states):
+        for h, (new, new_total, new_mixed) in zip(heads, states):
+            largest[h], total[h], mixed[h] = new, new_total, new_mixed
+
+    def own_head(h):
         scores, values = scores_of(h, place, True)
         new = jnp.max(scores, axis=0, keepdims=True)
         weights = jnp.exp(scores - new)
-        largest[h] = new
-        total[h] = jnp.sum(weights, axis=0, keepdims=True)
-        mixed[h] = outer(values, weights.astype(jnp.bfloat16))
+        return (
+            new,
+            jnp.sum(weights, axis=0, keepdims=True),
+            outer(values, weights.astype(jnp.bfloat16)),
+        )
+
+    def own_chip(i, _):
+        heads = (2 * i, 2 * i + 1)
+        keep(heads, [own_head(h) for h in heads])
         return 0
 
     kv_copy(1, s ^ 1, s ^ 1).wait_recv()
-    lax.fori_loop(0, KV_HEADS, own_chip, 0)
+    lax.fori_loop(0, KV_HEADS // 2, own_chip, 0)
 
     @pl.when(place == 0)
     def _():
@@ -451,7 +463,7 @@
     def earlier_chip(turn, _):
         chip = place - 1 - turn
 
-        @pl.when(turn == jnp.minimum(place - 1, 1))
+        @pl.when(turn == 0)
         def _():
             links_late()
 
@@ -460,17 +472,24 @@
         hand_on(chip, core).start()
         hand_on(chip, 1 - core).wait_recv()
 
-        def head(h, _):
+        def head(h):
             scores, values = scores_of(h, chip, False)
-            new = jnp.maximum(largest[h], jnp.max(scores, axis=0, keepdims=True))
-            fade = jnp.exp(largest[h] - new)
+            old = largest[h]
+            new = jnp.maximum(old, jnp.max(scores, axis=0, keepdims=True))
+            fade = jnp.exp(old - new)
             weights = jnp.exp(scores - new)
-            largest[h] = new
-            total[h] = total[h] * fade + jnp.sum(weights, axis=0, keepdims=True)
-            mixed[h] = mixed[h] * fade + outer(values, weights.astype(jnp.bfloat16))
+            return (
+                new,
+                total[h] * fade + jnp.sum(weights, axis=0, keepdims=True),
+                mixed[h] * fade + outer(values, weights.astype(jnp.bfloat16)),
+            )
+
+        def two_heads(i, _):
+            heads = (2 * i, 2 * i + 1)
+            keep(heads, [head(h) for h in heads])
             return 0
 
-        lax.fori_loop(0, KV_HEADS, head, 0)
+        lax.fori_loop(0, KV_HEADS // 2, two_heads, 0)
         return 0
 
     lax.fori_loop(0, place, earlier_chip, 0)
@@ -600,9 +619,18 @@
         value_grad = dot(shares.astype(jnp.bfloat16), grads[h])
         key_grad = dot(score_grad, queries[h])
         part = jnp.concatenate([key_grad, value_grad], axis=1).astype(jnp.bfloat16)
-        parts[chip, :, :, columns] = part.reshape(2, local, pair)
-        query_sum[h] += outer(keys, score_grad)
-        return 0
+        return columns, part.reshape(2, local, pair), query_sum[h] + outer(keys, score_grad)
+
+    def all_heads(chip, masked):
+        def two_heads(i, _):
+            heads = (2 * i, 2 * i + 1)
+            done = [head_grads(h, chip, masked) for h in heads]
+            for h, (columns, part, total) in zip(heads, done):
+                parts[chip, :, :, columns] = part
+                query_sum[h] = total
+            return 0
+
+        lax.fori_loop(0, KV_HEADS // 2, two_heads, 0)
 
     def finish_chip(chip):
         part_copy(chip, core).wait_recv()
@@ -616,7 +644,7 @@
         def _():
             gathers_early()
 
-        lax.fori_loop(0, KV_HEADS, lambda h, c: head_grads(h, chip, False), 0)
+        all_heads(chip, False)
         part_copy(chip, 1 - core).start()
 
         @pl.when(chip > 0)
@@ -631,7 +659,7 @@
     def _():
         finish_chip(place - 1)
 
-    lax.fori_loop(0, KV_HEADS, lambda h, c: head_grads(h, place, True), 0)
+    all_heads(place, True)
 
     @pl.when(core == 1)
     def _():

time: 573 us -> 566 us (0.988)
  Pallas kernels: 471 us -> 461 us
    pallas_call x1, Pallas kernels: 117 us -> 108 us  [attend_backward(): pl.pallas_call(backward_kernel, in_specs=[VMEM] * 10 + [ANY], out_specs=[...]
  transfers between devices with their start and end apart: 8 -> 8, of which waited for: 4 -> 4; matrix products, arithmetic and copies ran while one was open for 8% -> 8% of each run, Pallas kernels for 75% -> 74%
where the time goes in v7:
time: 566 us; the launch traced here: 556 us
  Pallas kernels  461 us (81%)
  other arithmetic  23.4 us (4%)
  matrix products  22.7 us (4%)
  waiting for transfers between devices  16.5 us (3%)
  between operations  14.6 us (3%)
  local copies, waits for them, and re-layouts  14.2 us (3%)
    pallas_call x1, Pallas kernels, attend_forward(): pl.pallas_call(forward_kernel, in_specs=[VMEM] * 5 + [ANY], out_specs=[VM...  149 us
    pallas_call x1, Pallas kernels, attend_backward(): pl.pallas_call(backward_kernel, in_specs=[VMEM] * 10 + [ANY], out_specs=[...  108 us
    pallas_call x1, Pallas kernels, feed_second(): pl.pallas_call(functools.partial(feed_second_kernel, slices=slices, strip...  64.2 us
    pallas_call x1, Pallas kernels, feed_first(): pl.pallas_call(functools.partial(feed_first_kernel, slices=slices, strip=...  63.3 us
    pallas_call x1, Pallas kernels, share_weights(): pl.pallas_call(share_kernel, in_specs=[VMEM] * 4, out_specs=[VMEM] * 3, o...  40.3 us
    pallas_call x2, Pallas kernels, bring_home(): pl.pallas_call(functools.partial(home_kernel, count=len(sources), results...  36.2 us
    dot_general x2, matrix products, against(): lax.dot_general(left, right, (((1,), (1,)), ((), ())), preferred_element_...  14.1 us
    sub x5, other arithmetic, adam_update(): weight - rate * (first_hat / (jnp.sqrt(second_hat) + adam_epsilon) + deca...  11.4 us
  transfers between devices with their start and end apart: 8, of which 4 were waited for; matrix products, arithmetic and copies ran while one was open for 8% of the time, Pallas kernels for 74%

profile of v7, /device:TPU:9, one launch (start us, length us, event | category | flops | bytes accessed | tf_op | source)
XLA Modules:
  0.0 556.1 jit_solution(14179778410782120378)
XLA Ops:
  7.2 0.0 all-gather.3.cloned.1.call-start
  7.2 0.7 convert_element_type.75
  7.9 0.1 copy.50
  8.1 1.4 copy-done
  9.4 1.1 copy-done.2
  10.5 40.3 %shard_map.296 = (bf16[256,2816]{1,0:T(8,128)(2,1)}, bf16[256,1408]{1,0:T(8,128)(2,1)}, bf16[4,2,64,2688]{3,2,1,0:T(8,128)(2,1)}) custom-call(f32[64,2560]{1,0:T(8,128)S(1)} %copy-done.2, bf16[64,128]{1,0:T(8,128)(2,1)S(1)} %pad.8.gain_ref, f32[64,11264]{1,0:T(8,128)} %gate_up_ref.1, f32[64,5632]{1,0:T(8,128)S(1)} %copy-done), custom_call_target="tpu_custom_call" | custom-call | tf_op jit(solution)/shard_map/pallas_call | solution.py:180
  50.8 0.0 all-gather.3.cloned.1.call-update
  50.8 0.0 all-gather.5.cloned.1.call-start
  50.9 0.7 all-gather.5.cloned.1.call-update
  51.6 0.0 reduce-scatter.4.cloned.1.call-start
  51.7 0.5 fusion.25
  52.3 0.6 copy-done.24
  52.9 0.1 pad_maximum_fusion.1
  53.0 0.1 copy.53
  53.1 0.8 copy.55.sine_ref
  53.9 0.1 copy.52
  54.0 0.8 copy.54.cosine_ref
  54.7 149.4 %shard_map.297 = (bf16[4,2,4,64,2688]{4,3,2,1,0:T(8,128)(2,1)}, bf16[256,2048]{1,0:T(8,128)(2,1)}, bf16[256,2048]{1,0:T(8,128)(2,1)}, f32[2,2048]{1,0:T(2,128)},...) custom-call(bf16[4,2,64,2688]{3,2,1,0:T(8,128)(2,1)} %get-tuple-elem, ...), custom_call_target="tpu_custom_call" | custom-call | flops 171798691840 | bytes 20971520 | tf_op jit(solution)/shard_map/pallas_call | solution.py:744
  204.2 0.0 all-gather.3.cloned.1.call-done.refs_2_.refs_5_
  204.2 63.3 %shard_map.298 = (bf16[4,256,2048]{2,1,0:T(8,128)(2,1)}, bf16[1024,1408]{1,0:T(8,128)(2,1)}, bf16[1024,1408]{1,0:T(8,128)(2,1)}, bf16[1024,1408]{1,0:T(8,128)(2,...) custom-call(bf16[4,256,2048]{2,1,0:T(8,128)(2,1)} %get-tuple-element.63.refs_0_, ...), custom_call_target="tpu_custom_call" | custom-call | flops 29527900160 | bytes 31457280 | tf_op jit(solution)/shard_map/pallas_call | solution.py:1064
  267.5 0.0 reduce-scatter.4.cloned.1.call-update
  267.6 0.0 reduce-scatter.6.cloned.1.call-start
  267.6 0.0 all-gather.5.cloned.1.call-done.refs_6_
  267.6 64.2 %shard_map.299 = (f32[256,2048]{1,0:T(8,128)}, bf16[4,256,2048]{2,1,0:T(8,128)(2,1)}, bf16[2048,2816]{1,0:T(8,128)(2,1)}, bf16[256,2048]{1,0:T(8,128)(2,1)}) custom-call(bf16[4,256,2048]{2,1,0:T(8,128)(2,1)} %get-tuple-element.63.refs_0_, bf16[4,256,2048]{2,1,0:T(8,128)(2,1)} %get-tuple-element.67.refs_1_, bf16[1024,1408]{1,0:T(8,128)(2,1)} %get-tuple-element.68.refs_2_, ...), custom_call_target="tpu_custom_call" | custom-call | flops 59055800320 | bytes 41943040 | tf_op jit(solution)/shard_map/pallas_call | solution.py:1107
  331.9 0.3 reduce-scatter.8.cloned.1.call-start
  332.2 0.3 copy-done.31
  332.5 0.2 multiply_sine_fusion.1
  332.8 0.8 copy.67
  333.6 0.8 copy.68
  334.4 0.2 multiply_reduce_fusion.2
  334.6 1.3 copy-done.10
  336.0 0.6 multiply_reduce_fusion
  336.6 0.6 copy-done.20
  337.2 2.0 fusion.37
  339.2 7.1 %convolution_convert_fusion.grad_ref = bf16[256,2048]{1,0:T(8,128)(2,1)} fusion(bf16[256,2048]{1,0:T(8,128)(2,1)S(1)} %get-tuple-element.124.branch_ref, bf16[2048,2048]{1,0:T(8,128)(2,1)} %bitcast.71), kind=kOutput, calls=%fused_computation.12 | convolution fusion | flops 2148007936 | bytes 10485760 | tf_op jit(solution)/shard_map/dot_general | solution.py:65
  346.3 108.0 %shard_map.300 = (bf16[256,2688]{1,0:T(8,128)(2,1)}, bf16[4,256,640]{2,1,0:T(8,128)(2,1)}, bf16[4,256,2048]{2,1,0:T(8,128)(2,1)}, bf16[4,256,512]{2,1,0:T(8,128)(2,1)}, bf16[3,256,2048]{2,1,0:T(8,128)(2,1)}) custom-call(bf16[256,2048]{1,0:T(8,128)(2,1)} %convolution_convert_fusion.grad_ref, bf16[256,2048]{1,0:T(8,128)(2,1)} %get-tuple-element.77.query_ref, ...), custom_call_target="tpu_custom_call" | custom-call | flops 85899345920 | bytes 20971520 | tf_op jit(solution)/shard_map/pallas_call | solution.py:801
  454.3 0.0 reduce-scatter.4.cloned.1.call-done.refs_1_
  454.3 1.5 dynamic-slice_bitcast_fusion.3
  455.8 0.4 collective-permute-start
  456.2 1.3 collective-permute-start.1
  457.5 1.1 collective-permute-start.2
  458.6 4.6 bitcast_convert_fusion
  463.2 1.5 collective-permute-done
  464.7 1.9 fusion.16
  466.7 1.1 fusion.22
  467.7 5.0 collective-permute-done.2
  472.7 1.1 add_convert_fusion
  473.8 2.5 pad_maximum_fusion
  476.3 3.7 reduce-scatter.6.cloned.1.call-done.refs_0_
  480.0 0.3 fusion.2
  480.4 7.0 %fusion.9 = (f32[2048]{0:T(1024)S(1)}, f32[256]{0:T(256)S(1)}, f32[256,2048]{1,0:T(8,128)S(1)}) fusion(f32[256]{0:T(256)S(1)} %get-tuple-element.138, bf16[1,256,2048]{2,1,0:T(8,128)(2,1)S(1)} %copy-done.11, f32[2048]{0:T(1024)S(1)} %bitcast.66, bf16[256,2688]{1,0:T(8,128)(2,1)} %get-tuple-element.95, bf16[2048,2688]{1,0:T(8,128)(2,1)} %bitcast.70), kind=kOutput, calls=%fused_computation.21 | convolution fusion | flops 2822240000 | bytes 15550464 | tf_op jit(solution)/shard_map/dot_general | solution.py:65
  487.5 27.2 %shard_map.302 = (bf16[64,11264]{1,0:T(8,128)(2,1)S(1)}, bf16[64,5632]{1,0:T(8,128)(2,1)S(1)}, f32[8,128]{1,0:T(8,128)S(1)}) custom-call(bf16[256,2816]{1,0:T(8,128)(2,1)S(1)} %copy-done.4, bf16[256,1408]{1,0:T(8,128)(2,1)S(1)} %copy-done.5, f32[8,8,256]{2,1,0:T(8,128)S(1)} %pad.9.refs_2_), custom_call_target="tpu_custom_call" | custom-call | flops 10737418240 | bytes 4194304 | tf_op jit(solution)/shard_map/pallas_call | solution.py:1227
  514.8 0.6 multiply_subtract_fusion.4
  515.4 4.8 fusion.6
  520.2 2.8 multiply_subtract_fusion.1
  523.0 1.5 copy-done.13
  524.5 0.9 copy-done.14
  525.4 5.0 multiply_subtract_fusion
  530.4 5.5 reduce-scatter.8.cloned.1.call-done.refs_0_
  535.9 1.1 copy-done.6
  537.0 9.0 %shard_map.301 = (bf16[64,2560]{1,0:T(8,128)(2,1)S(1)}, bf16[64,2048]{1,0:T(8,128)(2,1)S(1)}) custom-call(bf16[256,1152]{1,0:T(8,128)(2,1)S(1)} %copy-done.6), custom_call_target="tpu_custom_call" | custom-call | flops 10737418240 | bytes 4194304 | tf_op jit(solution)/shard_map/pallas_call | solution.py:1227
  546.0 1.6 multiply_subtract_fusion.2
  547.6 0.3 copy-done.28
  547.9 1.4 multiply_subtract_fusion.3
  (84 shorter events, 0.4 us)
Async XLA Ops:
  7.2 197.0 %all-gather.3.cloned.1.call-start = ((), (), s32[]{:S(2)}) async-start(), calls=%async_computation.3 | async-start | bytes 12976128 | tf_op jit(solution)/shard_map/all_gather | solution.py:1317
  8.0 1.4 copy-start
  9.4 1.1 copy-start.2
  50.8 216.8 %all-gather.5.cloned.1.call-start = ((), (), s32[]{:S(2)}) async-start(), calls=%async_computation.4 | async-start | bytes 6488064 | tf_op jit(solution)/shard_map/all_gather | solution.py:1328
  51.6 402.7 %reduce-scatter.4.cloned.1.call-start = ((), (), s32[]{:S(2)}) async-start(), calls=%async_computation.5 | async-start | bytes 6488064 | tf_op jit(solution)/shard_map/reduce_scatter | solution.py:1269
  51.7 0.6 copy-start.32
  51.7 0.6 copy-start.30
  52.2 0.7 copy-start.24
  52.3 151.9 %copy-start.25 = (f32[256,32]{1,0:T(8,128)}, f32[256,32]{1,0:T(8,128)S(1)}, u32[]{:S(2)}) copy-start(f32[256,32]{1,0:T(8,128)S(1)} %get-tuple-element.136.cosine_rows) | copy-start | bytes 98308
  267.6 212.5 %reduce-scatter.6.cloned.1.call-start = ((), (), s32[]{:S(2)}) async-start(), calls=%async_computation.6 | async-start | bytes 12976128 | tf_op jit(solution)/shard_map/reduce_scatter | solution.py:1269
  331.8 0.7 copy-start.31
  331.9 0.7 copy-start.33
  331.9 2.5 copy-start.7
  331.9 2.7 copy-start.29
  331.9 204.0 %reduce-scatter.8.cloned.1.call-start = ((), (), s32[]{:S(2)}) async-start(), calls=%async_computation.7 | async-start | bytes 5308416 | tf_op jit(solution)/shard_map/reduce_scatter | solution.py:1269
  334.3 1.6 copy-start.10
  336.0 1.2 copy-start.20
  339.2 7.1 %copy-start.21 = (bf16[256,2048]{1,0:T(8,128)(2,1)}, bf16[256,2048]{1,0:T(8,128)(2,1)S(1)}, u32[]{:S(2)}) copy-start(bf16[256,2048]{1,0:T(8,128)(2,1)S(1)} %get-tuple-element.124.branch_ref) | copy-start | bytes 3145732
  454.2 4.4 copy-start.37
  455.8 8.9 %collective-permute-start = (bf16[256,640]{1,0:T(8,128)(2,1)S(1)}, bf16[256,640]{1,0:T(8,128)(2,1)S(1)}, u32[]{:S(2)}, u32[]{:S(2)}) collective-permute-start(bf16[256,640]{1,0:T(8,128)(2,1)S(1)} %get-tuple-element.129), channel_id=1, source_target_pairs={{0,2},{1,3},{2,0},{3,1},{4,6},{5,7},{6,4},{7,5},{8,10},{9,11},{10,... | collective-permute-start | bytes 983048 | tf_op jit(solution)/shard_map/ppermute | solution.py:1244
  456.2 8.4 %collective-permute-start.1 = (bf16[256,640]{1,0:T(8,128)(2,1)S(1)}, bf16[256,640]{1,0:T(8,128)(2,1)S(1)}, u32[]{:S(2)}, u32[]{:S(2)}) collective-permute-start(bf16[256,640]{1,0:T(8,128)(2,1)S(1)} %get-tuple-element.128), channel_id=1, source_target_pairs={{0,1},{1,0},{2,3},{3,2},{4,5},{5,4},{6,7},{7,6},{8,9},{9,8},{10,11... | collective-permute-start | bytes 983048 | tf_op jit(solution)/shard_map/ppermute | solution.py:1244
  457.5 7.2 %copy-start.16 = (bf16[2,256,2048]{2,1,0:T(8,128)(2,1)S(1)}, bf16[2,256,2048]{2,1,0:T(8,128)(2,1)}, u32[]{:S(2)}) copy-start(bf16[2,256,2048]{2,1,0:T(8,128)(2,1)} %get-tuple-element.72.refs_7_) | copy-start | bytes 6291460
  457.5 15.2 %collective-permute-start.2 = (bf16[256,640]{1,0:T(8,128)(2,1)S(1)}, bf16[256,640]{1,0:T(8,128)(2,1)S(1)}, u32[]{:S(2)}, u32[]{:S(2)}) collective-permute-start(bf16[256,640]{1,0:T(8,128)(2,1)S(1)} %get-tuple-element.127), channel_id=1, source_target_pairs={{0,3},{1,2},{2,1},{3,0},{4,7},{5,6},{6,5},{7,4},{8,11},{9,10},{10,... | collective-permute-start | bytes 983048 | tf_op jit(solution)/shard_map/ppermute | solution.py:1244
  464.7 1.9 copy-start.15
  466.7 6.1 %copy-start.19 = (bf16[256,2048]{1,0:T(8,128)(2,1)S(1)}, bf16[256,2048]{1,0:T(8,128)(2,1)}, u32[]{:S(2)}) copy-start(bf16[256,2048]{1,0:T(8,128)(2,1)} %get-tuple-element.90) | copy-start | bytes 3145732
  476.3 3.7 copy-start.11
  480.3 7.1 %copy-start.4 = (bf16[256,2816]{1,0:T(8,128)(2,1)S(1)}, bf16[256,2816]{1,0:T(8,128)(2,1)}, u32[]{:S(2)}) copy-start(bf16[256,2816]{1,0:T(8,128)(2,1)} %reduce-scatter.6.cloned.1.call-done.refs_0_) | copy-start | bytes 4325380
  480.4 7.1 %copy-start.5 = (bf16[256,1408]{1,0:T(8,128)(2,1)S(1)}, bf16[256,1408]{1,0:T(8,128)(2,1)}, u32[]{:S(2)}) copy-start(bf16[256,1408]{1,0:T(8,128)(2,1)} %reduce-scatter.4.cloned.1.call-done.refs_1_) | copy-start | bytes 2162692
  487.5 27.3 %copy-start.34 = (f32[2,64]{1,0:T(2,128)S(1)}, f32[2,64]{1,0:T(2,128)}, u32[]{:S(2)}) copy-start(f32[2,64]{1,0:T(2,128)} %param.23) | copy-start | bytes 1540
  487.5 27.3 %copy-start.35 = (f32[2,64]{1,0:T(2,128)S(1)}, f32[2,64]{1,0:T(2,128)}, u32[]{:S(2)}) copy-start(f32[2,64]{1,0:T(2,128)} %param.33) | copy-start | bytes 1540
  487.5 27.3 %copy-start.36 = (f32[2,64]{1,0:T(2,128)S(1)}, f32[2,64]{1,0:T(2,128)}, u32[]{:S(2)}) copy-start(f32[2,64]{1,0:T(2,128)} %param.28) | copy-start | bytes 1540
  487.5 27.9 %copy-start.9 = (f32[256,2048]{1,0:T(8,128)S(1)}, f32[256,2048]{1,0:T(8,128)}, u32[]{:S(2)}) copy-start(f32[256,2048]{1,0:T(8,128)} %get-tuple-element.125) | copy-start | bytes 6291460
  487.5 27.9 %copy-start.12 = (bf16[3,256,2048]{2,1,0:T(8,128)(2,1)S(1)}, bf16[3,256,2048]{2,1,0:T(8,128)(2,1)}, u32[]{:S(2)}) copy-start(bf16[3,256,2048]{2,1,0:T(8,128)(2,1)} %get-tuple-element.81) | copy-start | bytes 9437188
  515.4 4.8 copy-start.1
  515.4 4.8 copy-start.17
  515.4 4.8 copy-start.18
  520.2 2.8 copy-start.8
  520.2 4.3 copy-start.13
  520.2 5.2 copy-start.14
  530.4 15.6 %copy-start.3 = (f32[64,2560]{1,0:T(8,128)S(1)}, f32[64,2560]{1,0:T(8,128)}, u32[]{:S(2)}) copy-start(f32[64,2560]{1,0:T(8,128)} %in_ref.1) | copy-start | bytes 1966084
  535.9 1.1 copy-start.6
  537.0 9.0 %copy-start.22 = (f32[64,2560]{1,0:T(8,128)S(1)}, f32[64,2560]{1,0:T(8,128)}, u32[]{:S(2)}) copy-start(f32[64,2560]{1,0:T(8,128)} %param.29) | copy-start | bytes 1966084
  537.0 9.0 %copy-start.23 = (f32[64,2560]{1,0:T(8,128)S(1)}, f32[64,2560]{1,0:T(8,128)}, u32[]{:S(2)}) copy-start(f32[64,2560]{1,0:T(8,128)} %param.24) | copy-start | bytes 1966084
  546.0 1.6 copy-start.26
  546.0 1.6 copy-start.27
  546.0 1.9 copy-start.28
Sparse Core Ops, SparseCore 0:
  51.0 145.5 all-gather.2
  198.2 61.2 all-gather.4
  267.7 67.9 reduce-scatter.3
  337.9 142.1 reduce-scatter.5
  482.2 53.6 reduce-scatter.7

commit v8 on v7

--- a/solution.py
+++ b/solution.py
@@ -640,10 +640,6 @@
         final_copy(chip, place).start()
 
     def earlier_chip(chip, _):
-        @pl.when(chip == place - 1)
-        def _():
-            gathers_early()
-
         all_heads(chip, False)
         part_copy(chip, 1 - core).start()
 
@@ -658,6 +654,7 @@
     @pl.when(place > 0)
     def _():
         finish_chip(place - 1)
+        gathers_early()
 
     all_heads(place, True)
 

time: 566 us -> 566 us (level)
  no operation moved by 1% of the time
where the time goes in v8:
time: 566 us; the launch traced here: 556 us
  Pallas kernels  461 us (81%)
  other arithmetic  23.4 us (4%)
  matrix products  22.7 us (4%)
  waiting for transfers between devices  16.5 us (3%)
  between operations  14.6 us (3%)
  local copies, waits for them, and re-layouts  14.2 us (3%)
    pallas_call x1, Pallas kernels, attend_forward(): pl.pallas_call(forward_kernel, in_specs=[VMEM] * 5 + [ANY], out_specs=[VM...  149 us
    pallas_call x1, Pallas kernels, attend_backward(): pl.pallas_call(backward_kernel, in_specs=[VMEM] * 10 + [ANY], out_specs=[...  108 us
    pallas_call x1, Pallas kernels, feed_second(): pl.pallas_call(functools.partial(feed_second_kernel, slices=slices, strip...  64.2 us
    pallas_call x1, Pallas kernels, feed_first(): pl.pallas_call(functools.partial(feed_first_kernel, slices=slices, strip=...  63.3 us
    pallas_call x1, Pallas kernels, share_weights(): pl.pallas_call(share_kernel, in_specs=[VMEM] * 4, out_specs=[VMEM] * 3, o...  40.3 us
    pallas_call x2, Pallas kernels, bring_home(): pl.pallas_call(functools.partial(home_kernel, count=len(sources), results...  36.2 us
    dot_general x2, matrix products, against(): lax.dot_general(left, right, (((1,), (1,)), ((), ())), preferred_element_...  14.1 us
    sub x5, other arithmetic, adam_update(): weight - rate * (first_hat / (jnp.sqrt(second_hat) + adam_epsilon) + deca...  11.4 us
  transfers between devices with their start and end apart: 8, of which 4 were waited for; matrix products, arithmetic and copies ran while one was open for 8% of the time, Pallas kernels for 74%

profile of v8, /device:TPU:9, one launch (start us, length us, event | category | flops | bytes accessed | tf_op | source)
XLA Modules:
  0.0 556.1 jit_solution(14382895772021714463)
XLA Ops:
  7.2 0.0 all-gather.3.cloned.1.call-start
  7.2 0.7 convert_element_type.75
  7.9 0.1 copy.50
  8.1 1.4 copy-done
  9.4 1.1 copy-done.2
  10.5 40.3 %shard_map.296 = (bf16[256,2816]{1,0:T(8,128)(2,1)}, bf16[256,1408]{1,0:T(8,128)(2,1)}, bf16[4,2,64,2688]{3,2,1,0:T(8,128)(2,1)}) custom-call(f32[64,2560]{1,0:T(8,128)S(1)} %copy-done.2, bf16[64,128]{1,0:T(8,128)(2,1)S(1)} %pad.8.gain_ref, f32[64,11264]{1,0:T(8,128)} %gate_up_ref.1, f32[64,5632]{1,0:T(8,128)S(1)} %copy-done), custom_call_target="tpu_custom_call" | custom-call | tf_op jit(solution)/shard_map/pallas_call | solution.py:180
  50.8 0.0 all-gather.3.cloned.1.call-update
  50.8 0.0 all-gather.5.cloned.1.call-start
  50.9 0.7 all-gather.5.cloned.1.call-update
  51.6 0.0 reduce-scatter.4.cloned.1.call-start
  51.7 0.5 fusion.25
  52.3 0.6 copy-done.24
  52.9 0.1 pad_maximum_fusion.1
  53.0 0.1 copy.53
  53.1 0.8 copy.55.sine_ref
  53.9 0.1 copy.52
  54.0 0.8 copy.54.cosine_ref
  54.7 149.4 %shard_map.297 = (bf16[4,2,4,64,2688]{4,3,2,1,0:T(8,128)(2,1)}, bf16[256,2048]{1,0:T(8,128)(2,1)}, bf16[256,2048]{1,0:T(8,128)(2,1)}, f32[2,2048]{1,0:T(2,128)},...) custom-call(bf16[4,2,64,2688]{3,2,1,0:T(8,128)(2,1)} %get-tuple-elem, ...), custom_call_target="tpu_custom_call" | custom-call | flops 171798691840 | bytes 20971520 | tf_op jit(solution)/shard_map/pallas_call | solution.py:741
  204.2 0.0 all-gather.3.cloned.1.call-done.refs_2_.refs_5_
  204.2 63.3 %shard_map.298 = (bf16[4,256,2048]{2,1,0:T(8,128)(2,1)}, bf16[1024,1408]{1,0:T(8,128)(2,1)}, bf16[1024,1408]{1,0:T(8,128)(2,1)}, bf16[1024,1408]{1,0:T(8,128)(2,...) custom-call(bf16[4,256,2048]{2,1,0:T(8,128)(2,1)} %get-tuple-element.63.refs_0_, ...), custom_call_target="tpu_custom_call" | custom-call | flops 29527900160 | bytes 31457280 | tf_op jit(solution)/shard_map/pallas_call | solution.py:1061
  267.5 0.0 reduce-scatter.4.cloned.1.call-update
  267.6 0.0 reduce-scatter.6.cloned.1.call-start
  267.6 0.0 all-gather.5.cloned.1.call-done.refs_6_
  267.6 64.2 %shard_map.299 = (f32[256,2048]{1,0:T(8,128)}, bf16[4,256,2048]{2,1,0:T(8,128)(2,1)}, bf16[2048,2816]{1,0:T(8,128)(2,1)}, bf16[256,2048]{1,0:T(8,128)(2,1)}) custom-call(bf16[4,256,2048]{2,1,0:T(8,128)(2,1)} %get-tuple-element.63.refs_0_, bf16[4,256,2048]{2,1,0:T(8,128)(2,1)} %get-tuple-element.67.refs_1_, bf16[1024,1408]{1,0:T(8,128)(2,1)} %get-tuple-element.68.refs_2_, ...), custom_call_target="tpu_custom_call" | custom-call | flops 59055800320 | bytes 41943040 | tf_op jit(solution)/shard_map/pallas_call | solution.py:1104
  331.9 0.3 reduce-scatter.8.cloned.1.call-start
  332.2 0.3 copy-done.31
  332.5 0.2 multiply_sine_fusion.1
  332.8 0.8 copy.67
  333.6 0.8 copy.68
  334.4 0.2 multiply_reduce_fusion.2
  334.6 1.3 copy-done.10
  336.0 0.6 multiply_reduce_fusion
  336.6 0.6 copy-done.20
  337.2 2.0 fusion.37
  339.2 7.1 %convolution_convert_fusion.grad_ref = bf16[256,2048]{1,0:T(8,128)(2,1)} fusion(bf16[256,2048]{1,0:T(8,128)(2,1)S(1)} %get-tuple-element.124.branch_ref, bf16[2048,2048]{1,0:T(8,128)(2,1)} %bitcast.71), kind=kOutput, calls=%fused_computation.12 | convolution fusion | flops 2148007936 | bytes 10485760 | tf_op jit(solution)/shard_map/dot_general | solution.py:65
  346.3 108.0 %shard_map.300 = (bf16[256,2688]{1,0:T(8,128)(2,1)}, bf16[4,256,640]{2,1,0:T(8,128)(2,1)}, bf16[4,256,2048]{2,1,0:T(8,128)(2,1)}, bf16[4,256,512]{2,1,0:T(8,128)(2,1)}, bf16[3,256,2048]{2,1,0:T(8,128)(2,1)}) custom-call(bf16[256,2048]{1,0:T(8,128)(2,1)} %convolution_convert_fusion.grad_ref, bf16[256,2048]{1,0:T(8,128)(2,1)} %get-tuple-element.77.query_ref, ...), custom_call_target="tpu_custom_call" | custom-call | flops 85899345920 | bytes 20971520 | tf_op jit(solution)/shard_map/pallas_call | solution.py:798
  454.3 0.0 reduce-scatter.4.cloned.1.call-done.refs_1_
  454.3 1.5 dynamic-slice_bitcast_fusion.3
  455.8 0.4 collective-permute-start
  456.2 1.3 collective-permute-start.1
  457.5 1.1 collective-permute-start.2
  458.6 4.6 bitcast_convert_fusion
  463.2 1.5 collective-permute-done
  464.7 1.9 fusion.16
  466.7 1.1 fusion.22
  467.7 5.0 collective-permute-done.2
  472.7 1.1 add_convert_fusion
  473.8 2.5 pad_maximum_fusion
  476.3 3.7 reduce-scatter.6.cloned.1.call-done.refs_0_
  480.0 0.3 fusion.2
  480.4 7.0 %fusion.9 = (f32[2048]{0:T(1024)S(1)}, f32[256]{0:T(256)S(1)}, f32[256,2048]{1,0:T(8,128)S(1)}) fusion(f32[256]{0:T(256)S(1)} %get-tuple-element.138, bf16[1,256,2048]{2,1,0:T(8,128)(2,1)S(1)} %copy-done.11, f32[2048]{0:T(1024)S(1)} %bitcast.66, bf16[256,2688]{1,0:T(8,128)(2,1)} %get-tuple-element.95, bf16[2048,2688]{1,0:T(8,128)(2,1)} %bitcast.70), kind=kOutput, calls=%fused_computation.21 | convolution fusion | flops 2822240000 | bytes 15550464 | tf_op jit(solution)/shard_map/dot_general | solution.py:65
  487.5 27.2 %shard_map.302 = (bf16[64,11264]{1,0:T(8,128)(2,1)S(1)}, bf16[64,5632]{1,0:T(8,128)(2,1)S(1)}, f32[8,128]{1,0:T(8,128)S(1)}) custom-call(bf16[256,2816]{1,0:T(8,128)(2,1)S(1)} %copy-done.4, bf16[256,1408]{1,0:T(8,128)(2,1)S(1)} %copy-done.5, f32[8,8,256]{2,1,0:T(8,128)S(1)} %pad.9.refs_2_), custom_call_target="tpu_custom_call" | custom-call | flops 10737418240 | bytes 4194304 | tf_op jit(solution)/shard_map/pallas_call | solution.py:1224
  514.8 0.6 multiply_subtract_fusion.4
  515.4 4.8 fusion.6
  520.2 2.8 multiply_subtract_fusion.1
  523.0 1.5 copy-done.13
  524.5 0.9 copy-done.14
  525.4 5.0 multiply_subtract_fusion
  530.4 5.5 reduce-scatter.8.cloned.1.call-done.refs_0_
  535.9 1.1 copy-done.6
  537.0 9.0 %shard_map.301 = (bf16[64,2560]{1,0:T(8,128)(2,1)S(1)}, bf16[64,2048]{1,0:T(8,128)(2,1)S(1)}) custom-call(bf16[256,1152]{1,0:T(8,128)(2,1)S(1)} %copy-done.6), custom_call_target="tpu_custom_call" | custom-call | flops 10737418240 | bytes 4194304 | tf_op jit(solution)/shard_map/pallas_call | solution.py:1224
  546.0 1.6 multiply_subtract_fusion.2
  547.6 0.3 copy-done.28
  547.9 1.4 multiply_subtract_fusion.3
  (84 shorter events, 0.4 us)
Async XLA Ops:
  7.2 197.0 %all-gather.3.cloned.1.call-start = ((), (), s32[]{:S(2)}) async-start(), calls=%async_computation.3 | async-start | bytes 12976128 | tf_op jit(solution)/shard_map/all_gather | solution.py:1314
  8.0 1.4 copy-start
  9.4 1.1 copy-start.2
  50.8 216.8 %all-gather.5.cloned.1.call-start = ((), (), s32[]{:S(2)}) async-start(), calls=%async_computation.4 | async-start | bytes 6488064 | tf_op jit(solution)/shard_map/all_gather | solution.py:1325
  51.6 402.7 %reduce-scatter.4.cloned.1.call-start = ((), (), s32[]{:S(2)}) async-start(), calls=%async_computation.5 | async-start | bytes 6488064 | tf_op jit(solution)/shard_map/reduce_scatter | solution.py:1266
  51.7 0.6 copy-start.32
  51.7 0.6 copy-start.30
  52.2 0.7 copy-start.24
  52.3 151.9 %copy-start.25 = (f32[256,32]{1,0:T(8,128)}, f32[256,32]{1,0:T(8,128)S(1)}, u32[]{:S(2)}) copy-start(f32[256,32]{1,0:T(8,128)S(1)} %get-tuple-element.136.cosine_rows) | copy-start | bytes 98308
  267.6 212.5 %reduce-scatter.6.cloned.1.call-start = ((), (), s32[]{:S(2)}) async-start(), calls=%async_computation.6 | async-start | bytes 12976128 | tf_op jit(solution)/shard_map/reduce_scatter | solution.py:1266
  331.8 0.7 copy-start.31
  331.9 0.7 copy-start.33
  331.9 2.5 copy-start.7
  331.9 2.7 copy-start.29
  331.9 204.0 %reduce-scatter.8.cloned.1.call-start = ((), (), s32[]{:S(2)}) async-start(), calls=%async_computation.7 | async-start | bytes 5308416 | tf_op jit(solution)/shard_map/reduce_scatter | solution.py:1266
  334.3 1.6 copy-start.10
  336.0 1.2 copy-start.20
  339.2 7.1 %copy-start.21 = (bf16[256,2048]{1,0:T(8,128)(2,1)}, bf16[256,2048]{1,0:T(8,128)(2,1)S(1)}, u32[]{:S(2)}) copy-start(bf16[256,2048]{1,0:T(8,128)(2,1)S(1)} %get-tuple-element.124.branch_ref) | copy-start | bytes 3145732
  454.2 4.4 copy-start.37
  455.8 8.9 %collective-permute-start = (bf16[256,640]{1,0:T(8,128)(2,1)S(1)}, bf16[256,640]{1,0:T(8,128)(2,1)S(1)}, u32[]{:S(2)}, u32[]{:S(2)}) collective-permute-start(bf16[256,640]{1,0:T(8,128)(2,1)S(1)} %get-tuple-element.129), channel_id=1, source_target_pairs={{0,2},{1,3},{2,0},{3,1},{4,6},{5,7},{6,4},{7,5},{8,10},{9,11},{10,... | collective-permute-start | bytes 983048 | tf_op jit(solution)/shard_map/ppermute | solution.py:1241
  456.2 8.4 %collective-permute-start.1 = (bf16[256,640]{1,0:T(8,128)(2,1)S(1)}, bf16[256,640]{1,0:T(8,128)(2,1)S(1)}, u32[]{:S(2)}, u32[]{:S(2)}) collective-permute-start(bf16[256,640]{1,0:T(8,128)(2,1)S(1)} %get-tuple-element.128), channel_id=1, source_target_pairs={{0,1},{1,0},{2,3},{3,2},{4,5},{5,4},{6,7},{7,6},{8,9},{9,8},{10,11... | collective-permute-start | bytes 983048 | tf_op jit(solution)/shard_map/ppermute | solution.py:1241
  457.5 7.2 %copy-start.16 = (bf16[2,256,2048]{2,1,0:T(8,128)(2,1)S(1)}, bf16[2,256,2048]{2,1,0:T(8,128)(2,1)}, u32[]{:S(2)}) copy-start(bf16[2,256,2048]{2,1,0:T(8,128)(2,1)} %get-tuple-element.72.refs_7_) | copy-start | bytes 6291460
  457.5 15.2 %collective-permute-start.2 = (bf16[256,640]{1,0:T(8,128)(2,1)S(1)}, bf16[256,640]{1,0:T(8,128)(2,1)S(1)}, u32[]{:S(2)}, u32[]{:S(2)}) collective-permute-start(bf16[256,640]{1,0:T(8,128)(2,1)S(1)} %get-tuple-element.127), channel_id=1, source_target_pairs={{0,3},{1,2},{2,1},{3,0},{4,7},{5,6},{6,5},{7,4},{8,11},{9,10},{10,... | collective-permute-start | bytes 983048 | tf_op jit(solution)/shard_map/ppermute | solution.py:1241
  464.7 1.9 copy-start.15
  466.7 6.1 %copy-start.19 = (bf16[256,2048]{1,0:T(8,128)(2,1)S(1)}, bf16[256,2048]{1,0:T(8,128)(2,1)}, u32[]{:S(2)}) copy-start(bf16[256,2048]{1,0:T(8,128)(2,1)} %get-tuple-element.90) | copy-start | bytes 3145732
  476.3 3.7 copy-start.11
  480.3 7.1 %copy-start.4 = (bf16[256,2816]{1,0:T(8,128)(2,1)S(1)}, bf16[256,2816]{1,0:T(8,128)(2,1)}, u32[]{:S(2)}) copy-start(bf16[256,2816]{1,0:T(8,128)(2,1)} %reduce-scatter.6.cloned.1.call-done.refs_0_) | copy-start | bytes 4325380
  480.4 7.1 %copy-start.5 = (bf16[256,1408]{1,0:T(8,128)(2,1)S(1)}, bf16[256,1408]{1,0:T(8,128)(2,1)}, u32[]{:S(2)}) copy-start(bf16[256,1408]{1,0:T(8,128)(2,1)} %reduce-scatter.4.cloned.1.call-done.refs_1_) | copy-start | bytes 2162692
  487.5 27.3 %copy-start.34 = (f32[2,64]{1,0:T(2,128)S(1)}, f32[2,64]{1,0:T(2,128)}, u32[]{:S(2)}) copy-start(f32[2,64]{1,0:T(2,128)} %param.23) | copy-start | bytes 1540
  487.5 27.3 %copy-start.35 = (f32[2,64]{1,0:T(2,128)S(1)}, f32[2,64]{1,0:T(2,128)}, u32[]{:S(2)}) copy-start(f32[2,64]{1,0:T(2,128)} %param.33) | copy-start | bytes 1540
  487.5 27.3 %copy-start.36 = (f32[2,64]{1,0:T(2,128)S(1)}, f32[2,64]{1,0:T(2,128)}, u32[]{:S(2)}) copy-start(f32[2,64]{1,0:T(2,128)} %param.28) | copy-start | bytes 1540
  487.5 27.9 %copy-start.9 = (f32[256,2048]{1,0:T(8,128)S(1)}, f32[256,2048]{1,0:T(8,128)}, u32[]{:S(2)}) copy-start(f32[256,2048]{1,0:T(8,128)} %get-tuple-element.125) | copy-start | bytes 6291460
  487.5 27.9 %copy-start.12 = (bf16[3,256,2048]{2,1,0:T(8,128)(2,1)S(1)}, bf16[3,256,2048]{2,1,0:T(8,128)(2,1)}, u32[]{:S(2)}) copy-start(bf16[3,256,2048]{2,1,0:T(8,128)(2,1)} %get-tuple-element.81) | copy-start | bytes 9437188
  515.4 4.8 copy-start.1
  515.4 4.8 copy-start.17
  515.4 4.8 copy-start.18
  520.2 2.8 copy-start.8
  520.2 4.3 copy-start.13
  520.2 5.2 copy-start.14
  530.4 15.6 %copy-start.3 = (f32[64,2560]{1,0:T(8,128)S(1)}, f32[64,2560]{1,0:T(8,128)}, u32[]{:S(2)}) copy-start(f32[64,2560]{1,0:T(8,128)} %in_ref.1) | copy-start | bytes 1966084
  535.9 1.1 copy-start.6
  537.0 9.0 %copy-start.22 = (f32[64,2560]{1,0:T(8,128)S(1)}, f32[64,2560]{1,0:T(8,128)}, u32[]{:S(2)}) copy-start(f32[64,2560]{1,0:T(8,128)} %param.29) | copy-start | bytes 1966084
  537.0 9.0 %copy-start.23 = (f32[64,2560]{1,0:T(8,128)S(1)}, f32[64,2560]{1,0:T(8,128)}, u32[]{:S(2)}) copy-start(f32[64,2560]{1,0:T(8,128)} %param.24) | copy-start | bytes 1966084
  546.0 1.6 copy-start.26
  546.0 1.6 copy-start.27
  546.0 1.9 copy-start.28
Sparse Core Ops, SparseCore 0:
  51.0 145.5 all-gather.2
  198.2 61.2 all-gather.4
  267.7 67.9 reduce-scatter.3
  337.9 142.1 reduce-scatter.5
  482.2 53.6 reduce-scatter.7
